TPU v7x, 32 devices: a whole 2x2x4 slice. The times are simulated.
32 devices in a mesh: tok: 8 (over y, x, core), mlp: 4 (over z).
Axes of the slice: x: 2, y: 2, z: 4, core: 2. Of those that a mesh axis runs over, the one named last changes fastest.
Arguments:
- tokens: bfloat16 [8192, 2048], P('tok'), may hold values from -6 to 6
- segment_ids: int32 [8192], P('tok'), may hold values from 0 to 1, as said below
- owner_table: int32 [8], replicated, may hold values from 0 to 7, each once
- cotangent: bfloat16 [8192, 2048], P('tok'), may hold values from -6 to 6
- w_in_rec: float32 [2, 2048, 2816], P(None, 'tok', 'mlp'), may hold values from -0.125 to 0.125
- m_in_rec: float32 [2, 2048, 2816], P(None, 'tok', 'mlp'), may hold values from -32 to 32
- v_in_rec: float32 [2, 2048, 2816], P(None, 'tok', 'mlp'), may hold values from 2.048 to 8.192
- q_in_rec: float32 [2, 32, 44, 2, 64, 64], P(None, 'tok', 'mlp'), may hold values from -1 to 1, as said below
- w_out_rec: float32 [2816, 2048], P('mlp', 'tok'), may hold values from -0.375 to 0.375
- m_out_rec: float32 [2816, 2048], P('mlp', 'tok'), may hold values from -32 to 32
- v_out_rec: float32 [2816, 2048], P('mlp', 'tok'), may hold values from 2.048 to 8.192
- q_out_rec: float32 [44, 32, 2, 64, 64], P('mlp', 'tok'), may hold values from -1 to 1, as said below
- w_in_mlp: float32 [2, 2048, 6144], P(None, 'tok', 'mlp'), may hold values from -0.125 to 0.125
- m_in_mlp: float32 [2, 2048, 6144], P(None, 'tok', 'mlp'), may hold values from -32 to 32
- v_in_mlp: float32 [2, 2048, 6144], P(None, 'tok', 'mlp'), may hold values from 2.048 to 8.192
- q_in_mlp: float32 [2, 32, 96, 2, 64, 64], P(None, 'tok', 'mlp'), may hold values from -1 to 1, as said below
- w_out_mlp: float32 [6144, 2048], P('mlp', 'tok'), may hold values from -0.109375 to 0.109375
- m_out_mlp: float32 [6144, 2048], P('mlp', 'tok'), may hold values from -32 to 32
- v_out_mlp: float32 [6144, 2048], P('mlp', 'tok'), may hold values from 2.048 to 8.192
- q_out_mlp: float32 [96, 32, 2, 64, 64], P('mlp', 'tok'), may hold values from -1 to 1, as said below
- w_gates: float32 [2, 16, 30976], P(None, 'mlp', 'tok'), may hold values from -0.4375 to 0.4375
- m_gates: float32 [2, 16, 30976], P(None, 'mlp', 'tok'), may hold values from -32 to 32
- v_gates: float32 [2, 16, 30976], P(None, 'mlp', 'tok'), may hold values from 2.048 to 8.192
- w_rnn: float32 [8, 2816], P(None, ('mlp', 'tok')), may hold values from -13 to 3
- m_rnn: float32 [8, 2816], P(None, ('mlp', 'tok')), may hold values from -768 to 768
- v_rnn: float32 [8, 2816], P(None, ('mlp', 'tok')), may hold values from 2048 to 8192
- w_gains: float32 [2, 2048], P(None, 'tok'), may hold values from 0.5 to 1.5
- m_gains: float32 [2, 2048], P(None, 'tok'), may hold values from -768 to 768
- v_gains: float32 [2, 2048], P(None, 'tok'), may hold values from 573.44 to 2293.76
Outputs:
- block_out: bfloat16 [8192, 2048], P('tok')
- grad_tokens: float32 [8192, 2048], P('tok')
- new_m_in_rec: float32 [2, 2048, 2816], P(None, 'tok', 'mlp')
- new_v_in_rec: float32 [2, 2048, 2816], P(None, 'tok', 'mlp')
- new_w_in_rec: float32 [2, 2048, 2816], P(None, 'tok', 'mlp')
- new_m_out_rec: float32 [2816, 2048], P('mlp', 'tok')
- new_v_out_rec: float32 [2816, 2048], P('mlp', 'tok')
- new_w_out_rec: float32 [2816, 2048], P('mlp', 'tok')
- new_m_in_mlp: float32 [2, 2048, 6144], P(None, 'tok', 'mlp')
- new_v_in_mlp: float32 [2, 2048, 6144], P(None, 'tok', 'mlp')
- new_w_in_mlp: float32 [2, 2048, 6144], P(None, 'tok', 'mlp')
- new_m_out_mlp: float32 [6144, 2048], P('mlp', 'tok')
- new_v_out_mlp: float32 [6144, 2048], P('mlp', 'tok')
- new_w_out_mlp: float32 [6144, 2048], P('mlp', 'tok')
- new_m_gates: float32 [2, 16, 30976], P(None, 'mlp', 'tok')
- new_v_gates: float32 [2, 16, 30976], P(None, 'mlp', 'tok')
- new_w_gates: float32 [2, 16, 30976], P(None, 'mlp', 'tok')
- new_m_rnn: float32 [8, 2816], P(None, ('mlp', 'tok'))
- new_v_rnn: float32 [8, 2816], P(None, ('mlp', 'tok'))
- new_m_gains: float32 [2, 2048], P(None, 'tok')
- new_v_gains: float32 [2, 2048], P(None, 'tok')
Inputs may be any that keep to these rules, and one draw needn't show every extreme that they name: `owner_table`: a permutation of the indices of tok. `segment_ids`: never falls, starts at 0 and rises by one at each new document; no document starts at a multiple of 1024 other than token 0. `q_in_rec`: every 64 x 64 matrix q[..., 0, :, :] and q[..., 1, :, :] is orthogonal. `q_out_rec`: every 64 x 64 matrix q[..., 0, :, :] and q[..., 1, :, :] is orthogonal. `q_in_mlp`: every 64 x 64 matrix q[..., 0, :, :] and q[..., 1, :, :] is orthogonal. `q_out_mlp`: every 64 x 64 matrix q[..., 0, :, :] and q[..., 1, :, :] is orthogonal.
All inputs are finite; a program needn't handle non-finite values.
Results may differ from a plain program's by a relative error of at most 0.01.
The roundings to bfloat16 on the way count: a program that leaves them out, or rounds other values in their place, can miss the bound.
Values may be sent and summed in bfloat16 or wider, within the bound.
No kernel may reach another device: no remote copies, remote signals or barrier semaphores. Data moves between devices by JAX's collectives and lax.ppermute only.
A program may use at most 384 MiB of HBM per device.

v0:
```python
import math

import jax
import jax.numpy as jnp
from jax import lax
from jax.sharding import PartitionSpec as P

BW = 176
CONV = 4
TILE = 64
STEP = 7


norm_eps = 1e-06
learn_rate = 0.02
beta_first = 0.9
beta_second = 0.999
adam_eps = 1e-08
decay_rate = 0.1
highest = lax.Precision.HIGHEST


def passed_along(array, axis, by):
    count = lax.axis_size(axis)
    pairs = [(i, i + by) for i in range(count) if 0 <= i + by < count]
    return lax.ppermute(array, axis, pairs)


def gelu_tanh(value):
    return (
        0.5
        * value
        * (1.0 + jnp.tanh(0.7978845608028654 * (value + 0.044715 * value * value * value)))
    )


def rms_norm(value, gain):
    return value * lax.rsqrt(jnp.mean(value * value, axis=-1, keepdims=True) + norm_eps) * gain


def gated_hidden(gate_in, up_in):
    return gelu_tanh(gate_in) * up_in


def link_pairs(earlier, later):
    return (earlier[0] * later[0], later[0] * earlier[1] + later[1])


def linear_blocks(decay, drive, backward):
    total_rows, width_cols = decay.shape
    span_rows = math.gcd(total_rows, 128)
    block_count = total_rows // span_rows

    def spread(array):
        return (
            array.reshape(block_count, span_rows, width_cols)
            .transpose(1, 0, 2)
            .reshape(span_rows, block_count * width_cols)
        )

    def step_once(carry, inputs):
        state_now = inputs[0] * carry[0] + inputs[1]
        prod_now = inputs[0] * carry[1]
        return ((state_now, prod_now), (state_now, prod_now))

    start_pair = (
        jnp.zeros((block_count * width_cols,), jnp.float32),
        jnp.ones((block_count * width_cols,), jnp.float32),
    )
    _, (state_loc, prod_loc) = lax.scan(
        step_once, start_pair, (spread(decay), spread(drive)), reverse=backward, unroll=8
    )
    edge_row = 0 if backward else span_rows - 1
    ends_state = state_loc[edge_row].reshape(block_count, width_cols)
    ends_prod = prod_loc[edge_row].reshape(block_count, width_cols)
    _, through = lax.associative_scan(link_pairs, (ends_prod, ends_state), reverse=backward, axis=0)
    zero_row = jnp.zeros((1, width_cols), jnp.float32)
    if backward:
        incoming = jnp.concatenate([through[1:], zero_row])
    else:
        incoming = jnp.concatenate([zero_row, through[:-1]])
    state_all = state_loc + prod_loc * incoming.reshape(1, block_count * width_cols)
    return (
        state_all.reshape(span_rows, block_count, width_cols)
        .transpose(1, 0, 2)
        .reshape(total_rows, width_cols)
    )


def matmul_plain(left, right):
    return jnp.dot(left, right, preferred_element_type=jnp.float32)


def matmul_left_t(left, right):
    return lax.dot_general(
        left, right, (((0,), (0,)), ((), ())), preferred_element_type=jnp.float32
    )


def matmul_right_t(left, right):
    return lax.dot_general(
        left, right, (((1,), (1,)), ((), ())), preferred_element_type=jnp.float32
    )


def reorder(array, dim, order):
    shape = array.shape
    parts = order.shape[0]
    reshaped = array.reshape(shape[:dim] + (parts, shape[dim] // parts) + shape[dim + 1 :])
    return jnp.take(reshaped, order, axis=dim).reshape(shape)


def to_tiles(array):
    leading = array.shape[:-2]
    row_count = array.shape[-2]
    col_count = array.shape[-1]
    reshaped = array.reshape(leading + (row_count // TILE, TILE, col_count // TILE, TILE))
    return jnp.swapaxes(reshaped, -3, -2)


def from_tiles(array):
    leading = array.shape[:-4]
    joined = jnp.swapaxes(array, -3, -2)
    return joined.reshape(leading + (array.shape[-4] * TILE, array.shape[-3] * TILE))


def soap_update(master, first, second, gradient, bases):
    left_basis = bases[..., 0, :, :]
    right_basis = bases[..., 1, :, :]
    rotated = jnp.einsum(
        "...ki,...kl,...lj->...ij", left_basis, to_tiles(gradient), right_basis, precision=highest
    )
    new_first = beta_first * to_tiles(first) + (1.0 - beta_first) * rotated
    new_second = beta_second * to_tiles(second) + (1.0 - beta_second) * rotated * rotated
    normalized = (
        new_first
        / (1.0 - beta_first**STEP)
        / (jnp.sqrt(new_second / (1.0 - beta_second**STEP)) + adam_eps)
    )
    turned = jnp.einsum(
        "...ik,...kl,...jl->...ij", left_basis, normalized, right_basis, precision=highest
    )
    new_master = master - learn_rate * (from_tiles(turned) + decay_rate * master)
    return (from_tiles(new_first), from_tiles(new_second), new_master)


def adam_update(master, first, second, gradient, decay):
    new_first = beta_first * first + (1.0 - beta_first) * gradient
    new_second = beta_second * second + (1.0 - beta_second) * gradient * gradient
    normalized = (
        new_first
        / (1.0 - beta_first**STEP)
        / (jnp.sqrt(new_second / (1.0 - beta_second**STEP)) + adam_eps)
    )
    return (new_first, new_second, master - learn_rate * (normalized + decay * master))


def moment_update(first, second, gradient):
    new_first = beta_first * first + (1.0 - beta_first) * gradient
    new_second = beta_second * second + (1.0 - beta_second) * gradient * gradient
    return (new_first, new_second)


def reduce_branch(branch_part):
    return lax.psum(branch_part, "mlp")


def reduce_input(input_part):
    return lax.psum(input_part, "mlp")


def on_device(
    tokens,
    segment_ids,
    owner_table,
    cotangent,
    w_in_rec,
    m_in_rec,
    v_in_rec,
    q_in_rec,
    w_out_rec,
    m_out_rec,
    v_out_rec,
    q_out_rec,
    w_in_mlp,
    m_in_mlp,
    v_in_mlp,
    q_in_mlp,
    w_out_mlp,
    m_out_mlp,
    v_out_mlp,
    q_out_mlp,
    w_gates,
    m_gates,
    v_gates,
    w_rnn,
    m_rnn,
    v_rnn,
    w_gains,
    m_gains,
    v_gains,
):
    parts = lax.axis_size("tok")
    rank = lax.axis_index("tok")
    count = tokens.shape[0]
    length = count * parts
    lag = CONV - 1
    gathered = (
        lax.all_gather(w_in_rec.astype(jnp.bfloat16), "tok", axis=1, tiled=True),
        lax.all_gather(w_out_rec.astype(jnp.bfloat16), "tok", axis=1, tiled=True),
        lax.all_gather(w_in_mlp.astype(jnp.bfloat16), "tok", axis=1, tiled=True),
        lax.all_gather(w_out_mlp.astype(jnp.bfloat16), "tok", axis=1, tiled=True),
        lax.all_gather(w_gates.astype(jnp.bfloat16), "tok", axis=2, tiled=True),
        lax.all_gather(w_rnn.astype(jnp.bfloat16), "tok", axis=1, tiled=True),
        lax.all_gather(w_gains.astype(jnp.bfloat16), "tok", axis=1, tiled=True),
    )
    in_rec = reorder(gathered[0], 1, owner_table)
    out_rec = reorder(gathered[1], 1, owner_table)
    in_mlp = reorder(gathered[2], 1, owner_table)
    out_mlp = reorder(gathered[3], 1, owner_table)
    gate_flat = reorder(gathered[4], 2, owner_table)
    rnn_f = reorder(gathered[5], 1, owner_table).astype(jnp.float32)
    gains_f = reorder(gathered[6], 1, owner_table).astype(jnp.float32)
    channels = out_rec.shape[0]
    blocks = gate_flat.shape[1]
    gate_mats = gate_flat.reshape(2, blocks, BW, BW)
    x_float = tokens.astype(jnp.float32)
    normed_one, norm_one_back = jax.vjp(rms_norm, x_float, gains_f[0])
    xn_one = normed_one.astype(jnp.bfloat16)
    y_pre = matmul_plain(xn_one, in_rec[0])
    u_low = matmul_plain(xn_one, in_rec[1]).astype(jnp.bfloat16)
    rim_values, rim_ids = passed_along(
        (u_low[count - lag :].astype(jnp.float32), segment_ids[count - lag :].astype(jnp.float32)),
        "tok",
        1,
    )
    position = rank * count - lag + jnp.arange(count + lag, dtype=jnp.int32)
    ids_ext = jnp.concatenate([rim_ids, segment_ids.astype(jnp.float32)])
    starts = (position % length == 0) | (ids_ext != jnp.concatenate([ids_ext[:1], ids_ext[:-1]]))
    live_ext = jnp.where(starts, 0.0, 1.0).astype(jnp.float32)
    live = live_ext[lag:]
    reset = 1.0 - live
    u_ext = jnp.concatenate([rim_values, u_low.astype(jnp.float32)])
    conv_val = rnn_f[CONV] + rnn_f[0] * u_ext[lag:]
    valid_rows = []
    valid = jnp.ones((count,), jnp.float32)
    for offset in range(1, CONV):
        valid = valid * live_ext[lag - offset + 1 : lag - offset + 1 + count]
        valid_rows.append(valid)
        conv_val = (
            conv_val + rnn_f[offset] * valid[:, None] * u_ext[lag - offset : lag - offset + count]
        )
    conv_low = conv_val.astype(jnp.bfloat16)
    blocked = conv_low.reshape(count, blocks, BW)
    pre_decay = (
        jnp.einsum(
            "tnb,nbc->tnc", blocked, gate_mats[0], preferred_element_type=jnp.float32
        ).reshape(count, channels)
        + rnn_f[CONV + 2]
    )
    pre_input = (
        jnp.einsum(
            "tnb,nbc->tnc", blocked, gate_mats[1], preferred_element_type=jnp.float32
        ).reshape(count, channels)
        + rnn_f[CONV + 3]
    )

    def gate_math(decay_in, input_in, conv_in, lam_in):
        rate_gate = jax.nn.sigmoid(decay_in)
        input_gate = jax.nn.sigmoid(input_in)
        log_decay = -8.0 * jax.nn.softplus(lam_in) * rate_gate
        scale = reset[:, None] + live[:, None] * jnp.sqrt(-jnp.expm1(2.0 * log_decay))
        return (jnp.exp(log_decay) * live[:, None], input_gate * conv_in * scale)

    (decay_eff, drive), gate_back = jax.vjp(
        gate_math, pre_decay, pre_input, conv_low.astype(jnp.float32), rnn_f[CONV + 1]
    )
    decay_ch, drive_ch = (
        lax.all_to_all(decay_eff, "tok", split_axis=1, concat_axis=0, tiled=True),
        lax.all_to_all(drive, "tok", split_axis=1, concat_axis=0, tiled=True),
    )
    state_ch = linear_blocks(decay_ch, drive_ch, False)
    state = lax.all_to_all(state_ch, "tok", split_axis=0, concat_axis=1, tiled=True)
    gelu_y, gelu_back = jax.vjp(gelu_tanh, y_pre)
    mixed = (state * gelu_y).astype(jnp.bfloat16)
    second = x_float + reduce_branch(matmul_plain(mixed, out_rec))
    normed_two, norm_two_back = jax.vjp(rms_norm, second, gains_f[1])
    xn_two = normed_two.astype(jnp.bfloat16)
    z_gate = matmul_plain(xn_two, in_mlp[0])
    z_up = matmul_plain(xn_two, in_mlp[1])
    hidden_f, hidden_back = jax.vjp(gated_hidden, z_gate, z_up)
    hidden = hidden_f.astype(jnp.bfloat16)
    result = (second + reduce_branch(matmul_plain(hidden, out_mlp))).astype(jnp.bfloat16)
    inverse = jnp.sum(
        jnp.where(
            owner_table[None, :] == jnp.arange(parts, dtype=jnp.int32)[:, None],
            jnp.arange(parts, dtype=jnp.int32)[None, :],
            0,
        ),
        axis=1,
    )
    d_hidden = matmul_right_t(cotangent, out_mlp)
    g_out_mlp = matmul_left_t(hidden, cotangent)
    d_gate, d_up = hidden_back(d_hidden)
    d_gate_low = d_gate.astype(jnp.bfloat16)
    d_up_low = d_up.astype(jnp.bfloat16)
    g_in_mlp = jnp.stack([matmul_left_t(xn_two, d_gate_low), matmul_left_t(xn_two, d_up_low)])
    partial_xn_two = matmul_right_t(d_gate_low, in_mlp[0]) + matmul_right_t(d_up_low, in_mlp[1])
    d_xn_two = reduce_input(partial_xn_two)
    d_second_norm, g_gain_two = norm_two_back(d_xn_two)
    d_second = cotangent.astype(jnp.float32) + d_second_norm
    d_rec = d_second.astype(jnp.bfloat16)
    g_out_rec = matmul_left_t(mixed, d_rec)
    d_mixed = matmul_right_t(d_rec, out_rec)
    d_state = d_mixed * gelu_y
    d_ypre_low = gelu_back(d_mixed * state)[0].astype(jnp.bfloat16)
    d_state_ch = lax.all_to_all(d_state, "tok", split_axis=1, concat_axis=0, tiled=True)
    carried = linear_blocks(decay_ch, decay_ch * d_state_ch, True)
    grad_total = d_state_ch + jnp.concatenate([carried[1:], jnp.zeros_like(carried[:1])])
    previous_state = jnp.concatenate([jnp.zeros_like(state_ch[:1]), state_ch[:-1]])
    d_decay, d_drive = (
        lax.all_to_all(grad_total * previous_state, "tok", split_axis=0, concat_axis=1, tiled=True),
        lax.all_to_all(grad_total, "tok", split_axis=0, concat_axis=1, tiled=True),
    )
    d_pre_decay, d_pre_input, d_conv_direct, g_lam = gate_back((d_decay, d_drive))
    decay_low = d_pre_decay.astype(jnp.bfloat16)
    input_low = d_pre_input.astype(jnp.bfloat16)
    decay_blk = decay_low.reshape(count, blocks, BW)
    input_blk = input_low.reshape(count, blocks, BW)
    g_gates = jnp.stack(
        [
            jnp.einsum("tnb,tnc->nbc", blocked, decay_blk, preferred_element_type=jnp.float32),
            jnp.einsum("tnb,tnc->nbc", blocked, input_blk, preferred_element_type=jnp.float32),
        ]
    ).reshape(2, blocks, BW * BW)
    d_conv = d_conv_direct + jnp.einsum(
        "tnc,nbc->tnb", decay_blk, gate_mats[0], preferred_element_type=jnp.float32
    ).reshape(count, channels)
    d_conv = d_conv + jnp.einsum(
        "tnc,nbc->tnb", input_blk, gate_mats[1], preferred_element_type=jnp.float32
    ).reshape(count, channels)
    tap_grads = [jnp.sum(d_conv * u_ext[lag:], axis=0)]
    d_u_ext = jnp.pad(rnn_f[0] * d_conv, ((lag, 0), (0, 0)))
    for offset in range(1, CONV):
        weighted_conv = valid_rows[offset - 1][:, None] * d_conv
        tap_grads.append(
            jnp.sum(weighted_conv * u_ext[lag - offset : lag - offset + count], axis=0)
        )
        d_u_ext = d_u_ext + jnp.pad(rnn_f[offset] * weighted_conv, ((lag - offset, offset), (0, 0)))
    from_next = passed_along(d_u_ext[:lag], "tok", -1)
    d_u_low = (d_u_ext[lag:] + jnp.pad(from_next, ((count - lag, 0), (0, 0)))).astype(jnp.bfloat16)
    g_in_rec = jnp.stack([matmul_left_t(xn_one, d_ypre_low), matmul_left_t(xn_one, d_u_low)])
    d_xn_one = reduce_input(
        matmul_right_t(d_ypre_low, in_rec[0]) + matmul_right_t(d_u_low, in_rec[1])
    )
    d_first_norm, g_gain_one = norm_one_back(d_xn_one)
    d_input = d_second + d_first_norm
    g_rnn = jnp.stack(
        tap_grads
        + [
            jnp.sum(d_conv, axis=0),
            g_lam,
            jnp.sum(decay_low.astype(jnp.float32), axis=0),
            jnp.sum(input_low.astype(jnp.float32), axis=0),
        ]
    )
    g_gains = jnp.stack([g_gain_one, g_gain_two])
    sum_in_rec, sum_out_rec, sum_in_mlp, sum_out_mlp, sum_gates, sum_rnn, sum_gains = (
        lax.psum_scatter(reorder(g_in_rec, 1, inverse), "tok", scatter_dimension=1, tiled=True),
        lax.psum_scatter(reorder(g_out_rec, 1, inverse), "tok", scatter_dimension=1, tiled=True),
        lax.psum_scatter(reorder(g_in_mlp, 1, inverse), "tok", scatter_dimension=1, tiled=True),
        lax.psum_scatter(reorder(g_out_mlp, 1, inverse), "tok", scatter_dimension=1, tiled=True),
        lax.psum_scatter(reorder(g_gates, 2, inverse), "tok", scatter_dimension=2, tiled=True),
        lax.psum_scatter(reorder(g_rnn, 1, inverse), "tok", scatter_dimension=1, tiled=True),
        lax.psum_scatter(reorder(g_gains, 1, inverse), "tok", scatter_dimension=1, tiled=True),
    )
    in_rec_new = soap_update(w_in_rec, m_in_rec, v_in_rec, sum_in_rec, q_in_rec)
    out_rec_new = soap_update(w_out_rec, m_out_rec, v_out_rec, sum_out_rec, q_out_rec)
    in_mlp_new = soap_update(w_in_mlp, m_in_mlp, v_in_mlp, sum_in_mlp, q_in_mlp)
    out_mlp_new = soap_update(w_out_mlp, m_out_mlp, v_out_mlp, sum_out_mlp, q_out_mlp)
    gates_new = adam_update(w_gates, m_gates, v_gates, sum_gates, decay_rate)
    rnn_new = moment_update(m_rnn, v_rnn, sum_rnn)
    gains_new = moment_update(m_gains, v_gains, sum_gains)
    return (
        result,
        d_input,
        in_rec_new[0],
        in_rec_new[1],
        in_rec_new[2],
        out_rec_new[0],
        out_rec_new[1],
        out_rec_new[2],
        in_mlp_new[0],
        in_mlp_new[1],
        in_mlp_new[2],
        out_mlp_new[0],
        out_mlp_new[1],
        out_mlp_new[2],
        gates_new[0],
        gates_new[1],
        gates_new[2],
        rnn_new[0],
        rnn_new[1],
        gains_new[0],
        gains_new[1],
    )


def solution(mesh):
    in_specs = (
        P("tok", None),
        P("tok"),
        P(),
        P("tok", None),
        P(None, "tok", "mlp"),
        P(None, "tok", "mlp"),
        P(None, "tok", "mlp"),
        P(None, "tok", "mlp", None, None, None),
        P("mlp", "tok"),
        P("mlp", "tok"),
        P("mlp", "tok"),
        P("mlp", "tok", None, None, None),
        P(None, "tok", "mlp"),
        P(None, "tok", "mlp"),
        P(None, "tok", "mlp"),
        P(None, "tok", "mlp", None, None, None),
        P("mlp", "tok"),
        P("mlp", "tok"),
        P("mlp", "tok"),
        P("mlp", "tok", None, None, None),
        P(None, "mlp", "tok"),
        P(None, "mlp", "tok"),
        P(None, "mlp", "tok"),
        P(None, ("mlp", "tok")),
        P(None, ("mlp", "tok")),
        P(None, ("mlp", "tok")),
        P(None, "tok"),
        P(None, "tok"),
        P(None, "tok"),
    )
    out_specs = (
        P("tok", None),
        P("tok", None),
        P(None, "tok", "mlp"),
        P(None, "tok", "mlp"),
        P(None, "tok", "mlp"),
        P("mlp", "tok"),
        P("mlp", "tok"),
        P("mlp", "tok"),
        P(None, "tok", "mlp"),
        P(None, "tok", "mlp"),
        P(None, "tok", "mlp"),
        P("mlp", "tok"),
        P("mlp", "tok"),
        P("mlp", "tok"),
        P(None, "mlp", "tok"),
        P(None, "mlp", "tok"),
        P(None, "mlp", "tok"),
        P(None, ("mlp", "tok")),
        P(None, ("mlp", "tok")),
        P(None, "tok"),
        P(None, "tok"),
    )
    return jax.shard_map(
        on_device, mesh=mesh, in_specs=in_specs, out_specs=out_specs, check_vma=False
    )
```

profile of v0, /device:TPU:0, one launch (start us, length us, event | category | flops | bytes accessed | tf_op | source)
XLA Modules:
  0.0 2795.6 jit_solution(14603839988798849890)
XLA Ops:
  22.4 102.6 %all_gather.22 = bf16[2,4,30976]{1,0,2:T(2,128)(2,1)} all-gather(bf16[2,4,3872]{1,0,2:T(2,128)(2,1)S(1)} %copy.435), channel_id=1, replica_groups=mesh['tok'=8,'mlp'=4] {'tok'}, dimensions={2}, use_global_device_ids=true | all-gather | bytes 557568 | tf_op jit(solution)/shard_map/all_gather | solution.py:213
  125.0 34.4 %copy.437 = bf16[2,4,8,3872]{3,1,2,0:T(4,128)(2,1)S(1)} copy(bf16[2,4,8,3872]{1,0,3,2:T(2,128)(2,1)} %bitcast.545) | data formatting | bytes 991232 | tf_op jit(solution)/shard_map/reshape | solution.py:109
  161.5 8.8 all_gather.23
  171.0 8.0 all-gather
  221.9 8.8 all-to-all-start
  239.4 26.5 all-to-all-done
  289.2 33.4 %all-to-all-done.1 = f32[1024,8,88]{0,2,1:T(8,128)} async-done(((f32[1024,8,88]{0,2,1:T(8,128)}), f32[1024,8,88]{0,2,1:T(8,128)}, u32[]{:S(2)}, u32[]{:S(2)}) %all-to-all-start.1) | async-done | bytes 2883616 | tf_op jit(solution)/shard_map/all_to_all | solution.py:280
  342.1 102.9 %while.38 = (s32[]{:T(128)}, f32[5632]{0:T(1024)S(1)}, f32[5632]{0:T(1024)S(1)}, f32[16,8,5632]{2,1,0:T(8,128)S(1)}, f32[16,8,5632]{2,1,0:T(8,128)}, /*index=5*/...) while((s32[]{:T(128)}, f32[5632]{0:T(1024)S(1)}, ...), condition=%wide.region_2.3_spmd.clone, body=%wide.region_1.2_spmd.clone.sunk | while | flops 146442 | bytes 3649855 | solution.py:70
  491.9 26.3 all-to-all-done.2
  518.2 8.6 fusion.125
  533.7 8.9 copy.454
  549.0 8.7 copy.455
  563.8 11.2 gather_fusion.5
  586.4 237.2 %all-reduce.39.cloned.1.call-done = f32[1024,2048]{1,0:T(8,128)} async-done(((f32[1024,2048]{1,0:T(8,128)}), f32[1024,2048]{1,0:T(8,128)}) %all-reduce.39.cloned.1.call-update) | async-done | bytes 8388624 | tf_op jit(solution)/shard_map/psum | solution.py:165
  834.2 11.8 fusion.288
  846.0 8.6 fusion.289
  854.6 17.8 fusion.36
  872.4 9.9 fusion.291
  882.3 9.1 convolution_add_fusion.1
  891.4 290.0 %all-reduce.41.cloned.1.call-done = f32[1024,2048]{1,0:T(8,128)} async-done(((f32[1024,2048]{1,0:T(8,128)}), f32[1024,2048]{1,0:T(8,128)}) %all-reduce.41.cloned.1.call-update) | async-done | bytes 8388624 | tf_op jit(solution)/shard_map/psum | solution.py:169
  1181.4 7.7 multiply_reduce_fusion
  1195.6 10.9 fusion.202
  1215.2 31.6 %all-to-all-done.3 = f32[1024,8,88]{0,2,1:T(8,128)} async-done(((f32[1024,8,88]{0,2,1:T(8,128)}), f32[1024,8,88]{0,2,1:T(8,128)}, u32[]{:S(2)}, u32[]{:S(2)}) %all-to-all-start.3) | async-done | bytes 2883616 | tf_op jit(solution)/shard_map/all_to_all | solution.py:317
  1272.7 103.0 %while.39 = (s32[]{:T(128)}, f32[5632]{0:T(1024)S(1)}, f32[5632]{0:T(1024)S(1)}, f32[16,8,5632]{2,1,0:T(8,128)S(1)}, f32[16,8,5632]{2,1,0:T(8,128)}, /*index=5*/...) while((s32[]{:T(128)}, f32[5632]{0:T(1024)S(1)}, ...), condition=%wide.region_9.10_spmd.clone, body=%wide.region_8.9_spmd.clone.sunk | while | flops 146443 | bytes 3649875 | solution.py:70
  1423.0 30.9 %all-to-all-done.5 = f32[8,1024,88]{1,2,0:T(8,128)S(1)} async-done(((f32[8,1024,88]{1,2,0:T(8,128)}), f32[8,1024,88]{1,2,0:T(8,128)S(1)}, u32[]{:S(2)}, u32[]{:S(2)}) %all-to-all-start.5) | async-done | bytes 2883616 | tf_op jit(solution)/shard_map/all_to_all | solution.py:322
  1460.0 12.2 fusion.290
  1478.1 16.9 all-to-all-done.4
  1495.1 8.0 fusion.106
  1531.1 8.7 convolution_add_fusion
  1551.6 28.0 %copy.554 = f32[2,4,30976]{1,0,2:T(2,128)} copy(f32[2,4,30976]{2,1,0:T(4,128)S(1)} %broadcast_select_fusion.5) | data formatting | bytes 1982464
  1579.7 29.8 %reshape.690 = f32[30976,8]{1,0:T(8,128)} reshape(f32[30976,2,4]{2,1,0:T(2,128)} %bitcast.539) | data formatting | bytes 1982464
  1634.2 11.4 fusion.296
  1645.7 10.5 copy.636
  1656.1 10.6 gather_fusion.10
  1666.7 12.7 copy.511
  1679.4 10.1 bitcast_select_fusion.1
  1713.1 7.7 pad_maximum_fusion.1
  1720.8 9.9 gather_fusion.7
  1730.7 10.8 copy.582
  1741.5 362.8 %all-reduce.43.cloned.1.call-done = (f32[1024,2048]{1,0:T(8,128)}, f32[1024,2048]{1,0:T(8,128)}) async-done(((f32[1024,2048]{1,0:T(8,128)}, f32[1024,2048]{1,0:T(8,128)}), (f32[1024,2048]{1,0:T(8,128)}, f32[1024,2048]{1,0:T(8,128)})) %all-reduce.43.cloned.1.call-update) | async-done | bytes 16777232 | tf_op jit(solution)/shard_map/psum | solution.py:165
  2113.0 14.7 broadcast_select_fusion
  2127.8 10.8 fusion.295
  2138.6 7.0 fusion.294
  2145.6 9.1 pad_maximum_fusion
  2154.7 19.5 gather_fusion.9
  2174.2 11.2 copy.495
  2185.3 9.9 bitcast_select_fusion
  2238.6 24.8 all-reduce.33
  2317.0 60.5 %reduce-scatter.18.cloned.1.call-done = f32[1536,256]{0,1:T(8,128)} async-done(((f32[1536,2048]{0,1:T(8,128)}), f32[1536,256]{0,1:T(8,128)}) %reduce-scatter.18.cloned.1.call-update) | async-done | bytes 1572880 | tf_op jit(solution)/shard_map/reduce_scatter | solution.py:372
  2380.9 8.0 fusion.57
  2388.9 7.8 fusion.44
  2412.2 8.6 fusion.50
  2440.3 9.4 add_convert_fusion
  2449.7 10.0 fusion.7
  2461.3 45.7 %reduce-scatter.12.cloned.1.call-done = f32[2,256,704]{1,2,0:T(8,128)} async-done(((f32[2,2048,704]{1,2,0:T(8,128)}), f32[2,256,704]{1,2,0:T(8,128)}) %reduce-scatter.12.cloned.1.call-update) | async-done | bytes 1441808 | tf_op jit(solution)/shard_map/reduce_scatter | solution.py:369
  2516.4 9.0 fusion.89
  2542.1 9.9 fusion.95
  2567.9 99.6 %reduce-scatter.16.cloned.1.call-done = f32[2,256,1536]{2,1,0:T(8,128)} async-done(((f32[2,2048,1536]{2,1,0:T(8,128)}), f32[2,256,1536]{2,1,0:T(8,128)}) %reduce-scatter.16.cloned.1.call-update) | async-done | bytes 3145744 | tf_op jit(solution)/shard_map/reduce_scatter | solution.py:371
  2679.7 15.2 fusion.29
  2695.0 16.8 fusion.16
  2711.8 8.9 copy.501
  2727.3 8.9 copy.503
  2742.4 16.8 fusion.22
  2759.2 12.8 fusion.149
  (1418 shorter events, 816.5 us)
Async XLA Ops:
  7.2 179.0 %all-gather.6.cloned.1.call-start = ((), (), s32[]{:S(2)}) async-start(), calls=%async_computation.12 | async-start | bytes 6488064 | tf_op jit(solution)/shard_map/all_gather | solution.py:209
  9.7 473.5 %all-gather.8.cloned.1.call-start = ((), (), s32[]{:S(2)}) async-start(), calls=%async_computation.13 | async-start | bytes 3244032 | tf_op jit(solution)/shard_map/all_gather | solution.py:210
  10.6 523.2 %all-gather.12.cloned.1.call-start = ((), (), s32[]{:S(2)}) async-start(), calls=%async_computation.16 | async-start | bytes 7077888 | tf_op jit(solution)/shard_map/all_gather | solution.py:212
  11.9 172.1 %collective-permute-start = (f32[3]{0:T(128)}, f32[3]{0:T(128)}, u32[]{:S(2)}, u32[]{:S(2)}) collective-permute-start(f32[3]{0:T(128)} %slice_convert_fusion.1), channel_id=1, source_target_pairs={{0,4},{4,8},{8,12},{12,16},{16,20},{20,24},{24,28},{1,5},{5,9},{9,... | collective-permute-start | bytes 44 | tf_op jit(solution)/shard_map/ppermute | solution.py:26
  15.4 109.6 %copy-start.18 = (f32[1536,256]{0,1:T(8,128)}, f32[1536,256]{0,1:T(8,128)S(1)}, u32[]{:S(2)}) copy-start(f32[1536,256]{0,1:T(8,128)S(1)} %copy.453) | copy-start | bytes 4718596
  125.0 34.4 %copy-start.116 = (s32[8]{0:T(128)S(1)}, s32[8]{0:T(128)}, u32[]{:S(2)}) copy-start(s32[8]{0:T(128)} %compare_select_fusion.5) | copy-start | bytes 100
  125.0 35.4 %copy-start.105 = (pred[8]{0:T(512)(128)(4,1)S(1)}, pred[8]{0:T(512)(128)(4,1)}, u32[]{:S(2)}) copy-start(pred[8]{0:T(512)(128)(4,1)} %compare_and_fusion.1) | copy-start | bytes 28
  161.4 55.4 %copy-start.39 = (bf16[4,176,176]{2,1,0:T(8,128)(2,1)}, bf16[4,176,176]{2,1,0:T(8,128)(2,1)S(1)}, u32[]{:S(2)}) copy-start(bf16[4,176,176]{2,1,0:T(8,128)(2,1)S(1)} %squeeze.246) | copy-start | bytes 743428
  180.0 12.0 copy-start.68
  180.7 32.8 %copy-start.85 = (f32[704]{0:T(1024)}, f32[704]{0:T(1024)S(1)}, u32[]{:S(2)}) copy-start(f32[704]{0:T(1024)S(1)} %get-tuple-element.533) | copy-start | bytes 8452
  180.7 32.8 %copy-start.87 = (f32[704]{0:T(1024)}, f32[704]{0:T(1024)S(1)}, u32[]{:S(2)}) copy-start(f32[704]{0:T(1024)S(1)} %get-tuple-element.534) | copy-start | bytes 8452
  180.7 32.8 %copy-start.89 = (f32[704]{0:T(1024)}, f32[704]{0:T(1024)S(1)}, u32[]{:S(2)}) copy-start(f32[704]{0:T(1024)S(1)} %get-tuple-element.535) | copy-start | bytes 8452
  180.7 32.8 %copy-start.91 = (f32[704]{0:T(1024)}, f32[704]{0:T(1024)S(1)}, u32[]{:S(2)}) copy-start(f32[704]{0:T(1024)S(1)} %get-tuple-element.532) | copy-start | bytes 8452
  180.7 51.1 %copy-start.64 = (f32[704]{0:T(1024)}, f32[704]{0:T(1024)S(1)}, u32[]{:S(2)}) copy-start(f32[704]{0:T(1024)S(1)} %get-tuple-element.480) | copy-start | bytes 8452
  180.7 51.1 %copy-start.69 = (f32[704]{0:T(1024)}, f32[704]{0:T(1024)S(1)}, u32[]{:S(2)}) copy-start(f32[704]{0:T(1024)S(1)} %get-tuple-element.537) | copy-start | bytes 8452
  180.7 51.1 %copy-start.76 = (f32[704]{0:T(1024)}, f32[704]{0:T(1024)S(1)}, u32[]{:S(2)}) copy-start(f32[704]{0:T(1024)S(1)} %get-tuple-element.536) | copy-start | bytes 8452
  184.0 334.3 %copy-start.82 = (f32[1024]{0:T(1024)}, f32[1024]{0:T(1024)S(1)}, u32[]{:S(2)}) copy-start(f32[1024]{0:T(1024)S(1)} %fusion.227) | copy-start | bytes 12292
  184.0 334.2 %copy-start.71 = (f32[1,2048]{1,0:T(1,128)}, f32[1,2048]{1,0:T(1,128)S(1)}, u32[]{:S(2)}) copy-start(f32[1,2048]{1,0:T(1,128)S(1)} %get-tuple-element.541) | copy-start | bytes 24580
  209.9 3.5 collective-permute-start.1
  212.4 19.4 copy-start.62
  212.4 19.4 copy-start.74
  216.9 15.0 copy-start.1
  221.9 44.0 %all-to-all-start = ((f32[1024,8,88]{0,2,1:T(8,128)}), f32[1024,8,88]{0,2,1:T(8,128)}, u32[]{:S(2)}, u32[]{:S(2)}) async-start(f32[1024,8,88]{0,2,1:T(8,128)} %exponential_multiply_fusion), calls=%async_computation | async-start | bytes 5767168 | tf_op jit(solution)/shard_map/all_to_all | solution.py:279
  265.9 56.6 %all-to-all-start.1 = ((f32[1024,8,88]{0,2,1:T(8,128)}), f32[1024,8,88]{0,2,1:T(8,128)}, u32[]{:S(2)}, u32[]{:S(2)}) async-start(f32[1024,8,88]{0,2,1:T(8,128)} %bitcast.596), calls=%async_computation.1 | async-start | bytes 5767168 | tf_op jit(solution)/shard_map/all_to_all | solution.py:280
  270.6 293.1 %all-gather.10.cloned.1.call-start = ((), (), s32[]{:S(2)}) async-start(), calls=%async_computation.15 | async-start | bytes 14155776 | tf_op jit(solution)/shard_map/all_gather | solution.py:211
  478.7 39.5 %all-to-all-start.2 = ((f32[8,1024,88]{1,2,0:T(8,128)}), f32[8,1024,88]{1,2,0:T(8,128)}, u32[]{:S(2)}, u32[]{:S(2)}) async-start(f32[8,1024,88]{1,2,0:T(8,128)} %copy.449), calls=%async_computation.2 | async-start | bytes 5767168 | tf_op jit(solution)/shard_map/all_to_all | solution.py:283
  483.1 340.5 %all-reduce.39.cloned.1.call-start = ((), (), s32[]{:S(2)}) async-start(), calls=%async_computation.14 | async-start | bytes 16777216 | tf_op jit(solution)/shard_map/psum | solution.py:165
  491.9 34.9 %copy-start.43 = (bf16[88,8,8,256]{3,1,2,0:T(8,128)(2,1)}, bf16[88,8,8,256]{3,1,2,0:T(8,128)(2,1)S(1)}, u32[]{:S(2)}) copy-start(bf16[88,8,8,256]{3,1,2,0:T(8,128)(2,1)S(1)} %copy.585) | copy-start | bytes 8650756
  533.7 647.7 %all-reduce.41.cloned.1.call-start = ((), (), s32[]{:S(2)}) async-start(), calls=%async_computation.17 | async-start | bytes 16777216 | tf_op jit(solution)/shard_map/psum | solution.py:169
  829.4 16.6 slice-start.10
  834.2 11.8 slice-start.11
  834.2 11.8 copy-start.35
  834.2 20.4 slice-start.8
  872.4 9.9 copy-start.128
  1195.6 11.0 copy-start.9
  1206.6 40.2 %all-to-all-start.3 = ((f32[1024,8,88]{0,2,1:T(8,128)}), f32[1024,8,88]{0,2,1:T(8,128)}, u32[]{:S(2)}, u32[]{:S(2)}) async-start(f32[1024,8,88]{0,2,1:T(8,128)} %bitcast.620), calls=%async_computation.3 | async-start | bytes 5767168 | tf_op jit(solution)/shard_map/all_to_all | solution.py:317
  1415.1 38.8 %all-to-all-start.5 = ((f32[8,1024,88]{1,2,0:T(8,128)}), f32[8,1024,88]{1,2,0:T(8,128)S(1)}, u32[]{:S(2)}, u32[]{:S(2)}) async-start(f32[8,1024,88]{1,2,0:T(8,128)} %bitcast.590), calls=%async_computation.5 | async-start | bytes 5767168 | tf_op jit(solution)/shard_map/all_to_all | solution.py:322
  1455.5 39.5 %all-to-all-start.4 = ((f32[8,1024,88]{1,2,0:T(8,128)}), f32[8,1024,88]{1,2,0:T(8,128)}, u32[]{:S(2)}, u32[]{:S(2)}) async-start(f32[8,1024,88]{1,2,0:T(8,128)} %bitcast.589), calls=%async_computation.4 | async-start | bytes 5767168 | tf_op jit(solution)/shard_map/all_to_all | solution.py:323
  1460.0 644.3 %all-reduce.43.cloned.1.call-start = ((), (), s32[]{:S(2)}) async-start(), calls=%async_computation.24 | async-start | bytes 33554432 | tf_op jit(solution)/shard_map/psum | solution.py:165
  1460.0 12.2 copy-start.44
  1460.0 12.2 copy-start.124
  1472.2 22.8 copy-start.2
  1472.2 22.8 copy-start.63
  1472.3 22.8 copy-start.75
  1524.6 4.1 collective-permute-start.2
  1539.9 724.2 %reduce-scatter.20.cloned.1.call-start = ((), (), s32[]{:S(2)}) async-start(), calls=%async_computation.22 | async-start | bytes 17842176
  1609.5 672.3 %reduce-scatter.14.cloned.1.call-start = ((), (), s32[]{:S(2)}) async-start(), calls=%async_computation.19 | async-start | bytes 6488064 | tf_op jit(solution)/shard_map/reduce_scatter | solution.py:370
  1632.3 745.2 %reduce-scatter.18.cloned.1.call-start = ((), (), s32[]{:S(2)}) async-start(), calls=%async_computation.21 | async-start | bytes 14155776 | tf_op jit(solution)/shard_map/reduce_scatter | solution.py:372
  1689.5 770.2 %reduce-scatter.22.cloned.1.call-start = ((), (), s32[]{:S(2)}) async-start(), calls=%async_computation.23 | async-start | bytes 1179648
  2113.0 394.0 %reduce-scatter.12.cloned.1.call-start = ((), (), s32[]{:S(2)}) async-start(), calls=%async_computation.18 | async-start | bytes 12976128 | tf_op jit(solution)/shard_map/reduce_scatter | solution.py:369
  2127.7 10.9 copy-start.126
  2127.7 539.7 %reduce-scatter.16.cloned.1.call-start = ((), (), s32[]{:S(2)}) async-start(), calls=%async_computation.20 | async-start | bytes 28311552 | tf_op jit(solution)/shard_map/reduce_scatter | solution.py:371
  2127.8 10.9 copy-start.36
  2232.4 31.0 %copy-start.109 = (f32[8,88]{1,0:T(8,128)S(1)}, f32[8,88]{1,0:T(8,128)}, u32[]{:S(2)}) copy-start(f32[8,88]{1,0:T(8,128)} %param.58) | copy-start | bytes 8452
  2232.4 31.0 %copy-start.110 = (f32[8,88]{1,0:T(8,128)S(1)}, f32[8,88]{1,0:T(8,128)}, u32[]{:S(2)}) copy-start(f32[8,88]{1,0:T(8,128)} %param.57) | copy-start | bytes 8452
  2274.4 12.7 copy-start.31
  2316.0 72.8 %slice-start.2 = ((s8[6291456]{0:T(1024)(128)(4,1)}), s8[2097152]{0:T(1024)(128)(4,1)S(1)}, s32[]{:S(2)}) async-start(s8[6291456]{0:T(1024)(128)(4,1)} %bitcast.563), calls=%async_computation.27 | async-start | bytes 4194304
  2401.8 19.0 slice-start.4
  2449.7 11.0 copy-start.113
  2449.7 11.0 copy-start.114
  2532.2 19.8 slice-start.6
  2542.1 9.9 slice-start.7
  2672.9 22.0 slice-start
  2679.7 15.2 slice-start.1
  (99 other events, 436.4 us)
Sparse Core Ops, SparseCore 0:
  10.5 63.4 all-gather.5
  76.4 43.5 all-gather.7
  122.5 45.5 all-gather.11
  273.6 91.4 all-gather.9
  533.8 289.7 all-reduce.38
  891.5 289.8 all-reduce.40
  1540.0 564.1 all-reduce.42
  2107.9 110.6 reduce-scatter.19
  2222.5 59.2 reduce-scatter.13
  2285.1 92.3 reduce-scatter.17
  2380.7 36.0 reduce-scatter.21
  2420.2 86.7 reduce-scatter.11
  2510.6 156.8 reduce-scatter.15
where the time goes:
time: 2810 us; the launch traced here: 2800 us
  waiting for transfers between devices  1270 us (45%)
  local copies, waits for them, and re-layouts  797 us (28%)
  matrix products  308 us (11%)
  other arithmetic  216 us (8%)
  blocking collectives  144 us (5%)
  starting transfers between devices  38.9 us (1%)
    psum x2, waiting for transfers between devices, reduce_branch(): return lax.psum(branch_part, 'mlp')  600 us
    psum x1, waiting for transfers between devices, reduce_input(): return lax.psum(input_part, 'mlp')  290 us
    slice x64, local copies, waits for them, and re-layouts, linear_blocks(): lax.scan(step_once, start_pair, (spread(decay), spread(drive)), reverse=b...  150 us
    unnamed x304, local copies, waits for them, and re-layouts  129 us
    gather x26, local copies, waits for them, and re-layouts, reorder(): return jnp.take(reshaped, order, axis=dim).reshape(shape)  129 us
    all_gather x1, blocking collectives, on_device(): lax.all_gather(w_gates.astype(jnp.bfloat16), 'tok', axis=2, tiled=True)  103 us
    reduce_scatter x1, waiting for transfers between devices, on_device(): lax.psum_scatter(reorder(g_in_mlp, 1, inverse), 'tok', scatter_dimension=...  99.6 us
    dot_general x8, matrix products, soap_update(): jnp.einsum('...ki,...kl,...lj->...ij', left_basis, to_tiles(gradient), ri...  71.3 us
  transfers between devices with their start and end apart: 22, of which 14 were waited for; matrix products, arithmetic and copies ran while one was open for 31% of the time, Pallas kernels for 0%

commit v1 on v0

v1 whole, which is shorter than its diff:
```python
import functools

import jax
import jax.numpy as jnp
from jax import lax
from jax.experimental import pallas as pl
from jax.experimental.pallas import tpu as pltpu
from jax.sharding import PartitionSpec as P

BW = 176
CONV = 4
TILE = 64
STEP = 7
HALO = 16
LANES = 128

norm_eps = 1e-06
learn_rate = 0.02
beta_first = 0.9
beta_second = 0.999
adam_eps = 1e-08
decay_rate = 0.1

f32 = jnp.float32
bf16 = jnp.bfloat16


def params(limit=56):
    return pltpu.CompilerParams(
        dimension_semantics=("arbitrary",), vmem_limit_bytes=limit * 1024 * 1024
    )


def whole(shape):
    return pl.BlockSpec(shape, lambda *_: (0,) * len(shape), pipeline_mode=pl.Buffered(1))


def nn(left, right):
    return lax.dot_general(left, right, (((1,), (0,)), ((), ())), preferred_element_type=f32)


def nt(left, right):
    return lax.dot_general(left, right, (((1,), (1,)), ((), ())), preferred_element_type=f32)


def tn(left, right):
    return lax.dot_general(left, right, (((0,), (0,)), ((), ())), preferred_element_type=f32)


def gelu_both(value):
    square = value * value
    bent = jnp.tanh(0.7978845608028654 * (value + 0.044715 * value * square))
    half = 0.5 * (1.0 + bent)
    slope = half + (0.5 * 0.7978845608028654) * value * (1.0 - bent * bent) * (
        1.0 + (3.0 * 0.044715) * square
    )
    return value * half, slope


def gelu_tanh(value):
    return (
        0.5
        * value
        * (1.0 + jnp.tanh(0.7978845608028654 * (value + 0.044715 * value * value * value)))
    )


def one_less_exp(value):
    series = 1.0 + value * (1.0 / 9.0)
    for order in range(8, 1, -1):
        series = 1.0 + value * series * (1.0 / order)
    return jnp.where(value > -0.5, -value * series, 1.0 - jnp.exp(value))


def gate_terms(pre_decay, pre_input, slope, live):
    rate = 1.0 / (1.0 + jnp.exp(-pre_decay))
    gate = 1.0 / (1.0 + jnp.exp(-pre_input))
    log_decay = slope * rate
    raw = jnp.exp(log_decay)
    root = jnp.sqrt(one_less_exp(2.0 * log_decay))
    mult = (1.0 - live) + live * root
    return rate, gate, raw, root, mult


def put_tiles(buffer, value):
    width = value.shape[1]
    for tile in range(pl.cdiv(width, LANES)):
        size = min(LANES, width - tile * LANES)
        buffer[tile, :, :size] = value[:, tile * LANES : tile * LANES + size]


def scan_tiles(first, second, carry_state, carry_prod, out_state, out_prod, width, backward):
    rows = first.shape[1]
    span = rows // 8
    for tile in range(pl.cdiv(width, LANES)):
        size = min(LANES, width - tile * LANES)
        cols = slice(tile * LANES, tile * LANES + size)

        def body(step, held, tile=tile):
            state, prod = held
            row = (span - 1 - step) if backward else step
            at = pl.ds(row, 8, stride=span)
            decay = first[tile, at, :]
            drive = second[tile, at, :]
            if backward:
                total = drive + state
                second[tile, at, :] = total
                first[tile, at, :] = prod
                return decay * total, decay * prod
            state = decay * state + drive
            prod = decay * prod
            second[tile, at, :] = state
            first[tile, at, :] = prod
            return state, prod

        state, prod = lax.fori_loop(
            0,
            span,
            body,
            (jnp.zeros((8, LANES), f32), jnp.ones((8, LANES), f32)),
            unroll=8,
        )
        state_in = carry_state[0:1, tile * LANES : (tile + 1) * LANES]
        prod_in = carry_prod[0:1, tile * LANES : (tile + 1) * LANES]
        for chunk in range(7, -1, -1) if backward else range(8):
            at = slice(chunk * span, (chunk + 1) * span)
            local = first[tile, at, :]
            out_state[at, cols] = (second[tile, at, :] + local * state_in)[:, :size]
            out_prod[at, cols] = (local * prod_in)[:, :size]
            state_in = state[chunk : chunk + 1] + prod[chunk : chunk + 1] * state_in
            prod_in = prod[chunk : chunk + 1] * prod_in
        carry_state[0:1, tile * LANES : (tile + 1) * LANES] = state_in
        carry_prod[0:1, tile * LANES : (tile + 1) * LANES] = prod_in


def rms_low(value, gain):
    return (
        value * lax.rsqrt(jnp.mean(value * value, axis=-1, keepdims=True) + norm_eps) * gain
    ).astype(bf16)


def front_kernel(
    tok, halo, gain, w_in, w_a, w_i, vec, mask,
    xn_o, y_o, u_o, uh_o, xc_o, pa_o, pi_o, a_o, h_o, p_o, end_o,
    ubuf, abuf, bbuf, car_s, car_p,
):
    step = pl.program_id(0)
    rows = tok.shape[0]
    width = y_o.shape[1]

    @pl.when(step == 0)
    def _():
        low = nn(rms_low(halo[...].astype(f32), gain[...]), w_in[1]).astype(bf16)
        uh_o[...] = low
        ubuf[0:HALO, :] = low.astype(f32)
        car_s[...] = jnp.zeros_like(car_s)
        car_p[...] = jnp.ones_like(car_p)

    xn = rms_low(tok[...].astype(f32), gain[...])
    xn_o[...] = xn
    y_o[...] = nn(xn, w_in[0])
    u_low = nn(xn, w_in[1]).astype(bf16)
    u_o[...] = u_low
    u_now = u_low.astype(f32)
    ubuf[HALO : HALO + rows, :] = u_now
    conv = vec[CONV : CONV + 1] + vec[0:1] * u_now
    for back in range(1, CONV):
        conv = conv + vec[back : back + 1] * mask[:, back : back + 1] * ubuf[
            HALO - back : HALO - back + rows, :
        ]
    ubuf[0:HALO, :] = u_now[rows - HALO :, :]
    conv_low = conv.astype(bf16)
    xc_o[...] = conv_low
    pre_decay = nn(conv_low, w_a[...]) + vec[CONV + 2 : CONV + 3]
    pre_input = nn(conv_low, w_i[...]) + vec[CONV + 3 : CONV + 4]
    pa_o[...] = pre_decay
    pi_o[...] = pre_input
    live = mask[:, 0:1]
    _, gate, raw, _, mult = gate_terms(pre_decay, pre_input, vec[CONV + 1 : CONV + 2], live)
    decay = raw * live
    a_o[...] = decay
    put_tiles(abuf, decay)
    put_tiles(bbuf, gate * conv_low.astype(f32) * mult)
    scan_tiles(abuf, bbuf, car_s, car_p, h_o, p_o, width, False)
    end_o[0:1, :] = car_s[0:1, :width]
    end_o[1:2, :] = car_p[0:1, :width]


def front(tok, halo, gain, w_in, w_a, w_i, vec, mask, rows):
    count, model = tok.shape
    width = w_in.shape[2]
    tiles = pl.cdiv(width, LANES)
    row = lambda size: pl.BlockSpec((rows, size), lambda i: (i, 0))
    like = lambda size, kind: jax.ShapeDtypeStruct((count, size), kind)
    return pl.pallas_call(
        front_kernel,
        grid=(count // rows,),
        in_specs=[
            row(model), whole(halo.shape), whole(gain.shape), whole(w_in.shape), whole(w_a.shape),
            whole(w_i.shape), whole(vec.shape), row(mask.shape[1]),
        ],
        out_specs=[
            row(model), row(width), row(width), whole((HALO, width)), row(width), row(width),
            row(width), row(width), row(width), row(width), whole((8, width)),
        ],
        out_shape=[
            like(model, bf16), like(width, f32), like(width, bf16),
            jax.ShapeDtypeStruct((HALO, width), bf16), like(width, bf16), like(width, f32),
            like(width, f32), like(width, f32), like(width, f32), like(width, f32),
            jax.ShapeDtypeStruct((8, width), f32),
        ],
        scratch_shapes=[
            pltpu.VMEM((HALO + rows, width), f32),
            pltpu.VMEM((tiles, rows, LANES), f32),
            pltpu.VMEM((tiles, rows, LANES), f32),
            pltpu.VMEM((8, tiles * LANES), f32),
            pltpu.VMEM((8, tiles * LANES), f32),
        ],
        compiler_params=params(),
        name="front",
    )(tok, halo, gain, w_in, w_a, w_i, vec, mask)


def state_kernel(rank, ends, h_l, p_l, y, w_o, h_o, hp_o, o_o, part_o, hin, hbuf):
    step = pl.program_id(0)
    rows = h_l.shape[0]

    @pl.when(step == 0)
    def _():
        def fold(at, held):
            return jnp.where(at < rank[0], ends[at, 0:1, :] + ends[at, 1:2, :] * held, held)

        start = lax.fori_loop(0, ends.shape[0], fold, jnp.zeros((1, h_l.shape[1]), f32))
        hin[0:1, :] = start
        hbuf[7:8, :] = start

    state = h_l[...] + p_l[...] * hin[0:1, :]
    h_o[...] = state
    hbuf[8 : 8 + rows, :] = state
    hp_o[...] = hbuf[7 : 7 + rows, :]
    hbuf[7:8, :] = state[rows - 1 :, :]
    mixed = (state * gelu_tanh(y[...])).astype(bf16)
    o_o[...] = mixed
    part_o[...] = nt(mixed, w_o[...]).astype(bf16)


def finish_state(rank, ends, h_l, p_l, y, w_o, rows):
    count, width = h_l.shape
    model = w_o.shape[0]
    row = lambda size: pl.BlockSpec((rows, size), lambda i: (i, 0))
    like = lambda size, kind: jax.ShapeDtypeStruct((count, size), kind)
    return pl.pallas_call(
        state_kernel,
        grid=(count // rows,),
        in_specs=[
            pl.BlockSpec(memory_space=pltpu.SMEM), whole(ends.shape), row(width), row(width),
            row(width), whole(w_o.shape),
        ],
        out_specs=[row(width), row(width), row(width), row(model)],
        out_shape=[like(width, f32), like(width, f32), like(width, bf16), like(model, bf16)],
        scratch_shapes=[pltpu.VMEM((8, width), f32), pltpu.VMEM((8 + rows, width), f32)],
        compiler_params=params(),
        name="finish_state",
    )(rank, ends, h_l, p_l, y, w_o)


def mlp_kernel(xn, dhid, w_g, w_u, hm_o, dg_o, du_o, part_o):
    hidden = dhid.shape[1]
    piece = hidden // 3
    total = None
    for at in range(0, hidden, piece):
        cols = slice(at, at + piece)
        z_gate = nn(xn[...], w_g[:, cols])
        z_up = nn(xn[...], w_u[:, cols])
        d_hid = dhid[:, cols]
        act, slope = gelu_both(z_gate)
        hm_o[:, cols] = (act * z_up).astype(bf16)
        d_gate = (d_hid * z_up * slope).astype(bf16)
        d_up = (d_hid * act).astype(bf16)
        dg_o[:, cols] = d_gate
        du_o[:, cols] = d_up
        more = nt(d_gate, w_g[:, cols]) + nt(d_up, w_u[:, cols])
        total = more if total is None else total + more
    part_o[...] = total.astype(bf16)


def mlp(xn, dhid, w_g, w_u, rows):
    count, model = xn.shape
    hidden = dhid.shape[1]
    row = lambda size: pl.BlockSpec((rows, size), lambda i: (i, 0))
    like = lambda size: jax.ShapeDtypeStruct((count, size), bf16)
    return pl.pallas_call(
        mlp_kernel,
        grid=(count // rows,),
        in_specs=[row(model), row(hidden), whole(w_g.shape), whole(w_u.shape)],
        out_specs=[row(hidden), row(hidden), row(hidden), row(model)],
        out_shape=[like(hidden), like(hidden), like(hidden), like(model)],
        compiler_params=params(),
        name="mlp",
    )(xn, dhid, w_g, w_u)


def back_kernel(
    d_rec, w_o, y, h, a, dy_o, g_o, p_o, end_o, abuf, bbuf, car_s, car_p
):
    step = pl.program_id(0)
    width = y.shape[1]

    @pl.when(step == 0)
    def _():
        car_s[...] = jnp.zeros_like(car_s)
        car_p[...] = jnp.ones_like(car_p)

    d_mixed = nn(d_rec[...], w_o[...])
    act, slope = gelu_both(y[...])
    dy_o[...] = (d_mixed * h[...] * slope).astype(bf16)
    put_tiles(abuf, a[...])
    put_tiles(bbuf, d_mixed * act)
    scan_tiles(abuf, bbuf, car_s, car_p, g_o, p_o, width, True)
    end_o[0:1, :] = car_s[0:1, :width]
    end_o[1:2, :] = car_p[0:1, :width]


def back_scan(d_rec, w_o, y, h, a, rows):
    count, model = d_rec.shape
    width = y.shape[1]
    tiles = pl.cdiv(width, LANES)
    steps = count // rows
    row = lambda size: pl.BlockSpec((rows, size), lambda i: (steps - 1 - i, 0))
    like = lambda size, kind: jax.ShapeDtypeStruct((count, size), kind)
    return pl.pallas_call(
        back_kernel,
        grid=(steps,),
        in_specs=[row(model), whole(w_o.shape), row(width), row(width), row(width)],
        out_specs=[row(width), row(width), row(width), whole((8, width))],
        out_shape=[
            like(width, bf16), like(width, f32), like(width, f32),
            jax.ShapeDtypeStruct((8, width), f32),
        ],
        scratch_shapes=[
            pltpu.VMEM((tiles, rows, LANES), f32),
            pltpu.VMEM((tiles, rows, LANES), f32),
            pltpu.VMEM((8, tiles * LANES), f32),
            pltpu.VMEM((8, tiles * LANES), f32),
        ],
        compiler_params=params(),
        name="back_scan",
    )(d_rec, w_o, y, h, a)


def gates_kernel(
    rank, ends, g_l, p_l, pa, pi, xc, hp, u, u_prev, u_halo, mask, w_a, w_i, vec,
    dpa_o, dpi_o, du_o, tail_o, head_o, sum_o,
    qin, dbuf, ubuf,
):
    step = pl.program_id(0)
    steps = pl.num_programs(0)
    rows, width = g_l.shape

    @pl.when(step == 0)
    def _():
        count = ends.shape[0]

        def fold(back, held):
            at = count - 1 - back
            return jnp.where(at > rank[0], ends[at, 0:1, :] + ends[at, 1:2, :] * held, held)

        qin[0:1, :] = lax.fori_loop(0, count, fold, jnp.zeros((1, width), f32))
        sum_o[...] = jnp.zeros_like(sum_o)
        dbuf[rows : rows + 8, :] = jnp.zeros((8, width), f32)

    grad = g_l[...] + p_l[...] * qin[0:1, :]
    live = mask[:, 0:1]
    slope = vec[CONV + 1 : CONV + 2]
    rate, gate, raw, root, mult = gate_terms(pa[...], pi[...], slope, live)
    conv = xc[...].astype(f32)
    d_mult = grad * gate * conv
    d_log = live * (grad * hp[...] * raw - d_mult * (raw * raw) / root)
    d_log_rate = d_log * rate
    d_conv = grad * gate * mult
    d_pa = (d_log_rate * slope * (1.0 - rate)).astype(bf16)
    d_pi = (grad * mult * conv * gate * (1.0 - gate)).astype(bf16)
    dpa_o[...] = d_pa
    dpi_o[...] = d_pi
    d_conv = d_conv + nt(d_pa, w_a[...]) + nt(d_pi, w_i[...])
    total = lambda value: jnp.sum(value, axis=0, keepdims=True)
    u_now = u[...].astype(f32)
    before = jnp.where(step == steps - 1, u_halo[...], u_prev[...]).astype(f32)
    ubuf[0:HALO, :] = before
    ubuf[HALO : HALO + rows, :] = u_now
    dbuf[0:rows, :] = d_conv
    sum_o[0:1, :] += total(d_conv * u_now)
    d_u = vec[0:1] * d_conv
    for back in range(1, CONV):
        sum_o[back : back + 1, :] += total(
            d_conv * mask[:, back : back + 1] * ubuf[HALO - back : HALO - back + rows, :]
        )
        d_u = d_u + vec[back : back + 1] * mask[:, CONV - 1 + back : CONV + back] * dbuf[
            back : back + rows, :
        ]
    sum_o[CONV : CONV + 1, :] += total(d_conv)
    sum_o[CONV + 1 : CONV + 2, :] += total(d_log_rate)
    sum_o[CONV + 2 : CONV + 3, :] += total(d_pa.astype(f32))
    sum_o[CONV + 3 : CONV + 4, :] += total(d_pi.astype(f32))
    du_o[...] = d_u.astype(bf16)

    @pl.when(step == 0)
    def _():
        tail_o[...] = d_u[rows - HALO :, :]

    head = d_conv[0:8, :]
    dbuf[rows : rows + 8, :] = head
    head_o[...] = head


def gates_back(rank, ends, g_l, p_l, pa, pi, xc, hp, u, u_halo, mask, w_a, w_i, vec, rows):
    count, width = g_l.shape
    steps = count // rows
    at = lambda i: steps - 1 - i
    row = lambda size: pl.BlockSpec((rows, size), lambda i: (at(i), 0))
    like = lambda size, kind: jax.ShapeDtypeStruct((count, size), kind)
    per = rows // HALO
    return pl.pallas_call(
        gates_kernel,
        grid=(steps,),
        in_specs=[
            pl.BlockSpec(memory_space=pltpu.SMEM), whole(ends.shape), row(width), row(width),
            row(width), row(width), row(width), row(width), row(width),
            pl.BlockSpec((HALO, width), lambda i: (jnp.maximum(at(i) * per - 1, 0), 0)),
            whole(u_halo.shape), row(mask.shape[1]), whole(w_a.shape), whole(w_i.shape),
            whole(vec.shape),
        ],
        out_specs=[
            row(width), row(width), row(width), whole((HALO, width)), whole((8, width)),
            whole((8, width)),
        ],
        out_shape=[
            like(width, bf16), like(width, bf16), like(width, bf16),
            jax.ShapeDtypeStruct((HALO, width), f32), jax.ShapeDtypeStruct((8, width), f32),
            jax.ShapeDtypeStruct((8, width), f32),
        ],
        scratch_shapes=[
            pltpu.VMEM((8, width), f32),
            pltpu.VMEM((rows + 8, width), f32),
            pltpu.VMEM((HALO + rows, width), f32),
        ],
        compiler_params=params(),
        name="gates_back",
    )(rank, ends, g_l, p_l, pa, pi, xc, hp, u, u, u_halo, mask, w_a, w_i, vec)


def pair_kernel(left, right, weights, out):
    out[...] = (nt(left[...], weights[0]) + nt(right[...], weights[1])).astype(bf16)


def pair_back(left, right, weights, rows):
    count, width = left.shape
    model = weights.shape[1]
    row = lambda size: pl.BlockSpec((rows, size), lambda i: (i, 0))
    return pl.pallas_call(
        pair_kernel,
        grid=(count // rows,),
        in_specs=[row(width), row(width), whole(weights.shape)],
        out_specs=row(model),
        out_shape=jax.ShapeDtypeStruct((count, model), bf16),
        compiler_params=params(),
        name="pair_back",
    )(left, right, weights)


def moments_step(first, second, grad):
    new_first = beta_first * first + (1.0 - beta_first) * grad
    new_second = beta_second * second + (1.0 - beta_second) * grad * grad
    normal = (
        new_first
        * (1.0 / (1.0 - beta_first**STEP))
        / (jnp.sqrt(new_second * (1.0 / (1.0 - beta_second**STEP))) + adam_eps)
    )
    return new_first, new_second, normal


def soap_body(turned, w, m, v, q, nm, nv, nw):
    tile_rows = w.shape[0] // TILE
    tile_cols = w.shape[1] // TILE
    side = lax.broadcasted_iota(jnp.int32, (TILE, 2 * TILE), 1) < TILE
    square = (lax.broadcasted_iota(jnp.int32, (2 * TILE, 2 * TILE), 0) < TILE) == (
        lax.broadcasted_iota(jnp.int32, (2 * TILE, 2 * TILE), 1) < TILE
    )
    for i in range(tile_rows):
        for j in range(0, tile_cols, 2):
            pair = j + 1 < tile_cols
            rows = slice(i * TILE, (i + 1) * TILE)
            cols = slice(j * TILE, (j + (2 if pair else 1)) * TILE)
            lefts = [q[i, j, 0].astype(bf16)]
            right = q[i, j, 1].astype(bf16)
            if pair:
                lefts.append(q[i, j + 1, 0].astype(bf16))
                both = jnp.concatenate([q[i, j, 1], q[i, j + 1, 1]], axis=0)
                right = jnp.where(
                    square, jnp.concatenate([both, both], axis=1), 0.0
                ).astype(bf16)
            choose = lambda parts: jnp.where(side, parts[0], parts[1]) if pair else parts[0]
            inner = choose([turned(rows, cols, left) for left in lefts]).astype(bf16)
            grad = nn(inner, right)
            new_first, new_second, normal = moments_step(m[rows, cols], v[rows, cols], grad)
            nm[rows, cols] = new_first
            nv[rows, cols] = new_second
            low = normal.astype(bf16)
            outer = choose([nn(left, low) for left in lefts]).astype(bf16)
            master = w[rows, cols]
            nw[rows, cols] = master - learn_rate * (nt(outer, right) + decay_rate * master)


def soap_in_kernel(w, m, v, g, q, nm, nv, nw):
    soap_body(lambda rows, cols, left: tn(left, g[rows, cols]), w, m, v, q, nm, nv, nw)


def soap_out_kernel(w, m, v, g, q, nm, nv, nw):
    def turned(rows, cols, left):
        return lax.dot_general(
            left, g[cols, rows], (((0,), (1,)), ((), ())), preferred_element_type=f32
        )

    soap_body(turned, w, m, v, q, nm, nv, nw)


def soap_in(w, m, v, g, q):
    shape = w.shape
    flat = lambda array: array.reshape((-1, shape[-1]))
    w, m, v, g = flat(w), flat(m), flat(v), flat(g)
    height, width = w.shape
    q = q.reshape((height // TILE, width // TILE, 2, TILE, TILE))
    row = pl.BlockSpec((TILE, width), lambda i: (i, 0))
    out = jax.ShapeDtypeStruct(w.shape, f32)
    results = pl.pallas_call(
        soap_in_kernel,
        grid=(height // TILE,),
        in_specs=[row] * 4
        + [pl.BlockSpec((1, width // TILE, 2, TILE, TILE), lambda i: (i, 0, 0, 0, 0))],
        out_specs=[row] * 3,
        out_shape=[out] * 3,
        compiler_params=params(),
        name="soap_in",
    )(w, m, v, g, q)
    return [array.reshape(shape) for array in results]


def soap_out(w, m, v, g, q):
    height, width = w.shape
    rows = height
    for parts in (4, 3, 2):
        if height % (parts * 2 * TILE) == 0:
            rows = height // parts
            break
    row = pl.BlockSpec((rows, width), lambda i: (i, 0))
    out = jax.ShapeDtypeStruct(w.shape, f32)
    return pl.pallas_call(
        soap_out_kernel,
        grid=(height // rows,),
        in_specs=[row] * 3
        + [
            pl.BlockSpec((width, rows), lambda i: (0, i)),
            pl.BlockSpec((rows // TILE, width // TILE, 2, TILE, TILE), lambda i: (i, 0, 0, 0, 0)),
        ],
        out_specs=[row] * 3,
        out_shape=[out] * 3,
        compiler_params=params(),
        name="soap_out",
    )(w, m, v, g, q)


def reorder(array, dim, order):
    shape = array.shape
    parts = order.shape[0]
    reshaped = array.reshape(shape[:dim] + (parts, shape[dim] // parts) + shape[dim + 1 :])
    return jnp.take(reshaped, order, axis=dim, mode="clip").reshape(shape)


def gather_slabs(array):
    return lax.all_gather(array, "mlp", axis=0, tiled=True)


def scatter_slabs(array):
    return lax.psum_scatter(array, "mlp", scatter_dimension=0, tiled=True)


def line_scatter(array):
    count = lax.axis_size("mlp")
    slab = lax.axis_index("mlp")
    share = array.shape[0] // count
    piece = lambda at: lax.dynamic_slice_in_dim(
        array, jnp.clip(at, 0, count - 1) * share, share, 0
    ).astype(f32)
    up = down = 0.0
    for step in range(1, count):
        send_up = (piece(slab + count - step) + up).astype(bf16)
        send_down = (piece(slab - count + step) + down).astype(bf16)
        up = lax.ppermute(send_up, "mlp", [(i, i + 1) for i in range(step)]).astype(f32)
        down = lax.ppermute(
            send_down, "mlp", [(i, i - 1) for i in range(count - step, count)]
        ).astype(f32)
    return piece(slab) + up + down


def line_gather(array):
    count = lax.axis_size("mlp")
    slab = lax.axis_index("mlp")
    share = array.shape[0]
    ups, downs = [array], [array]
    for step in range(1, count):
        ups.append(lax.ppermute(ups[-1], "mlp", [(i, i + 1) for i in range(step - 1, count - 1)]))
        downs.append(lax.ppermute(downs[-1], "mlp", [(i, i - 1) for i in range(1, count - step + 1)]))
    out = jnp.zeros((count * share,) + array.shape[1:], array.dtype)
    out = lax.dynamic_update_slice_in_dim(out, array, slab * share, 0)
    for step in range(1, count):
        part = jnp.where(slab >= step, ups[step], downs[count - step])
        out = lax.dynamic_update_slice_in_dim(out, part, (slab - step) % count * share, 0)
    return out


def hop(array, pairs):
    count = lax.axis_size("tok")
    return lax.ppermute(array, "tok", [(i, i ^ pairs[i % 2]) for i in range(count)])


CORE, NEAR, FAR = (1, 1), (2, 4), (4, 2)


def stored_order(parts, rank):
    indices = jnp.arange(parts, dtype=jnp.int32)
    if parts != 8:
        return indices, indices
    near, far = indices // 2 % 2, indices % 2
    spots = rank ^ (
        indices // 4 + jnp.where(rank % 2 == 0, near * 2 + far * 4, near * 4 + far * 2)
    )
    return spots, invert(spots)


def invert(order):
    indices = jnp.arange(order.shape[0], dtype=jnp.int32)
    return jnp.sum(jnp.where(order[None, :] == indices[:, None], indices[None, :], 0), axis=1)


def gather_tok(array, dim):
    if lax.axis_size("tok") != 8:
        return lax.all_gather(array, "tok", axis=dim, tiled=True)
    two = jnp.concatenate([array, hop(array, FAR)], axis=dim)
    other = hop(two, NEAR)
    four = jnp.concatenate([two, other], axis=dim)
    rest = jnp.split(hop(four, CORE), 4, axis=dim)
    return jnp.concatenate([four, rest[0], rest[2], rest[1], rest[3]], axis=dim)


def scatter_tok(keep, send):
    if lax.axis_size("tok") != 8:
        whole_sum = jnp.concatenate([keep.astype(send.dtype), send], axis=0)
        return lax.psum_scatter(whole_sum, "tok", scatter_dimension=0, tiled=True)
    rows = keep.shape[0] // 4
    low = send.dtype
    got = hop(send, CORE).reshape((2, 2, rows) + keep.shape[1:])
    keep = keep.reshape(got.shape)
    added = lambda at: keep[at].astype(f32) + got[:, at].astype(f32)
    near = hop(added(1).astype(low), NEAR)
    stay = added(0)
    summed = lambda at: stay[at] + near[at].astype(f32)
    far = hop(summed(1).astype(low), FAR)
    return summed(0) + far.astype(f32)


def grad_owned(left, right):
    half = left.shape[1] // 2
    return scatter_tok(
        tn(left[:, :half], right), tn(left[:, half:], right).astype(bf16)
    )


def permute_kernel(order, array, out):
    out[...] = array[...]


def permute_columns(array, order):
    parts = order.shape[0]
    rows, width = array.shape
    size = width // parts
    if size % LANES:
        return reorder(array, 1, order)
    return pl.pallas_call(
        permute_kernel,
        grid_spec=pltpu.PrefetchScalarGridSpec(
            num_scalar_prefetch=1,
            grid=(parts,),
            in_specs=[pl.BlockSpec((rows, size), lambda i, order: (0, order[i]))],
            out_specs=pl.BlockSpec((rows, size), lambda i, order: (0, i)),
        ),
        out_shape=jax.ShapeDtypeStruct(array.shape, array.dtype),
        compiler_params=params(),
        name="permute_columns",
    )(order, array)


def norm_back(value, upstream, gain):
    scale = lax.rsqrt(jnp.mean(value * value, axis=-1, keepdims=True) + norm_eps)
    weighted = upstream * gain
    inner = jnp.mean(value * weighted, axis=-1, keepdims=True)
    d_value = scale * weighted - value * (scale * scale * scale) * inner
    return d_value, jnp.sum(upstream * value * scale, axis=0)


def block_diagonal(blocks):
    count, width, _ = blocks.shape
    return jnp.concatenate(
        [
            jnp.pad(blocks[n], ((0, 0), (n * width, (count - 1 - n) * width)))
            for n in range(count)
        ],
        axis=0,
    )


def diagonal_blocks(array, count):
    width = array.shape[0] // count
    return jnp.stack(
        [array[n * width : (n + 1) * width, n * width : (n + 1) * width] for n in range(count)]
    )


def on_device(
    tokens, segment_ids, owner_table, cotangent,
    w_in_rec, m_in_rec, v_in_rec, q_in_rec,
    w_out_rec, m_out_rec, v_out_rec, q_out_rec,
    w_in_mlp, m_in_mlp, v_in_mlp, q_in_mlp,
    w_out_mlp, m_out_mlp, v_out_mlp, q_out_mlp,
    w_gates, m_gates, v_gates, w_rnn, m_rnn, v_rnn, w_gains, m_gains, v_gains,
):
    parts = lax.axis_size("tok")
    rank = lax.axis_index("tok")
    slabs = lax.axis_size("mlp")
    slab = lax.axis_index("mlp")
    count, model = tokens.shape
    length = count * parts
    share = count // slabs
    rows = min(256, count)
    half = parts // 2
    spots, places = stored_order(parts, rank)
    into_local = jnp.take(invert(owner_table), spots, mode="clip")
    from_local = jnp.take(places, owner_table, mode="clip")
    rank_ref = rank.reshape(1).astype(jnp.int32)

    in_rec = gather_tok(w_in_rec.astype(bf16), 1)
    out_rec_own, in_rec = lax.optimization_barrier((w_out_rec.T.astype(bf16), in_rec))
    out_rec = gather_tok(out_rec_own, 0)
    mlp_own = jnp.concatenate([w_in_mlp[0], w_in_mlp[1], w_out_mlp.T], axis=1).astype(bf16)
    mlp_own, out_rec = lax.optimization_barrier((mlp_own, out_rec))
    mlp_all = gather_tok(mlp_own, 0)
    hid = w_in_mlp.shape[2]

    blocks = w_gates.shape[1]
    gate_part = w_gates.shape[2]
    lead = 2 * blocks
    rnn_part = w_rnn.shape[1]
    small = jnp.concatenate(
        [w_gates.reshape(lead, gate_part), w_rnn, w_gains.reshape(lead, -1)], axis=1
    ).astype(bf16)
    small_all = lax.all_gather(small, "tok", axis=0, tiled=False)
    gains_all = small_all[:, :, gate_part + rnn_part :].reshape(parts, 2, model // parts)
    gains_f = (
        jnp.take(gains_all, spots, axis=0, mode="clip")
        .transpose(1, 0, 2)
        .reshape(2, model)
        .astype(f32)
    )
    ordered = jnp.take(small_all[:, :, : gate_part + rnn_part], owner_table, axis=0, mode="clip")
    gate_mats = ordered[:, :, :gate_part].transpose(1, 0, 2).reshape(2, blocks, BW, BW)
    w_a = block_diagonal(gate_mats[0])
    w_i = block_diagonal(gate_mats[1])
    rnn_f = ordered[:, :, gate_part:].transpose(1, 0, 2).reshape(lead, -1).astype(f32)
    lam = rnn_f[CONV + 1]
    vec = rnn_f.at[CONV + 1].set(-8.0 * jax.nn.softplus(lam))

    tok_s = permute_columns(tokens, into_local)
    cot_s = permute_columns(cotangent, into_local)
    forward_pairs = [(i, i + 1) for i in range(parts - 1)]
    rim = lax.ppermute(tokens[count - HALO :], "tok", forward_pairs)
    halo = reorder(rim, 1, into_local)
    rim_ids = lax.ppermute(segment_ids[count - HALO :], "tok", forward_pairs)
    position = rank * count - HALO + jnp.arange(count + HALO, dtype=jnp.int32)
    ids_ext = jnp.concatenate([rim_ids, segment_ids])
    starts = (position % length == 0) | (ids_ext != jnp.concatenate([ids_ext[:1], ids_ext[:-1]]))
    live_ext = jnp.where(starts, 0.0, 1.0).astype(f32)
    live = live_ext[HALO:]
    valid = [live]
    for back in range(1, CONV):
        before = valid[-1] if back > 1 else jnp.ones((count,), f32)
        valid.append(before * live_ext[HALO - back + 1 : HALO - back + 1 + count])
    ahead = [jnp.concatenate([valid[k][k:], jnp.zeros((k,), f32)]) for k in range(1, CONV)]
    mask = jnp.stack(valid + ahead + [live], axis=1)

    xn_one, y_pre, u_low, u_halo, conv_low, pre_decay, pre_input, decay, h_loc, p_loc, ends = front(
        tok_s, halo, gains_f[0:1], in_rec, w_a, w_i, vec, mask, rows
    )
    ends_all = lax.all_gather(ends[0:2], "tok", axis=0, tiled=False)
    state, state_prev, mixed, branch = finish_state(
        rank_ref, ends_all, h_loc, p_loc, y_pre, out_rec, rows
    )
    own = lambda array: lax.dynamic_slice_in_dim(array, slab * share, share, 0)
    second = own(tok_s).astype(f32) + scatter_slabs(branch).astype(f32)
    second_low = rms_low(second, gains_f[1])
    w_g, w_u, w_d = mlp_all[:, :hid], mlp_all[:, hid : 2 * hid], mlp_all[:, 2 * hid :]
    d_hidden = nn(cot_s, w_d)
    xn_two = gather_slabs(second_low)
    hidden, d_gate, d_up, d_branch = mlp(xn_two, d_hidden, w_g, w_u, rows)
    d_xn_two = scatter_slabs(d_branch).astype(f32)
    g_out_mlp = grad_owned(cot_s, hidden)
    g_in_mlp = jnp.stack([grad_owned(xn_two, d_gate), grad_owned(xn_two, d_up)])
    result_own = second + line_scatter(nt(hidden, w_d).astype(bf16))
    result = line_gather(permute_columns(result_own.astype(bf16), from_local))

    d_value, g_gain_two = norm_back(second, d_xn_two, gains_f[1])
    d_second = own(cot_s).astype(f32) + d_value
    d_rec = gather_slabs(d_second.astype(bf16))
    d_ypre, g_loc, q_loc, ends_back = back_scan(d_rec, out_rec, y_pre, state, decay, rows)
    ends_back_all = lax.all_gather(ends_back[0:2], "tok", axis=0, tiled=False)
    d_pa, d_pi, d_u, d_u_tail, d_conv_head, sums = gates_back(
        rank_ref, ends_back_all, g_loc, q_loc, pre_decay, pre_input, conv_low, state_prev,
        u_low, u_halo, mask, w_a, w_i, vec, rows,
    )
    spill = []
    for ahead_by in range(CONV - 1, 0, -1):
        row_sum = 0.0
        for back in range(ahead_by, CONV):
            at = back - ahead_by
            row_sum = row_sum + rnn_f[back] * mask[at, back] * d_conv_head[at]
        spill.append(row_sum)
    from_next = lax.ppermute(jnp.stack(spill), "tok", [(i + 1, i) for i in range(parts - 1)])
    d_u_tail = d_u_tail + jnp.pad(from_next, ((HALO - CONV + 1, 0), (0, 0)))
    d_u = lax.dynamic_update_slice_in_dim(d_u, d_u_tail.astype(bf16), count - HALO, 0)
    d_xn_one = scatter_slabs(pair_back(d_ypre, d_u, in_rec, rows)).astype(f32)
    g_out_rec = grad_owned(d_rec, mixed)
    g_in_rec = jnp.stack([grad_owned(xn_one, d_ypre), grad_owned(xn_one, d_u)])
    d_value_one, g_gain_one = norm_back(own(tok_s).astype(f32), d_xn_one, gains_f[0])
    d_input_own = (d_second + d_value_one).astype(bf16)
    d_input = gather_slabs(permute_columns(d_input_own, from_local)).astype(f32)

    g_gates = jnp.stack(
        [
            diagonal_blocks(tn(conv_low, d_pa), blocks),
            diagonal_blocks(tn(conv_low, d_pi), blocks),
        ]
    )
    g_rnn = sums.at[CONV + 1].multiply(-8.0 * jax.nn.sigmoid(lam))
    g_small = jnp.concatenate(
        [g_gates.reshape(lead, parts, gate_part), g_rnn.reshape(lead, parts, rnn_part)], axis=2
    ).transpose(1, 0, 2)
    g_small = jnp.take(g_small, into_local, axis=0, mode="clip")
    sum_small = scatter_tok(g_small[:half], g_small[half:])[0]
    sum_gates = sum_small[:, :gate_part].reshape(w_gates.shape)
    sum_rnn = sum_small[:, gate_part:]
    g_gains = jnp.stack([g_gain_one, g_gain_two]).reshape(2, parts, -1).transpose(1, 0, 2)
    sum_gains = lax.psum(scatter_tok(g_gains[:half], g_gains[half:])[0], "mlp")

    low = lambda array: array.astype(bf16)
    out_mlp_new = soap_out(w_out_mlp, m_out_mlp, v_out_mlp, low(g_out_mlp), q_out_mlp)
    in_mlp_new = soap_in(w_in_mlp, m_in_mlp, v_in_mlp, low(g_in_mlp), q_in_mlp)
    out_rec_new = soap_out(w_out_rec, m_out_rec, v_out_rec, low(g_out_rec), q_out_rec)
    in_rec_new = soap_in(w_in_rec, m_in_rec, v_in_rec, low(g_in_rec), q_in_rec)
    gates_m, gates_v, gates_n = moments_step(m_gates, v_gates, sum_gates)
    gates_w = w_gates - learn_rate * (gates_n + decay_rate * w_gates)
    rnn_m, rnn_v, _ = moments_step(m_rnn, v_rnn, sum_rnn)
    gains_m, gains_v, _ = moments_step(m_gains, v_gains, sum_gains)
    return (
        result, d_input,
        in_rec_new[0], in_rec_new[1], in_rec_new[2],
        out_rec_new[0], out_rec_new[1], out_rec_new[2],
        in_mlp_new[0], in_mlp_new[1], in_mlp_new[2],
        out_mlp_new[0], out_mlp_new[1], out_mlp_new[2],
        gates_m, gates_v, gates_w, rnn_m, rnn_v, gains_m, gains_v,
    )


def solution(mesh):
    in_specs = (
        P("tok", None),
        P("tok"),
        P(),
        P("tok", None),
        P(None, "tok", "mlp"),
        P(None, "tok", "mlp"),
        P(None, "tok", "mlp"),
        P(None, "tok", "mlp", None, None, None),
        P("mlp", "tok"),
        P("mlp", "tok"),
        P("mlp", "tok"),
        P("mlp", "tok", None, None, None),
        P(None, "tok", "mlp"),
        P(None, "tok", "mlp"),
        P(None, "tok", "mlp"),
        P(None, "tok", "mlp", None, None, None),
        P("mlp", "tok"),
        P("mlp", "tok"),
        P("mlp", "tok"),
        P("mlp", "tok", None, None, None),
        P(None, "mlp", "tok"),
        P(None, "mlp", "tok"),
        P(None, "mlp", "tok"),
        P(None, ("mlp", "tok")),
        P(None, ("mlp", "tok")),
        P(None, ("mlp", "tok")),
        P(None, "tok"),
        P(None, "tok"),
        P(None, "tok"),
    )
    out_specs = (
        P("tok", None),
        P("tok", None),
        P(None, "tok", "mlp"),
        P(None, "tok", "mlp"),
        P(None, "tok", "mlp"),
        P("mlp", "tok"),
        P("mlp", "tok"),
        P("mlp", "tok"),
        P(None, "tok", "mlp"),
        P(None, "tok", "mlp"),
        P(None, "tok", "mlp"),
        P("mlp", "tok"),
        P("mlp", "tok"),
        P("mlp", "tok"),
        P(None, "mlp", "tok"),
        P(None, "mlp", "tok"),
        P(None, "mlp", "tok"),
        P(None, ("mlp", "tok")),
        P(None, ("mlp", "tok")),
        P(None, "tok"),
        P(None, "tok"),
    )
    return jax.shard_map(
        on_device, mesh=mesh, in_specs=in_specs, out_specs=out_specs, check_vma=False
    )
```

time: 2810 us -> 1160 us (0.41)
  waiting for transfers between devices: 1270 us -> 358 us
  local copies, waits for them, and re-layouts: 797 us -> 168 us
  Pallas kernels: 0 us -> 247 us
  matrix products: 308 us -> 71.7 us
  other arithmetic: 216 us -> 116 us
  blocking collectives: 144 us -> 90 us
  starting transfers between devices: 38.9 us -> 71.7 us
    psum x3 -> x0, waiting for transfers between devices: 890 us -> none  [the longest x2 600 us: reduce_branch(): return lax.psum(branch_part, 'mlp')]
    pallas_call x0 -> x14, Pallas kernels: none -> 247 us  [the longest x2 51.9 us: soap_in(): pl.pallas_call(soap_in_kernel, grid=(height // TILE,), in_specs=[row] * 4...]
    ppermute x3 -> x48, waiting for transfers between devices: 1 us -> 242 us  [the longest x33 120 us: hop(): lax.ppermute(array, 'tok', [(i, i ^ pairs[i % 2]) for i in range(count)])]
    dot_general x40 -> x16, matrix products: 308 us -> 71.7 us  [the longest x14 52.4 us: tn(): lax.dot_general(left, right, (((0,), (0,)), ((), ())), preferred_element_...]
    all_to_all x6 -> x0, waiting for transfers between devices: 166 us -> none  [the longest x1 33.4 us: on_device(): lax.all_to_all(drive, 'tok', split_axis=1, concat_axis=0, tiled=True)]
    reduce_scatter x4 -> x3, waiting for transfers between devices: 212 us -> 68.3 us  [scatter_slabs(): return lax.psum_scatter(array, 'mlp', scatter_dimension=0, tiled=True)]
    gather x26 -> x6, local copies, waits for them, and re-layouts: 129 us -> 6.26 us  [the longest x1 1.95 us: on_device(): g_small = jnp.take(g_small, into_local, axis=0, mode='clip')]
    slice x148 -> x25, local copies, waits for them, and re-layouts: 161 us -> 41.5 us  [the longest x9 21 us: scatter_tok(): added = lambda at: keep[at].astype(f32) + got[:, at].astype(f32)]
  transfers between devices with their start and end apart: 22 -> 54, of which waited for: 14 -> 17; matrix products, arithmetic and copies ran while one was open for 31% -> 27% of each run, Pallas kernels for 0% -> 19%
where the time goes in v1:
time: 1160 us; the launch traced here: 1140 us
  waiting for transfers between devices  358 us (31%)
  Pallas kernels  247 us (21%)
  local copies, waits for them, and re-layouts  168 us (14%)
  other arithmetic  116 us (10%)
  blocking collectives  90 us (8%)
  starting transfers between devices  71.7 us (6%)
  matrix products  71.7 us (6%)
  between operations  16 us (1%)
    ppermute x33, waiting for transfers between devices, hop(): lax.ppermute(array, 'tok', [(i, i ^ pairs[i % 2]) for i in range(count)])  120 us
    unnamed x192, local copies, waits for them, and re-layouts  72.6 us
    reduce_scatter x3, waiting for transfers between devices, scatter_slabs(): return lax.psum_scatter(array, 'mlp', scatter_dimension=0, tiled=True)  68.3 us
    ppermute x3, waiting for transfers between devices, line_scatter(): lax.ppermute(send_up, 'mlp', [(i, i + 1) for i in range(step)]).astype(f32)  61.1 us
    ppermute x3, waiting for transfers between devices, line_gather(): lax.ppermute(downs[-1], 'mlp', [(i, i - 1) for i in range(1, count - step...  60.8 us
    all_gather x1, blocking collectives, on_device(): small_all = lax.all_gather(small, 'tok', axis=0, tiled=False)  52.6 us
    dot_general x14, matrix products, tn(): lax.dot_general(left, right, (((0,), (0,)), ((), ())), preferred_element_...  52.4 us
    pallas_call x2, Pallas kernels, soap_in(): pl.pallas_call(soap_in_kernel, grid=(height // TILE,), in_specs=[row] * 4...  51.9 us
  transfers between devices with their start and end apart: 54, of which 17 were waited for; matrix products, arithmetic and copies ran while one was open for 27% of the time, Pallas kernels for 19%

profile of v1, /device:TPU:0, one launch (start us, length us, event | category | flops | bytes accessed | tf_op | source)
XLA Modules:
  0.0 1138.7 jit_solution(2645176052326211180)
XLA Ops:
  11.7 9.3 collective-permute-done.1
  23.1 17.0 %collective-permute-done.2 = bf16[2,512,704]{1,2,0:T(8,128)(2,1)S(1)} collective-permute-done((bf16[2,512,704]{1,2,0:T(8,128)(2,1)S(1)}, bf16[2,512,704]{1,2,0:T(8,128)(2,1)S(1)}, u32[]{:S(2)}, u32[]{:S(2)}) %collective-permute-start.2) | collective-permute-done | bytes 1441824 | tf_op jit(solution)/shard_map/ppermute | solution.py:623
  63.6 5.8 collective-permute-done.5
  79.6 5.3 collective-permute-done.6
  104.4 26.8 %collective-permute-done.8 = bf16[256,4608]{1,0:T(8,128)(2,1)S(1)} collective-permute-done((bf16[256,4608]{1,0:T(8,128)(2,1)S(1)}, bf16[256,4608]{1,0:T(8,128)(2,1)S(1)}, u32[]{:S(2)}, u32[]{:S(2)}) %collective-permute-start.8) | collective-permute-done | bytes 2359328 | tf_op jit(solution)/shard_map/ppermute | solution.py:623
  143.1 52.6 %all_gather.25 = bf16[8,8,4024]{2,1,0:T(8,128)(2,1)S(1)} all-gather(bf16[1,8,4024]{2,1,0:T(8,128)(2,1)S(1)} %concatenate.86), channel_id=1, replica_groups=mesh['tok'=8,'mlp'=4] {'tok'}, dimensions={0}, use_global_device_ids=true | all-gather | bytes 579456 | tf_op jit(solution)/shard_map/all_gather | solution.py:765
  205.8 7.4 permute_columns.4.tok
  220.5 4.0 multiply_reduce_fusion.5
  228.3 33.9 %front.1 = (bf16[1024,2048]{1,0:T(8,128)(2,1)}, f32[1024,704]{1,0:T(8,128)}, bf16[1024,704]{1,0:T(8,128)(2,1)}, bf16[16,704]{1,0:T(8,128)(2,1)}, bf16[1024,704]{...) custom-call(bf16[1024,2048]{1,0:T(8,128)(2,1)} %permute_columns.4.to, ...), custom_call_target="tpu_custom_call" | custom-call | tf_op jit(solution)/shard_map/front/pallas_call | solution.py:195
  262.2 6.6 pad_maximum_fusion
  269.9 15.4 %all-gather.2.ends = f32[8,2,704]{2,1,0:T(2,128)} all-gather(f32[1,2,704]{2,1,0:T(2,128)S(1)} %slice_bitcast_fusion.22), channel_id=2, replica_groups=mesh['tok'=8,'mlp'=4] {'tok'}, dimensions={0}, use_global_device_ids=true | all-gather | bytes 50688 | tf_op jit(solution)/shard_map/all_gather | solution.py:802
  285.3 10.7 finish_state.1
  299.1 7.4 permute_columns.5
  318.4 4.9 constant_dynamic-update-slice_fusion.14
  323.3 49.9 %reduce-scatter.4.cloned.1.call-done = bf16[256,2048]{1,0:T(8,128)(2,1)} async-done(((bf16[1024,2048]{1,0:T(8,128)(2,1)}), bf16[256,2048]{1,0:T(8,128)(2,1)}) %reduce-scatter.4.cloned.1.call-update) | async-done | bytes 1048592 | tf_op jit(solution)/shard_map/reduce_scatter | solution.py:584
  378.0 3.3 slice_dynamic-update-slice_fusion.3
  381.3 3.2 slice_dynamic-update-slice_fusion.2
  384.5 3.4 slice_dynamic-update-slice_fusion.1
  387.9 3.4 slice_dynamic-update-slice_fusion
  391.3 10.4 fusion.147
  401.7 10.4 fusion.2.dhid
  412.2 47.1 %all-gather.8.cloned.1.call-done.xn = bf16[1024,2048]{1,0:T(8,128)(2,1)} async-done(((bf16[256,2048]{1,0:T(8,128)(2,1)}), bf16[1024,2048]{1,0:T(8,128)(2,1)}) %all-gather.8.cloned.1.call-update) | async-done | bytes 4194320 | tf_op jit(solution)/shard_map/all_gather | solution.py:580
  459.3 33.8 %mlp.1 = (bf16[1024,1536]{1,0:T(8,128)(2,1)}, bf16[1024,1536]{1,0:T(8,128)(2,1)}, bf16[1024,1536]{1,0:T(8,128)(2,1)}, bf16[1024,2048]{1,0:T(8,128)(2,1)}) custom-call(bf16[1024,2048]{1,0:T(8,128)(2,1)} %all-gather.8.cloned.1.call-done.xn, f32[1024,1536]{1,0:T(8,128)} %fusion.2.dhid, bf16[2048,1536]{1,0:T(8,128)(2,1)} %get-tuple-element.287.w_g, ...), custom_call_target="tpu_custom_call" | custom-call | tf_op jit(solution)/shard_map/mlp/pallas_call | solution.py:292
  493.5 7.8 convolution_convert_fusion
  501.3 4.9 convolution_convert_fusion.2
  506.7 4.8 convolution_convert_fusion.1
  511.6 8.9 fusion.4
  524.1 3.6 fusion.33
  530.8 3.5 fusion.43
  537.4 30.8 %collective-permute-done.11 = bf16[256,2048]{1,0:T(8,128)(2,1)S(1)} collective-permute-done((bf16[256,2048]{1,0:T(8,128)(2,1)S(1)}, bf16[256,2048]{1,0:T(8,128)(2,1)S(1)}, u32[]{:S(2)}, u32[]{:S(2)}) %collective-permute-start.11) | collective-permute-done | bytes 1048608 | tf_op jit(solution)/shard_map/ppermute | solution.py:598
  568.7 4.6 collective-permute-start.12
  573.3 3.5 fusion.41
  580.0 30.2 %collective-permute-done.12 = bf16[256,2048]{1,0:T(8,128)(2,1)S(1)} collective-permute-done((bf16[256,2048]{1,0:T(8,128)(2,1)S(1)}, bf16[256,2048]{1,0:T(8,128)(2,1)S(1)}, u32[]{:S(2)}, u32[]{:S(2)}) %collective-permute-start.12) | collective-permute-done | bytes 1048608 | tf_op jit(solution)/shard_map/ppermute | solution.py:598
  613.1 6.0 collective-permute-start.13
  621.6 3.4 fusion.145
  625.1 4.9 fusion.7
  631.8 3.5 fusion.9
  644.7 5.9 collective-permute-done.40
  653.8 22.0 %collective-permute-done.34 = bf16[2,256,1536]{2,1,0:T(8,128)(2,1)S(1)} collective-permute-done((bf16[2,256,1536]{2,1,0:T(8,128)(2,1)S(1)}, bf16[2,256,1536]{2,1,0:T(8,128)(2,1)S(1)}, u32[]{:S(2)}, u32[]{:S(2)}) %collective-permute-start.34) | collective-permute-done | bytes 1572896 | tf_op jit(solution)/shard_map/ppermute | solution.py:623
  677.8 23.3 %collective-permute-done.37 = bf16[2,256,1536]{2,1,0:T(8,128)(2,1)S(1)} collective-permute-done((bf16[2,256,1536]{2,1,0:T(8,128)(2,1)S(1)}, bf16[2,256,1536]{2,1,0:T(8,128)(2,1)S(1)}, u32[]{:S(2)}, u32[]{:S(2)}) %collective-permute-start.37) | collective-permute-done | bytes 1572896 | tf_op jit(solution)/shard_map/ppermute | solution.py:623
  706.4 23.7 %soap_out.3 = (f32[1536,256]{1,0:T(8,128)}, f32[1536,256]{1,0:T(8,128)}, f32[1536,256]{1,0:T(8,128)}) custom-call(f32[1536,256]{1,0:T(8,128)} %w.3, f32[1536,256]{1,0:T(8,128)} %m.3, f32[1536,256]{1,0:T(8,128)} %v.3, bf16[256,1536]{1,0:T(8,128)(2,1)} %fusion.69.g, f32[24,4,2,64,64]{4,3,2,1,0:T(8,128)} %q.3), custom_call_target="tpu_custom_call" | custom-call | tf_op jit(solution)/shard_map/soap_out/pallas_call | solution.py:557
  735.3 33.3 %soap_in.3 = (f32[512,1536]{1,0:T(8,128)}, f32[512,1536]{1,0:T(8,128)}, f32[512,1536]{1,0:T(8,128)}) custom-call(f32[512,1536]{1,0:T(8,128)} %bitcast.344, f32[512,1536]{1,0:T(8,128)} %bitcast.360, f32[512,1536]{1,0:T(8,128)} %bitcast.361, bf16[512,1536]{1,0:T(8,128)(2,1)} %bitcast.345, f32[8,24,2,64,64]{4,3,2,1,0:T(8,128)} %bitcast.337), custom_call_target="tpu_custom_call" | custom-call | tf_op jit(solution)/shard_map/soap_in/pallas_call | solution.py:535
  769.2 21.3 %back_scan.1 = (bf16[1024,704]{1,0:T(8,128)(2,1)}, f32[1024,704]{1,0:T(8,128)}, f32[1024,704]{1,0:T(8,128)}, f32[8,704]{1,0:T(8,128)}) custom-call(bf16[1024,2048]{1,0:T(8,128)(2,1)} %all-gather.10.cloned.1.call-done.d_rec, bf16[2048,704]{1,0:T(8,128)(2,1)} %constant_dynamic-update-slice_fusion.7.w_o, f32[1024,704]{1,0:T(8,128)} %get-tuple-element.94.y, ...), custom_call_target="tpu_custom_call" | custom-call | tf_op jit(solution)/shard_map/back_scan/pallas_call | solution.py:331
  791.3 10.0 all-gather.3.ends
  801.3 20.5 %gates_back.1 = (bf16[1024,704]{1,0:T(8,128)(2,1)}, bf16[1024,704]{1,0:T(8,128)(2,1)}, bf16[1024,704]{1,0:T(8,128)(2,1)}, f32[16,704]{1,0:T(8,128)}, f32[8,704]{1,0:T(8,128)}, /*index=5*/f32[8,704]{1,0:T(8,128)}) custom-call(s32[1]{0:T(128)} %bitcast.1.rank, f32[8,2,704]{2,1,0:T(2,128)} %all-gather.3.ends, f32[1024,704]{1,0:T(8,128)} %get-tuple-element.105.g_l, ...), custom_call_target="tpu_custom_call" | custom-call | tf_op jit(solution)/shard_map/gates_back/pallas_call | solution.py:423
  840.6 4.9 fusion.63
  846.8 11.4 %pair_back.1 = bf16[1024,2048]{1,0:T(8,128)(2,1)} custom-call(bf16[1024,704]{1,0:T(8,128)(2,1)} %get-tuple-element.103.left, bf16[1024,704]{1,0:T(8,128)(2,1)} %fusion.117.right, bf16[2,2048,704]{2,1,0:T(8,128)(2,1)} %constant_dynamic-update-slice_fusion.w_in.weights), custom_call_target="tpu_custom_call" | custom-call | tf_op jit(solution)/shard_map/pair_back/pallas_call | solution.py:460
  858.2 3.8 fusion.37
  872.2 3.2 squeeze.196
  877.5 5.2 fusion.60
  896.9 3.8 reshape.654
  907.2 4.0 reshape.648
  915.8 18.4 %reduce-scatter.8.cloned.1.call-done = bf16[256,2048]{1,0:T(8,128)(2,1)} async-done(((bf16[1024,2048]{1,0:T(8,128)(2,1)}), bf16[256,2048]{1,0:T(8,128)(2,1)}) %reduce-scatter.8.cloned.1.call-update) | async-done | bytes 1048592 | tf_op jit(solution)/shard_map/reduce_scatter | solution.py:584
  937.1 4.8 fusion.21
  942.0 6.0 permute_columns.7
  955.1 3.8 reshape.649
  963.6 5.9 permute_columns.6
  984.1 5.5 collective-permute-start.17
  989.6 52.8 %collective-permute-done.18 = bf16[256,2048]{1,0:T(8,128)(2,1)} collective-permute-done((bf16[256,2048]{1,0:T(8,128)(2,1)}, bf16[256,2048]{1,0:T(8,128)(2,1)}, u32[]{:S(2)}, u32[]{:S(2)}) %collective-permute-start.18) | collective-permute-done | bytes 1048608 | tf_op jit(solution)/shard_map/ppermute | solution.py:612
  1045.8 13.1 %soap_out.2 = (f32[704,256]{1,0:T(8,128)}, f32[704,256]{1,0:T(8,128)}, f32[704,256]{1,0:T(8,128)}) custom-call(f32[704,256]{1,0:T(8,128)} %w.2, f32[704,256]{1,0:T(8,128)} %m.2, f32[704,256]{1,0:T(8,128)} %v.2, bf16[256,704]{1,0:T(8,128)(2,1)} %fusion.95.g, f32[11,4,2,64,64]{4,3,2,1,0:T(8,128)} %q.2), custom_call_target="tpu_custom_call" | custom-call | tf_op jit(solution)/shard_map/soap_out/pallas_call | solution.py:557
  1064.1 8.0 collective-permute-done.19
  1074.7 18.5 %soap_in.2 = (f32[512,704]{1,0:T(8,128)}, f32[512,704]{1,0:T(8,128)}, f32[512,704]{1,0:T(8,128)}) custom-call(f32[512,704]{1,0:T(8,128)} %bitcast.351, f32[512,704]{1,0:T(8,128)} %bitcast.352, f32[512,704]{1,0:T(8,128)} %bitcast.353, bf16[512,704]{1,0:T(8,128)(2,1)} %bitcast.362, f32[8,11,2,64,64]{4,3,2,1,0:T(8,128)} %bitcast.354), custom_call_target="tpu_custom_call" | custom-call | tf_op jit(solution)/shard_map/soap_in/pallas_call | solution.py:535
  1103.7 12.0 %psum.7 = f32[2,256]{1,0:T(2,128)S(1)} all-reduce(f32[2,256]{1,0:T(2,128)S(1)} %fusion.137), channel_id=1, replica_groups=mesh['tok'=8,'mlp'=4] {'mlp'}, use_global_device_ids=true, to_apply=%region_11.12 | all-reduce | flops 512 | bytes 4096 | tf_op jit(solution)/shard_map/psum | solution.py:860
  1124.8 6.7 convert_element_type.394
  (454 shorter events, 278.2 us)
Async XLA Ops:
  7.2 366.0 %reduce-scatter.4.cloned.1.call-start = ((), (), s32[]{:S(2)}) async-start(), calls=%async_computation.3 | async-start | bytes 5242880 | tf_op jit(solution)/shard_map/reduce_scatter | solution.py:584
  8.7 12.3 %collective-permute-start.1 = (bf16[2,256,704]{1,2,0:T(8,128)(2,1)S(1)}, bf16[2,256,704]{1,2,0:T(8,128)(2,1)S(1)}, u32[]{:S(2)}, u32[]{:S(2)}) collective-permute-start(bf16[2,256,704]{1,2,0:T(8,128)(2,1)S(1)} %convert_element_type.365), channel_id=1, source_target_pairs={{0,16},{4,12},{8,24},{12,4},{16,0},{20,28},{24,8},{28,20},{1,17},{... | collective-permute-start | bytes 2162696 | tf_op jit(solution)/shard_map/ppermute | solution.py:623
  21.1 19.1 %collective-permute-start.2 = (bf16[2,512,704]{1,2,0:T(8,128)(2,1)S(1)}, bf16[2,512,704]{1,2,0:T(8,128)(2,1)S(1)}, u32[]{:S(2)}, u32[]{:S(2)}) collective-permute-start(bf16[2,512,704]{1,2,0:T(8,128)(2,1)S(1)} %pad_maximum_fusion.5), channel_id=1, source_target_pairs={{0,8},{4,20},{8,0},{12,28},{16,24},{20,4},{24,16},{28,12},{1,9},{5... | collective-permute-start | bytes 4325384 | tf_op jit(solution)/shard_map/ppermute | solution.py:623
  42.2 9.7 collective-permute-start.3
  61.6 7.8 collective-permute-start.5
  73.3 11.6 %collective-permute-start.6 = (bf16[512,704]{0,1:T(8,128)(2,1)}, bf16[512,704]{0,1:T(8,128)(2,1)}, u32[]{:S(2)}, u32[]{:S(2)}) collective-permute-start(bf16[512,704]{0,1:T(8,128)(2,1)} %copy.291), channel_id=1, source_target_pairs={{0,8},{4,20},{8,0},{12,28},{16,24},{20,4},{24,16},{28,12},{1,9},{5... | collective-permute-start | bytes 2162696 | tf_op jit(solution)/shard_map/ppermute | solution.py:623
  87.3 5.2 collective-permute-start.7
  102.3 40.5 %copy-start.43 = (f32[2,4,3872]{2,1,0:T(4,128)S(1)}, f32[2,4,3872]{2,1,0:T(4,128)}, u32[]{:S(2)}) copy-start(f32[2,4,3872]{2,1,0:T(4,128)} %param.53) | copy-start | bytes 371716
  102.3 40.6 %copy-start.69 = (f32[2,256]{1,0:T(2,128)S(1)}, f32[2,256]{1,0:T(2,128)}, u32[]{:S(2)}) copy-start(f32[2,256]{1,0:T(2,128)} %param.59) | copy-start | bytes 6148
  102.3 40.7 %copy-start.66 = (f32[8,88]{1,0:T(8,128)S(1)}, f32[8,88]{1,0:T(8,128)}, u32[]{:S(2)}) copy-start(f32[8,88]{1,0:T(8,128)} %param.56) | copy-start | bytes 8452
  102.3 28.9 %collective-permute-start.8 = (bf16[256,4608]{1,0:T(8,128)(2,1)S(1)}, bf16[256,4608]{1,0:T(8,128)(2,1)S(1)}, u32[]{:S(2)}, u32[]{:S(2)}) collective-permute-start(bf16[256,4608]{1,0:T(8,128)(2,1)S(1)} %pad_maximum_fusion.3), channel_id=1, source_target_pairs={{0,16},{4,12},{8,24},{12,4},{16,0},{20,28},{24,8},{28,20},{1,17},{... | collective-permute-start | bytes 7077896 | tf_op jit(solution)/shard_map/ppermute | solution.py:623
  134.2 61.7 %copy-start.70 = (s32[8]{0:T(128)S(1)}, s32[8]{0:T(128)}, u32[]{:S(2)}) copy-start(s32[8]{0:T(128)} %param.35) | copy-start | bytes 100
  134.2 128.0 %collective-permute-start.9 = (bf16[512,4608]{1,0:T(8,128)(2,1)}, bf16[512,4608]{1,0:T(8,128)(2,1)}, u32[]{:S(2)}, u32[]{:S(2)}) collective-permute-start(bf16[512,4608]{1,0:T(8,128)(2,1)} %pad_maximum_fusion.1), channel_id=1, source_target_pairs={{0,8},{4,20},{8,0},{12,28},{16,24},{20,4},{24,16},{28,12},{1,9},{5... | collective-permute-start | bytes 14155784 | tf_op jit(solution)/shard_map/ppermute | solution.py:623
  136.8 80.2 %collective-permute-start.4 = (s32[16]{0:T(128)}, s32[16]{0:T(128)}, u32[]{:S(2)}, u32[]{:S(2)}) collective-permute-start(s32[16]{0:T(128)} %slice.512), channel_id=1, source_target_pairs={{0,4},{4,8},{8,12},{12,16},{16,20},{20,24},{24,28},{1,5},{5,9},{9,... | collective-permute-start | bytes 200 | tf_op jit(solution)/shard_map/ppermute | solution.py:786
  140.0 86.2 %collective-permute-start = (bf16[16,2048]{1,0:T(8,128)(2,1)}, bf16[16,2048]{1,0:T(8,128)(2,1)}, u32[]{:S(2)}, u32[]{:S(2)}) collective-permute-start(bf16[16,2048]{1,0:T(8,128)(2,1)} %slice.495), channel_id=1, source_target_pairs={{0,4},{4,8},{8,12},{12,16},{16,20},{20,24},{24,28},{1,5},{5,9},{9,... | collective-permute-start | bytes 196616 | tf_op jit(solution)/shard_map/ppermute | solution.py:784
  214.0 48.2 %copy-start.62 = (s32[1024]{0:T(1024)}, s32[1024]{0:T(1024)S(1)}, u32[]{:S(2)}) copy-start(s32[1024]{0:T(1024)S(1)} %pad_clamp_fusion) | copy-start | bytes 12292
  228.3 34.0 %copy-start.2 = (bf16[256,4608]{1,0:T(8,128)(2,1)S(1)}, bf16[256,4608]{1,0:T(8,128)(2,1)}, u32[]{:S(2)}) copy-start(bf16[256,4608]{1,0:T(8,128)(2,1)} %copy-done.1) | copy-start | bytes 7077892
  268.8 109.1 %collective-permute-start.10 = (bf16[1024,4608]{1,0:T(8,128)(2,1)}, bf16[1024,4608]{1,0:T(8,128)(2,1)}, u32[]{:S(2)}, u32[]{:S(2)}) collective-permute-start(bf16[1024,4608]{1,0:T(8,128)(2,1)} %pad_maximum_fusion), channel_id=1, source_target_pairs={{0,4},{4,0},{8,12},{12,8},{16,20},{20,16},{24,28},{28,24},{1,5},{5... | collective-permute-start | bytes 28311560 | tf_op jit(solution)/shard_map/ppermute | solution.py:623
  296.0 163.3 %all-gather.8.cloned.1.call-start = ((), (), s32[]{:S(2)}) async-start(), calls=%async_computation.4 | async-start | bytes 5242880 | tf_op jit(solution)/shard_map/all_gather | solution.py:580
  375.2 246.4 %copy-start.53 = (f32[256]{0:T(256)}, f32[256]{0:T(256)S(1)}, u32[]{:S(2)}) copy-start(f32[256]{0:T(256)S(1)} %get-tuple-element.360) | copy-start | bytes 3076
  375.3 246.4 %copy-start.57 = (f32[256]{0:T(256)}, f32[256]{0:T(256)S(1)}, u32[]{:S(2)}) copy-start(f32[256]{0:T(256)S(1)} %get-tuple-element.359) | copy-start | bytes 3076
  377.9 241.1 %reduce-scatter.6.cloned.1.call-start = ((), (), s32[]{:S(2)}) async-start(), calls=%async_computation.5 | async-start | bytes 5242880 | tf_op jit(solution)/shard_map/reduce_scatter | solution.py:584
  493.2 276.0 %all-gather.10.cloned.1.call-start = ((), (), s32[]{:S(2)}) async-start(), calls=%async_computation.6 | async-start | bytes 5242880 | tf_op jit(solution)/shard_map/all_gather | solution.py:580
  501.2 123.8 %collective-permute-start.39 = (bf16[1024,1536]{1,0:T(8,128)(2,1)}, bf16[1024,1536]{1,0:T(8,128)(2,1)}, u32[]{:S(2)}, u32[]{:S(2)}) collective-permute-start(bf16[1024,1536]{1,0:T(8,128)(2,1)} %convolution_convert_fusion), channel_id=1, source_target_pairs={{0,4},{4,0},{8,12},{12,8},{16,20},{20,16},{24,28},{28,24},{1,5},{5... | collective-permute-start | bytes 9437192 | tf_op jit(solution)/shard_map/ppermute | solution.py:623
  506.2 125.6 %collective-permute-start.33 = (bf16[1024,1536]{1,0:T(8,128)(2,1)}, bf16[1024,1536]{1,0:T(8,128)(2,1)}, u32[]{:S(2)}, u32[]{:S(2)}) collective-permute-start(bf16[1024,1536]{1,0:T(8,128)(2,1)} %convolution_convert_fusion.2), channel_id=1, source_target_pairs={{0,4},{4,0},{8,12},{12,8},{16,20},{20,16},{24,28},{28,24},{1,5},{5... | collective-permute-start | bytes 9437192 | tf_op jit(solution)/shard_map/ppermute | solution.py:623
  511.5 124.5 %collective-permute-start.36 = (bf16[1024,1536]{1,0:T(8,128)(2,1)}, bf16[1024,1536]{1,0:T(8,128)(2,1)}, u32[]{:S(2)}, u32[]{:S(2)}) collective-permute-start(bf16[1024,1536]{1,0:T(8,128)(2,1)} %convolution_convert_fusion.1), channel_id=1, source_target_pairs={{0,4},{4,0},{8,12},{12,8},{16,20},{20,16},{24,28},{28,24},{1,5},{5... | collective-permute-start | bytes 9437192 | tf_op jit(solution)/shard_map/ppermute | solution.py:623
  520.4 89.8 %copy-start.4 = (bf16[1024,2048]{1,0:T(8,128)(2,1)}, bf16[1024,2048]{1,0:T(8,128)(2,1)S(1)}, u32[]{:S(2)}) copy-start(bf16[1024,2048]{1,0:T(8,128)(2,1)S(1)} %fusion.4) | copy-start | bytes 12582916
  520.7 47.6 %collective-permute-start.11 = (bf16[256,2048]{1,0:T(8,128)(2,1)S(1)}, bf16[256,2048]{1,0:T(8,128)(2,1)S(1)}, u32[]{:S(2)}, u32[]{:S(2)}) collective-permute-start(bf16[256,2048]{1,0:T(8,128)(2,1)S(1)} %get-tuple-element.298), channel_id=1, source_target_pairs={{0,1},{4,5},{8,9},{12,13},{16,17},{20,21},{24,25},{28,29}} | collective-permute-start | bytes 3145736 | tf_op jit(solution)/shard_map/ppermute | solution.py:598
  522.3 57.6 %collective-permute-start.14 = (bf16[256,2048]{1,0:T(8,128)(2,1)S(1)}, bf16[256,2048]{1,0:T(8,128)(2,1)S(1)}, u32[]{:S(2)}, u32[]{:S(2)}) collective-permute-start(bf16[256,2048]{1,0:T(8,128)(2,1)S(1)} %get-tuple-element.299), channel_id=1, source_target_pairs={{3,2},{7,6},{11,10},{15,14},{19,18},{23,22},{27,26},{31,30}} | collective-permute-start | bytes 3145736 | tf_op jit(solution)/shard_map/ppermute | solution.py:599
  568.7 41.5 %collective-permute-start.12 = (bf16[256,2048]{1,0:T(8,128)(2,1)S(1)}, bf16[256,2048]{1,0:T(8,128)(2,1)S(1)}, u32[]{:S(2)}, u32[]{:S(2)}) collective-permute-start(bf16[256,2048]{1,0:T(8,128)(2,1)S(1)} %add_convert_fusion.4), channel_id=1, source_target_pairs={{0,1},{1,2},{4,5},{5,6},{8,9},{9,10},{12,13},{13,14},{16,17},{17,1... | collective-permute-start | bytes 3145736 | tf_op jit(solution)/shard_map/ppermute | solution.py:598
  612.3 28.3 %collective-permute-start.15 = (bf16[256,2048]{1,0:T(8,128)(2,1)}, bf16[256,2048]{1,0:T(8,128)(2,1)S(1)}, u32[]{:S(2)}, u32[]{:S(2)}) collective-permute-start(bf16[256,2048]{1,0:T(8,128)(2,1)} %get-tuple-element.297), channel_id=1, source_target_pairs={{2,1},{3,2},{6,5},{7,6},{10,9},{11,10},{14,13},{15,14},{18,17},{19... | collective-permute-start | bytes 3145736 | tf_op jit(solution)/shard_map/ppermute | solution.py:599
  613.1 324.0 %collective-permute-start.13 = (bf16[256,2048]{1,0:T(8,128)(2,1)}, bf16[256,2048]{1,0:T(8,128)(2,1)}, u32[]{:S(2)}, u32[]{:S(2)}) collective-permute-start(bf16[256,2048]{1,0:T(8,128)(2,1)} %get-tuple-element.296), channel_id=1, source_target_pairs={{0,1},{1,2},{2,3},{4,5},{5,6},{6,7},{8,9},{9,10},{10,11},{12,13},{... | collective-permute-start | bytes 3145736 | tf_op jit(solution)/shard_map/ppermute | solution.py:598
  625.0 309.2 %reduce-scatter.8.cloned.1.call-start = ((), (), s32[]{:S(2)}) async-start(), calls=%async_computation.7 | async-start | bytes 5242880 | tf_op jit(solution)/shard_map/reduce_scatter | solution.py:584
  630.0 20.6 %collective-permute-start.40 = (bf16[2,256,1536]{2,1,0:T(8,128)(2,1)S(1)}, bf16[2,256,1536]{2,1,0:T(8,128)(2,1)}, u32[]{:S(2)}, u32[]{:S(2)}) collective-permute-start(bf16[2,256,1536]{2,1,0:T(8,128)(2,1)S(1)} %get-tuple-element.300), channel_id=1, source_target_pairs={{0,8},{4,20},{8,0},{12,28},{16,24},{20,4},{24,16},{28,12},{1,9},{5... | collective-permute-start | bytes 4718600 | tf_op jit(solution)/shard_map/ppermute | solution.py:623
  635.4 40.4 %collective-permute-start.34 = (bf16[2,256,1536]{2,1,0:T(8,128)(2,1)S(1)}, bf16[2,256,1536]{2,1,0:T(8,128)(2,1)S(1)}, u32[]{:S(2)}, u32[]{:S(2)}) collective-permute-start(bf16[2,256,1536]{2,1,0:T(8,128)(2,1)S(1)} %get-tuple-element.302), channel_id=1, source_target_pairs={{0,8},{4,20},{8,0},{12,28},{16,24},{20,4},{24,16},{28,12},{1,9},{5... | collective-permute-start | bytes 4718600 | tf_op jit(solution)/shard_map/ppermute | solution.py:623
  639.3 61.8 %copy-start.9 = (f32[2,256,1536]{2,1,0:T(8,128)}, f32[2,256,1536]{2,1,0:T(8,128)S(1)}, u32[]{:S(2)}) copy-start(f32[2,256,1536]{2,1,0:T(8,128)S(1)} %get-tuple-element.305) | copy-start | bytes 9437188
  639.3 61.7 %collective-permute-start.37 = (bf16[2,256,1536]{2,1,0:T(8,128)(2,1)S(1)}, bf16[2,256,1536]{2,1,0:T(8,128)(2,1)S(1)}, u32[]{:S(2)}, u32[]{:S(2)}) collective-permute-start(bf16[2,256,1536]{2,1,0:T(8,128)(2,1)S(1)} %get-tuple-element.304), channel_id=1, source_target_pairs={{0,8},{4,20},{8,0},{12,28},{16,24},{20,4},{24,16},{28,12},{1,9},{5... | collective-permute-start | bytes 4718600 | tf_op jit(solution)/shard_map/ppermute | solution.py:623
  643.2 293.9 %collective-permute-start.16 = (bf16[256,2048]{1,0:T(8,128)(2,1)}, bf16[256,2048]{1,0:T(8,128)(2,1)}, u32[]{:S(2)}, u32[]{:S(2)}) collective-permute-start(bf16[256,2048]{1,0:T(8,128)(2,1)} %add_convert_fusion.1), channel_id=1, source_target_pairs={{1,0},{2,1},{3,2},{5,4},{6,5},{7,6},{9,8},{10,9},{11,10},{13,12},{... | collective-permute-start | bytes 3145736 | tf_op jit(solution)/shard_map/ppermute | solution.py:599
  652.0 52.1 %collective-permute-start.41 = (bf16[256,1536]{1,0:T(8,128)(2,1)S(1)}, bf16[256,1536]{1,0:T(8,128)(2,1)S(1)}, u32[]{:S(2)}, u32[]{:S(2)}) collective-permute-start(bf16[256,1536]{1,0:T(8,128)(2,1)S(1)} %fusion.91), channel_id=1, source_target_pairs={{0,16},{4,12},{8,24},{12,4},{16,0},{20,28},{24,8},{28,20},{1,17},{... | collective-permute-start | bytes 2359304 | tf_op jit(solution)/shard_map/ppermute | solution.py:623
  676.0 54.1 %collective-permute-start.35 = (bf16[256,1536]{1,0:T(8,128)(2,1)S(1)}, bf16[256,1536]{1,0:T(8,128)(2,1)}, u32[]{:S(2)}, u32[]{:S(2)}) collective-permute-start(bf16[256,1536]{1,0:T(8,128)(2,1)S(1)} %fusion.88), channel_id=1, source_target_pairs={{0,16},{4,12},{8,24},{12,4},{16,0},{20,28},{24,8},{28,20},{1,17},{... | collective-permute-start | bytes 2359304 | tf_op jit(solution)/shard_map/ppermute | solution.py:623
  702.3 29.4 %collective-permute-start.38 = (bf16[256,1536]{1,0:T(8,128)(2,1)}, bf16[256,1536]{1,0:T(8,128)(2,1)}, u32[]{:S(2)}, u32[]{:S(2)}) collective-permute-start(bf16[256,1536]{1,0:T(8,128)(2,1)} %fusion.90), channel_id=1, source_target_pairs={{0,16},{4,12},{8,24},{12,4},{16,0},{20,28},{24,8},{28,20},{1,17},{... | collective-permute-start | bytes 2359304 | tf_op jit(solution)/shard_map/ppermute | solution.py:623
  823.2 22.2 %collective-permute-start.23 = (f32[3,704]{1,0:T(4,128)}, f32[3,704]{1,0:T(4,128)}, u32[]{:S(2)}, u32[]{:S(2)}) collective-permute-start(f32[3,704]{1,0:T(4,128)} %pad_maximum_fusion.10), channel_id=1, source_target_pairs={{4,0},{8,4},{12,8},{16,12},{20,16},{24,20},{28,24},{5,1},{9,5},{13... | collective-permute-start | bytes 25352 | tf_op jit(solution)/shard_map/ppermute | solution.py:835
  839.4 43.2 %collective-permute-start.42 = (f32[4,8,3960]{2,1,0:T(8,128)}, f32[4,8,3960]{2,1,0:T(8,128)}, u32[]{:S(2)}, u32[]{:S(2)}) collective-permute-start(f32[4,8,3960]{2,1,0:T(8,128)} %slice.731), channel_id=1, source_target_pairs={{0,4},{4,0},{8,12},{12,8},{16,20},{20,16},{24,28},{28,24},{1,5},{5... | collective-permute-start | bytes 1520648 | tf_op jit(solution)/shard_map/ppermute | solution.py:623
  845.4 51.4 %collective-permute-start.30 = (bf16[1024,704]{0,1:T(8,128)(2,1)}, bf16[1024,704]{0,1:T(8,128)(2,1)}, u32[]{:S(2)}, u32[]{:S(2)}) collective-permute-start(bf16[1024,704]{0,1:T(8,128)(2,1)} %fusion.63), channel_id=1, source_target_pairs={{0,4},{4,0},{8,12},{12,8},{16,20},{20,16},{24,28},{28,24},{1,5},{5... | collective-permute-start | bytes 4325384 | tf_op jit(solution)/shard_map/ppermute | solution.py:623
  858.2 266.6 %all-gather.12.cloned.1.call-start = ((), (), s32[]{:S(2)}) async-start(), calls=%async_computation.8 | async-start | bytes 5242880 | tf_op jit(solution)/shard_map/all_gather | solution.py:580
  877.0 30.2 %collective-permute-start.24 = (bf16[1024,704]{0,1:T(8,128)(2,1)}, bf16[1024,704]{0,1:T(8,128)(2,1)}, u32[]{:S(2)}, u32[]{:S(2)}) collective-permute-start(bf16[1024,704]{0,1:T(8,128)(2,1)} %fusion.57), channel_id=1, source_target_pairs={{0,4},{4,0},{8,12},{12,8},{16,20},{20,16},{24,28},{28,24},{1,5},{5... | collective-permute-start | bytes 4325384 | tf_op jit(solution)/shard_map/ppermute | solution.py:623
  883.7 6.3 collective-permute-start.43
  890.2 5.0 collective-permute-start.44
  895.2 59.9 %collective-permute-start.27 = (bf16[1024,704]{0,1:T(8,128)(2,1)}, bf16[1024,704]{0,1:T(8,128)(2,1)}, u32[]{:S(2)}, u32[]{:S(2)}) collective-permute-start(bf16[1024,704]{0,1:T(8,128)(2,1)} %fusion.60), channel_id=1, source_target_pairs={{0,4},{4,0},{8,12},{12,8},{16,20},{20,16},{24,28},{28,24},{1,5},{5... | collective-permute-start | bytes 4325384 | tf_op jit(solution)/shard_map/ppermute | solution.py:623
  905.7 66.4 %collective-permute-start.31 = (bf16[2,256,704]{1,2,0:T(8,128)(2,1)}, bf16[2,256,704]{1,2,0:T(8,128)(2,1)}, u32[]{:S(2)}, u32[]{:S(2)}) collective-permute-start(bf16[2,256,704]{1,2,0:T(8,128)(2,1)} %copy.314), channel_id=1, source_target_pairs={{0,8},{4,20},{8,0},{12,28},{16,24},{20,4},{24,16},{28,12},{1,9},{5... | collective-permute-start | bytes 2162696 | tf_op jit(solution)/shard_map/ppermute | solution.py:623
  915.2 62.5 %collective-permute-start.25 = (bf16[2,256,704]{1,2,0:T(8,128)(2,1)}, bf16[2,256,704]{1,2,0:T(8,128)(2,1)}, u32[]{:S(2)}, u32[]{:S(2)}) collective-permute-start(bf16[2,256,704]{1,2,0:T(8,128)(2,1)} %fusion.79), channel_id=1, source_target_pairs={{0,8},{4,20},{8,0},{12,28},{16,24},{20,4},{24,16},{28,12},{1,9},{5... | collective-permute-start | bytes 2162696 | tf_op jit(solution)/shard_map/ppermute | solution.py:623
  962.1 19.1 %collective-permute-start.28 = (bf16[2,256,704]{1,2,0:T(8,128)(2,1)}, bf16[2,256,704]{1,2,0:T(8,128)(2,1)}, u32[]{:S(2)}, u32[]{:S(2)}) collective-permute-start(bf16[2,256,704]{1,2,0:T(8,128)(2,1)} %fusion.78), channel_id=1, source_target_pairs={{0,8},{4,20},{8,0},{12,28},{16,24},{20,4},{24,16},{28,12},{1,9},{5... | collective-permute-start | bytes 2162696 | tf_op jit(solution)/shard_map/ppermute | solution.py:623
  969.5 72.9 %collective-permute-start.18 = (bf16[256,2048]{1,0:T(8,128)(2,1)}, bf16[256,2048]{1,0:T(8,128)(2,1)}, u32[]{:S(2)}, u32[]{:S(2)}) collective-permute-start(bf16[256,2048]{1,0:T(8,128)(2,1)} %permute_columns.6), channel_id=1, source_target_pairs={{1,0},{2,1},{3,2},{5,4},{6,5},{7,6},{9,8},{10,9},{11,10},{13,12},{... | collective-permute-start | bytes 3145736 | tf_op jit(solution)/shard_map/ppermute | solution.py:612
  976.2 67.7 %collective-permute-start.32 = (bf16[256,704]{1,0:T(8,128)(2,1)}, bf16[256,704]{1,0:T(8,128)(2,1)}, u32[]{:S(2)}, u32[]{:S(2)}) collective-permute-start(bf16[256,704]{1,0:T(8,128)(2,1)} %fusion.104), channel_id=1, source_target_pairs={{0,16},{4,12},{8,24},{12,4},{16,0},{20,28},{24,8},{28,20},{1,17},{... | collective-permute-start | bytes 1081352 | tf_op jit(solution)/shard_map/ppermute | solution.py:623
  980.7 78.3 %collective-permute-start.26 = (bf16[256,704]{0,1:T(8,128)(2,1)}, bf16[256,704]{0,1:T(8,128)(2,1)S(1)}, u32[]{:S(2)}, u32[]{:S(2)}) collective-permute-start(bf16[256,704]{0,1:T(8,128)(2,1)} %fusion.106), channel_id=1, source_target_pairs={{0,16},{4,12},{8,24},{12,4},{16,0},{20,28},{24,8},{28,20},{1,17},{... | collective-permute-start | bytes 1081352 | tf_op jit(solution)/shard_map/ppermute | solution.py:623
  982.5 77.7 %collective-permute-start.29 = (bf16[256,704]{0,1:T(8,128)(2,1)S(1)}, bf16[256,704]{0,1:T(8,128)(2,1)S(1)}, u32[]{:S(2)}, u32[]{:S(2)}) collective-permute-start(bf16[256,704]{0,1:T(8,128)(2,1)S(1)} %fusion.108), channel_id=1, source_target_pairs={{0,16},{4,12},{8,24},{12,4},{16,0},{20,28},{24,8},{28,20},{1,17},{... | collective-permute-start | bytes 1081352 | tf_op jit(solution)/shard_map/ppermute | solution.py:623
  984.1 78.3 %collective-permute-start.17 = (bf16[256,2048]{1,0:T(8,128)(2,1)}, bf16[256,2048]{1,0:T(8,128)(2,1)}, u32[]{:S(2)}, u32[]{:S(2)}) collective-permute-start(bf16[256,2048]{1,0:T(8,128)(2,1)} %permute_columns.6), channel_id=1, source_target_pairs={{0,1},{1,2},{2,3},{4,5},{5,6},{6,7},{8,9},{9,10},{10,11},{12,13},{... | collective-permute-start | bytes 3145736 | tf_op jit(solution)/shard_map/ppermute | solution.py:611
  1042.4 29.7 %collective-permute-start.19 = (bf16[256,2048]{1,0:T(8,128)(2,1)}, bf16[256,2048]{1,0:T(8,128)(2,1)}, u32[]{:S(2)}, u32[]{:S(2)}) collective-permute-start(bf16[256,2048]{1,0:T(8,128)(2,1)} %collective-permute-done.18), channel_id=1, source_target_pairs={{1,0},{2,1},{5,4},{6,5},{9,8},{10,9},{13,12},{14,13},{17,16},{18,1... | collective-permute-start | bytes 3145736 | tf_op jit(solution)/shard_map/ppermute | solution.py:612
  1060.2 1.3 collective-permute-start.45
  1061.5 37.9 %collective-permute-start.46 = (f32[2,1,2,256]{3,2,0,1:T(2,128)S(1)}, f32[2,1,2,256]{3,2,0,1:T(2,128)S(1)}, u32[]{:S(2)}, u32[]{:S(2)}) collective-permute-start(f32[2,1,2,256]{3,2,0,1:T(2,128)S(1)} %get-tuple-element.343), channel_id=1, source_target_pairs={{0,8},{4,20},{8,0},{12,28},{16,24},{20,4},{24,16},{28,12},{1,9},{5... | collective-permute-start | bytes 12296 | tf_op jit(solution)/shard_map/ppermute | solution.py:623
  1062.4 53.8 %collective-permute-start.21 = (bf16[256,2048]{1,0:T(8,128)(2,1)}, bf16[256,2048]{1,0:T(8,128)(2,1)}, u32[]{:S(2)}, u32[]{:S(2)}) collective-permute-start(bf16[256,2048]{1,0:T(8,128)(2,1)} %collective-permute-done.17), channel_id=1, source_target_pairs={{1,2},{2,3},{5,6},{6,7},{9,10},{10,11},{13,14},{14,15},{17,18},{18... | collective-permute-start | bytes 3145736 | tf_op jit(solution)/shard_map/ppermute | solution.py:611
  1072.1 44.8 %collective-permute-start.20 = (bf16[256,2048]{1,0:T(8,128)(2,1)}, bf16[256,2048]{1,0:T(8,128)(2,1)}, u32[]{:S(2)}, u32[]{:S(2)}) collective-permute-start(bf16[256,2048]{1,0:T(8,128)(2,1)} %collective-permute-done.19), channel_id=1, source_target_pairs={{1,0},{5,4},{9,8},{13,12},{17,16},{21,20},{25,24},{29,28}} | collective-permute-start | bytes 3145736 | tf_op jit(solution)/shard_map/ppermute | solution.py:612
  1099.4 4.2 collective-permute-start.47
  1116.2 5.9 collective-permute-start.22
  (67 other events, 537.1 us)
Sparse Core Ops, SparseCore 0:
  296.1 77.0 reduce-scatter.3
  378.0 81.2 all-gather.7
  493.3 109.9 reduce-scatter.5
  625.1 106.3 all-gather.9
  858.3 75.8 reduce-scatter.7
  948.1 106.5 all-gather.11

commit v2 on v1

v2 whole, which is shorter than its diff:
```python
import functools

import jax
import jax.numpy as jnp
from jax import lax
from jax.experimental import pallas as pl
from jax.experimental.pallas import tpu as pltpu
from jax.sharding import PartitionSpec as P

BW = 176
CONV = 4
TILE = 64
STEP = 7
HALO = 16
LANES = 128

norm_eps = 1e-06
learn_rate = 0.02
beta_first = 0.9
beta_second = 0.999
adam_eps = 1e-08
decay_rate = 0.1

f32 = jnp.float32
bf16 = jnp.bfloat16


def params(limit=56):
    return pltpu.CompilerParams(
        dimension_semantics=("arbitrary",), vmem_limit_bytes=limit * 1024 * 1024
    )


def whole(shape):
    return pl.BlockSpec(shape, lambda *_: (0,) * len(shape), pipeline_mode=pl.Buffered(1))


def nn(left, right):
    return lax.dot_general(left, right, (((1,), (0,)), ((), ())), preferred_element_type=f32)


def nt(left, right):
    return lax.dot_general(left, right, (((1,), (1,)), ((), ())), preferred_element_type=f32)


def tn(left, right):
    return lax.dot_general(left, right, (((0,), (0,)), ((), ())), preferred_element_type=f32)


def gelu_both(value):
    square = value * value
    bent = jnp.tanh(0.7978845608028654 * (value + 0.044715 * value * square))
    half = 0.5 * (1.0 + bent)
    slope = half + (0.5 * 0.7978845608028654) * value * (1.0 - bent * bent) * (
        1.0 + (3.0 * 0.044715) * square
    )
    return value * half, slope


def gelu_tanh(value):
    return (
        0.5
        * value
        * (1.0 + jnp.tanh(0.7978845608028654 * (value + 0.044715 * value * value * value)))
    )


def one_less_square(log_value, value):
    twice = 2.0 * log_value
    series = 1.0 + twice * (1.0 / 6.0)
    for order in range(5, 1, -1):
        series = 1.0 + twice * series * (1.0 / order)
    return jnp.where(twice > -0.0625, -twice * series, 1.0 - value * value)


def gate_terms(pre_decay, pre_input, slope, live):
    rate = 0.5 + 0.5 * jnp.tanh(0.5 * pre_decay)
    gate = 0.5 + 0.5 * jnp.tanh(0.5 * pre_input)
    log_decay = slope * rate
    raw = jnp.exp(log_decay)
    root = jnp.sqrt(one_less_square(log_decay, raw))
    mult = (1.0 - live) + live * root
    return rate, gate, raw, root, mult


def put_tiles(buffer, value):
    width = value.shape[1]
    for tile in range(pl.cdiv(width, LANES)):
        size = min(LANES, width - tile * LANES)
        buffer[tile, :, :size] = value[:, tile * LANES : tile * LANES + size]


def scan_tiles(first, second, carry_state, carry_prod, out_state, out_prod, width, backward):
    tiles, rows, _ = first.shape
    span = rows // 8

    def body(step, held):
        row = (span - 1 - step) if backward else step
        at = pl.ds(row, 8, stride=span)
        states, prods = [], []
        for tile in range(tiles):
            state, prod = held[0][tile], held[1][tile]
            decay = first[tile, at, :]
            drive = second[tile, at, :]
            if backward:
                total = drive + state
                second[tile, at, :] = total
                first[tile, at, :] = prod
                states.append(decay * total)
                prods.append(decay * prod)
            else:
                states.append(decay * state + drive)
                prods.append(decay * prod)
                second[tile, at, :] = states[-1]
                first[tile, at, :] = prods[-1]
        return tuple(states), tuple(prods)

    states, prods = lax.fori_loop(
        0,
        span,
        body,
        (
            (jnp.zeros((8, LANES), f32),) * tiles,
            (jnp.ones((8, LANES), f32),) * tiles,
        ),
        unroll=4,
    )
    for tile in range(tiles):
        size = min(LANES, width - tile * LANES)
        cols = slice(tile * LANES, tile * LANES + size)
        wide = slice(tile * LANES, (tile + 1) * LANES)
        state, prod = states[tile], prods[tile]
        state_in = carry_state[0:1, wide]
        prod_in = carry_prod[0:1, wide]
        for chunk in range(7, -1, -1) if backward else range(8):
            at = slice(chunk * span, (chunk + 1) * span)
            local = first[tile, at, :]
            out_state[at, cols] = (second[tile, at, :] + local * state_in)[:, :size]
            out_prod[at, cols] = (local * prod_in)[:, :size]
            state_in = state[chunk : chunk + 1] + prod[chunk : chunk + 1] * state_in
            prod_in = prod[chunk : chunk + 1] * prod_in
        carry_state[0:1, wide] = state_in
        carry_prod[0:1, wide] = prod_in


def piece_spot(array, piece):
    return (0, 2, 1, 3)[piece] if array == 1 else piece


def load_pieces(arrays, which, held, sem, along):
    copies = []
    for number, array in enumerate(arrays):
        size = array.shape[1 + along]
        base = sum(before.shape[0] for before in arrays[:number])
        if base * size >= held.shape[along]:
            break
        for piece in range(array.shape[0]):
            at = pl.ds((base + piece_spot(number, piece)) * size, size)
            for slot, kind in enumerate(which):
                place = held.at[slot, at, :] if along == 1 else held.at[slot, :, at]
                copies.append(pltpu.make_async_copy(array.at[piece, kind], place, sem))
    for copy in copies:
        copy.start()
    for copy in copies:
        copy.wait()


def any_spec():
    return pl.BlockSpec(memory_space=pl.ANY)


def rms_low(value, gain):
    return (
        value * lax.rsqrt(jnp.mean(value * value, axis=-1, keepdims=True) + norm_eps) * gain
    ).astype(bf16)


def front_kernel(
    tok, halo, gain, w_own, w_far, w_a, w_i, vec, mask,
    xn_o, y_o, u_o, uh_o, xc_o, pa_o, pi_o, a_o, h_o, p_o, end_o,
    ubuf, abuf, bbuf, car_s, car_p, w_in, sem,
):
    step = pl.program_id(0)
    rows = tok.shape[0]
    width = y_o.shape[1]

    @pl.when(step == 0)
    def _():
        load_pieces((w_own, w_far), (0, 1), w_in, sem, 2)
        low = nt(rms_low(halo[...].astype(f32), gain[...]), w_in[1]).astype(bf16)
        uh_o[...] = low
        ubuf[0:HALO, :] = low.astype(f32)
        car_s[...] = jnp.zeros_like(car_s)
        car_p[...] = jnp.ones_like(car_p)

    xn = rms_low(tok[...].astype(f32), gain[...])
    xn_o[...] = xn
    y_o[...] = nt(xn, w_in[0])
    u_low = nt(xn, w_in[1]).astype(bf16)
    u_o[...] = u_low
    u_now = u_low.astype(f32)
    ubuf[HALO : HALO + rows, :] = u_now
    conv = vec[CONV : CONV + 1] + vec[0:1] * u_now
    for back in range(1, CONV):
        conv = conv + vec[back : back + 1] * mask[:, back : back + 1] * ubuf[
            HALO - back : HALO - back + rows, :
        ]
    ubuf[0:HALO, :] = u_now[rows - HALO :, :]
    conv_low = conv.astype(bf16)
    xc_o[...] = conv_low
    pre_decay = nn(conv_low, w_a[...]) + vec[CONV + 2 : CONV + 3]
    pre_input = nn(conv_low, w_i[...]) + vec[CONV + 3 : CONV + 4]
    pa_o[...] = pre_decay
    pi_o[...] = pre_input
    live = mask[:, 0:1]
    _, gate, raw, _, mult = gate_terms(pre_decay, pre_input, vec[CONV + 1 : CONV + 2], live)
    decay = raw * live
    a_o[...] = decay
    put_tiles(abuf, decay)
    put_tiles(bbuf, gate * conv_low.astype(f32) * mult)
    scan_tiles(abuf, bbuf, car_s, car_p, h_o, p_o, width, False)
    end_o[0:1, :] = car_s[0:1, :width]
    end_o[1:2, :] = car_p[0:1, :width]


def front(tok, halo, gain, weights, w_a, w_i, vec, mask, rows):
    count, model = tok.shape
    width = weights[0].shape[2]
    tiles = pl.cdiv(width, LANES)
    row = lambda size: pl.BlockSpec((rows, size), lambda i: (i, 0))
    like = lambda size, kind: jax.ShapeDtypeStruct((count, size), kind)
    return pl.pallas_call(
        front_kernel,
        grid=(count // rows,),
        in_specs=[
            row(model), whole(halo.shape), whole(gain.shape), any_spec(), any_spec(),
            whole(w_a.shape), whole(w_i.shape), whole(vec.shape), row(mask.shape[1]),
        ],
        out_specs=[
            row(model), row(width), row(width), whole((HALO, width)), row(width), row(width),
            row(width), row(width), row(width), row(width), whole((8, width)),
        ],
        out_shape=[
            like(model, bf16), like(width, f32), like(width, bf16),
            jax.ShapeDtypeStruct((HALO, width), bf16), like(width, bf16), like(width, f32),
            like(width, f32), like(width, f32), like(width, f32), like(width, f32),
            jax.ShapeDtypeStruct((8, width), f32),
        ],
        scratch_shapes=[
            pltpu.VMEM((HALO + rows, width), f32),
            pltpu.VMEM((tiles, rows, LANES), f32),
            pltpu.VMEM((tiles, rows, LANES), f32),
            pltpu.VMEM((8, tiles * LANES), f32),
            pltpu.VMEM((8, tiles * LANES), f32),
            pltpu.VMEM((2, width, model), bf16),
            pltpu.SemaphoreType.DMA,
        ],
        compiler_params=params(),
        name="front",
    )(tok, halo, gain, *weights, w_a, w_i, vec, mask)


def state_kernel(
    rank, ends, h_l, p_l, y, w_own, w_far, h_o, hp_o, o_o, part_o, hin, hbuf, w_o, sem
):
    step = pl.program_id(0)
    rows = h_l.shape[0]

    @pl.when(step == 0)
    def _():
        load_pieces((w_own, w_far), (2,), w_o, sem, 2)

        def fold(at, held):
            return jnp.where(at < rank[0], ends[at, 0:1, :] + ends[at, 1:2, :] * held, held)

        start = lax.fori_loop(0, ends.shape[0], fold, jnp.zeros((1, h_l.shape[1]), f32))
        hin[0:1, :] = start
        hbuf[7:8, :] = start

    state = h_l[...] + p_l[...] * hin[0:1, :]
    h_o[...] = state
    hbuf[8 : 8 + rows, :] = state
    hp_o[...] = hbuf[7 : 7 + rows, :]
    hbuf[7:8, :] = state[rows - 1 :, :]
    mixed = (state * gelu_tanh(y[...])).astype(bf16)
    o_o[...] = mixed
    part_o[...] = nn(mixed, w_o[0]).astype(bf16)


def finish_state(rank, ends, h_l, p_l, y, weights, model, rows):
    count, width = h_l.shape
    row = lambda size: pl.BlockSpec((rows, size), lambda i: (i, 0))
    like = lambda size, kind: jax.ShapeDtypeStruct((count, size), kind)
    return pl.pallas_call(
        state_kernel,
        grid=(count // rows,),
        in_specs=[
            pl.BlockSpec(memory_space=pltpu.SMEM), whole(ends.shape), row(width), row(width),
            row(width), any_spec(), any_spec(),
        ],
        out_specs=[row(width), row(width), row(width), row(model)],
        out_shape=[like(width, f32), like(width, f32), like(width, bf16), like(model, bf16)],
        scratch_shapes=[
            pltpu.VMEM((8, width), f32),
            pltpu.VMEM((8 + rows, width), f32),
            pltpu.VMEM((1, width, model), bf16),
            pltpu.SemaphoreType.DMA,
        ],
        compiler_params=params(),
        name="finish_state",
    )(rank, ends, h_l, p_l, y, *weights)


def mlp_kernel(xn, dhid, w_own, w_far, hm_o, dg_o, du_o, part_o, held, sem):
    @pl.when(pl.program_id(0) == 0)
    def _():
        load_pieces((w_own, w_far), (0, 1), held, sem, 1)

    w_g, w_u = held.at[0], held.at[1]
    hidden = dhid.shape[1]
    piece = hidden // 3
    for at in range(0, hidden, piece):
        cols = slice(at, at + piece)
        z_gate = nn(xn[...], w_g[:, cols])
        z_up = nn(xn[...], w_u[:, cols])
        d_hid = dhid[:, cols]
        act, slope = gelu_both(z_gate)
        hm_o[:, cols] = (act * z_up).astype(bf16)
        dg_o[:, cols] = (d_hid * z_up * slope).astype(bf16)
        du_o[:, cols] = (d_hid * act).astype(bf16)
    model = xn.shape[1]
    piece = model // 4
    for at in range(0, model, piece):
        cols = slice(at, at + piece)
        part_o[:, cols] = (nt(dg_o[...], w_g[cols, :]) + nt(du_o[...], w_u[cols, :])).astype(bf16)


def mlp(xn, dhid, weights, rows):
    count, model = xn.shape
    hidden = dhid.shape[1]
    row = lambda size: pl.BlockSpec((rows, size), lambda i: (i, 0))
    like = lambda size: jax.ShapeDtypeStruct((count, size), bf16)
    return pl.pallas_call(
        mlp_kernel,
        grid=(count // rows,),
        in_specs=[row(model), row(hidden), any_spec(), any_spec()],
        out_specs=[row(hidden), row(hidden), row(hidden), row(model)],
        out_shape=[like(hidden), like(hidden), like(hidden), like(model)],
        scratch_shapes=[pltpu.VMEM((2, model, hidden), bf16), pltpu.SemaphoreType.DMA],
        compiler_params=params(),
        name="mlp",
    )(xn, dhid, *weights)


def back_kernel(
    d_rec, w_own, w_far, y, h, a, dy_o, g_o, p_o, end_o, abuf, bbuf, car_s, car_p, w_o, sem
):
    step = pl.program_id(0)
    width = y.shape[1]

    @pl.when(step == 0)
    def _():
        load_pieces((w_own, w_far), (2,), w_o, sem, 2)
        car_s[...] = jnp.zeros_like(car_s)
        car_p[...] = jnp.ones_like(car_p)

    d_mixed = nt(d_rec[...], w_o[0])
    act, slope = gelu_both(y[...])
    dy_o[...] = (d_mixed * h[...] * slope).astype(bf16)
    put_tiles(abuf, a[...])
    put_tiles(bbuf, d_mixed * act)
    scan_tiles(abuf, bbuf, car_s, car_p, g_o, p_o, width, True)
    end_o[0:1, :] = car_s[0:1, :width]
    end_o[1:2, :] = car_p[0:1, :width]


def back_scan(d_rec, weights, y, h, a, rows):
    count, model = d_rec.shape
    width = y.shape[1]
    tiles = pl.cdiv(width, LANES)
    steps = count // rows
    row = lambda size: pl.BlockSpec((rows, size), lambda i: (steps - 1 - i, 0))
    like = lambda size, kind: jax.ShapeDtypeStruct((count, size), kind)
    return pl.pallas_call(
        back_kernel,
        grid=(steps,),
        in_specs=[row(model), any_spec(), any_spec(), row(width), row(width), row(width)],
        out_specs=[row(width), row(width), row(width), whole((8, width))],
        out_shape=[
            like(width, bf16), like(width, f32), like(width, f32),
            jax.ShapeDtypeStruct((8, width), f32),
        ],
        scratch_shapes=[
            pltpu.VMEM((tiles, rows, LANES), f32),
            pltpu.VMEM((tiles, rows, LANES), f32),
            pltpu.VMEM((8, tiles * LANES), f32),
            pltpu.VMEM((8, tiles * LANES), f32),
            pltpu.VMEM((1, width, model), bf16),
            pltpu.SemaphoreType.DMA,
        ],
        compiler_params=params(),
        name="back_scan",
    )(d_rec, *weights, y, h, a)


def gates_kernel(
    rank, ends, g_l, p_l, pa, pi, xc, hp, u, u_prev, u_halo, mask, w_a, w_i, vec,
    dpa_o, dpi_o, du_o, tail_o, spill_o, sum_o,
    qin, dbuf, ubuf,
):
    step = pl.program_id(0)
    steps = pl.num_programs(0)
    rows, width = g_l.shape

    @pl.when(step == 0)
    def _():
        count = ends.shape[0]

        def fold(back, held):
            at = count - 1 - back
            return jnp.where(at > rank[0], ends[at, 0:1, :] + ends[at, 1:2, :] * held, held)

        qin[0:1, :] = lax.fori_loop(0, count, fold, jnp.zeros((1, width), f32))
        sum_o[...] = jnp.zeros_like(sum_o)
        dbuf[rows : rows + 8, :] = jnp.zeros((8, width), f32)

    grad = g_l[...] + p_l[...] * qin[0:1, :]
    live = mask[:, 0:1]
    slope = vec[CONV + 1 : CONV + 2]
    rate, gate, raw, root, mult = gate_terms(pa[...], pi[...], slope, live)
    conv = xc[...].astype(f32)
    d_mult = grad * gate * conv
    d_log = live * (grad * hp[...] * raw - d_mult * (raw * raw) / root)
    d_log_rate = d_log * rate
    d_conv = grad * gate * mult
    d_pa = (d_log_rate * slope * (1.0 - rate)).astype(bf16)
    d_pi = (grad * mult * conv * gate * (1.0 - gate)).astype(bf16)
    dpa_o[...] = d_pa
    dpi_o[...] = d_pi
    d_conv = d_conv + nt(d_pa, w_a[...]) + nt(d_pi, w_i[...])
    total = lambda value: jnp.sum(value, axis=0, keepdims=True)
    u_now = u[...].astype(f32)
    before = jnp.where(step == steps - 1, u_halo[...], u_prev[...]).astype(f32)
    ubuf[0:HALO, :] = before
    ubuf[HALO : HALO + rows, :] = u_now
    dbuf[0:rows, :] = d_conv
    sum_o[0:1, :] += total(d_conv * u_now)
    d_u = vec[0:1] * d_conv
    for back in range(1, CONV):
        sum_o[back : back + 1, :] += total(
            d_conv * mask[:, back : back + 1] * ubuf[HALO - back : HALO - back + rows, :]
        )
        d_u = d_u + vec[back : back + 1] * mask[:, CONV - 1 + back : CONV + back] * dbuf[
            back : back + rows, :
        ]
    sum_o[CONV : CONV + 1, :] += total(d_conv)
    sum_o[CONV + 1 : CONV + 2, :] += total(d_log_rate)
    sum_o[CONV + 2 : CONV + 3, :] += total(d_pa.astype(f32))
    sum_o[CONV + 3 : CONV + 4, :] += total(d_pi.astype(f32))
    du_o[...] = d_u.astype(bf16)

    @pl.when(step == 0)
    def _():
        tail_o[...] = d_u[rows - HALO :, :]

    head = d_conv[0:8, :]
    dbuf[rows : rows + 8, :] = head

    @pl.when(step == steps - 1)
    def _():
        spill_o[...] = jnp.zeros_like(spill_o)
        for ahead in range(CONV - 1, 0, -1):
            row = 0.0
            for back in range(ahead, CONV):
                at = back - ahead
                row = row + vec[back : back + 1] * mask[at : at + 1, back : back + 1] * d_conv[
                    at : at + 1, :
                ]
            spill_o[HALO - ahead : HALO - ahead + 1, :] = row


def gates_back(rank, ends, g_l, p_l, pa, pi, xc, hp, u, u_halo, mask, w_a, w_i, vec, rows):
    count, width = g_l.shape
    steps = count // rows
    at = lambda i: steps - 1 - i
    row = lambda size: pl.BlockSpec((rows, size), lambda i: (at(i), 0))
    like = lambda size, kind: jax.ShapeDtypeStruct((count, size), kind)
    per = rows // HALO
    return pl.pallas_call(
        gates_kernel,
        grid=(steps,),
        in_specs=[
            pl.BlockSpec(memory_space=pltpu.SMEM), whole(ends.shape), row(width), row(width),
            row(width), row(width), row(width), row(width), row(width),
            pl.BlockSpec((HALO, width), lambda i: (jnp.maximum(at(i) * per - 1, 0), 0)),
            whole(u_halo.shape), row(mask.shape[1]), whole(w_a.shape), whole(w_i.shape),
            whole(vec.shape),
        ],
        out_specs=[
            row(width), row(width), row(width), whole((HALO, width)), whole((HALO, width)),
            whole((8, width)),
        ],
        out_shape=[
            like(width, bf16), like(width, bf16), like(width, bf16),
            jax.ShapeDtypeStruct((HALO, width), f32), jax.ShapeDtypeStruct((HALO, width), f32),
            jax.ShapeDtypeStruct((8, width), f32),
        ],
        scratch_shapes=[
            pltpu.VMEM((8, width), f32),
            pltpu.VMEM((rows + 8, width), f32),
            pltpu.VMEM((HALO + rows, width), f32),
        ],
        compiler_params=params(),
        name="gates_back",
    )(rank, ends, g_l, p_l, pa, pi, xc, hp, u, u, u_halo, mask, w_a, w_i, vec)


def pair_kernel(left, right, tail, more, w_own, w_far, out, right_o, held, sem):
    step = pl.program_id(0)
    rows = left.shape[0]

    @pl.when(step == 0)
    def _():
        load_pieces((w_own, w_far), (0, 1), held, sem, 2)

    right_o[...] = right[...]

    @pl.when(step == pl.num_programs(0) - 1)
    def _():
        right_o[rows - HALO :, :] = (tail[...] + more[...]).astype(bf16)

    out[...] = (nn(left[...], held[0]) + nn(right_o[...], held[1])).astype(bf16)


def pair_back(left, right, tail, more, weights, model, rows):
    count, width = left.shape
    row = lambda size: pl.BlockSpec((rows, size), lambda i: (i, 0))
    return pl.pallas_call(
        pair_kernel,
        grid=(count // rows,),
        in_specs=[
            row(width), row(width), whole(tail.shape), whole(more.shape), any_spec(), any_spec(),
        ],
        out_specs=[row(model), row(width)],
        out_shape=[
            jax.ShapeDtypeStruct((count, model), bf16),
            jax.ShapeDtypeStruct((count, width), bf16),
        ],
        scratch_shapes=[pltpu.VMEM((2, width, model), bf16), pltpu.SemaphoreType.DMA],
        compiler_params=params(),
        name="pair_back",
    )(left, right, tail, more, *weights)


def mask_kernel(ids, out):
    rows = out.shape[0]
    now = ids[HALO : HALO + rows, :]
    same = lambda by: (now == ids[HALO + by : HALO + by + rows, :]).astype(f32)
    out[...] = jnp.zeros_like(out)
    out[:, 0:1] = same(-1)
    for back in range(1, CONV):
        out[:, back : back + 1] = same(-back)
        out[:, CONV - 1 + back : CONV + back] = same(back)


def masks(ids, count):
    return pl.pallas_call(
        mask_kernel,
        out_shape=jax.ShapeDtypeStruct((count, 8), f32),
        compiler_params=pltpu.CompilerParams(vmem_limit_bytes=16 * 1024 * 1024),
        name="masks",
    )(ids)


def moments_step(first, second, grad):
    new_first = beta_first * first + (1.0 - beta_first) * grad
    new_second = beta_second * second + (1.0 - beta_second) * grad * grad
    normal = (
        new_first
        * (1.0 / (1.0 - beta_first**STEP))
        / (jnp.sqrt(new_second * (1.0 / (1.0 - beta_second**STEP))) + adam_eps)
    )
    return new_first, new_second, normal


def soap_tiles(turned, tile_rows, tile_cols, w, m, v, bases, nm, nv, nw):
    side = lax.broadcasted_iota(jnp.int32, (TILE, 2 * TILE), 1) < TILE
    square = (lax.broadcasted_iota(jnp.int32, (2 * TILE, 2 * TILE), 0) < TILE) == (
        lax.broadcasted_iota(jnp.int32, (2 * TILE, 2 * TILE), 1) < TILE
    )
    for i in range(tile_rows):
        for j in range(0, tile_cols, 2):
            rows = slice(i * TILE, (i + 1) * TILE)
            cols = slice(j * TILE, (j + 2) * TILE)
            left_a, right_a = bases(i, j)
            left_b, right_b = bases(i, j + 1)
            lefts = [left_a.astype(bf16), left_b.astype(bf16)]
            both = jnp.concatenate([right_a, right_b], axis=0)
            right = jnp.where(square, jnp.concatenate([both, both], axis=1), 0.0).astype(bf16)
            choose = lambda parts: jnp.where(side, parts[0], parts[1])
            inner = choose([turned(rows, cols, left) for left in lefts]).astype(bf16)
            grad = nn(inner, right)
            new_first, new_second, normal = moments_step(m[rows, cols], v[rows, cols], grad)
            nm[rows, cols] = new_first
            nv[rows, cols] = new_second
            low = normal.astype(bf16)
            outer = choose([nn(left, low) for left in lefts]).astype(bf16)
            master = w[rows, cols]
            nw[rows, cols] = master - learn_rate * (nt(outer, right) + decay_rate * master)


def soap_kernel(turned, swapped, w, m, v, g, q, nm, nv, nw):
    def plain(rows, cols, left):
        return tn(left, g[0, rows, cols])

    def across(rows, cols, left):
        return lax.dot_general(
            left, g[0, cols, rows], (((0,), (1,)), ((), ())), preferred_element_type=f32
        )

    if swapped:
        bases = lambda i, j: (q[0, j, i, 1], q[0, j, i, 0])
    else:
        bases = lambda i, j: (q[0, i, j, 0], q[0, i, j, 1])
    soap_tiles(
        across if turned else plain, w.shape[1] // TILE, w.shape[2] // TILE,
        w.at[0], m.at[0], v.at[0], bases, nm.at[0], nv.at[0], nw.at[0],
    )


def soap(w, m, v, g, q, rows, turned=False, swapped=False):
    group, height, width = w.shape
    if width < 2 * TILE:
        q = jnp.concatenate([q, q], axis=1 if swapped else 2)
        padded = [jnp.concatenate([array, array], axis=2) for array in (w, m, v)]
        g = jnp.concatenate([g, g], axis=1 if turned else 2)
        results = soap(*padded, g, q, rows, turned, swapped)
        return [array[:, :, :width] for array in results]
    row = pl.BlockSpec((1, rows, width), lambda n, i: (n, i, 0))
    out = jax.ShapeDtypeStruct(w.shape, f32)
    if swapped:
        q_block = (1, width // TILE, rows // TILE, 2, TILE, TILE)
        q_at = lambda n, i: (n, 0, i, 0, 0, 0)
    else:
        q_block = (1, rows // TILE, width // TILE, 2, TILE, TILE)
        q_at = lambda n, i: (n, i, 0, 0, 0, 0)
    return pl.pallas_call(
        functools.partial(soap_kernel, turned, swapped),
        grid=(group, height // rows),
        in_specs=[row] * 3
        + [
            pl.BlockSpec((1, width, rows), lambda n, i: (n, 0, i)) if turned else row,
            pl.BlockSpec(q_block, q_at),
        ],
        out_specs=[row] * 3,
        out_shape=[out] * 3,
        compiler_params=pltpu.CompilerParams(
            dimension_semantics=("arbitrary", "arbitrary"), vmem_limit_bytes=56 * 1024 * 1024
        ),
        name="soap",
    )(w, m, v, g, q)


def reorder(array, dim, order):
    shape = array.shape
    parts = order.shape[0]
    reshaped = array.reshape(shape[:dim] + (parts, shape[dim] // parts) + shape[dim + 1 :])
    return jnp.take(reshaped, order, axis=dim, mode="clip").reshape(shape)


def gather_slabs(array):
    return lax.all_gather(array, "mlp", axis=0, tiled=True)


def scatter_slabs(array):
    return lax.psum_scatter(array, "mlp", scatter_dimension=0, tiled=True)


def hop(array, pairs):
    count = lax.axis_size("tok")
    return lax.ppermute(array, "tok", [(i, i ^ pairs[i % 2]) for i in range(count)])


CORE, NEAR, FAR = (1, 1), (2, 4), (4, 2)


def stored_order(parts, rank):
    indices = jnp.arange(parts, dtype=jnp.int32)
    if parts != 8:
        return indices, indices
    near, far = indices // 2 % 2, indices % 2
    spots = rank ^ (
        indices // 4 + jnp.where(rank % 2 == 0, near * 2 + far * 4, near * 4 + far * 2)
    )
    return spots, invert(spots)


def invert(order):
    indices = jnp.arange(order.shape[0], dtype=jnp.int32)
    return jnp.sum(jnp.where(order[None, :] == indices[:, None], indices[None, :], 0), axis=1)


def gather_start(own):
    two = jnp.concatenate([own, hop(own, FAR)], axis=0)
    return jnp.concatenate([two, hop(two, NEAR)], axis=0)


class Sums:
    def __init__(self, keep, send, dim):
        self.keep, self.send, self.dim = keep, send, dim
        self.whole = lax.axis_size("tok") != 8

    def cut(self, array, blocks, at):
        size = array.shape[self.dim] // blocks
        return lax.slice_in_dim(array, at * size, (at + 1) * size, axis=self.dim).astype(f32)

    def mixed(self, at, there):
        return self.cut(self.keep, 4, at) + self.cut(self.got, 4, there)

    def first(self, *before):
        if self.whole:
            return self.send
        self.got = hop(self.send, CORE)
        self.near_send = after(
            jnp.concatenate([self.mixed(2, 1), self.mixed(3, 3)], axis=self.dim).astype(
                self.send.dtype
            ),
            *before,
        )
        return self.near_send

    def second(self, *before):
        if self.whole:
            return self.send
        self.near = hop(self.near_send, NEAR)
        self.far_send = after(
            (self.mixed(1, 2) + self.cut(self.near, 2, 1)).astype(self.send.dtype), *before
        )
        return self.far_send

    def third(self):
        if self.whole:
            both = jnp.concatenate([self.keep.astype(self.send.dtype), self.send], axis=self.dim)
            return lax.psum_scatter(both, "tok", scatter_dimension=self.dim, tiled=True)
        far = hop(self.far_send, FAR)
        return self.mixed(0, 0) + self.cut(self.near, 2, 0) + far.astype(f32)


def sums_of(array):
    half = array.shape[0] // 2
    sums = Sums(array[:half], array[half:], 0)
    sums.first()
    sums.second()
    return sums.third()


def halves(array):
    half = array.shape[1] // 2
    return array[:, :half], array[:, half:]


def grad_rows(left, right):
    keep, send = halves(left)
    return Sums(tn(keep, right), tn(send, right).astype(bf16), 0)


def grad_columns(left, right):
    keep, send = halves(right)
    return Sums(tn(left, keep), tn(left, send).astype(bf16), 1)


def permute_kernel(order, array, out):
    parts = order.shape[0]
    size = array.shape[1] // parts
    for part in range(parts):
        at = pl.multiple_of(order[part] * size, LANES)
        out[:, part * size : (part + 1) * size] = array[:, pl.ds(at, size)]


def permute_columns(array, order):
    parts = order.shape[0]
    count, width = array.shape
    if width // parts % LANES:
        return reorder(array, 1, order)
    rows = min(256, count)
    row = pl.BlockSpec((rows, width), lambda i: (i, 0))
    return pl.pallas_call(
        permute_kernel,
        grid=(count // rows,),
        in_specs=[pl.BlockSpec(memory_space=pltpu.SMEM), row],
        out_specs=row,
        out_shape=jax.ShapeDtypeStruct(array.shape, array.dtype),
        compiler_params=params(),
        name="permute_columns",
    )(order, array)


def settle_kernel(move, order, value, upstream, gain, base, total_o, low_o, sum_o, hold):
    @pl.when(pl.program_id(0) == 0)
    def _():
        sum_o[...] = jnp.zeros_like(sum_o)

    held = value[...].astype(f32)
    grad = upstream[...].astype(f32)
    scale = lax.rsqrt(jnp.mean(held * held, axis=-1, keepdims=True) + norm_eps)
    weighted = grad * gain[...]
    inner = jnp.mean(held * weighted, axis=-1, keepdims=True)
    total = base[...].astype(f32) + (scale * weighted - held * (scale * scale * scale * inner))
    sum_o[0:1, :] += jnp.sum(grad * held * scale, axis=0, keepdims=True)
    total_o[...] = total
    low = total.astype(bf16)
    if not move:
        low_o[...] = low
        return
    hold[...] = low
    parts = order.shape[0]
    size = low.shape[1] // parts
    for part in range(parts):
        at = pl.multiple_of(order[part] * size, LANES)
        low_o[:, part * size : (part + 1) * size] = hold[:, pl.ds(at, size)]


def settle(value, upstream, gain, base, order, move):
    count, model = value.shape
    inside = move and (model // order.shape[0]) % LANES == 0
    rows = min(128, count)
    row = pl.BlockSpec((rows, model), lambda i: (i, 0))
    total, low, sums = pl.pallas_call(
        functools.partial(settle_kernel, inside),
        grid=(count // rows,),
        in_specs=[pl.BlockSpec(memory_space=pltpu.SMEM), row, row, whole(gain.shape), row],
        out_specs=[row, row, whole((8, model))],
        out_shape=[
            jax.ShapeDtypeStruct((count, model), f32),
            jax.ShapeDtypeStruct((count, model), bf16),
            jax.ShapeDtypeStruct((8, model), f32),
        ],
        scratch_shapes=[pltpu.VMEM((rows, model), bf16)],
        compiler_params=params(),
        name="settle",
    )(order, value, upstream, gain, base)
    if move and not inside:
        low = reorder(low, 1, order)
    return total, low, sums[0]


def after(array, *others):
    return lax.optimization_barrier((array,) + others)[0]


def block_diagonal(blocks):
    count, width, _ = blocks.shape
    return jnp.concatenate(
        [
            jnp.pad(blocks[n], ((0, 0), (n * width, (count - 1 - n) * width)))
            for n in range(count)
        ],
        axis=0,
    )


def diagonal_blocks(array, count):
    width = array.shape[0] // count
    return jnp.stack(
        [array[n * width : (n + 1) * width, n * width : (n + 1) * width] for n in range(count)]
    )


def on_device(
    tokens, segment_ids, owner_table, cotangent,
    w_in_rec, m_in_rec, v_in_rec, q_in_rec,
    w_out_rec, m_out_rec, v_out_rec, q_out_rec,
    w_in_mlp, m_in_mlp, v_in_mlp, q_in_mlp,
    w_out_mlp, m_out_mlp, v_out_mlp, q_out_mlp,
    w_gates, m_gates, v_gates, w_rnn, m_rnn, v_rnn, w_gains, m_gains, v_gains,
):
    parts = lax.axis_size("tok")
    rank = lax.axis_index("tok")
    slabs = lax.axis_size("mlp")
    slab = lax.axis_index("mlp")
    count, model = tokens.shape
    length = count * parts
    share = count // slabs
    rows = min(256, count)
    spots, places = stored_order(parts, rank)
    into_local = jnp.take(invert(owner_table), spots, mode="clip")
    from_local = jnp.take(places, owner_table, mode="clip")
    rank_ref = rank.reshape(1).astype(jnp.int32)

    blocks = w_gates.shape[1]
    gate_part = w_gates.shape[2]
    lead = 2 * blocks
    rnn_part = w_rnn.shape[1]
    small = jnp.concatenate(
        [w_gates.reshape(lead, gate_part), w_rnn, w_gains.reshape(lead, -1)], axis=1
    ).astype(bf16)
    if parts == 8:
        small_four = gather_start(small[None])
        small_rest = hop(small_four, CORE)
        small_all = jnp.concatenate(
            [small_four] + [small_rest[p : p + 1] for p in (0, 2, 1, 3)], axis=0
        )
    else:
        small_all = lax.all_gather(small, "tok", axis=0, tiled=False)
    turn = lambda array: jnp.swapaxes(array, 1, 2)
    rec_own = jnp.concatenate([turn(w_in_rec), w_out_rec[None]], axis=0).astype(bf16)[None]
    join = lambda *arrays: jnp.concatenate(arrays, axis=0)
    if parts == 8:
        rec_far = hop(rec_own, FAR)
        rec_two = join(rec_own, rec_far)
        rec_near = hop(rec_two, NEAR)
    gains_all = small_all[:, :, gate_part + rnn_part :].reshape(parts, 2, model // parts)
    gains_f = (
        gains_all
        .transpose(1, 0, 2)
        .reshape(2, model)
        .astype(f32)
    )
    ordered = jnp.take(small_all[:, :, : gate_part + rnn_part], from_local, axis=0, mode="clip")
    gate_mats = ordered[:, :, :gate_part].transpose(1, 0, 2).reshape(2, blocks, BW, BW)
    w_a = block_diagonal(gate_mats[0])
    w_i = block_diagonal(gate_mats[1])
    rnn_f = ordered[:, :, gate_part:].transpose(1, 0, 2).reshape(lead, -1).astype(f32)
    lam = rnn_f[CONV + 1]
    vec = rnn_f.at[CONV + 1].set(-8.0 * jax.nn.softplus(lam))

    tok_s = permute_columns(tokens, into_local)
    cot_s = permute_columns(cotangent, into_local)
    forward_pairs = [(i, i + 1) for i in range(parts - 1)]
    rim = lax.ppermute(tokens[count - HALO :], "tok", forward_pairs)
    halo = permute_columns(rim, into_local)
    rim_ids = lax.ppermute(segment_ids[count - HALO :], "tok", forward_pairs)
    ids = jnp.concatenate(
        [
            jnp.where(rank == 0, -1, rim_ids).astype(f32),
            segment_ids.astype(f32),
            jnp.full((HALO,), -1.0, f32),
        ]
    )
    mask = masks(ids[:, None], count)
    if parts == 8:
        rec_near = after(rec_near, tok_s, halo, mask, w_a, w_i, vec)
        rec_four = join(rec_two, rec_near)
        rec_w = (rec_four, hop(rec_four, CORE))
    else:
        rec_all = lax.all_gather(rec_own[0], "tok", axis=2, tiled=True)[None]
        rec_w = (rec_all, rec_all)

    xn_one, y_pre, u_low, u_halo, conv_low, pre_decay, pre_input, decay, h_loc, p_loc, ends = front(
        tok_s, halo, gains_f[0:1], rec_w, w_a, w_i, vec, mask, rows
    )
    ends_all = lax.all_gather(ends[0:2], "tok", axis=0, tiled=False)
    state, state_prev, mixed, branch = finish_state(
        rank_ref, ends_all, h_loc, p_loc, y_pre, rec_w, model, rows
    )
    own = lambda array: lax.dynamic_slice_in_dim(array, slab * share, share, 0)
    own_tok = own(tok_s)
    second = own_tok.astype(f32) + scatter_slabs(branch).astype(f32)
    second_low = rms_low(second, gains_f[1])
    up_own = after(w_in_mlp.astype(bf16)[None], branch)
    down_own = after(w_out_mlp.astype(bf16)[None], branch)
    if parts == 8:
        down_four = gather_start(down_own)
        down_rest = hop(down_four, CORE)
        down = jnp.concatenate(
            [down_four[p] for p in range(4)] + [down_rest[p] for p in (0, 2, 1, 3)], axis=1
        )
        up_two = join(up_own, hop(after(up_own, down_four), FAR))
        up_near = after(hop(up_two, NEAR), second_low)
        up_four = join(up_two, up_near)
        up_w = (up_four, hop(up_four, CORE))
    else:
        down = lax.all_gather(down_own[0], "tok", axis=1, tiled=True)
        up_all = lax.all_gather(up_own[0], "tok", axis=1, tiled=True)[None]
        up_w = (up_all, up_all)
    cot_s = permute_columns(after(cotangent, branch), into_local)
    d_hidden = nt(cot_s, down)
    xn_two = gather_slabs(second_low)
    hidden, d_gate, d_up, d_branch = mlp(xn_two, d_hidden, up_w, min(512, count))
    d_xn_two = scatter_slabs(d_branch)
    low = lambda array: array.astype(bf16)
    sum_gate = grad_rows(xn_two, d_gate)
    sum_up = grad_rows(xn_two, d_up)
    sum_down = grad_rows(cot_s, hidden)
    branch_two = nn(hidden, down).astype(bf16)
    d_xn_two = after(
        d_xn_two, sum_gate.first(), sum_up.first(), sum_down.first(), branch_two
    )
    sum_gate.second()
    sum_up.second()
    sum_down.second()
    g_in_mlp = jnp.stack([low(sum_gate.third()), low(sum_up.third())])
    g_out_mlp = low(sum_down.third())

    lead_one = lambda *arrays: [array[None] for array in arrays]
    split = lambda height: max(
        n for n in range(2 * TILE, height + 1, 2 * TILE) if height % n == 0 and n <= 512
    )
    in_mlp_new = soap(w_in_mlp, m_in_mlp, v_in_mlp, g_in_mlp, q_in_mlp, TILE)

    d_second, d_second_low, g_gain_two = settle(
        second, d_xn_two, gains_f[1:2], own(cot_s), from_local, False
    )
    d_rec = gather_slabs(d_second_low)
    branch_two = after(branch_two, in_mlp_new[0])
    d_rec = after(d_rec, in_mlp_new[0])
    result_own = second + scatter_slabs(branch_two).astype(f32)
    result_low = permute_columns(result_own.astype(bf16), from_local)
    d_ypre, g_loc, q_loc, ends_back = back_scan(d_rec, rec_w, y_pre, state, decay, rows)
    ends_back_all = lax.all_gather(ends_back[0:2], "tok", axis=0, tiled=False)
    d_pa, d_pi, d_u, d_u_tail, spill, sums = gates_back(
        rank_ref, ends_back_all, g_loc, q_loc, pre_decay, pre_input, conv_low, state_prev,
        u_low, u_halo, mask, w_a, w_i, vec, rows,
    )
    from_next = lax.ppermute(spill, "tok", [(i + 1, i) for i in range(parts - 1)])
    d_pair, d_u = pair_back(d_ypre, d_u, d_u_tail, from_next, rec_w, model, rows)
    d_xn_one = scatter_slabs(d_pair)
    out_mlp_new = soap(
        *lead_one(w_out_mlp, m_out_mlp, v_out_mlp, after(g_out_mlp, d_pair), q_out_mlp),
        split(w_out_mlp.shape[0]), turned=True,
    )
    d_rec, mixed, xn_one, d_ypre, d_u, d_pa, d_pi, conv_low = lax.optimization_barrier(
        (d_rec, mixed, xn_one, d_ypre, d_u, d_pa, d_pi, conv_low, d_pair)
    )[:8]
    sum_out = grad_columns(mixed, d_rec)
    sum_y = grad_columns(d_ypre, xn_one)
    sum_u = grad_columns(d_u, xn_one)
    d_xn_one = after(
        d_xn_one, sum_out.first(), sum_y.first(), sum_u.first(), out_mlp_new[0]
    )
    _, d_input_low, g_gain_one = settle(
        own_tok, d_xn_one, gains_f[0:1], d_second, from_local, True
    )
    d_input = gather_slabs(d_input_low)
    sum_out.second()
    sum_y.second()
    sum_u.second()
    g_out_rec = low(sum_out.third())
    g_in_rec = jnp.stack([low(sum_y.third()), low(sum_u.third())])
    result = gather_slabs(after(result_low, d_input_low))

    g_gates = jnp.stack(
        [
            diagonal_blocks(tn(conv_low, d_pa), blocks),
            diagonal_blocks(tn(conv_low, d_pi), blocks),
        ]
    )
    g_rnn = sums.at[CONV + 1].multiply(-8.0 * jax.nn.sigmoid(lam))
    g_small = jnp.concatenate(
        [g_gates.reshape(lead, parts, gate_part), g_rnn.reshape(lead, parts, rnn_part)], axis=2
    ).transpose(1, 0, 2)
    g_small = jnp.take(g_small, into_local, axis=0, mode="clip")
    sum_small = sums_of(g_small)[0]
    sum_gates = sum_small[:, :gate_part].reshape(w_gates.shape)
    sum_rnn = sum_small[:, gate_part:]
    g_gains = jnp.stack([g_gain_one, g_gain_two]).reshape(2, parts, -1).transpose(1, 0, 2)
    sum_gains = lax.psum(sums_of(g_gains)[0], "mlp")

    out_rec_new = soap(
        *lead_one(w_out_rec, m_out_rec, v_out_rec, g_out_rec, q_out_rec), w_out_rec.shape[0]
    )
    in_rec_new = soap(
        turn(w_in_rec), turn(m_in_rec), turn(v_in_rec), g_in_rec, q_in_rec, w_in_rec.shape[2],
        swapped=True,
    )
    out_mlp_new = [array[0] for array in out_mlp_new]
    out_rec_new = [array[0] for array in out_rec_new]
    in_rec_new = [turn(array) for array in in_rec_new]
    gates_m, gates_v, gates_n = moments_step(m_gates, v_gates, sum_gates)
    gates_w = w_gates - learn_rate * (gates_n + decay_rate * w_gates)
    rnn_m, rnn_v, _ = moments_step(m_rnn, v_rnn, sum_rnn)
    gains_m, gains_v, _ = moments_step(m_gains, v_gains, sum_gains)
    d_input = after(
        d_input, in_rec_new[0], out_rec_new[0], gates_w, rnn_m
    ).astype(f32)
    return (
        result, d_input,
        in_rec_new[0], in_rec_new[1], in_rec_new[2],
        out_rec_new[0], out_rec_new[1], out_rec_new[2],
        in_mlp_new[0], in_mlp_new[1], in_mlp_new[2],
        out_mlp_new[0], out_mlp_new[1], out_mlp_new[2],
        gates_m, gates_v, gates_w, rnn_m, rnn_v, gains_m, gains_v,
    )


def solution(mesh):
    in_specs = (
        P("tok", None),
        P("tok"),
        P(),
        P("tok", None),
        P(None, "tok", "mlp"),
        P(None, "tok", "mlp"),
        P(None, "tok", "mlp"),
        P(None, "tok", "mlp", None, None, None),
        P("mlp", "tok"),
        P("mlp", "tok"),
        P("mlp", "tok"),
        P("mlp", "tok", None, None, None),
        P(None, "tok", "mlp"),
        P(None, "tok", "mlp"),
        P(None, "tok", "mlp"),
        P(None, "tok", "mlp", None, None, None),
        P("mlp", "tok"),
        P("mlp", "tok"),
        P("mlp", "tok"),
        P("mlp", "tok", None, None, None),
        P(None, "mlp", "tok"),
        P(None, "mlp", "tok"),
        P(None, "mlp", "tok"),
        P(None, ("mlp", "tok")),
        P(None, ("mlp", "tok")),
        P(None, ("mlp", "tok")),
        P(None, "tok"),
        P(None, "tok"),
        P(None, "tok"),
    )
    out_specs = (
        P("tok", None),
        P("tok", None),
        P(None, "tok", "mlp"),
        P(None, "tok", "mlp"),
        P(None, "tok", "mlp"),
        P("mlp", "tok"),
        P("mlp", "tok"),
        P("mlp", "tok"),
        P(None, "tok", "mlp"),
        P(None, "tok", "mlp"),
        P(None, "tok", "mlp"),
        P("mlp", "tok"),
        P("mlp", "tok"),
        P("mlp", "tok"),
        P(None, "mlp", "tok"),
        P(None, "mlp", "tok"),
        P(None, "mlp", "tok"),
        P(None, ("mlp", "tok")),
        P(None, ("mlp", "tok")),
        P(None, "tok"),
        P(None, "tok"),
    )
    return jax.shard_map(
        on_device, mesh=mesh, in_specs=in_specs, out_specs=out_specs, check_vma=False
    )
```

time: 1160 us -> 934 us (0.81); the launches traced: 1140 us -> 927 us
  local copies, waits for them, and re-layouts: 168 us -> 55.9 us
  blocking collectives: 90 us -> 33.2 us
  other arithmetic: 116 us -> 77.2 us
  waiting for transfers between devices: 358 us -> 384 us
  starting transfers between devices: 71.7 us -> 47.2 us
    ppermute x13 -> x1, waiting for transfers between devices: 122 us -> 2.03 us  [on_device(): lax.ppermute(spill, 'tok', [(i + 1, i) for i in range(parts - 1)])]
    ppermute x33 -> x36, waiting for transfers between devices: 120 us -> 193 us  [hop(): lax.ppermute(array, 'tok', [(i, i ^ pairs[i % 2]) for i in range(count)])]
    all_gather x3 -> x4, waiting for transfers between devices: 47.1 us -> 103 us  [gather_slabs(): return lax.all_gather(array, 'mlp', axis=0, tiled=True)]
    all_gather x1 -> x0, blocking collectives: 52.6 us -> none  [on_device(): small_all = lax.all_gather(small, 'tok', axis=0, tiled=False)]
    unnamed x192 -> x140, local copies, waits for them, and re-layouts: 72.6 us -> 33.3 us
    slice x20 -> x5, local copies, waits for them, and re-layouts: 36.5 us -> 2.34 us  [the longest x2 1.69 us: settle(): return (total, low, sums[0])]
    ppermute x13 -> x1, starting transfers between devices: 29.4 us -> 1.29 us  [on_device(): lax.ppermute(spill, 'tok', [(i + 1, i) for i in range(parts - 1)])]
    convert_element_type x22 -> x11, other arithmetic: 47 us -> 19 us  [the longest x6 8.79 us: second(): (self.mixed(1, 2) + self.cut(self.near, 2, 1)).astype(self.send.dtype)]
  transfers between devices with their start and end apart: 54 -> 47, of which waited for: 17 -> 26; matrix products, arithmetic and copies ran while one was open for 27% -> 18% of each run, Pallas kernels for 19% -> 11%
where the time goes in v2:
time: 934 us; the launch traced here: 927 us
  waiting for transfers between devices  384 us (41%)
  Pallas kernels  240 us (26%)
  other arithmetic  77.2 us (8%)
  matrix products  73.8 us (8%)
  local copies, waits for them, and re-layouts  55.9 us (6%)
  starting transfers between devices  47.2 us (5%)
  blocking collectives  33.2 us (4%)
  between operations  15.4 us (2%)
    ppermute x36, waiting for transfers between devices, hop(): lax.ppermute(array, 'tok', [(i, i ^ pairs[i % 2]) for i in range(count)])  193 us
    all_gather x4, waiting for transfers between devices, gather_slabs(): return lax.all_gather(array, 'mlp', axis=0, tiled=True)  103 us
    reduce_scatter x4, waiting for transfers between devices, scatter_slabs(): return lax.psum_scatter(array, 'mlp', scatter_dimension=0, tiled=True)  85.6 us
    pallas_call x4, Pallas kernels, soap(): pl.pallas_call(functools.partial(soap_kernel, turned, swapped), grid=(gro...  85.2 us
    dot_general x14, matrix products, tn(): lax.dot_general(left, right, (((0,), (0,)), ((), ())), preferred_element_...  56.6 us
    ppermute x36, starting transfers between devices, hop(): lax.ppermute(array, 'tok', [(i, i ^ pairs[i % 2]) for i in range(count)])  41.1 us
    pallas_call x1, Pallas kernels, mlp(): pl.pallas_call(mlp_kernel, grid=(count // rows,), in_specs=[row(model), r...  36.2 us
    pallas_call x1, Pallas kernels, front(): pl.pallas_call(front_kernel, grid=(count // rows,), in_specs=[row(model),...  33.8 us
  transfers between devices with their start and end apart: 47, of which 26 were waited for; matrix products, arithmetic and copies ran while one was open for 18% of the time, Pallas kernels for 11%

profile of v2, /device:TPU:0, one launch (start us, length us, event | category | flops | bytes accessed | tf_op | source)
XLA Modules:
  0.0 927.3 jit_solution(9428133251029858180)
XLA Ops:
  9.9 3.0 collective-permute-start.1
  24.3 4.9 permute_columns.4.tok
  30.8 5.1 collective-permute-start.2
  52.5 6.1 fusion.63
  58.5 14.8 %collective-permute-done.5 = bf16[2,3,704,256]{3,2,1,0:T(8,128)(2,1)} collective-permute-done((bf16[2,3,704,256]{3,2,1,0:T(8,128)(2,1)}, bf16[2,3,704,256]{3,2,1,0:T(8,128)(2,1)}, u32[]{:S(2)}, u32[]{:S(2)}) %collective-permute-start.5) | collective-permute-done | bytes 2162720 | tf_op jit(solution)/shard_map/ppermute | solution.py:681
  73.3 3.5 pad_maximum_fusion.w_own
  78.7 5.8 collective-permute-done.7.w_far
  84.5 33.8 %front.1 = (bf16[1024,2048]{1,0:T(8,128)(2,1)}, f32[1024,704]{1,0:T(8,128)}, bf16[1024,704]{1,0:T(8,128)(2,1)}, bf16[16,704]{1,0:T(8,128)(2,1)}, bf16[1024,704]{...) custom-call(bf16[1024,2048]{1,0:T(8,128)(2,1)} %permute_columns.4.to, ...), custom_call_target="tpu_custom_call" | custom-call | tf_op jit(solution)/shard_map/front/pallas_call | solution.py:232
  119.1 11.7 %all-gather.2.ends = f32[8,2,704]{2,1,0:T(2,128)} all-gather(f32[1,2,704]{2,1,0:T(2,128)S(1)} %slice_bitcast_fusion.16), channel_id=2, replica_groups=mesh['tok'=8,'mlp'=4] {'tok'}, dimensions={0}, use_global_device_ids=true | all-gather | bytes 50688 | tf_op jit(solution)/shard_map/all_gather | solution.py:952
  130.7 11.6 %finish_state.1 = (f32[1024,704]{1,0:T(8,128)}, f32[1024,704]{1,0:T(8,128)}, bf16[1024,704]{1,0:T(8,128)(2,1)}, bf16[1024,2048]{1,0:T(8,128)(2,1)}) custom-call(s32[1]{0:T(128)} %bitcast.1.rank, f32[8,2,704]{2,1,0:T(2,128)} %all-gather.2.ends, f32[1024,704]{1,0:T(8,128)} %get-tuple-element.116.h_l, f32[1024,704]{1,0:T(8,128)} %get-tuple-element.117.p_l, ...), custom_call_target="tpu_custom_call" | custom-call | tf_op jit(solution)/shard_map/finish_state/pallas_call | solution.py:294
  144.5 11.4 %collective-permute-done.8 = bf16[1,1536,256]{2,1,0:T(8,128)(2,1)S(1)} collective-permute-done((bf16[1,1536,256]{2,1,0:T(8,128)(2,1)S(1)}, bf16[1,1536,256]{2,1,0:T(8,128)(2,1)S(1)}, u32[]{:S(2)}, u32[]{:S(2)}) %collective-permute-start.8) | collective-permute-done | bytes 786464 | tf_op jit(solution)/shard_map/ppermute | solution.py:681
  158.8 17.8 %collective-permute-done.9 = bf16[2,1536,256]{2,1,0:T(8,128)(2,1)S(1)} collective-permute-done((bf16[2,1536,256]{2,1,0:T(8,128)(2,1)S(1)}, bf16[2,1536,256]{2,1,0:T(8,128)(2,1)S(1)}, u32[]{:S(2)}, u32[]{:S(2)}) %collective-permute-start.9) | collective-permute-done | bytes 1572896 | tf_op jit(solution)/shard_map/ppermute | solution.py:681
  179.5 19.8 %collective-permute-done.11 = bf16[1,2,256,1536]{3,2,1,0:T(8,128)(2,1)S(1)} collective-permute-done((bf16[1,2,256,1536]{3,2,1,0:T(8,128)(2,1)S(1)}, bf16[1,2,256,1536]{3,2,1,0:T(8,128)(2,1)S(1)}, u32[]{:S(2)}, u32[]{:S(2)}) %collective-permute-start.11) | collective-permute-done | bytes 1572896 | tf_op jit(solution)/shard_map/ppermute | solution.py:681
  202.1 5.0 permute_columns.6
  210.3 9.3 %reduce-scatter.5.cloned.1.call-done = bf16[256,2048]{1,0:T(8,128)(2,1)} async-done(((bf16[1024,2048]{1,0:T(8,128)(2,1)}), bf16[256,2048]{1,0:T(8,128)(2,1)}) %reduce-scatter.5.cloned.1.call-update) | async-done | bytes 1048592 | tf_op jit(solution)/shard_map/reduce_scatter | solution.py:676
  219.7 3.3 convert_add_fusion
  225.0 14.1 %collective-permute-done.12 = bf16[2,2,256,1536]{3,2,1,0:T(8,128)(2,1)} collective-permute-done((bf16[2,2,256,1536]{3,2,1,0:T(8,128)(2,1)}, bf16[2,2,256,1536]{3,2,1,0:T(8,128)(2,1)}, u32[]{:S(2)}, u32[]{:S(2)}) %collective-permute-start.12) | collective-permute-done | bytes 3145760 | tf_op jit(solution)/shard_map/ppermute | solution.py:681
  239.1 3.7 constant_dynamic-update-slice_fusion.6.w_own
  250.1 2.7 copy-done.33
  252.8 9.0 fusion.117.dhid
  261.8 44.5 %all-gather.9.cloned.1.call-done.xn = bf16[1024,2048]{1,0:T(8,128)(2,1)} async-done(((bf16[256,2048]{1,0:T(8,128)(2,1)}), bf16[1024,2048]{1,0:T(8,128)(2,1)}) %all-gather.9.cloned.1.call-update) | async-done | bytes 4194320 | tf_op jit(solution)/shard_map/all_gather | solution.py:672
  306.4 36.2 %mlp.1 = (bf16[1024,1536]{1,0:T(8,128)(2,1)}, bf16[1024,1536]{1,0:T(8,128)(2,1)}, bf16[1024,1536]{1,0:T(8,128)(2,1)}, bf16[1024,2048]{1,0:T(8,128)(2,1)}) custom-call(bf16[1024,2048]{1,0:T(8,128)(2,1)} %all-gather.9.cloned.1.call-done.xn, f32[1024,1536]{1,0:T(8,128)} %fusion.117.dhid, bf16[4,2,256,1536]{3,2,1,0:T(8,128)(2,1)} %constant_dynamic-update-slice_fusion.6.w_own, ...), custom_call_target="tpu_custom_call" | custom-call | tf_op jit(solution)/shard_map/mlp/pallas_call | solution.py:343
  342.6 6.9 convolution_convert_fusion.2
  349.6 7.8 convolution_convert_fusion.3
  358.0 4.8 convolution_convert_fusion.1
  362.8 5.3 fusion.7
  368.2 5.4 fusion.15
  373.5 5.4 fusion.17
  378.9 8.2 convolution_convert_fusion
  387.2 3.0 fusion.50
  392.0 2.7 fusion.57
  398.0 27.1 %reduce-scatter.9.cloned.1.call-done.upstream = bf16[256,2048]{1,0:T(8,128)(2,1)} async-done(((bf16[1024,2048]{1,0:T(8,128)(2,1)}), bf16[256,2048]{1,0:T(8,128)(2,1)}) %reduce-scatter.9.cloned.1.call-update) | async-done | bytes 1048592 | tf_op jit(solution)/shard_map/reduce_scatter | solution.py:676
  425.2 4.2 settle.2
  431.9 18.6 %collective-permute-done.18 = bf16[512,1536]{1,0:T(8,128)(2,1)S(1)} collective-permute-done((bf16[512,1536]{1,0:T(8,128)(2,1)}, bf16[512,1536]{1,0:T(8,128)(2,1)S(1)}, u32[]{:S(2)}, u32[]{:S(2)}) %collective-permute-start.18) | collective-permute-done | bytes 1572896 | tf_op jit(solution)/shard_map/ppermute | solution.py:681
  454.0 21.7 %collective-permute-done.15 = bf16[512,1536]{1,0:T(8,128)(2,1)S(1)} collective-permute-done((bf16[512,1536]{1,0:T(8,128)(2,1)}, bf16[512,1536]{1,0:T(8,128)(2,1)S(1)}, u32[]{:S(2)}, u32[]{:S(2)}) %collective-permute-start.15) | collective-permute-done | bytes 1572896 | tf_op jit(solution)/shard_map/ppermute | solution.py:681
  481.3 8.5 collective-permute-done.16
  493.0 33.3 %soap.4 = (f32[2,256,1536]{2,1,0:T(8,128)}, f32[2,256,1536]{2,1,0:T(8,128)}, f32[2,256,1536]{2,1,0:T(8,128)}) custom-call(f32[2,256,1536]{2,1,0:T(8,128)} %w.1, f32[2,256,1536]{2,1,0:T(8,128)} %m.1, f32[2,256,1536]{2,1,0:T(8,128)} %v.1, bf16[2,256,1536]{2,1,0:T(8,128)(2,1)} %pad_maximum_fusion.6.g, f32[2,4,24,2,64,64]{5,4,3,2,1,0:T(8,128)} %q.2), custom_call_target="tpu_custom_call" | custom-call | tf_op jit(solution)/shard_map/soap/pallas_call | solution.py:647
  526.4 19.6 %back_scan.1 = (bf16[1024,704]{1,0:T(8,128)(2,1)}, f32[1024,704]{1,0:T(8,128)}, f32[1024,704]{1,0:T(8,128)}, f32[8,704]{1,0:T(8,128)}) custom-call(bf16[1024,2048]{1,0:T(8,128)(2,1)} %all-gather.11.cloned.1.call-done.d_rec, bf16[4,3,704,256]{3,2,1,0:T(8,128)(2,1)} %pad_maximum_fusion.w_own, bf16[4,3,704,256]{3,2,1,0:T(8,128)(2,1)} %collective-permute-done.7.w_far, ...), custom_call_target="tpu_custom_call" | custom-call | tf_op jit(solution)/shard_map/back_scan/pallas_call | solution.py:384
  546.7 10.1 %all-gather.3.ends = f32[8,2,704]{2,1,0:T(2,128)} all-gather(f32[1,2,704]{2,1,0:T(2,128)S(1)} %slice_bitcast_fusion.15), channel_id=3, replica_groups=mesh['tok'=8,'mlp'=4] {'tok'}, dimensions={0}, use_global_device_ids=true | all-gather | bytes 50688 | tf_op jit(solution)/shard_map/all_gather | solution.py:1010
  556.8 18.8 %gates_back.1 = (bf16[1024,704]{1,0:T(8,128)(2,1)}, bf16[1024,704]{1,0:T(8,128)(2,1)}, bf16[1024,704]{1,0:T(8,128)(2,1)}, f32[16,704]{1,0:T(8,128)}, f32[16,704]{1,0:T(8,128)}, /*index=5*/f32[8,704]{1,0:T(8,128)}) custom-call(s32[1]{0:T(128)} %bitcast.1.rank, f32[8,2,704]{2,1,0:T(2,128)} %all-gather.3.ends, f32[1024,704]{1,0:T(8,128)} %get-tuple-element.138.g_l, ...), custom_call_target="tpu_custom_call" | custom-call | tf_op jit(solution)/shard_map/gates_back/pallas_call | solution.py:489
  579.5 12.2 %pair_back.1 = (bf16[1024,2048]{1,0:T(8,128)(2,1)}, bf16[1024,704]{1,0:T(8,128)(2,1)}) custom-call(bf16[1024,704]{1,0:T(8,128)(2,1)} %get-tuple-element.157.left, bf16[1024,704]{1,0:T(8,128)(2,1)} %get-tuple-element.146.right, f32[16,704]{1,0:T(8,128)} %get-tuple-element.147.tail, f32[16,704]{1,0:T(8,128)} %copy-done.36, ...), custom_call_target="tpu_custom_call" | custom-call | tf_op jit(solution)/shard_map/pair_back/pallas_call | solution.py:538
  595.2 18.4 %collective-permute-done.25 = bf16[512,1536]{1,0:T(8,128)(2,1)S(1)} collective-permute-done((bf16[512,1536]{1,0:T(8,128)(2,1)S(1)}, bf16[512,1536]{1,0:T(8,128)(2,1)S(1)}, u32[]{:S(2)}, u32[]{:S(2)}) %collective-permute-start.25) | collective-permute-done | bytes 1572896 | tf_op jit(solution)/shard_map/ppermute | solution.py:681
  615.6 3.1 collective-permute-start.26
  618.7 10.0 %collective-permute-done.26 = bf16[256,1536]{1,0:T(8,128)(2,1)S(1)} collective-permute-done((bf16[256,1536]{1,0:T(8,128)(2,1)S(1)}, bf16[256,1536]{1,0:T(8,128)(2,1)S(1)}, u32[]{:S(2)}, u32[]{:S(2)}) %collective-permute-start.26) | collective-permute-done | bytes 786464 | tf_op jit(solution)/shard_map/ppermute | solution.py:681
  628.7 3.0 fusion.44
  631.7 2.8 fusion.37
  637.2 2.8 fusion.31
  640.2 2.8 fusion.34
  643.3 3.3 fusion.25
  646.7 23.9 %soap.5 = (f32[1,1536,256]{2,1,0:T(8,128)}, f32[1,1536,256]{2,1,0:T(8,128)}, f32[1,1536,256]{2,1,0:T(8,128)}) custom-call(f32[1,1536,256]{2,1,0:T(8,128)} %bitcast.140, f32[1,1536,256]{2,1,0:T(8,128)} %bitcast.145, f32[1,1536,256]{2,1,0:T(8,128)} %bitcast.146, bf16[1,256,1536]{2,1,0:T(8,128)(2,1)} %bitcast.142, f32[1,24,4,2,64,64]{5,4,3,2,1,0:T(8,128)} %bitcast.137), custom_call_target="tpu_custom_call" | custom-call | tf_op jit(solution)/shard_map/soap/pallas_call | solution.py:647
  670.6 3.4 fusion.23
  682.3 4.4 settle.3
  687.3 2.7 fusion.119
  701.8 49.2 %reduce-scatter.7.cloned.1.call-done = bf16[256,2048]{1,0:T(8,128)(2,1)} async-done(((bf16[1024,2048]{1,0:T(8,128)(2,1)}), bf16[256,2048]{1,0:T(8,128)(2,1)}) %reduce-scatter.7.cloned.1.call-update) | async-done | bytes 1048592 | tf_op jit(solution)/shard_map/reduce_scatter | solution.py:676
  751.0 2.7 add_convert_fusion.array
  767.5 5.4 collective-permute-done.29
  775.8 9.4 %collective-permute-done.27 = bf16[704,512]{1,0:T(8,128)(2,1)S(1)} collective-permute-done((bf16[704,512]{1,0:T(8,128)(2,1)S(1)}, bf16[704,512]{1,0:T(8,128)(2,1)S(1)}, u32[]{:S(2)}, u32[]{:S(2)}) %collective-permute-start.27) | collective-permute-done | bytes 720928 | tf_op jit(solution)/shard_map/ppermute | solution.py:681
  788.2 10.5 %collective-permute-done.31 = bf16[704,512]{1,0:T(8,128)(2,1)S(1)} collective-permute-done((bf16[704,512]{1,0:T(8,128)(2,1)S(1)}, bf16[704,512]{1,0:T(8,128)(2,1)S(1)}, u32[]{:S(2)}, u32[]{:S(2)}) %collective-permute-start.31) | collective-permute-done | bytes 720928 | tf_op jit(solution)/shard_map/ppermute | solution.py:681
  809.9 17.4 %soap.6 = (f32[2,704,256]{2,1,0:T(8,128)}, f32[2,704,256]{2,1,0:T(8,128)}, f32[2,704,256]{2,1,0:T(8,128)}) custom-call(f32[2,704,256]{2,1,0:T(8,128)} %bitcast.141, f32[2,704,256]{2,1,0:T(8,128)} %bitcast.147, f32[2,704,256]{2,1,0:T(8,128)} %bitcast.148, bf16[2,704,256]{2,1,0:T(8,128)(2,1)} %pad_maximum_fusion.13.g, f32[2,4,11,2,64,64]{5,4,3,2,1,0:T(8,128)} %q.3), custom_call_target="tpu_custom_call" | custom-call | tf_op jit(solution)/shard_map/soap/pallas_call | solution.py:647
  827.3 10.4 %soap.7 = (f32[1,704,256]{2,1,0:T(8,128)}, f32[1,704,256]{2,1,0:T(8,128)}, f32[1,704,256]{2,1,0:T(8,128)}) custom-call(f32[1,704,256]{2,1,0:T(8,128)} %bitcast.143, f32[1,704,256]{2,1,0:T(8,128)} %bitcast.149, f32[1,704,256]{2,1,0:T(8,128)} %bitcast.150, bf16[1,704,256]{2,1,0:T(8,128)(2,1)} %fusion.98.g, f32[1,11,4,2,64,64]{5,4,3,2,1,0:T(8,128)} %bitcast.144), custom_call_target="tpu_custom_call" | custom-call | tf_op jit(solution)/shard_map/soap/pallas_call | solution.py:647
  837.8 11.4 %psum.7 = f32[2,256]{1,0:T(2,128)S(1)} all-reduce(f32[2,256]{1,0:T(2,128)S(1)} %fusion.106), channel_id=1, replica_groups=mesh['tok'=8,'mlp'=4] {'mlp'}, use_global_device_ids=true, to_apply=%region_7.8 | all-reduce | flops 512 | bytes 4096 | tf_op jit(solution)/shard_map/psum | solution.py:1057
  849.8 6.7 convert_element_type.342
  856.5 58.9 %all-gather.13.cloned.1.call-done = bf16[1024,2048]{1,0:T(8,128)(2,1)} async-done(((bf16[256,2048]{1,0:T(8,128)(2,1)}), bf16[1024,2048]{1,0:T(8,128)(2,1)}) %all-gather.13.cloned.1.call-update) | async-done | bytes 4194320 | tf_op jit(solution)/shard_map/all_gather | solution.py:672
  915.4 4.8 copy.91
  (340 shorter events, 143.7 us)
Async XLA Ops:
  7.2 212.4 %reduce-scatter.5.cloned.1.call-start = ((), (), s32[]{:S(2)}) async-start(), calls=%async_computation.4 | async-start | bytes 5242880 | tf_op jit(solution)/shard_map/reduce_scatter | solution.py:676
  9.9 20.9 %collective-permute-start.1 = (bf16[1,8,4024]{2,1,0:T(8,128)(2,1)S(1)}, bf16[1,8,4024]{2,1,0:T(8,128)(2,1)S(1)}, u32[]{:S(2)}, u32[]{:S(2)}) collective-permute-start(bf16[1,8,4024]{2,1,0:T(8,128)(2,1)S(1)} %concatenate.116), channel_id=1, source_target_pairs={{0,16},{4,12},{8,24},{12,4},{16,0},{20,28},{24,8},{28,20},{1,17},{... | collective-permute-start | bytes 193160 | tf_op jit(solution)/shard_map/ppermute | solution.py:681
  13.7 22.8 %collective-permute-start = (bf16[16,2048]{1,0:T(8,128)(2,1)S(1)}, bf16[16,2048]{1,0:T(8,128)(2,1)S(1)}, u32[]{:S(2)}, u32[]{:S(2)}) collective-permute-start(bf16[16,2048]{1,0:T(8,128)(2,1)S(1)} %slice.470), channel_id=1, source_target_pairs={{0,4},{4,8},{8,12},{12,16},{16,20},{20,24},{24,28},{1,5},{5,9},{9,... | collective-permute-start | bytes 196616 | tf_op jit(solution)/shard_map/ppermute | solution.py:930
  17.4 27.2 %collective-permute-start.4 = (bf16[1,3,704,256]{3,2,1,0:T(8,128)(2,1)}, bf16[1,3,704,256]{3,2,1,0:T(8,128)(2,1)S(1)}, u32[]{:S(2)}, u32[]{:S(2)}) collective-permute-start(bf16[1,3,704,256]{3,2,1,0:T(8,128)(2,1)} %pad_maximum_fusion.9), channel_id=1, source_target_pairs={{0,16},{4,12},{8,24},{12,4},{16,0},{20,28},{24,8},{28,20},{1,17},{... | collective-permute-start | bytes 3244040 | tf_op jit(solution)/shard_map/ppermute | solution.py:681
  19.0 10.1 %collective-permute-start.6 = (s32[16]{0:T(128)S(1)}, s32[16]{0:T(128)S(1)}, u32[]{:S(2)}, u32[]{:S(2)}) collective-permute-start(s32[16]{0:T(128)S(1)} %slice.478), channel_id=1, source_target_pairs={{0,4},{4,8},{8,12},{12,16},{16,20},{20,24},{24,28},{1,5},{5,9},{9,... | collective-permute-start | bytes 200 | tf_op jit(solution)/shard_map/ppermute | solution.py:932
  30.8 8.0 collective-permute-start.2
  38.9 1.6 collective-permute-start.3
  46.3 27.1 %collective-permute-start.5 = (bf16[2,3,704,256]{3,2,1,0:T(8,128)(2,1)}, bf16[2,3,704,256]{3,2,1,0:T(8,128)(2,1)}, u32[]{:S(2)}, u32[]{:S(2)}) collective-permute-start(bf16[2,3,704,256]{3,2,1,0:T(8,128)(2,1)} %pad_maximum_fusion.2), channel_id=1, source_target_pairs={{0,8},{4,20},{8,0},{12,28},{16,24},{20,4},{24,16},{28,12},{1,9},{5... | collective-permute-start | bytes 6488072 | tf_op jit(solution)/shard_map/ppermute | solution.py:681
  52.1 24.6 %copy-start.38 = (f32[1,704]{1,0:T(1,128)}, f32[1,704]{1,0:T(1,128)S(1)}, u32[]{:S(2)}) copy-start(f32[1,704]{1,0:T(1,128)S(1)} %slice.491) | copy-start | bytes 8452
  52.4 24.3 %copy-start.32 = (f32[8,704]{1,0:T(8,128)}, f32[8,704]{1,0:T(8,128)S(1)}, u32[]{:S(2)}) copy-start(f32[8,704]{1,0:T(8,128)S(1)} %scatter.4.vec) | copy-start | bytes 67588
  76.8 7.8 collective-permute-start.7
  78.7 144.7 %copy-start.34 = (f32[1,8,256]{2,0,1:T(1,128)}, f32[1,8,256]{2,0,1:T(1,128)S(1)}, u32[]{:S(2)}) copy-start(f32[1,8,256]{2,0,1:T(1,128)S(1)} %get-tuple-element.223) | copy-start | bytes 24580
  142.4 163.9 %all-gather.9.cloned.1.call-start = ((), (), s32[]{:S(2)}) async-start(), calls=%async_computation.5 | async-start | bytes 5242880 | tf_op jit(solution)/shard_map/all_gather | solution.py:672
  143.9 12.9 %copy-start.4 = (f32[2,256,1536]{2,1,0:T(8,128)S(1)}, f32[2,256,1536]{2,1,0:T(8,128)}, u32[]{:S(2)}) copy-start(f32[2,256,1536]{2,1,0:T(8,128)} %w.1) | copy-start | bytes 9437188
  143.9 12.1 %collective-permute-start.8 = (bf16[1,1536,256]{2,1,0:T(8,128)(2,1)S(1)}, bf16[1,1536,256]{2,1,0:T(8,128)(2,1)S(1)}, u32[]{:S(2)}, u32[]{:S(2)}) collective-permute-start(bf16[1,1536,256]{2,1,0:T(8,128)(2,1)S(1)} %convert_bitcast_fusion.1), channel_id=1, source_target_pairs={{0,16},{4,12},{8,24},{12,4},{16,0},{20,28},{24,8},{28,20},{1,17},{... | collective-permute-start | bytes 2359304 | tf_op jit(solution)/shard_map/ppermute | solution.py:681
  156.1 20.5 %collective-permute-start.9 = (bf16[2,1536,256]{2,1,0:T(8,128)(2,1)S(1)}, bf16[2,1536,256]{2,1,0:T(8,128)(2,1)S(1)}, u32[]{:S(2)}, u32[]{:S(2)}) collective-permute-start(bf16[2,1536,256]{2,1,0:T(8,128)(2,1)S(1)} %pad_maximum_fusion.3), channel_id=1, source_target_pairs={{0,8},{4,20},{8,0},{12,28},{16,24},{20,4},{24,16},{28,12},{1,9},{5... | collective-permute-start | bytes 4718600 | tf_op jit(solution)/shard_map/ppermute | solution.py:681
  179.0 20.4 %collective-permute-start.11 = (bf16[1,2,256,1536]{3,2,1,0:T(8,128)(2,1)S(1)}, bf16[1,2,256,1536]{3,2,1,0:T(8,128)(2,1)S(1)}, u32[]{:S(2)}, u32[]{:S(2)}) collective-permute-start(bf16[1,2,256,1536]{3,2,1,0:T(8,128)(2,1)S(1)} %convert_bitcast_fusion), channel_id=1, source_target_pairs={{0,16},{4,12},{8,24},{12,4},{16,0},{20,28},{24,8},{28,20},{1,17},{... | collective-permute-start | bytes 4718600 | tf_op jit(solution)/shard_map/ppermute | solution.py:681
  201.6 37.6 %collective-permute-start.12 = (bf16[2,2,256,1536]{3,2,1,0:T(8,128)(2,1)}, bf16[2,2,256,1536]{3,2,1,0:T(8,128)(2,1)}, u32[]{:S(2)}, u32[]{:S(2)}) collective-permute-start(bf16[2,2,256,1536]{3,2,1,0:T(8,128)(2,1)} %pad_maximum_fusion.1), channel_id=1, source_target_pairs={{0,8},{4,20},{8,0},{12,28},{16,24},{20,4},{24,16},{28,12},{1,9},{5... | collective-permute-start | bytes 9437192 | tf_op jit(solution)/shard_map/ppermute | solution.py:681
  208.3 36.8 %collective-permute-start.10 = (bf16[4,1536,256]{2,1,0:T(8,128)(2,1)}, bf16[4,1536,256]{2,1,0:T(8,128)(2,1)}, u32[]{:S(2)}, u32[]{:S(2)}) collective-permute-start(bf16[4,1536,256]{2,1,0:T(8,128)(2,1)} %constant_dynamic-update-slice_fusion.3), channel_id=1, source_target_pairs={{0,4},{4,0},{8,12},{12,8},{16,20},{20,16},{24,28},{28,24},{1,5},{5... | collective-permute-start | bytes 9437192 | tf_op jit(solution)/shard_map/ppermute | solution.py:681
  224.9 200.2 %reduce-scatter.9.cloned.1.call-start = ((), (), s32[]{:S(2)}) async-start(), calls=%async_computation.7 | async-start | bytes 5242880 | tf_op jit(solution)/shard_map/reduce_scatter | solution.py:676
  225.0 17.9 %copy-start.7 = (bf16[1024,2048]{1,0:T(8,128)(2,1)S(1)}, bf16[1024,2048]{1,0:T(8,128)(2,1)}, u32[]{:S(2)}) copy-start(bf16[1024,2048]{1,0:T(8,128)(2,1)} %permute_columns.6) | copy-start | bytes 12582916
  242.9 63.5 %collective-permute-start.13 = (bf16[4,2,256,1536]{3,2,1,0:T(8,128)(2,1)}, bf16[4,2,256,1536]{3,2,1,0:T(8,128)(2,1)}, u32[]{:S(2)}, u32[]{:S(2)}) collective-permute-start(bf16[4,2,256,1536]{3,2,1,0:T(8,128)(2,1)} %constant_dynamic-update-slice_fusion.6.w_own), channel_id=1, source_target_pairs={{0,4},{4,0},{8,12},{12,8},{16,20},{20,16},{24,28},{28,24},{1,5},{5... | collective-permute-start | bytes 18874376 | tf_op jit(solution)/shard_map/ppermute | solution.py:681
  306.3 36.2 %copy-start.17 = (bf16[1024,2048]{1,0:T(8,128)(2,1)S(1)}, bf16[1024,2048]{1,0:T(8,128)(2,1)}, u32[]{:S(2)}) copy-start(bf16[1024,2048]{1,0:T(8,128)(2,1)} %all-gather.9.cloned.1.call-done.xn) | copy-start | bytes 12582916
  349.5 37.6 %collective-permute-start.17 = (bf16[1024,1536]{1,0:T(8,128)(2,1)}, bf16[1024,1536]{1,0:T(8,128)(2,1)}, u32[]{:S(2)}, u32[]{:S(2)}) collective-permute-start(bf16[1024,1536]{1,0:T(8,128)(2,1)} %convolution_convert_fusion.2), channel_id=1, source_target_pairs={{0,4},{4,0},{8,12},{12,8},{16,20},{20,16},{24,28},{28,24},{1,5},{5... | collective-permute-start | bytes 9437192 | tf_op jit(solution)/shard_map/ppermute | solution.py:681
  349.6 176.8 %all-gather.11.cloned.1.call-start = ((), (), s32[]{:S(2)}) async-start(), calls=%async_computation.8 | async-start | bytes 5242880 | tf_op jit(solution)/shard_map/all_gather | solution.py:672
  357.5 33.9 %collective-permute-start.14 = (bf16[1024,1536]{1,0:T(8,128)(2,1)}, bf16[1024,1536]{1,0:T(8,128)(2,1)}, u32[]{:S(2)}, u32[]{:S(2)}) collective-permute-start(bf16[1024,1536]{1,0:T(8,128)(2,1)} %convolution_convert_fusion.3), channel_id=1, source_target_pairs={{0,4},{4,0},{8,12},{12,8},{16,20},{20,16},{24,28},{28,24},{1,5},{5... | collective-permute-start | bytes 9437192 | tf_op jit(solution)/shard_map/ppermute | solution.py:681
  362.8 33.1 %collective-permute-start.20 = (bf16[1024,1536]{1,0:T(8,128)(2,1)}, bf16[1024,1536]{1,0:T(8,128)(2,1)}, u32[]{:S(2)}, u32[]{:S(2)}) collective-permute-start(bf16[1024,1536]{1,0:T(8,128)(2,1)} %convolution_convert_fusion.1), channel_id=1, source_target_pairs={{0,4},{4,0},{8,12},{12,8},{16,20},{20,16},{24,28},{28,24},{1,5},{5... | collective-permute-start | bytes 9437192 | tf_op jit(solution)/shard_map/ppermute | solution.py:681
  368.2 10.8 %slice-start.2 = ((s8[6291456]{0:T(1024)(128)(4,1)}), s8[4194304]{0:T(1024)(128)(4,1)S(1)}, s32[]{:S(2)}) async-start(s8[6291456]{0:T(1024)(128)(4,1)} %bitcast.152), calls=%async_computation.14 | async-start | bytes 8388608
  429.3 253.0 %reduce-scatter.11.cloned.1.call-start = ((), (), s32[]{:S(2)}) async-start(), calls=%async_computation.9 | async-start | bytes 5242880 | tf_op jit(solution)/shard_map/reduce_scatter | solution.py:676
  429.8 20.7 %collective-permute-start.18 = (bf16[512,1536]{1,0:T(8,128)(2,1)}, bf16[512,1536]{1,0:T(8,128)(2,1)S(1)}, u32[]{:S(2)}, u32[]{:S(2)}) collective-permute-start(bf16[512,1536]{1,0:T(8,128)(2,1)} %pad_maximum_fusion.5), channel_id=1, source_target_pairs={{0,8},{4,20},{8,0},{12,28},{16,24},{20,4},{24,16},{28,12},{1,9},{5... | collective-permute-start | bytes 4718600 | tf_op jit(solution)/shard_map/ppermute | solution.py:681
  431.3 44.4 %collective-permute-start.15 = (bf16[512,1536]{1,0:T(8,128)(2,1)}, bf16[512,1536]{1,0:T(8,128)(2,1)S(1)}, u32[]{:S(2)}, u32[]{:S(2)}) collective-permute-start(bf16[512,1536]{1,0:T(8,128)(2,1)} %pad_maximum_fusion.4), channel_id=1, source_target_pairs={{0,8},{4,20},{8,0},{12,28},{16,24},{20,4},{24,16},{28,12},{1,9},{5... | collective-permute-start | bytes 4718600 | tf_op jit(solution)/shard_map/ppermute | solution.py:681
  452.4 26.8 %collective-permute-start.19 = (bf16[256,1536]{1,0:T(8,128)(2,1)S(1)}, bf16[256,1536]{1,0:T(8,128)(2,1)S(1)}, u32[]{:S(2)}, u32[]{:S(2)}) collective-permute-start(bf16[256,1536]{1,0:T(8,128)(2,1)S(1)} %fusion.48), channel_id=1, source_target_pairs={{0,16},{4,12},{8,24},{12,4},{16,0},{20,28},{24,8},{28,20},{1,17},{... | collective-permute-start | bytes 2359304 | tf_op jit(solution)/shard_map/ppermute | solution.py:681
  477.7 12.1 %collective-permute-start.16 = (bf16[256,1536]{1,0:T(8,128)(2,1)S(1)}, bf16[256,1536]{1,0:T(8,128)(2,1)S(1)}, u32[]{:S(2)}, u32[]{:S(2)}) collective-permute-start(bf16[256,1536]{1,0:T(8,128)(2,1)S(1)} %fusion.55), channel_id=1, source_target_pairs={{0,16},{4,12},{8,24},{12,4},{16,0},{20,28},{24,8},{28,20},{1,17},{... | collective-permute-start | bytes 2359304 | tf_op jit(solution)/shard_map/ppermute | solution.py:681
  575.6 3.3 collective-permute-start.21
  591.7 159.2 %reduce-scatter.7.cloned.1.call-start = ((), (), s32[]{:S(2)}) async-start(), calls=%async_computation.6 | async-start | bytes 5242880 | tf_op jit(solution)/shard_map/reduce_scatter | solution.py:676
  592.3 257.5 %all-gather.15.cloned.1.call-start = ((), (), s32[]{:S(2)}) async-start(), calls=%async_computation.11 | async-start | bytes 5242880 | tf_op jit(solution)/shard_map/all_gather | solution.py:672
  592.5 21.0 %collective-permute-start.25 = (bf16[512,1536]{1,0:T(8,128)(2,1)S(1)}, bf16[512,1536]{1,0:T(8,128)(2,1)S(1)}, u32[]{:S(2)}, u32[]{:S(2)}) collective-permute-start(bf16[512,1536]{1,0:T(8,128)(2,1)S(1)} %pad_maximum_fusion.7), channel_id=1, source_target_pairs={{0,8},{4,20},{8,0},{12,28},{16,24},{20,4},{24,16},{28,12},{1,9},{5... | collective-permute-start | bytes 4718600 | tf_op jit(solution)/shard_map/ppermute | solution.py:681
  613.6 18.1 %copy-start.52 = (bf16[1024,704]{1,0:T(8,128)(2,1)S(1)}, bf16[1024,704]{1,0:T(8,128)(2,1)}, u32[]{:S(2)}) copy-start(bf16[1024,704]{1,0:T(8,128)(2,1)} %get-tuple-element.155) | copy-start | bytes 4325380
  615.6 16.0 %copy-start.16 = (bf16[1024,2048]{1,0:T(8,128)(2,1)S(1)}, bf16[1024,2048]{1,0:T(8,128)(2,1)}, u32[]{:S(2)}) copy-start(bf16[1024,2048]{1,0:T(8,128)(2,1)} %all-gather.11.cloned.1.call-done.d_rec) | copy-start | bytes 12582916
  615.6 13.0 %collective-permute-start.26 = (bf16[256,1536]{1,0:T(8,128)(2,1)S(1)}, bf16[256,1536]{1,0:T(8,128)(2,1)S(1)}, u32[]{:S(2)}, u32[]{:S(2)}) collective-permute-start(bf16[256,1536]{1,0:T(8,128)(2,1)S(1)} %fusion.41), channel_id=1, source_target_pairs={{0,16},{4,12},{8,24},{12,4},{16,0},{20,28},{24,8},{28,20},{1,17},{... | collective-permute-start | bytes 2359304 | tf_op jit(solution)/shard_map/ppermute | solution.py:681
  634.5 39.6 %collective-permute-start.22 = (bf16[704,1024]{1,0:T(8,128)(2,1)}, bf16[704,1024]{1,0:T(8,128)(2,1)S(1)}, u32[]{:S(2)}, u32[]{:S(2)}) collective-permute-start(bf16[704,1024]{1,0:T(8,128)(2,1)} %fusion.37), channel_id=1, source_target_pairs={{0,4},{4,0},{8,12},{12,8},{16,20},{20,16},{24,28},{28,24},{1,5},{5... | collective-permute-start | bytes 4325384 | tf_op jit(solution)/shard_map/ppermute | solution.py:681
  637.2 36.8 %copy-start.19 = (f32[704,1024]{1,0:T(8,128)}, f32[704,1024]{1,0:T(8,128)S(1)}, u32[]{:S(2)}) copy-start(f32[704,1024]{1,0:T(8,128)S(1)} %fusion.11) | copy-start | bytes 8650756
  640.0 35.3 %collective-permute-start.23 = (bf16[704,1024]{1,0:T(8,128)(2,1)}, bf16[704,1024]{1,0:T(8,128)(2,1)}, u32[]{:S(2)}, u32[]{:S(2)}) collective-permute-start(bf16[704,1024]{1,0:T(8,128)(2,1)} %fusion.31), channel_id=1, source_target_pairs={{0,4},{4,0},{8,12},{12,8},{16,20},{20,16},{24,28},{28,24},{1,5},{5... | collective-permute-start | bytes 4325384 | tf_op jit(solution)/shard_map/ppermute | solution.py:681
  643.0 36.8 %collective-permute-start.24 = (bf16[704,1024]{1,0:T(8,128)(2,1)}, bf16[704,1024]{1,0:T(8,128)(2,1)}, u32[]{:S(2)}, u32[]{:S(2)}) collective-permute-start(bf16[704,1024]{1,0:T(8,128)(2,1)} %fusion.34), channel_id=1, source_target_pairs={{0,4},{4,0},{8,12},{12,8},{16,20},{20,16},{24,28},{28,24},{1,5},{5... | collective-permute-start | bytes 4325384 | tf_op jit(solution)/shard_map/ppermute | solution.py:681
  646.7 24.0 %copy-start.55 = (bf16[1024,704]{1,0:T(8,128)(2,1)S(1)}, bf16[1024,704]{1,0:T(8,128)(2,1)}, u32[]{:S(2)}) copy-start(bf16[1024,704]{1,0:T(8,128)(2,1)} %get-tuple-element.159) | copy-start | bytes 4325380
  686.7 228.6 %all-gather.13.cloned.1.call-start = ((), (), s32[]{:S(2)}) async-start(), calls=%async_computation.10 | async-start | bytes 5242880 | tf_op jit(solution)/shard_map/all_gather | solution.py:672
  694.8 56.1 %copy-start.2 = (bf16[256,2048]{1,0:T(8,128)(2,1)S(1)}, bf16[256,2048]{1,0:T(8,128)(2,1)}, u32[]{:S(2)}) copy-start(bf16[256,2048]{1,0:T(8,128)(2,1)} %copy-done.1) | copy-start | bytes 3145732
  696.8 2.0 collective-permute-start.33
  700.3 55.9 %collective-permute-start.34 = (f32[2,8,3960]{2,1,0:T(8,128)}, f32[2,8,3960]{2,1,0:T(8,128)S(1)}, u32[]{:S(2)}, u32[]{:S(2)}) collective-permute-start(f32[2,8,3960]{2,1,0:T(8,128)} %pad_maximum_fusion.15), channel_id=1, source_target_pairs={{0,8},{4,20},{8,0},{12,28},{16,24},{20,4},{24,16},{28,12},{1,9},{5... | collective-permute-start | bytes 760328 | tf_op jit(solution)/shard_map/ppermute | solution.py:681
  756.2 10.7 %copy-start.43 = (f32[8,88]{1,0:T(8,128)S(1)}, f32[8,88]{1,0:T(8,128)}, u32[]{:S(2)}) copy-start(f32[8,88]{1,0:T(8,128)} %param.57) | copy-start | bytes 8452
  756.2 5.0 collective-permute-start.35
  761.3 37.4 %copy-start.20 = (f32[704,1024]{1,0:T(8,128)S(1)}, f32[704,1024]{1,0:T(8,128)}, u32[]{:S(2)}) copy-start(f32[704,1024]{1,0:T(8,128)} %copy-done.19) | copy-start | bytes 8650756
  761.3 37.4 %copy-start.26 = (bf16[704,1024]{1,0:T(8,128)(2,1)S(1)}, bf16[704,1024]{1,0:T(8,128)(2,1)}, u32[]{:S(2)}) copy-start(bf16[704,1024]{1,0:T(8,128)(2,1)} %copy-done.25) | copy-start | bytes 4325380
  761.3 11.6 %collective-permute-start.29 = (bf16[704,512]{1,0:T(8,128)(2,1)}, bf16[704,512]{1,0:T(8,128)(2,1)S(1)}, u32[]{:S(2)}, u32[]{:S(2)}) collective-permute-start(bf16[704,512]{1,0:T(8,128)(2,1)} %pad_maximum_fusion.12), channel_id=1, source_target_pairs={{0,8},{4,20},{8,0},{12,28},{16,24},{20,4},{24,16},{28,12},{1,9},{5... | collective-permute-start | bytes 2162696 | tf_op jit(solution)/shard_map/ppermute | solution.py:681
  762.9 22.3 %collective-permute-start.27 = (bf16[704,512]{1,0:T(8,128)(2,1)S(1)}, bf16[704,512]{1,0:T(8,128)(2,1)S(1)}, u32[]{:S(2)}, u32[]{:S(2)}) collective-permute-start(bf16[704,512]{1,0:T(8,128)(2,1)S(1)} %copy-done.28), channel_id=1, source_target_pairs={{0,8},{4,20},{8,0},{12,28},{16,24},{20,4},{24,16},{28,12},{1,9},{5... | collective-permute-start | bytes 2162696 | tf_op jit(solution)/shard_map/ppermute | solution.py:681
  765.3 33.4 %collective-permute-start.31 = (bf16[704,512]{1,0:T(8,128)(2,1)S(1)}, bf16[704,512]{1,0:T(8,128)(2,1)S(1)}, u32[]{:S(2)}, u32[]{:S(2)}) collective-permute-start(bf16[704,512]{1,0:T(8,128)(2,1)S(1)} %copy-done.27), channel_id=1, source_target_pairs={{0,8},{4,20},{8,0},{12,28},{16,24},{20,4},{24,16},{28,12},{1,9},{5... | collective-permute-start | bytes 2162696 | tf_op jit(solution)/shard_map/ppermute | solution.py:681
  774.2 26.3 %collective-permute-start.30 = (bf16[704,256]{1,0:T(8,128)(2,1)S(1)}, bf16[704,256]{1,0:T(8,128)(2,1)S(1)}, u32[]{:S(2)}, u32[]{:S(2)}) collective-permute-start(bf16[704,256]{1,0:T(8,128)(2,1)S(1)} %fusion.81), channel_id=1, source_target_pairs={{0,16},{4,12},{8,24},{12,4},{16,0},{20,28},{24,8},{28,20},{1,17},{... | collective-permute-start | bytes 1081352 | tf_op jit(solution)/shard_map/ppermute | solution.py:681
  786.6 16.3 %collective-permute-start.28 = (bf16[704,256]{1,0:T(8,128)(2,1)S(1)}, bf16[704,256]{1,0:T(8,128)(2,1)S(1)}, u32[]{:S(2)}, u32[]{:S(2)}) collective-permute-start(bf16[704,256]{1,0:T(8,128)(2,1)S(1)} %fusion.86), channel_id=1, source_target_pairs={{0,16},{4,12},{8,24},{12,4},{16,0},{20,28},{24,8},{28,20},{1,17},{... | collective-permute-start | bytes 1081352 | tf_op jit(solution)/shard_map/ppermute | solution.py:681
  798.9 7.5 collective-permute-start.32
  802.8 1.5 collective-permute-start.36
  804.3 3.7 collective-permute-start.37
  808.0 29.8 %collective-permute-start.38 = (f32[1,2,256]{2,1,0:T(2,128)S(1)}, f32[1,2,256]{2,1,0:T(2,128)S(1)}, u32[]{:S(2)}, u32[]{:S(2)}) collective-permute-start(f32[1,2,256]{2,1,0:T(2,128)S(1)} %slice_add_fusion.30), channel_id=1, source_target_pairs={{0,16},{4,12},{8,24},{12,4},{16,0},{20,28},{24,8},{28,20},{1,17},{... | collective-permute-start | bytes 6152 | tf_op jit(solution)/shard_map/ppermute | solution.py:681
  827.3 21.9 %copy-start.45 = (f32[2,256]{1,0:T(2,128)S(1)}, f32[2,256]{1,0:T(2,128)}, u32[]{:S(2)}) copy-start(f32[2,256]{1,0:T(2,128)} %param.61) | copy-start | bytes 6148
  827.3 21.9 %copy-start.46 = (f32[2,256]{1,0:T(2,128)S(1)}, f32[2,256]{1,0:T(2,128)}, u32[]{:S(2)}) copy-start(f32[2,256]{1,0:T(2,128)} %param.60) | copy-start | bytes 6148
  (43 other events, 179.6 us)
Sparse Core Ops, SparseCore 0:
  142.5 77.0 reduce-scatter.4
  225.1 81.2 all-gather.8
  349.7 75.4 reduce-scatter.8
  429.5 81.3 all-gather.10
  591.9 79.5 reduce-scatter.10
  673.7 77.2 reduce-scatter.6
  752.5 81.2 all-gather.14
  836.0 79.3 all-gather.12

commit v3 on v2

--- a/solution.py
+++ b/solution.py
@@ -28,6 +28,12 @@
 def params(limit=56):
     return pltpu.CompilerParams(
         dimension_semantics=("arbitrary",), vmem_limit_bytes=limit * 1024 * 1024
+    )
+
+
+def cost(micros):
+    return pl.CostEstimate(
+        flops=int(micros * 1.1e9), bytes_accessed=int(micros * 3.3e6), transcendentals=0
     )
 
 
@@ -143,30 +149,30 @@
         carry_prod[0:1, wide] = prod_in
 
 
-def piece_spot(array, piece):
-    return (0, 2, 1, 3)[piece] if array == 1 else piece
+SPOTS = ((0, 1), (2, 3), (4, 6), (5, 7))
 
 
 def load_pieces(arrays, which, held, sem, along):
     copies = []
-    for number, array in enumerate(arrays):
+    for array, spots in zip(arrays, SPOTS):
         size = array.shape[1 + along]
-        base = sum(before.shape[0] for before in arrays[:number])
-        if base * size >= held.shape[along]:
-            break
-        for piece in range(array.shape[0]):
-            at = pl.ds((base + piece_spot(number, piece)) * size, size)
+        if size == held.shape[along]:
+            spots = (0,)
+        for piece, spot in enumerate(spots):
+            at = pl.ds(spot * size, size)
             for slot, kind in enumerate(which):
                 place = held.at[slot, at, :] if along == 1 else held.at[slot, :, at]
                 copies.append(pltpu.make_async_copy(array.at[piece, kind], place, sem))
+        if size == held.shape[along]:
+            break
     for copy in copies:
         copy.start()
     for copy in copies:
         copy.wait()
 
 
-def any_spec():
-    return pl.BlockSpec(memory_space=pl.ANY)
+def any_specs():
+    return [pl.BlockSpec(memory_space=pl.ANY)] * len(SPOTS)
 
 
 def rms_low(value, gain):
@@ -176,7 +182,7 @@
 
 
 def front_kernel(
-    tok, halo, gain, w_own, w_far, w_a, w_i, vec, mask,
+    tok, halo, gain, w_0, w_1, w_2, w_3, w_a, w_i, vec, mask,
     xn_o, y_o, u_o, uh_o, xc_o, pa_o, pi_o, a_o, h_o, p_o, end_o,
     ubuf, abuf, bbuf, car_s, car_p, w_in, sem,
 ):
@@ -186,7 +192,7 @@
 
     @pl.when(step == 0)
     def _():
-        load_pieces((w_own, w_far), (0, 1), w_in, sem, 2)
+        load_pieces((w_0, w_1, w_2, w_3), (0, 1), w_in, sem, 2)
         low = nt(rms_low(halo[...].astype(f32), gain[...]), w_in[1]).astype(bf16)
         uh_o[...] = low
         ubuf[0:HALO, :] = low.astype(f32)
@@ -233,7 +239,7 @@
         front_kernel,
         grid=(count // rows,),
         in_specs=[
-            row(model), whole(halo.shape), whole(gain.shape), any_spec(), any_spec(),
+            row(model), whole(halo.shape), whole(gain.shape), *any_specs(),
             whole(w_a.shape), whole(w_i.shape), whole(vec.shape), row(mask.shape[1]),
         ],
         out_specs=[
@@ -256,20 +262,19 @@
             pltpu.SemaphoreType.DMA,
         ],
         compiler_params=params(),
+        cost_estimate=cost(34),
         name="front",
     )(tok, halo, gain, *weights, w_a, w_i, vec, mask)
 
 
 def state_kernel(
-    rank, ends, h_l, p_l, y, w_own, w_far, h_o, hp_o, o_o, part_o, hin, hbuf, w_o, sem
+    rank, ends, h_l, p_l, y, h_o, hp_o, o_o, hin, hbuf
 ):
     step = pl.program_id(0)
     rows = h_l.shape[0]
 
     @pl.when(step == 0)
     def _():
-        load_pieces((w_own, w_far), (2,), w_o, sem, 2)
-
         def fold(at, held):
             return jnp.where(at < rank[0], ends[at, 0:1, :] + ends[at, 1:2, :] * held, held)
 
@@ -282,12 +287,10 @@
     hbuf[8 : 8 + rows, :] = state
     hp_o[...] = hbuf[7 : 7 + rows, :]
     hbuf[7:8, :] = state[rows - 1 :, :]
-    mixed = (state * gelu_tanh(y[...])).astype(bf16)
-    o_o[...] = mixed
-    part_o[...] = nn(mixed, w_o[0]).astype(bf16)
-
-
-def finish_state(rank, ends, h_l, p_l, y, weights, model, rows):
+    o_o[...] = (state * gelu_tanh(y[...])).astype(bf16)
+
+
+def finish_state(rank, ends, h_l, p_l, y, rows):
     count, width = h_l.shape
     row = lambda size: pl.BlockSpec((rows, size), lambda i: (i, 0))
     like = lambda size, kind: jax.ShapeDtypeStruct((count, size), kind)
@@ -296,25 +299,67 @@
         grid=(count // rows,),
         in_specs=[
             pl.BlockSpec(memory_space=pltpu.SMEM), whole(ends.shape), row(width), row(width),
-            row(width), any_spec(), any_spec(),
-        ],
-        out_specs=[row(width), row(width), row(width), row(model)],
-        out_shape=[like(width, f32), like(width, f32), like(width, bf16), like(model, bf16)],
+            row(width),
+        ],
+        out_specs=[row(width), row(width), row(width)],
+        out_shape=[like(width, f32), like(width, f32), like(width, bf16)],
         scratch_shapes=[
             pltpu.VMEM((8, width), f32),
             pltpu.VMEM((8 + rows, width), f32),
-            pltpu.VMEM((1, width, model), bf16),
-            pltpu.SemaphoreType.DMA,
         ],
         compiler_params=params(),
+        cost_estimate=cost(8),
         name="finish_state",
-    )(rank, ends, h_l, p_l, y, *weights)
-
-
-def mlp_kernel(xn, dhid, w_own, w_far, hm_o, dg_o, du_o, part_o, held, sem):
+    )(rank, ends, h_l, p_l, y)
+
+
+def lift_kernel(slab, mixed, tok, gain, w_0, w_1, w_2, w_3, xn_o, own_o, w_o, sem):
+    step = pl.program_id(0)
+
+    @pl.when(step == 0)
+    def _():
+        load_pieces((w_0, w_1, w_2, w_3), range(w_o.shape[0]), w_o, sem, 2)
+
+    total = nn(mixed[0], w_o[0])
+    for kind in range(1, w_o.shape[0]):
+        total = total + nn(mixed[kind], w_o[kind])
+    second = tok[...].astype(f32) + total
+    xn_o[...] = rms_low(second, gain[...])
+
+    @pl.when(step == slab[0])
+    def _():
+        own_o[...] = second
+
+
+def lift(slab, mixed, tok, gain, weights):
+    count, model = tok.shape
+    slabs, _, width = mixed.shape
+    rows = count // slabs
+    row = lambda size: pl.BlockSpec((rows, size), lambda i: (i, 0))
+    return pl.pallas_call(
+        lift_kernel,
+        grid=(slabs,),
+        in_specs=[
+            pl.BlockSpec(memory_space=pltpu.SMEM),
+            pl.BlockSpec((slabs, rows, width), lambda i: (0, i, 0)),
+            row(model), whole(gain.shape), *any_specs(),
+        ],
+        out_specs=[row(model), whole((rows, model))],
+        out_shape=[
+            jax.ShapeDtypeStruct((count, model), bf16),
+            jax.ShapeDtypeStruct((rows, model), f32),
+        ],
+        scratch_shapes=[pltpu.VMEM((slabs, width, model), bf16), pltpu.SemaphoreType.DMA],
+        compiler_params=params(),
+        cost_estimate=cost(22),
+        name="lift",
+    )(slab, mixed, tok, gain, *weights)
+
+
+def mlp_kernel(xn, dhid, w_0, w_1, w_2, w_3, hm_o, dg_o, du_o, part_o, held, sem):
     @pl.when(pl.program_id(0) == 0)
     def _():
-        load_pieces((w_own, w_far), (0, 1), held, sem, 1)
+        load_pieces((w_0, w_1, w_2, w_3), (0, 1), held, sem, 1)
 
     w_g, w_u = held.at[0], held.at[1]
     hidden = dhid.shape[1]
@@ -343,24 +388,25 @@
     return pl.pallas_call(
         mlp_kernel,
         grid=(count // rows,),
-        in_specs=[row(model), row(hidden), any_spec(), any_spec()],
+        in_specs=[row(model), row(hidden), *any_specs()],
         out_specs=[row(hidden), row(hidden), row(hidden), row(model)],
         out_shape=[like(hidden), like(hidden), like(hidden), like(model)],
         scratch_shapes=[pltpu.VMEM((2, model, hidden), bf16), pltpu.SemaphoreType.DMA],
         compiler_params=params(),
+        cost_estimate=cost(36),
         name="mlp",
     )(xn, dhid, *weights)
 
 
 def back_kernel(
-    d_rec, w_own, w_far, y, h, a, dy_o, g_o, p_o, end_o, abuf, bbuf, car_s, car_p, w_o, sem
+    slab, d_rec, w_0, w_1, w_2, w_3, y, h, a, dy_o, g_o, p_o, end_o, abuf, bbuf, car_s, car_p, w_o, sem
 ):
     step = pl.program_id(0)
     width = y.shape[1]
 
     @pl.when(step == 0)
     def _():
-        load_pieces((w_own, w_far), (2,), w_o, sem, 2)
+        load_pieces((w_0, w_1, w_2, w_3), (slab[0],), w_o, sem, 2)
         car_s[...] = jnp.zeros_like(car_s)
         car_p[...] = jnp.ones_like(car_p)
 
@@ -374,7 +420,7 @@
     end_o[1:2, :] = car_p[0:1, :width]
 
 
-def back_scan(d_rec, weights, y, h, a, rows):
+def back_scan(slab, d_rec, weights, y, h, a, rows):
     count, model = d_rec.shape
     width = y.shape[1]
     tiles = pl.cdiv(width, LANES)
@@ -384,7 +430,10 @@
     return pl.pallas_call(
         back_kernel,
         grid=(steps,),
-        in_specs=[row(model), any_spec(), any_spec(), row(width), row(width), row(width)],
+        in_specs=[
+            pl.BlockSpec(memory_space=pltpu.SMEM), row(model), *any_specs(), row(width), row(width),
+            row(width),
+        ],
         out_specs=[row(width), row(width), row(width), whole((8, width))],
         out_shape=[
             like(width, bf16), like(width, f32), like(width, f32),
@@ -399,8 +448,9 @@
             pltpu.SemaphoreType.DMA,
         ],
         compiler_params=params(),
+        cost_estimate=cost(20),
         name="back_scan",
-    )(d_rec, *weights, y, h, a)
+    )(slab, d_rec, *weights, y, h, a)
 
 
 def gates_kernel(
@@ -511,17 +561,18 @@
             pltpu.VMEM((HALO + rows, width), f32),
         ],
         compiler_params=params(),
+        cost_estimate=cost(19),
         name="gates_back",
     )(rank, ends, g_l, p_l, pa, pi, xc, hp, u, u, u_halo, mask, w_a, w_i, vec)
 
 
-def pair_kernel(left, right, tail, more, w_own, w_far, out, right_o, held, sem):
+def pair_kernel(left, right, tail, more, w_0, w_1, w_2, w_3, out, right_o, held, sem):
     step = pl.program_id(0)
     rows = left.shape[0]
 
     @pl.when(step == 0)
     def _():
-        load_pieces((w_own, w_far), (0, 1), held, sem, 2)
+        load_pieces((w_0, w_1, w_2, w_3), (0, 1), held, sem, 2)
 
     right_o[...] = right[...]
 
@@ -539,7 +590,7 @@
         pair_kernel,
         grid=(count // rows,),
         in_specs=[
-            row(width), row(width), whole(tail.shape), whole(more.shape), any_spec(), any_spec(),
+            row(width), row(width), whole(tail.shape), whole(more.shape), *any_specs(),
         ],
         out_specs=[row(model), row(width)],
         out_shape=[
@@ -548,6 +599,7 @@
         ],
         scratch_shapes=[pltpu.VMEM((2, width, model), bf16), pltpu.SemaphoreType.DMA],
         compiler_params=params(),
+        cost_estimate=cost(12),
         name="pair_back",
     )(left, right, tail, more, *weights)
 
@@ -568,6 +620,7 @@
         mask_kernel,
         out_shape=jax.ShapeDtypeStruct((count, 8), f32),
         compiler_params=pltpu.CompilerParams(vmem_limit_bytes=16 * 1024 * 1024),
+        cost_estimate=cost(2),
         name="masks",
     )(ids)
 
@@ -657,6 +710,7 @@
         compiler_params=pltpu.CompilerParams(
             dimension_semantics=("arbitrary", "arbitrary"), vmem_limit_bytes=56 * 1024 * 1024
         ),
+        cost_estimate=cost(group * height * width / 24000),
         name="soap",
     )(w, m, v, g, q)
 
@@ -791,6 +845,7 @@
         out_specs=row,
         out_shape=jax.ShapeDtypeStruct(array.shape, array.dtype),
         compiler_params=params(),
+        cost_estimate=cost(count * width / 420000),
         name="permute_columns",
     )(order, array)
 
@@ -837,6 +892,7 @@
         ],
         scratch_shapes=[pltpu.VMEM((rows, model), bf16)],
         compiler_params=params(),
+        cost_estimate=cost(4),
         name="settle",
     )(order, value, upstream, gain, base)
     if move and not inside:
@@ -903,12 +959,13 @@
     else:
         small_all = lax.all_gather(small, "tok", axis=0, tiled=False)
     turn = lambda array: jnp.swapaxes(array, 1, 2)
-    rec_own = jnp.concatenate([turn(w_in_rec), w_out_rec[None]], axis=0).astype(bf16)[None]
+    rec_own = turn(w_in_rec).astype(bf16)[None]
     join = lambda *arrays: jnp.concatenate(arrays, axis=0)
+    out_own = lax.all_gather(w_out_rec.astype(bf16), "mlp", axis=0, tiled=False)[None]
     if parts == 8:
-        rec_far = hop(rec_own, FAR)
-        rec_two = join(rec_own, rec_far)
+        rec_two = join(rec_own, hop(rec_own, FAR))
         rec_near = hop(rec_two, NEAR)
+        rec_core = hop(rec_two, CORE)
     gains_all = small_all[:, :, gate_part + rnn_part :].reshape(parts, 2, model // parts)
     gains_f = (
         gains_all
@@ -940,42 +997,52 @@
     mask = masks(ids[:, None], count)
     if parts == 8:
         rec_near = after(rec_near, tok_s, halo, mask, w_a, w_i, vec)
-        rec_four = join(rec_two, rec_near)
-        rec_w = (rec_four, hop(rec_four, CORE))
+        rec_w = (rec_two, rec_near, rec_core, hop(rec_near, CORE))
+        up_own = w_in_mlp.astype(bf16)[None]
+        out_far = hop(after(out_own, rec_near), FAR)
+        up_far = hop(after(up_own, rec_near), FAR)
     else:
-        rec_all = lax.all_gather(rec_own[0], "tok", axis=2, tiled=True)[None]
-        rec_w = (rec_all, rec_all)
+        rec_w = (lax.all_gather(rec_own[0], "tok", axis=2, tiled=True)[None],) * 4
+        out_w = (lax.all_gather(out_own[0], "tok", axis=2, tiled=True)[None],) * 4
 
     xn_one, y_pre, u_low, u_halo, conv_low, pre_decay, pre_input, decay, h_loc, p_loc, ends = front(
         tok_s, halo, gains_f[0:1], rec_w, w_a, w_i, vec, mask, rows
     )
     ends_all = lax.all_gather(ends[0:2], "tok", axis=0, tiled=False)
-    state, state_prev, mixed, branch = finish_state(
-        rank_ref, ends_all, h_loc, p_loc, y_pre, rec_w, model, rows
-    )
+    state, state_prev, mixed = finish_state(rank_ref, ends_all, h_loc, p_loc, y_pre, rows)
     own = lambda array: lax.dynamic_slice_in_dim(array, slab * share, share, 0)
+    slab_ref = slab.reshape(1).astype(jnp.int32)
     own_tok = own(tok_s)
-    second = own_tok.astype(f32) + scatter_slabs(branch).astype(f32)
-    second_low = rms_low(second, gains_f[1])
-    up_own = after(w_in_mlp.astype(bf16)[None], branch)
-    down_own = after(w_out_mlp.astype(bf16)[None], branch)
+    mixed_all = lax.all_gather(mixed, "mlp", axis=0, tiled=False)
+    down_own = w_out_mlp.astype(bf16)[None]
     if parts == 8:
-        down_four = gather_start(down_own)
-        down_rest = hop(down_four, CORE)
+        out_two = join(out_own, after(out_far, ends))
+        up_two = join(up_own, after(up_far, ends))
+        out_near = hop(out_two, NEAR)
+        up_near = hop(up_two, NEAR)
+        down_far = hop(after(down_own, ends), FAR)
+        out_core = hop(after(out_two, mixed), CORE)
+        out_w = (out_two, out_near, out_core, hop(after(out_near, mixed), CORE))
+        down_two = join(down_own, after(down_far, mixed))
+        down_near = hop(down_two, NEAR)
+        down_core = hop(down_two, CORE)
+        up_core = hop(after(up_two, mixed), CORE)
+        up_w = (up_two, up_near, up_core, hop(after(up_near, mixed), CORE))
+        down_last = hop(down_near, CORE)
         down = jnp.concatenate(
-            [down_four[p] for p in range(4)] + [down_rest[p] for p in (0, 2, 1, 3)], axis=1
+            [
+                down_two[0], down_two[1], down_near[0], down_near[1],
+                down_core[0], down_last[0], down_core[1], down_last[1],
+            ],
+            axis=1,
         )
-        up_two = join(up_own, hop(after(up_own, down_four), FAR))
-        up_near = after(hop(up_two, NEAR), second_low)
-        up_four = join(up_two, up_near)
-        up_w = (up_four, hop(up_four, CORE))
     else:
         down = lax.all_gather(down_own[0], "tok", axis=1, tiled=True)
-        up_all = lax.all_gather(up_own[0], "tok", axis=1, tiled=True)[None]
-        up_w = (up_all, up_all)
-    cot_s = permute_columns(after(cotangent, branch), into_local)
+        up_own = w_in_mlp.astype(bf16)
+        up_w = (lax.all_gather(up_own, "tok", axis=1, tiled=True)[None],) * 4
+    cot_s = permute_columns(after(cotangent, mixed), into_local)
     d_hidden = nt(cot_s, down)
-    xn_two = gather_slabs(second_low)
+    xn_two, second = lift(slab_ref, mixed_all, tok_s, gains_f[1:2], out_w)
     hidden, d_gate, d_up, d_branch = mlp(xn_two, d_hidden, up_w, min(512, count))
     d_xn_two = scatter_slabs(d_branch)
     low = lambda array: array.astype(bf16)
@@ -1004,9 +1071,10 @@
     d_rec = gather_slabs(d_second_low)
     branch_two = after(branch_two, in_mlp_new[0])
     d_rec = after(d_rec, in_mlp_new[0])
-    result_own = second + scatter_slabs(branch_two).astype(f32)
+    branch_sum = scatter_slabs(branch_two)
+    result_own = second + branch_sum.astype(f32)
     result_low = permute_columns(result_own.astype(bf16), from_local)
-    d_ypre, g_loc, q_loc, ends_back = back_scan(d_rec, rec_w, y_pre, state, decay, rows)
+    d_ypre, g_loc, q_loc, ends_back = back_scan(slab_ref, d_rec, out_w, y_pre, state, decay, rows)
     ends_back_all = lax.all_gather(ends_back[0:2], "tok", axis=0, tiled=False)
     d_pa, d_pi, d_u, d_u_tail, spill, sums = gates_back(
         rank_ref, ends_back_all, g_loc, q_loc, pre_decay, pre_input, conv_low, state_prev,
@@ -1014,7 +1082,7 @@
     )
     from_next = lax.ppermute(spill, "tok", [(i + 1, i) for i in range(parts - 1)])
     d_pair, d_u = pair_back(d_ypre, d_u, d_u_tail, from_next, rec_w, model, rows)
-    d_xn_one = scatter_slabs(d_pair)
+    d_xn_one = scatter_slabs(after(d_pair, branch_sum))
     out_mlp_new = soap(
         *lead_one(w_out_mlp, m_out_mlp, v_out_mlp, after(g_out_mlp, d_pair), q_out_mlp),
         split(w_out_mlp.shape[0]), turned=True,

time: 934 us -> 797 us (0.85)
  waiting for transfers between devices: 384 us -> 255 us
  Pallas kernels: 240 us -> 260 us
  local copies, waits for them, and re-layouts: 55.9 us -> 38.1 us
    ppermute x36 -> x43, waiting for transfers between devices: 193 us -> 130 us  [hop(): lax.ppermute(array, 'tok', [(i, i ^ pairs[i % 2]) for i in range(count)])]
    reduce_scatter x4 -> x3, waiting for transfers between devices: 85.6 us -> 44.5 us  [scatter_slabs(): return lax.psum_scatter(array, 'mlp', scatter_dimension=0, tiled=True)]
    all_gather x4 -> x3, waiting for transfers between devices: 103 us -> 68.7 us  [gather_slabs(): return lax.all_gather(array, 'mlp', axis=0, tiled=True)]
    pallas_call x1 -> x2, Pallas kernels: 19.6 us -> 42.4 us  [the longest x1 22.8 us: lift(): pl.pallas_call(lift_kernel, grid=(slabs,), in_specs=[pl.BlockSpec(memory_...]
    unnamed x140 -> x127, local copies, waits for them, and re-layouts: 33.3 us -> 20.2 us
    all_gather x0 -> x2, waiting for transfers between devices: none -> 11.7 us  [the longest x1 11.7 us: on_device(): mixed_all = lax.all_gather(mixed, 'mlp', axis=0, tiled=False)]
    ppermute x36 -> x43, starting transfers between devices: 41.1 us -> 37.9 us  [hop(): lax.ppermute(array, 'tok', [(i, i ^ pairs[i % 2]) for i in range(count)])]
  transfers between devices with their start and end apart: 47 -> 54, of which waited for: 26 -> 23; matrix products, arithmetic and copies ran while one was open for 18% -> 21% of each run, Pallas kernels for 11% -> 28%
where the time goes in v3:
time: 797 us; the launch traced here: 790 us
  Pallas kernels  260 us (33%)
  waiting for transfers between devices  255 us (32%)
  other arithmetic  72.9 us (9%)
  matrix products  71.1 us (9%)
  starting transfers between devices  46.9 us (6%)
  local copies, waits for them, and re-layouts  38.1 us (5%)
  blocking collectives  31.2 us (4%)
  between operations  15.5 us (2%)
    ppermute x43, waiting for transfers between devices, hop(): lax.ppermute(array, 'tok', [(i, i ^ pairs[i % 2]) for i in range(count)])  130 us
    pallas_call x4, Pallas kernels, soap(): pl.pallas_call(functools.partial(soap_kernel, turned, swapped), grid=(gro...  85.5 us
    all_gather x3, waiting for transfers between devices, gather_slabs(): return lax.all_gather(array, 'mlp', axis=0, tiled=True)  68.7 us
    dot_general x14, matrix products, tn(): lax.dot_general(left, right, (((0,), (0,)), ((), ())), preferred_element_...  54.1 us
    reduce_scatter x3, waiting for transfers between devices, scatter_slabs(): return lax.psum_scatter(array, 'mlp', scatter_dimension=0, tiled=True)  44.5 us
    ppermute x43, starting transfers between devices, hop(): lax.ppermute(array, 'tok', [(i, i ^ pairs[i % 2]) for i in range(count)])  37.9 us
    pallas_call x1, Pallas kernels, mlp(): pl.pallas_call(mlp_kernel, grid=(count // rows,), in_specs=[row(model), r...  36.5 us
    pallas_call x1, Pallas kernels, front(): pl.pallas_call(front_kernel, grid=(count // rows,), in_specs=[row(model),...  33.8 us
  transfers between devices with their start and end apart: 54, of which 23 were waited for; matrix products, arithmetic and copies ran while one was open for 21% of the time, Pallas kernels for 28%

profile of v3, /device:TPU:0, one launch (start us, length us, event | category | flops | bytes accessed | tf_op | source)
XLA Modules:
  0.0 790.2 jit_solution(10105961551868082412)
XLA Ops:
  8.1 2.5 collective-permute-start.6
  11.4 4.5 collective-permute-start
  24.8 4.9 permute_columns.4.tok
  46.5 6.1 fusion.63
  52.6 7.4 collective-permute-done.5.w_1
  65.7 33.8 %front.1 = (bf16[1024,2048]{1,0:T(8,128)(2,1)}, f32[1024,704]{1,0:T(8,128)}, bf16[1024,704]{1,0:T(8,128)(2,1)}, bf16[16,704]{1,0:T(8,128)(2,1)}, bf16[1024,704]{...) custom-call(bf16[1024,2048]{1,0:T(8,128)(2,1)} %permute_columns.4.to, ...), custom_call_target="tpu_custom_call" | custom-call | flops 37399998464 | bytes 112200000 | tf_op jit(solution)/shard_map/front/pallas_call | solution.py:238
  100.2 10.1 %all-gather.4.ends = f32[8,2,704]{2,1,0:T(2,128)} all-gather(f32[1,2,704]{2,1,0:T(2,128)S(1)} %slice_bitcast_fusion.16), channel_id=2, replica_groups=mesh['tok'=8,'mlp'=4] {'tok'}, dimensions={0}, use_global_device_ids=true | all-gather | bytes 50688 | tf_op jit(solution)/shard_map/all_gather | solution.py:1011
  110.3 7.4 finish_state.1
  120.5 3.3 pad_maximum_fusion.1.w_0
  124.6 10.9 %collective-permute-done.13 = bf16[1,1536,256]{2,1,0:T(8,128)(2,1)S(1)} collective-permute-done((bf16[1,1536,256]{2,1,0:T(8,128)(2,1)S(1)}, bf16[1,1536,256]{2,1,0:T(8,128)(2,1)S(1)}, u32[]{:S(2)}, u32[]{:S(2)}) %collective-permute-start.13) | collective-permute-done | bytes 786464 | tf_op jit(solution)/shard_map/ppermute | solution.py:735
  138.3 3.4 pad_maximum_fusion.w_0
  144.0 5.2 permute_columns.6
  149.7 2.3 constant_dynamic-slice_fusion.base
  152.1 26.4 %collective-permute-done.14 = bf16[2,1536,256]{2,1,0:T(8,128)(2,1)} collective-permute-done((bf16[2,1536,256]{2,1,0:T(8,128)(2,1)}, bf16[2,1536,256]{2,1,0:T(8,128)(2,1)}, u32[]{:S(2)}, u32[]{:S(2)}) %collective-permute-start.14) | collective-permute-done | bytes 1572896 | tf_op jit(solution)/shard_map/ppermute | solution.py:735
  182.6 29.6 %collective-permute-done.18.w_1 = bf16[2,2,256,1536]{3,2,1,0:T(8,128)(2,1)} collective-permute-done((bf16[2,2,256,1536]{3,2,1,0:T(8,128)(2,1)}, bf16[2,2,256,1536]{3,2,1,0:T(8,128)(2,1)}, u32[]{:S(2)}, u32[]{:S(2)}) %collective-permute-start.18) | collective-permute-done | bytes 3145760 | tf_op jit(solution)/shard_map/ppermute | solution.py:735
  213.3 8.6 %fusion.117.dhid = f32[1024,1536]{1,0:T(8,128)} fusion(bf16[1024,2048]{1,0:T(8,128)(2,1)S(1)} %copy-done.20, bf16[1536,2048]{1,0:T(8,128)(2,1)S(1)} %fusion.69), kind=kOutput, calls=%fused_computation.267 | convolution fusion | flops 6442450944 | bytes 16777216 | tf_op jit(solution)/shard_map/dot_general | solution.py:49
  221.9 11.7 %all-gather.18.cloned.1.call-done = bf16[4096,704]{1,0:T(8,128)(2,1)} async-done(((bf16[1024,704]{1,0:T(8,128)(2,1)}), bf16[4096,704]{1,0:T(8,128)(2,1)}) %all-gather.18.cloned.1.call-update) | async-done | bytes 5767184 | tf_op jit(solution)/shard_map/all_gather | solution.py:1016
  233.5 22.8 %lift.1 = (bf16[1024,2048]{1,0:T(8,128)(2,1)}, f32[256,2048]{1,0:T(8,128)}) custom-call(s32[1]{0:T(128)} %bitcast.slab, bf16[4,1024,704]{2,1,0:T(8,128)(2,1)} %bitcast.156, bf16[1024,2048]{1,0:T(8,128)(2,1)} %permute_columns.4.tok, f32[1,2048]{1,0:T(1,128)} %bitcast.153, bf16[2,4,704,256]{3,2,1,0:T(8,128)(2,1)} %pad_maximum_fusion.1.w_0, ...), custom_call_target="tpu_custom_call" | custom-call | flops 24199999488 | bytes 72600000 | tf_op jit(solution)/shard_map/lift/pallas_call | solution.py:339
  256.3 36.5 %mlp.1 = (bf16[1024,1536]{1,0:T(8,128)(2,1)}, bf16[1024,1536]{1,0:T(8,128)(2,1)}, bf16[1024,1536]{1,0:T(8,128)(2,1)}, bf16[1024,2048]{1,0:T(8,128)(2,1)}) custom-call(bf16[1024,2048]{1,0:T(8,128)(2,1)} %get-tuple-element.133.xn, f32[1024,1536]{1,0:T(8,128)} %fusion.117.dhid, bf16[2,2,256,1536]{3,2,1,0:T(8,128)(2,1)} %pad_maximum_fusion.w_0, ...), custom_call_target="tpu_custom_call" | custom-call | flops 39600001024 | bytes 118800000 | tf_op jit(solution)/shard_map/mlp/pallas_call | solution.py:388
  294.7 6.8 convolution_convert_fusion.2
  301.6 4.8 convolution_convert_fusion.3
  306.4 5.3 fusion.25
  311.7 5.4 fusion.23
  317.1 4.8 convolution_convert_fusion.1
  322.4 5.3 fusion.7
  327.8 8.4 %convolution_convert_fusion = bf16[1024,2048]{1,0:T(8,128)(2,1)} fusion(bf16[1024,1536]{1,0:T(8,128)(2,1)S(1)} %copy-done.49, bf16[1536,2048]{1,0:T(8,128)(2,1)S(1)} %bitcast.145), kind=kOutput, calls=%fused_computation.4 | convolution fusion | flops 6444548096 | bytes 13631488 | tf_op jit(solution)/shard_map/dot_general | solution.py:45
  336.2 2.9 fusion.50
  341.8 2.9 fusion.57
  348.9 19.1 %reduce-scatter.6.cloned.1.call-done.upstream = bf16[256,2048]{1,0:T(8,128)(2,1)} async-done(((bf16[1024,2048]{1,0:T(8,128)(2,1)}), bf16[256,2048]{1,0:T(8,128)(2,1)}) %reduce-scatter.6.cloned.1.call-update) | async-done | bytes 1048592 | tf_op jit(solution)/shard_map/reduce_scatter | solution.py:730
  368.0 4.2 settle.2
  376.0 2.7 collective-permute-done.22
  378.7 2.4 fusion.55
  382.6 3.9 collective-permute-done.26
  388.7 6.2 collective-permute-done.23
  398.4 33.4 %soap.4 = (f32[2,256,1536]{2,1,0:T(8,128)}, f32[2,256,1536]{2,1,0:T(8,128)}, f32[2,256,1536]{2,1,0:T(8,128)}) custom-call(f32[2,256,1536]{2,1,0:T(8,128)} %w.1, f32[2,256,1536]{2,1,0:T(8,128)} %m.1, f32[2,256,1536]{2,1,0:T(8,128)} %v.1, bf16[2,256,1536]{2,1,0:T(8,128)(2,1)} %pad_maximum_fusion.5.g, f32[2,4,24,2,64,64]{5,4,3,2,1,0:T(8,128)} %q.2), custom_call_target="tpu_custom_call" | custom-call | flops 36044800000 | bytes 108134400 | tf_op jit(solution)/shard_map/soap/pallas_call | solution.py:700
  431.9 21.8 %all-gather.12.cloned.1.call-done.d_rec = bf16[1024,2048]{1,0:T(8,128)(2,1)} async-done(((bf16[256,2048]{1,0:T(8,128)(2,1)}), bf16[1024,2048]{1,0:T(8,128)(2,1)}) %all-gather.12.cloned.1.call-update) | async-done | bytes 4194320 | tf_op jit(solution)/shard_map/all_gather | solution.py:726
  453.7 19.6 %back_scan.1 = (bf16[1024,704]{1,0:T(8,128)(2,1)}, f32[1024,704]{1,0:T(8,128)}, f32[1024,704]{1,0:T(8,128)}, f32[8,704]{1,0:T(8,128)}) custom-call(s32[1]{0:T(128)} %bitcast.slab, bf16[1024,2048]{1,0:T(8,128)(2,1)} %all-gather.12.cloned.1.call-done.d_rec, bf16[2,4,704,256]{3,2,1,0:T(8,128)(2,1)} %pad_maximum_fusion.1.w_0, ...), custom_call_target="tpu_custom_call" | custom-call | flops 22000001024 | bytes 66000000 | tf_op jit(solution)/shard_map/back_scan/pallas_call | solution.py:430
  474.0 10.1 %all-gather.5.ends = f32[8,2,704]{2,1,0:T(2,128)} all-gather(f32[1,2,704]{2,1,0:T(2,128)S(1)} %slice_bitcast_fusion.15), channel_id=5, replica_groups=mesh['tok'=8,'mlp'=4] {'tok'}, dimensions={0}, use_global_device_ids=true | all-gather | bytes 50688 | tf_op jit(solution)/shard_map/all_gather | solution.py:1078
  484.1 19.2 %gates_back.1 = (bf16[1024,704]{1,0:T(8,128)(2,1)}, bf16[1024,704]{1,0:T(8,128)(2,1)}, bf16[1024,704]{1,0:T(8,128)(2,1)}, f32[16,704]{1,0:T(8,128)}, f32[16,704]{1,0:T(8,128)}, /*index=5*/f32[8,704]{1,0:T(8,128)}) custom-call(s32[1]{0:T(128)} %bitcast.1.rank, f32[8,2,704]{2,1,0:T(2,128)} %all-gather.5.ends, f32[1024,704]{1,0:T(8,128)} %get-tuple-element.154.g_l, ...), custom_call_target="tpu_custom_call" | custom-call | flops 20899999744 | bytes 62700000 | tf_op jit(solution)/shard_map/gates_back/pallas_call | solution.py:539
  504.6 2.6 collective-permute-start.32
  507.8 12.2 %pair_back.1 = (bf16[1024,2048]{1,0:T(8,128)(2,1)}, bf16[1024,704]{1,0:T(8,128)(2,1)}) custom-call(bf16[1024,704]{1,0:T(8,128)(2,1)} %get-tuple-element.173.left, bf16[1024,704]{1,0:T(8,128)(2,1)} %get-tuple-element.162.right, f32[16,704]{1,0:T(8,128)} %get-tuple-element.163.tail, f32[16,704]{1,0:T(8,128)} %copy-done.40, ...), custom_call_target="tpu_custom_call" | custom-call | flops 13200000000 | bytes 39600000 | tf_op jit(solution)/shard_map/pair_back/pallas_call | solution.py:589
  520.0 11.2 %reduce-scatter.4.cloned.1.call-done = bf16[256,2048]{1,0:T(8,128)(2,1)} async-done(((bf16[1024,2048]{1,0:T(8,128)(2,1)}), bf16[256,2048]{1,0:T(8,128)(2,1)}) %reduce-scatter.4.cloned.1.call-update) | async-done | bytes 1048592 | tf_op jit(solution)/shard_map/reduce_scatter | solution.py:730
  534.8 2.3 constant_dynamic-slice_fusion.1.value
  537.1 8.2 %collective-permute-done.33 = bf16[256,1536]{1,0:T(8,128)(2,1)S(1)} collective-permute-done((bf16[256,1536]{1,0:T(8,128)(2,1)S(1)}, bf16[256,1536]{1,0:T(8,128)(2,1)S(1)}, u32[]{:S(2)}, u32[]{:S(2)}) %collective-permute-start.33) | collective-permute-done | bytes 786464 | tf_op jit(solution)/shard_map/ppermute | solution.py:735
  545.3 2.9 fusion.44
  548.4 5.1 fusion.34
  553.5 2.8 fusion.31
  556.8 2.8 fusion.37
  559.6 24.1 %soap.5 = (f32[1,1536,256]{2,1,0:T(8,128)}, f32[1,1536,256]{2,1,0:T(8,128)}, f32[1,1536,256]{2,1,0:T(8,128)}) custom-call(f32[1,1536,256]{2,1,0:T(8,128)} %bitcast.135, f32[1,1536,256]{2,1,0:T(8,128)} %bitcast.158, f32[1,1536,256]{2,1,0:T(8,128)} %bitcast.159, bf16[1,256,1536]{2,1,0:T(8,128)(2,1)} %bitcast.141, f32[1,24,4,2,64,64]{5,4,3,2,1,0:T(8,128)} %bitcast.155), custom_call_target="tpu_custom_call" | custom-call | flops 18022400000 | bytes 54067200 | tf_op jit(solution)/shard_map/soap/pallas_call | solution.py:700
  583.8 3.4 fusion.11
  597.0 14.2 %reduce-scatter.8.cloned.1.call-done.upstream = bf16[256,2048]{1,0:T(8,128)(2,1)} async-done(((bf16[1024,2048]{1,0:T(8,128)(2,1)}), bf16[256,2048]{1,0:T(8,128)(2,1)}) %reduce-scatter.8.cloned.1.call-update) | async-done | bytes 1048592 | tf_op jit(solution)/shard_map/reduce_scatter | solution.py:730
  611.2 4.4 settle.3
  615.9 2.7 fusion.119
  628.1 3.5 collective-permute-done.41
  633.2 2.4 permute_columns.7
  641.9 6.4 collective-permute-done.36
  651.4 10.4 %collective-permute-done.34 = bf16[704,512]{1,0:T(8,128)(2,1)} collective-permute-done((bf16[704,512]{1,0:T(8,128)(2,1)}, bf16[704,512]{1,0:T(8,128)(2,1)}, u32[]{:S(2)}, u32[]{:S(2)}) %collective-permute-start.34) | collective-permute-done | bytes 720928 | tf_op jit(solution)/shard_map/ppermute | solution.py:735
  664.6 9.0 %collective-permute-done.38 = bf16[704,512]{1,0:T(8,128)(2,1)S(1)} collective-permute-done((bf16[704,512]{1,0:T(8,128)(2,1)}, bf16[704,512]{1,0:T(8,128)(2,1)S(1)}, u32[]{:S(2)}, u32[]{:S(2)}) %collective-permute-start.38) | collective-permute-done | bytes 720928 | tf_op jit(solution)/shard_map/ppermute | solution.py:735
  680.9 17.2 %soap.6 = (f32[2,704,256]{2,1,0:T(8,128)}, f32[2,704,256]{2,1,0:T(8,128)}, f32[2,704,256]{2,1,0:T(8,128)}) custom-call(f32[2,704,256]{2,1,0:T(8,128)} %bitcast.138, f32[2,704,256]{2,1,0:T(8,128)} %bitcast.160, f32[2,704,256]{2,1,0:T(8,128)} %bitcast.161, bf16[2,704,256]{2,1,0:T(8,128)(2,1)} %pad_maximum_fusion.12.g, f32[2,4,11,2,64,64]{5,4,3,2,1,0:T(8,128)} %q.3), custom_call_target="tpu_custom_call" | custom-call | flops 16520532992 | bytes 49561600 | tf_op jit(solution)/shard_map/soap/pallas_call | solution.py:700
  702.4 10.8 %soap.7 = (f32[1,704,256]{2,1,0:T(8,128)}, f32[1,704,256]{2,1,0:T(8,128)}, f32[1,704,256]{2,1,0:T(8,128)}) custom-call(f32[1,704,256]{2,1,0:T(8,128)} %bitcast.142, f32[1,704,256]{2,1,0:T(8,128)} %bitcast.162, f32[1,704,256]{2,1,0:T(8,128)} %bitcast.163, bf16[1,704,256]{2,1,0:T(8,128)(2,1)} %fusion.98.g, f32[1,11,4,2,64,64]{5,4,3,2,1,0:T(8,128)} %bitcast.157), custom_call_target="tpu_custom_call" | custom-call | flops 8260266496 | bytes 24780800 | tf_op jit(solution)/shard_map/soap/pallas_call | solution.py:700
  713.2 11.0 %psum.7 = f32[2,256]{1,0:T(2,128)S(1)} all-reduce(f32[2,256]{1,0:T(2,128)S(1)} %fusion.106), channel_id=1, replica_groups=mesh['tok'=8,'mlp'=4] {'mlp'}, use_global_device_ids=true, to_apply=%region_5.6 | all-reduce | flops 512 | bytes 4096 | tf_op jit(solution)/shard_map/psum | solution.py:1125
  724.8 6.7 convert_element_type.330
  731.4 46.9 %all-gather.14.cloned.1.call-done = bf16[1024,2048]{1,0:T(8,128)(2,1)} async-done(((bf16[256,2048]{1,0:T(8,128)(2,1)}), bf16[1024,2048]{1,0:T(8,128)(2,1)}) %all-gather.14.cloned.1.call-update) | async-done | bytes 4194320 | tf_op jit(solution)/shard_map/all_gather | solution.py:726
  778.3 4.8 copy.87
  (337 shorter events, 120.3 us)
Async XLA Ops:
  7.2 14.8 %copy-start.11 = (f32[2,256,704]{1,2,0:T(8,128)S(1)}, f32[2,256,704]{1,2,0:T(8,128)}, u32[]{:S(2)}) copy-start(f32[2,256,704]{1,2,0:T(8,128)} %param.37) | copy-start | bytes 4325380
  7.2 56.4 %all-gather.20.cloned.1.call-start = ((), (), s32[]{:S(2)}) async-start(), calls=%async_computation.10 | async-start | bytes 1802240 | tf_op jit(solution)/shard_map/all_gather | solution.py:964
  8.1 21.6 %collective-permute-start.6 = (s32[16]{0:T(128)S(1)}, s32[16]{0:T(128)S(1)}, u32[]{:S(2)}, u32[]{:S(2)}) collective-permute-start(s32[16]{0:T(128)S(1)} %slice.478), channel_id=1, source_target_pairs={{0,4},{4,8},{8,12},{12,16},{16,20},{20,24},{24,28},{1,5},{5,9},{9,... | collective-permute-start | bytes 200 | tf_op jit(solution)/shard_map/ppermute | solution.py:989
  11.4 21.5 %collective-permute-start = (bf16[16,2048]{1,0:T(8,128)(2,1)S(1)}, bf16[16,2048]{1,0:T(8,128)(2,1)S(1)}, u32[]{:S(2)}, u32[]{:S(2)}) collective-permute-start(bf16[16,2048]{1,0:T(8,128)(2,1)S(1)} %slice.470), channel_id=1, source_target_pairs={{0,4},{4,8},{8,12},{12,16},{16,20},{20,24},{24,28},{1,5},{5,9},{9,... | collective-permute-start | bytes 196616 | tf_op jit(solution)/shard_map/ppermute | solution.py:987
  18.5 12.9 %collective-permute-start.1 = (bf16[1,8,4024]{2,1,0:T(8,128)(2,1)S(1)}, bf16[1,8,4024]{2,1,0:T(8,128)(2,1)S(1)}, u32[]{:S(2)}, u32[]{:S(2)}) collective-permute-start(bf16[1,8,4024]{2,1,0:T(8,128)(2,1)S(1)} %concatenate.92), channel_id=1, source_target_pairs={{0,16},{4,12},{8,24},{12,4},{16,0},{20,28},{24,8},{28,20},{1,17},{... | collective-permute-start | bytes 193160 | tf_op jit(solution)/shard_map/ppermute | solution.py:735
  21.9 211.6 %all-gather.18.cloned.1.call-start = ((), (), s32[]{:S(2)}) async-start(), calls=%async_computation.9 | async-start | bytes 7864320 | tf_op jit(solution)/shard_map/all_gather | solution.py:1016
  22.0 17.5 %collective-permute-start.4 = (bf16[1,2,704,256]{3,2,1,0:T(8,128)(2,1)S(1)}, bf16[1,2,704,256]{3,2,1,0:T(8,128)(2,1)}, u32[]{:S(2)}, u32[]{:S(2)}) collective-permute-start(bf16[1,2,704,256]{3,2,1,0:T(8,128)(2,1)S(1)} %convert_bitcast_fusion.1), channel_id=1, source_target_pairs={{0,16},{4,12},{8,24},{12,4},{16,0},{20,28},{24,8},{28,20},{1,17},{... | collective-permute-start | bytes 2162696 | tf_op jit(solution)/shard_map/ppermute | solution.py:735
  31.3 5.0 collective-permute-start.2
  36.4 1.6 collective-permute-start.3
  40.8 19.2 %collective-permute-start.5 = (bf16[2,2,704,256]{3,2,1,0:T(8,128)(2,1)S(1)}, bf16[2,2,704,256]{3,2,1,0:T(8,128)(2,1)}, u32[]{:S(2)}, u32[]{:S(2)}) collective-permute-start(bf16[2,2,704,256]{3,2,1,0:T(8,128)(2,1)S(1)} %pad_maximum_fusion.7.w_0), channel_id=1, source_target_pairs={{0,8},{4,20},{8,0},{12,28},{16,24},{20,4},{24,16},{28,12},{1,9},{5... | collective-permute-start | bytes 4325384 | tf_op jit(solution)/shard_map/ppermute | solution.py:735
  46.5 15.5 %copy-start.29 = (f32[8,704]{1,0:T(8,128)}, f32[8,704]{1,0:T(8,128)S(1)}, u32[]{:S(2)}) copy-start(f32[8,704]{1,0:T(8,128)S(1)} %scatter.4.vec) | copy-start | bytes 67588
  52.6 13.0 %collective-permute-start.7 = (bf16[2,2,704,256]{3,2,1,0:T(8,128)(2,1)S(1)}, bf16[2,2,704,256]{3,2,1,0:T(8,128)(2,1)}, u32[]{:S(2)}, u32[]{:S(2)}) collective-permute-start(bf16[2,2,704,256]{3,2,1,0:T(8,128)(2,1)S(1)} %pad_maximum_fusion.7.w_0), channel_id=1, source_target_pairs={{0,4},{4,0},{8,12},{12,8},{16,20},{20,16},{24,28},{28,24},{1,5},{5... | collective-permute-start | bytes 4325384 | tf_op jit(solution)/shard_map/ppermute | solution.py:735
  60.0 5.7 collective-permute-start.8
  63.6 56.2 %collective-permute-start.9 = (bf16[1,4,704,256]{3,2,1,0:T(8,128)(2,1)}, bf16[1,4,704,256]{3,2,1,0:T(8,128)(2,1)}, u32[]{:S(2)}, u32[]{:S(2)}) collective-permute-start(bf16[1,4,704,256]{3,2,1,0:T(8,128)(2,1)} %bitcast.139), channel_id=1, source_target_pairs={{0,16},{4,12},{8,24},{12,4},{16,0},{20,28},{24,8},{28,20},{1,17},{... | collective-permute-start | bytes 4325384 | tf_op jit(solution)/shard_map/ppermute | solution.py:735
  65.2 59.5 %collective-permute-start.17 = (bf16[1,2,256,1536]{3,2,1,0:T(8,128)(2,1)S(1)}, bf16[1,2,256,1536]{3,2,1,0:T(8,128)(2,1)}, u32[]{:S(2)}, u32[]{:S(2)}) collective-permute-start(bf16[1,2,256,1536]{3,2,1,0:T(8,128)(2,1)S(1)} %convert_bitcast_fusion), channel_id=1, source_target_pairs={{0,16},{4,12},{8,24},{12,4},{16,0},{20,28},{24,8},{28,20},{1,17},{... | collective-permute-start | bytes 4718600 | tf_op jit(solution)/shard_map/ppermute | solution.py:735
  117.7 250.3 %reduce-scatter.6.cloned.1.call-start = ((), (), s32[]{:S(2)}) async-start(), calls=%async_computation.4 | async-start | bytes 5242880 | tf_op jit(solution)/shard_map/reduce_scatter | solution.py:730
  119.2 16.3 %collective-permute-start.13 = (bf16[1,1536,256]{2,1,0:T(8,128)(2,1)S(1)}, bf16[1,1536,256]{2,1,0:T(8,128)(2,1)S(1)}, u32[]{:S(2)}, u32[]{:S(2)}) collective-permute-start(bf16[1,1536,256]{2,1,0:T(8,128)(2,1)S(1)} %convert_bitcast_fusion.2), channel_id=1, source_target_pairs={{0,16},{4,12},{8,24},{12,4},{16,0},{20,28},{24,8},{28,20},{1,17},{... | collective-permute-start | bytes 2359304 | tf_op jit(solution)/shard_map/ppermute | solution.py:735
  123.8 58.3 %collective-permute-start.10 = (bf16[2,4,704,256]{3,2,1,0:T(8,128)(2,1)}, bf16[2,4,704,256]{3,2,1,0:T(8,128)(2,1)}, u32[]{:S(2)}, u32[]{:S(2)}) collective-permute-start(bf16[2,4,704,256]{3,2,1,0:T(8,128)(2,1)} %pad_maximum_fusion.1.w_0), channel_id=1, source_target_pairs={{0,8},{4,20},{8,0},{12,28},{16,24},{20,4},{24,16},{28,12},{1,9},{5... | collective-permute-start | bytes 8650760 | tf_op jit(solution)/shard_map/ppermute | solution.py:735
  137.7 40.8 %collective-permute-start.14 = (bf16[2,1536,256]{2,1,0:T(8,128)(2,1)}, bf16[2,1536,256]{2,1,0:T(8,128)(2,1)}, u32[]{:S(2)}, u32[]{:S(2)}) collective-permute-start(bf16[2,1536,256]{2,1,0:T(8,128)(2,1)} %pad_maximum_fusion.2), channel_id=1, source_target_pairs={{0,8},{4,20},{8,0},{12,28},{16,24},{20,4},{24,16},{28,12},{1,9},{5... | collective-permute-start | bytes 4718600 | tf_op jit(solution)/shard_map/ppermute | solution.py:735
  141.7 70.5 %collective-permute-start.18 = (bf16[2,2,256,1536]{3,2,1,0:T(8,128)(2,1)}, bf16[2,2,256,1536]{3,2,1,0:T(8,128)(2,1)}, u32[]{:S(2)}, u32[]{:S(2)}) collective-permute-start(bf16[2,2,256,1536]{3,2,1,0:T(8,128)(2,1)} %pad_maximum_fusion.w_0), channel_id=1, source_target_pairs={{0,8},{4,20},{8,0},{12,28},{16,24},{20,4},{24,16},{28,12},{1,9},{5... | collective-permute-start | bytes 9437192 | tf_op jit(solution)/shard_map/ppermute | solution.py:735
  144.0 77.8 %collective-permute-start.11 = (bf16[2,4,704,256]{3,2,1,0:T(8,128)(2,1)}, bf16[2,4,704,256]{3,2,1,0:T(8,128)(2,1)}, u32[]{:S(2)}, u32[]{:S(2)}) collective-permute-start(bf16[2,4,704,256]{3,2,1,0:T(8,128)(2,1)} %pad_maximum_fusion.1.w_0), channel_id=1, source_target_pairs={{0,4},{4,0},{8,12},{12,8},{16,20},{20,16},{24,28},{28,24},{1,5},{5... | collective-permute-start | bytes 8650760 | tf_op jit(solution)/shard_map/ppermute | solution.py:735
  144.0 35.2 %copy-start.24 = (bf16[1536,2048]{1,0:T(8,128)(2,1)S(1)}, bf16[1536,2048]{1,0:T(8,128)(2,1)}, u32[]{:S(2)}) copy-start(bf16[1536,2048]{1,0:T(8,128)(2,1)} %convert_dynamic-update-slice_fusion) | copy-start | bytes 18874372
  149.2 30.0 %copy-start.3 = (bf16[1,1536,256]{2,1,0:T(8,128)(2,1)S(1)}, bf16[1,1536,256]{2,1,0:T(8,128)(2,1)}, u32[]{:S(2)}) copy-start(bf16[1,1536,256]{2,1,0:T(8,128)(2,1)} %copy-done.2) | copy-start | bytes 2359300
  149.2 32.6 %collective-permute-start.15 = (bf16[2,1536,256]{2,1,0:T(8,128)(2,1)}, bf16[2,1536,256]{2,1,0:T(8,128)(2,1)S(1)}, u32[]{:S(2)}, u32[]{:S(2)}) collective-permute-start(bf16[2,1536,256]{2,1,0:T(8,128)(2,1)} %pad_maximum_fusion.2), channel_id=1, source_target_pairs={{0,4},{4,0},{8,12},{12,8},{16,20},{20,16},{24,28},{28,24},{1,5},{5... | collective-permute-start | bytes 4718600 | tf_op jit(solution)/shard_map/ppermute | solution.py:735
  178.5 34.5 %collective-permute-start.16 = (bf16[2,1536,256]{2,1,0:T(8,128)(2,1)}, bf16[2,1536,256]{2,1,0:T(8,128)(2,1)S(1)}, u32[]{:S(2)}, u32[]{:S(2)}) collective-permute-start(bf16[2,1536,256]{2,1,0:T(8,128)(2,1)} %collective-permute-done.14), channel_id=1, source_target_pairs={{0,4},{4,0},{8,12},{12,8},{16,20},{20,16},{24,28},{28,24},{1,5},{5... | collective-permute-start | bytes 4718600 | tf_op jit(solution)/shard_map/ppermute | solution.py:735
  181.8 74.5 %collective-permute-start.19 = (bf16[2,2,256,1536]{3,2,1,0:T(8,128)(2,1)}, bf16[2,2,256,1536]{3,2,1,0:T(8,128)(2,1)}, u32[]{:S(2)}, u32[]{:S(2)}) collective-permute-start(bf16[2,2,256,1536]{3,2,1,0:T(8,128)(2,1)} %pad_maximum_fusion.w_0), channel_id=1, source_target_pairs={{0,4},{4,0},{8,12},{12,8},{16,20},{20,16},{24,28},{28,24},{1,5},{5... | collective-permute-start | bytes 9437192 | tf_op jit(solution)/shard_map/ppermute | solution.py:735
  182.0 31.2 %copy-start.20 = (bf16[1024,2048]{1,0:T(8,128)(2,1)S(1)}, bf16[1024,2048]{1,0:T(8,128)(2,1)}, u32[]{:S(2)}) copy-start(bf16[1024,2048]{1,0:T(8,128)(2,1)} %permute_columns.6) | copy-start | bytes 12582916
  182.0 39.8 %collective-permute-start.12 = (bf16[2,4,704,256]{3,2,1,0:T(8,128)(2,1)}, bf16[2,4,704,256]{3,2,1,0:T(8,128)(2,1)}, u32[]{:S(2)}, u32[]{:S(2)}) collective-permute-start(bf16[2,4,704,256]{3,2,1,0:T(8,128)(2,1)} %collective-permute-done.10.w_1), channel_id=1, source_target_pairs={{0,4},{4,0},{8,12},{12,8},{16,20},{20,16},{24,28},{28,24},{1,5},{5... | collective-permute-start | bytes 8650760 | tf_op jit(solution)/shard_map/ppermute | solution.py:735
  212.2 44.2 %collective-permute-start.20 = (bf16[2,2,256,1536]{3,2,1,0:T(8,128)(2,1)}, bf16[2,2,256,1536]{3,2,1,0:T(8,128)(2,1)}, u32[]{:S(2)}, u32[]{:S(2)}) collective-permute-start(bf16[2,2,256,1536]{3,2,1,0:T(8,128)(2,1)} %collective-permute-done.18.w_1), channel_id=1, source_target_pairs={{0,4},{4,0},{8,12},{12,8},{16,20},{20,16},{24,28},{28,24},{1,5},{5... | collective-permute-start | bytes 9437192 | tf_op jit(solution)/shard_map/ppermute | solution.py:735
  292.9 160.8 %all-gather.12.cloned.1.call-start = ((), (), s32[]{:S(2)}) async-start(), calls=%async_computation.5 | async-start | bytes 5242880 | tf_op jit(solution)/shard_map/all_gather | solution.py:726
  301.5 34.7 %collective-permute-start.24 = (bf16[1024,1536]{1,0:T(8,128)(2,1)}, bf16[1024,1536]{1,0:T(8,128)(2,1)}, u32[]{:S(2)}, u32[]{:S(2)}) collective-permute-start(bf16[1024,1536]{1,0:T(8,128)(2,1)} %convolution_convert_fusion.2), channel_id=1, source_target_pairs={{0,4},{4,0},{8,12},{12,8},{16,20},{20,16},{24,28},{28,24},{1,5},{5... | collective-permute-start | bytes 9437192 | tf_op jit(solution)/shard_map/ppermute | solution.py:735
  311.7 16.0 %slice-start.2 = ((s8[6291456]{0:T(1024)(128)(4,1)}), s8[4194304]{0:T(1024)(128)(4,1)S(1)}, s32[]{:S(2)}) async-start(s8[6291456]{0:T(1024)(128)(4,1)} %bitcast.144), calls=%async_computation.13 | async-start | bytes 8388608
  321.9 19.8 %collective-permute-start.21 = (bf16[1024,1536]{1,0:T(8,128)(2,1)}, bf16[1024,1536]{1,0:T(8,128)(2,1)}, u32[]{:S(2)}, u32[]{:S(2)}) collective-permute-start(bf16[1024,1536]{1,0:T(8,128)(2,1)} %convolution_convert_fusion.3), channel_id=1, source_target_pairs={{0,4},{4,0},{8,12},{12,8},{16,20},{20,16},{24,28},{28,24},{1,5},{5... | collective-permute-start | bytes 9437192 | tf_op jit(solution)/shard_map/ppermute | solution.py:735
  327.7 19.3 %collective-permute-start.27 = (bf16[1024,1536]{1,0:T(8,128)(2,1)}, bf16[1024,1536]{1,0:T(8,128)(2,1)S(1)}, u32[]{:S(2)}, u32[]{:S(2)}) collective-permute-start(bf16[1024,1536]{1,0:T(8,128)(2,1)} %convolution_convert_fusion.1), channel_id=1, source_target_pairs={{0,4},{4,0},{8,12},{12,8},{16,20},{20,16},{24,28},{28,24},{1,5},{5... | collective-permute-start | bytes 9437192 | tf_op jit(solution)/shard_map/ppermute | solution.py:735
  340.3 32.0 %collective-permute-start.25 = (bf16[512,1536]{1,0:T(8,128)(2,1)}, bf16[512,1536]{1,0:T(8,128)(2,1)}, u32[]{:S(2)}, u32[]{:S(2)}) collective-permute-start(bf16[512,1536]{1,0:T(8,128)(2,1)} %pad_maximum_fusion.4), channel_id=1, source_target_pairs={{0,8},{4,20},{8,0},{12,28},{16,24},{20,4},{24,16},{28,12},{1,9},{5... | collective-permute-start | bytes 4718600 | tf_op jit(solution)/shard_map/ppermute | solution.py:735
  345.9 32.8 %collective-permute-start.22 = (bf16[512,1536]{1,0:T(8,128)(2,1)}, bf16[512,1536]{1,0:T(8,128)(2,1)}, u32[]{:S(2)}, u32[]{:S(2)}) collective-permute-start(bf16[512,1536]{1,0:T(8,128)(2,1)} %pad_maximum_fusion.3), channel_id=1, source_target_pairs={{0,8},{4,20},{8,0},{12,28},{16,24},{20,4},{24,16},{28,12},{1,9},{5... | collective-permute-start | bytes 4718600 | tf_op jit(solution)/shard_map/ppermute | solution.py:735
  372.2 159.0 %reduce-scatter.4.cloned.1.call-start = ((), (), s32[]{:S(2)}) async-start(), calls=%async_computation.3 | async-start | bytes 5242880 | tf_op jit(solution)/shard_map/reduce_scatter | solution.py:730
  374.4 12.1 %collective-permute-start.26 = (bf16[256,1536]{1,0:T(8,128)(2,1)S(1)}, bf16[256,1536]{1,0:T(8,128)(2,1)S(1)}, u32[]{:S(2)}, u32[]{:S(2)}) collective-permute-start(bf16[256,1536]{1,0:T(8,128)(2,1)S(1)} %fusion.48), channel_id=1, source_target_pairs={{0,16},{4,12},{8,24},{12,4},{16,0},{20,28},{24,8},{28,20},{1,17},{... | collective-permute-start | bytes 2359304 | tf_op jit(solution)/shard_map/ppermute | solution.py:735
  381.1 13.8 %collective-permute-start.23 = (bf16[256,1536]{1,0:T(8,128)(2,1)S(1)}, bf16[256,1536]{1,0:T(8,128)(2,1)S(1)}, u32[]{:S(2)}, u32[]{:S(2)}) collective-permute-start(bf16[256,1536]{1,0:T(8,128)(2,1)S(1)} %fusion.55), channel_id=1, source_target_pairs={{0,16},{4,12},{8,24},{12,4},{16,0},{20,28},{24,8},{28,20},{1,17},{... | collective-permute-start | bytes 2359304 | tf_op jit(solution)/shard_map/ppermute | solution.py:735
  431.8 179.4 %reduce-scatter.8.cloned.1.call-start = ((), (), s32[]{:S(2)}) async-start(), calls=%async_computation.6 | async-start | bytes 5242880 | tf_op jit(solution)/shard_map/reduce_scatter | solution.py:730
  503.3 3.9 collective-permute-start.28
  504.6 26.8 %collective-permute-start.32 = (bf16[512,1536]{1,0:T(8,128)(2,1)}, bf16[512,1536]{1,0:T(8,128)(2,1)}, u32[]{:S(2)}, u32[]{:S(2)}) collective-permute-start(bf16[512,1536]{1,0:T(8,128)(2,1)} %pad_maximum_fusion.6), channel_id=1, source_target_pairs={{0,8},{4,20},{8,0},{12,28},{16,24},{20,4},{24,16},{28,12},{1,9},{5... | collective-permute-start | bytes 4718600 | tf_op jit(solution)/shard_map/ppermute | solution.py:735
  531.3 193.5 %all-gather.16.cloned.1.call-start = ((), (), s32[]{:S(2)}) async-start(), calls=%async_computation.8 | async-start | bytes 5242880 | tf_op jit(solution)/shard_map/all_gather | solution.py:726
  533.2 12.1 %collective-permute-start.33 = (bf16[256,1536]{1,0:T(8,128)(2,1)S(1)}, bf16[256,1536]{1,0:T(8,128)(2,1)S(1)}, u32[]{:S(2)}, u32[]{:S(2)}) collective-permute-start(bf16[256,1536]{1,0:T(8,128)(2,1)S(1)} %fusion.41), channel_id=1, source_target_pairs={{0,16},{4,12},{8,24},{12,4},{16,0},{20,28},{24,8},{28,20},{1,17},{... | collective-permute-start | bytes 2359304 | tf_op jit(solution)/shard_map/ppermute | solution.py:735
  553.5 37.9 %collective-permute-start.31 = (bf16[704,1024]{1,0:T(8,128)(2,1)}, bf16[704,1024]{1,0:T(8,128)(2,1)S(1)}, u32[]{:S(2)}, u32[]{:S(2)}) collective-permute-start(bf16[704,1024]{1,0:T(8,128)(2,1)} %fusion.34), channel_id=1, source_target_pairs={{0,4},{4,0},{8,12},{12,8},{16,20},{20,16},{24,28},{28,24},{1,5},{5... | collective-permute-start | bytes 4325384 | tf_op jit(solution)/shard_map/ppermute | solution.py:735
  556.3 37.3 %collective-permute-start.30 = (bf16[704,1024]{1,0:T(8,128)(2,1)}, bf16[704,1024]{1,0:T(8,128)(2,1)S(1)}, u32[]{:S(2)}, u32[]{:S(2)}) collective-permute-start(bf16[704,1024]{1,0:T(8,128)(2,1)} %fusion.31), channel_id=1, source_target_pairs={{0,4},{4,0},{8,12},{12,8},{16,20},{20,16},{24,28},{28,24},{1,5},{5... | collective-permute-start | bytes 4325384 | tf_op jit(solution)/shard_map/ppermute | solution.py:735
  559.6 35.4 %collective-permute-start.29 = (bf16[704,1024]{1,0:T(8,128)(2,1)}, bf16[704,1024]{1,0:T(8,128)(2,1)S(1)}, u32[]{:S(2)}, u32[]{:S(2)}) collective-permute-start(bf16[704,1024]{1,0:T(8,128)(2,1)} %fusion.37), channel_id=1, source_target_pairs={{0,4},{4,0},{8,12},{12,8},{16,20},{20,16},{24,28},{28,24},{1,5},{5... | collective-permute-start | bytes 4325384 | tf_op jit(solution)/shard_map/ppermute | solution.py:735
  615.6 162.7 %all-gather.14.cloned.1.call-start = ((), (), s32[]{:S(2)}) async-start(), calls=%async_computation.7 | async-start | bytes 5242880 | tf_op jit(solution)/shard_map/all_gather | solution.py:726
  623.2 2.0 collective-permute-start.40
  625.2 6.3 collective-permute-start.41
  631.6 5.0 collective-permute-start.42
  636.6 25.1 %copy-start.7 = (f32[704,1024]{1,0:T(8,128)S(1)}, f32[704,1024]{1,0:T(8,128)}, u32[]{:S(2)}) copy-start(f32[704,1024]{1,0:T(8,128)} %copy-done.6) | copy-start | bytes 8650756
  636.7 11.7 %collective-permute-start.36 = (bf16[704,512]{1,0:T(8,128)(2,1)}, bf16[704,512]{1,0:T(8,128)(2,1)}, u32[]{:S(2)}, u32[]{:S(2)}) collective-permute-start(bf16[704,512]{1,0:T(8,128)(2,1)} %pad_maximum_fusion.11), channel_id=1, source_target_pairs={{0,8},{4,20},{8,0},{12,28},{16,24},{20,4},{24,16},{28,12},{1,9},{5... | collective-permute-start | bytes 2162696 | tf_op jit(solution)/shard_map/ppermute | solution.py:735
  638.2 23.5 %collective-permute-start.34 = (bf16[704,512]{1,0:T(8,128)(2,1)}, bf16[704,512]{1,0:T(8,128)(2,1)}, u32[]{:S(2)}, u32[]{:S(2)}) collective-permute-start(bf16[704,512]{1,0:T(8,128)(2,1)} %pad_maximum_fusion.10), channel_id=1, source_target_pairs={{0,8},{4,20},{8,0},{12,28},{16,24},{20,4},{24,16},{28,12},{1,9},{5... | collective-permute-start | bytes 2162696 | tf_op jit(solution)/shard_map/ppermute | solution.py:735
  638.8 34.7 %copy-start.5 = (f32[704,1024]{1,0:T(8,128)S(1)}, f32[704,1024]{1,0:T(8,128)}, u32[]{:S(2)}) copy-start(f32[704,1024]{1,0:T(8,128)} %copy-done.4) | copy-start | bytes 8650756
  639.8 33.8 %collective-permute-start.38 = (bf16[704,512]{1,0:T(8,128)(2,1)}, bf16[704,512]{1,0:T(8,128)(2,1)S(1)}, u32[]{:S(2)}, u32[]{:S(2)}) collective-permute-start(bf16[704,512]{1,0:T(8,128)(2,1)} %pad_maximum_fusion.9), channel_id=1, source_target_pairs={{0,8},{4,20},{8,0},{12,28},{16,24},{20,4},{24,16},{28,12},{1,9},{5... | collective-permute-start | bytes 2162696 | tf_op jit(solution)/shard_map/ppermute | solution.py:735
  649.8 26.4 %collective-permute-start.37 = (bf16[704,256]{1,0:T(8,128)(2,1)S(1)}, bf16[704,256]{1,0:T(8,128)(2,1)S(1)}, u32[]{:S(2)}, u32[]{:S(2)}) collective-permute-start(bf16[704,256]{1,0:T(8,128)(2,1)S(1)} %fusion.81), channel_id=1, source_target_pairs={{0,16},{4,12},{8,24},{12,4},{16,0},{20,28},{24,8},{28,20},{1,17},{... | collective-permute-start | bytes 1081352 | tf_op jit(solution)/shard_map/ppermute | solution.py:735
  663.0 14.7 %collective-permute-start.35 = (bf16[704,256]{1,0:T(8,128)(2,1)S(1)}, bf16[704,256]{1,0:T(8,128)(2,1)S(1)}, u32[]{:S(2)}, u32[]{:S(2)}) collective-permute-start(bf16[704,256]{1,0:T(8,128)(2,1)S(1)} %fusion.86), channel_id=1, source_target_pairs={{0,16},{4,12},{8,24},{12,4},{16,0},{20,28},{24,8},{28,20},{1,17},{... | collective-permute-start | bytes 1081352 | tf_op jit(solution)/shard_map/ppermute | solution.py:735
  674.7 25.0 %collective-permute-start.39 = (bf16[704,256]{1,0:T(8,128)(2,1)S(1)}, bf16[704,256]{1,0:T(8,128)(2,1)S(1)}, u32[]{:S(2)}, u32[]{:S(2)}) collective-permute-start(bf16[704,256]{1,0:T(8,128)(2,1)S(1)} %fusion.76), channel_id=1, source_target_pairs={{0,16},{4,12},{8,24},{12,4},{16,0},{20,28},{24,8},{28,20},{1,17},{... | collective-permute-start | bytes 1081352 | tf_op jit(solution)/shard_map/ppermute | solution.py:735
  680.8 17.3 %collective-permute-start.43 = (f32[4,2,256]{2,1,0:T(2,128)S(1)}, f32[4,2,256]{2,1,0:T(2,128)S(1)}, u32[]{:S(2)}, u32[]{:S(2)}) collective-permute-start(f32[4,2,256]{2,1,0:T(2,128)S(1)} %slice.722), channel_id=1, source_target_pairs={{0,4},{4,0},{8,12},{12,8},{16,20},{20,16},{24,28},{28,24},{1,5},{5... | collective-permute-start | bytes 24584 | tf_op jit(solution)/shard_map/ppermute | solution.py:735
  698.1 3.7 collective-permute-start.44
  701.8 11.4 %collective-permute-start.45 = (f32[1,2,256]{2,1,0:T(2,128)S(1)}, f32[1,2,256]{2,1,0:T(2,128)S(1)}, u32[]{:S(2)}, u32[]{:S(2)}) collective-permute-start(f32[1,2,256]{2,1,0:T(2,128)S(1)} %slice_add_fusion.30), channel_id=1, source_target_pairs={{0,16},{4,12},{8,24},{12,4},{16,0},{20,28},{24,8},{28,20},{1,17},{... | collective-permute-start | bytes 6152 | tf_op jit(solution)/shard_map/ppermute | solution.py:735
  702.3 21.8 %copy-start.33 = (f32[2,256]{1,0:T(2,128)S(1)}, f32[2,256]{1,0:T(2,128)}, u32[]{:S(2)}) copy-start(f32[2,256]{1,0:T(2,128)} %param.61) | copy-start | bytes 6148
  702.3 21.8 %copy-start.34 = (f32[2,256]{1,0:T(2,128)S(1)}, f32[2,256]{1,0:T(2,128)}, u32[]{:S(2)}) copy-start(f32[2,256]{1,0:T(2,128)} %param.60) | copy-start | bytes 6148
  (46 other events, 231.3 us)
Sparse Core Ops, SparseCore 0:
  22.0 35.1 all-gather.19
  117.8 115.6 all-gather.17
  293.0 74.9 reduce-scatter.5
  372.4 81.2 all-gather.11
  455.9 75.2 reduce-scatter.3
  534.0 77.2 reduce-scatter.7
  615.7 81.4 all-gather.15
  698.9 79.4 all-gather.13

commit v4 on v3

--- a/solution.py
+++ b/solution.py
@@ -91,18 +91,23 @@
 
 def put_tiles(buffer, value):
     width = value.shape[1]
+    span = value.shape[0] // 8
     for tile in range(pl.cdiv(width, LANES)):
         size = min(LANES, width - tile * LANES)
-        buffer[tile, :, :size] = value[:, tile * LANES : tile * LANES + size]
+        for chunk in range(8):
+            at = chunk * (span + 1)
+            buffer[tile, at : at + span, :size] = value[
+                chunk * span : (chunk + 1) * span, tile * LANES : tile * LANES + size
+            ]
 
 
 def scan_tiles(first, second, carry_state, carry_prod, out_state, out_prod, width, backward):
     tiles, rows, _ = first.shape
-    span = rows // 8
+    span = rows // 8 - 1
 
     def body(step, held):
         row = (span - 1 - step) if backward else step
-        at = pl.ds(row, 8, stride=span)
+        at = pl.ds(row, 8, stride=span + 1)
         states, prods = [], []
         for tile in range(tiles):
             state, prod = held[0][tile], held[1][tile]
@@ -140,8 +145,9 @@
         prod_in = carry_prod[0:1, wide]
         for chunk in range(7, -1, -1) if backward else range(8):
             at = slice(chunk * span, (chunk + 1) * span)
-            local = first[tile, at, :]
-            out_state[at, cols] = (second[tile, at, :] + local * state_in)[:, :size]
+            held = slice(chunk * (span + 1), chunk * (span + 1) + span)
+            local = first[tile, held, :]
+            out_state[at, cols] = (second[tile, held, :] + local * state_in)[:, :size]
             out_prod[at, cols] = (local * prod_in)[:, :size]
             state_in = state[chunk : chunk + 1] + prod[chunk : chunk + 1] * state_in
             prod_in = prod[chunk : chunk + 1] * prod_in
@@ -150,6 +156,22 @@
 
 
 SPOTS = ((0, 1), (2, 3), (4, 6), (5, 7))
+
+
+def piece_copies(arrays, which, held, sem, along):
+    copies = []
+    for array, spots in zip(arrays, SPOTS):
+        size = array.shape[1 + along]
+        if size == held.shape[along]:
+            spots = (0,)
+        for piece, spot in enumerate(spots):
+            at = pl.ds(spot * size, size)
+            for slot, kind in which:
+                place = held.at[slot, at, :] if along == 1 else held.at[slot, :, at]
+                copies.append(pltpu.make_async_copy(array.at[piece, kind], place, sem))
+        if size == held.shape[along]:
+            break
+    return copies
 
 
 def load_pieces(arrays, which, held, sem, along):
@@ -254,21 +276,21 @@
         ],
         scratch_shapes=[
             pltpu.VMEM((HALO + rows, width), f32),
-            pltpu.VMEM((tiles, rows, LANES), f32),
-            pltpu.VMEM((tiles, rows, LANES), f32),
+            pltpu.VMEM((tiles, rows + 8, LANES), f32),
+            pltpu.VMEM((tiles, rows + 8, LANES), f32),
             pltpu.VMEM((8, tiles * LANES), f32),
             pltpu.VMEM((8, tiles * LANES), f32),
             pltpu.VMEM((2, width, model), bf16),
             pltpu.SemaphoreType.DMA,
         ],
         compiler_params=params(),
-        cost_estimate=cost(34),
+        cost_estimate=cost(26),
         name="front",
     )(tok, halo, gain, *weights, w_a, w_i, vec, mask)
 
 
 def state_kernel(
-    rank, ends, h_l, p_l, y, h_o, hp_o, o_o, hin, hbuf
+    rank, ends, h_l, p_l, y, h_o, hp_o, o_o, packed_o, hin, hbuf
 ):
     step = pl.program_id(0)
     rows = h_l.shape[0]
@@ -287,11 +309,27 @@
     hbuf[8 : 8 + rows, :] = state
     hp_o[...] = hbuf[7 : 7 + rows, :]
     hbuf[7:8, :] = state[rows - 1 :, :]
-    o_o[...] = (state * gelu_tanh(y[...])).astype(bf16)
+    mixed = (state * gelu_tanh(y[...])).astype(bf16)
+    o_o[...] = mixed
+    odd = step % 2
+    full = mixed.shape[1] // LANES
+    for tile in range(full):
+        packed_o[2 * tile + odd] = mixed[:, tile * LANES : (tile + 1) * LANES]
+    rest = mixed[:, full * LANES :]
+    side = LANES // 2
+
+    @pl.when(odd == 0)
+    def _():
+        packed_o[2 * full, :, :side] = rest
+
+    @pl.when(odd == 1)
+    def _():
+        packed_o[2 * full, :, side:] = rest
 
 
 def finish_state(rank, ends, h_l, p_l, y, rows):
     count, width = h_l.shape
+    assert width % LANES == LANES // 2 and count // rows % 2 == 0
     row = lambda size: pl.BlockSpec((rows, size), lambda i: (i, 0))
     like = lambda size, kind: jax.ShapeDtypeStruct((count, size), kind)
     return pl.pallas_call(
@@ -301,8 +339,14 @@
             pl.BlockSpec(memory_space=pltpu.SMEM), whole(ends.shape), row(width), row(width),
             row(width),
         ],
-        out_specs=[row(width), row(width), row(width)],
-        out_shape=[like(width, f32), like(width, f32), like(width, bf16)],
+        out_specs=[
+            row(width), row(width), row(width),
+            pl.BlockSpec((2 * width // LANES, rows, LANES), lambda i: (0, i // 2, 0)),
+        ],
+        out_shape=[
+            like(width, f32), like(width, f32), like(width, bf16),
+            jax.ShapeDtypeStruct((2 * width // LANES, count // 2, LANES), bf16),
+        ],
         scratch_shapes=[
             pltpu.VMEM((8, width), f32),
             pltpu.VMEM((8 + rows, width), f32),
@@ -313,89 +357,114 @@
     )(rank, ends, h_l, p_l, y)
 
 
-def lift_kernel(slab, mixed, tok, gain, w_0, w_1, w_2, w_3, xn_o, own_o, w_o, sem):
+def middle_kernel(
+    slab, mixed, tok, gain, dhid, w_0, w_1, w_2, w_3, u_0, u_1, u_2, u_3, *rest
+):
+    xn_o, hm_o, dg_o, du_o, part_o, own_o, low, w_o, w_up, o_sems, up_sem = rest[-11:]
     step = pl.program_id(0)
+    kinds = w_o.shape[0]
+    out_copies = lambda kind: piece_copies(
+        (w_0, w_1, w_2, w_3), ((kind, kind),), w_o, o_sems.at[kind], 2
+    )
+    up_copies = lambda: piece_copies(
+        (u_0, u_1, u_2, u_3), ((0, 0), (1, 1)), w_up, up_sem, 1
+    )
 
     @pl.when(step == 0)
     def _():
-        load_pieces((w_0, w_1, w_2, w_3), range(w_o.shape[0]), w_o, sem, 2)
-
-    total = nn(mixed[0], w_o[0])
-    for kind in range(1, w_o.shape[0]):
-        total = total + nn(mixed[kind], w_o[kind])
+        for kind in range(kinds):
+            for copy in out_copies(kind):
+                copy.start()
+        for copy in up_copies():
+            copy.start()
+
+    odd = step % 2
+    full = low.shape[2] // LANES
+    for kind in range(kinds):
+        for tile in range(full):
+            low[kind, :, tile * LANES : (tile + 1) * LANES] = mixed[kind, 2 * tile + odd]
+        both = mixed[kind, 2 * full].astype(f32)
+        side = LANES // 2
+        low[kind, :, full * LANES :] = jnp.where(
+            odd == 0, both[:, :side], both[:, side:]
+        ).astype(bf16)
+
+    total = None
+    for kind in range(kinds):
+
+        @pl.when(step == 0)
+        def _():
+            for copy in out_copies(kind):
+                copy.wait()
+
+        more = nn(low[kind], w_o[kind])
+        total = more if kind == 0 else total + more
+    rows, model = xn_o.shape
     second = tok[...].astype(f32) + total
-    xn_o[...] = rms_low(second, gain[...])
+    xn = rms_low(second, gain[...])
+    xn_o[...] = xn
 
     @pl.when(step == slab[0])
     def _():
         own_o[...] = second
 
-
-def lift(slab, mixed, tok, gain, weights):
-    count, model = tok.shape
-    slabs, _, width = mixed.shape
-    rows = count // slabs
-    row = lambda size: pl.BlockSpec((rows, size), lambda i: (i, 0))
-    return pl.pallas_call(
-        lift_kernel,
-        grid=(slabs,),
-        in_specs=[
-            pl.BlockSpec(memory_space=pltpu.SMEM),
-            pl.BlockSpec((slabs, rows, width), lambda i: (0, i, 0)),
-            row(model), whole(gain.shape), *any_specs(),
-        ],
-        out_specs=[row(model), whole((rows, model))],
-        out_shape=[
-            jax.ShapeDtypeStruct((count, model), bf16),
-            jax.ShapeDtypeStruct((rows, model), f32),
-        ],
-        scratch_shapes=[pltpu.VMEM((slabs, width, model), bf16), pltpu.SemaphoreType.DMA],
-        compiler_params=params(),
-        cost_estimate=cost(22),
-        name="lift",
-    )(slab, mixed, tok, gain, *weights)
-
-
-def mlp_kernel(xn, dhid, w_0, w_1, w_2, w_3, hm_o, dg_o, du_o, part_o, held, sem):
-    @pl.when(pl.program_id(0) == 0)
-    def _():
-        load_pieces((w_0, w_1, w_2, w_3), (0, 1), held, sem, 1)
-
-    w_g, w_u = held.at[0], held.at[1]
+    @pl.when(step == 0)
+    def _():
+        for copy in up_copies():
+            copy.wait()
+
+    w_g, w_u = w_up.at[0], w_up.at[1]
     hidden = dhid.shape[1]
     piece = hidden // 3
     for at in range(0, hidden, piece):
         cols = slice(at, at + piece)
-        z_gate = nn(xn[...], w_g[:, cols])
-        z_up = nn(xn[...], w_u[:, cols])
+        z_gate = nn(xn_o[...], w_g[:, cols])
+        z_up = nn(xn_o[...], w_u[:, cols])
         d_hid = dhid[:, cols]
         act, slope = gelu_both(z_gate)
         hm_o[:, cols] = (act * z_up).astype(bf16)
         dg_o[:, cols] = (d_hid * z_up * slope).astype(bf16)
         du_o[:, cols] = (d_hid * act).astype(bf16)
-    model = xn.shape[1]
     piece = model // 4
     for at in range(0, model, piece):
         cols = slice(at, at + piece)
         part_o[:, cols] = (nt(dg_o[...], w_g[cols, :]) + nt(du_o[...], w_u[cols, :])).astype(bf16)
 
 
-def mlp(xn, dhid, weights, rows):
-    count, model = xn.shape
-    hidden = dhid.shape[1]
+def middle(slab, mixed, tok, gain, dhid, out_w, up_w):
+    slabs = mixed.shape[0]
+    width = out_w[0].shape[2]
+    count, hidden = dhid.shape
+    model = gain.shape[1]
+    rows = count // slabs
     row = lambda size: pl.BlockSpec((rows, size), lambda i: (i, 0))
     like = lambda size: jax.ShapeDtypeStruct((count, size), bf16)
     return pl.pallas_call(
-        mlp_kernel,
-        grid=(count // rows,),
-        in_specs=[row(model), row(hidden), *any_specs()],
-        out_specs=[row(hidden), row(hidden), row(hidden), row(model)],
-        out_shape=[like(hidden), like(hidden), like(hidden), like(model)],
-        scratch_shapes=[pltpu.VMEM((2, model, hidden), bf16), pltpu.SemaphoreType.DMA],
-        compiler_params=params(),
-        cost_estimate=cost(36),
-        name="mlp",
-    )(xn, dhid, *weights)
+        middle_kernel,
+        grid=(slabs,),
+        in_specs=[
+            pl.BlockSpec(memory_space=pltpu.SMEM),
+            pl.BlockSpec((slabs, mixed.shape[1], rows, LANES), lambda i: (0, 0, i // 2, 0)),
+            row(model), whole(gain.shape), row(hidden), *any_specs(), *any_specs(),
+        ],
+        out_specs=[
+            row(model), row(hidden), row(hidden), row(hidden), row(model), whole((rows, model)),
+        ],
+        out_shape=[
+            like(model), like(hidden), like(hidden), like(hidden), like(model),
+            jax.ShapeDtypeStruct((rows, model), f32),
+        ],
+        scratch_shapes=[
+            pltpu.VMEM((slabs, rows, width), bf16),
+            pltpu.VMEM((slabs, width, model), bf16),
+            pltpu.VMEM((2, model, hidden), bf16),
+            pltpu.SemaphoreType.DMA((slabs,)),
+            pltpu.SemaphoreType.DMA,
+        ],
+        compiler_params=params(61),
+        cost_estimate=cost(52),
+        name="middle",
+    )(slab, mixed, tok, gain, dhid, *out_w, *up_w)
 
 
 def back_kernel(
@@ -440,15 +509,15 @@
             jax.ShapeDtypeStruct((8, width), f32),
         ],
         scratch_shapes=[
-            pltpu.VMEM((tiles, rows, LANES), f32),
-            pltpu.VMEM((tiles, rows, LANES), f32),
+            pltpu.VMEM((tiles, rows + 8, LANES), f32),
+            pltpu.VMEM((tiles, rows + 8, LANES), f32),
             pltpu.VMEM((8, tiles * LANES), f32),
             pltpu.VMEM((8, tiles * LANES), f32),
             pltpu.VMEM((1, width, model), bf16),
             pltpu.SemaphoreType.DMA,
         ],
         compiler_params=params(),
-        cost_estimate=cost(20),
+        cost_estimate=cost(12),
         name="back_scan",
     )(slab, d_rec, *weights, y, h, a)
 
@@ -1009,11 +1078,11 @@
         tok_s, halo, gains_f[0:1], rec_w, w_a, w_i, vec, mask, rows
     )
     ends_all = lax.all_gather(ends[0:2], "tok", axis=0, tiled=False)
-    state, state_prev, mixed = finish_state(rank_ref, ends_all, h_loc, p_loc, y_pre, rows)
+    state, state_prev, mixed, packed = finish_state(rank_ref, ends_all, h_loc, p_loc, y_pre, rows)
     own = lambda array: lax.dynamic_slice_in_dim(array, slab * share, share, 0)
     slab_ref = slab.reshape(1).astype(jnp.int32)
     own_tok = own(tok_s)
-    mixed_all = lax.all_gather(mixed, "mlp", axis=0, tiled=False)
+    mixed_all = lax.all_gather(packed, "mlp", axis=0, tiled=False)
     down_own = w_out_mlp.astype(bf16)[None]
     if parts == 8:
         out_two = join(out_own, after(out_far, ends))
@@ -1022,12 +1091,10 @@
         up_near = hop(up_two, NEAR)
         down_far = hop(after(down_own, ends), FAR)
         out_core = hop(after(out_two, mixed), CORE)
-        out_w = (out_two, out_near, out_core, hop(after(out_near, mixed), CORE))
         down_two = join(down_own, after(down_far, mixed))
         down_near = hop(down_two, NEAR)
         down_core = hop(down_two, CORE)
         up_core = hop(after(up_two, mixed), CORE)
-        up_w = (up_two, up_near, up_core, hop(after(up_near, mixed), CORE))
         down_last = hop(down_near, CORE)
         down = jnp.concatenate(
             [
@@ -1042,8 +1109,13 @@
         up_w = (lax.all_gather(up_own, "tok", axis=1, tiled=True)[None],) * 4
     cot_s = permute_columns(after(cotangent, mixed), into_local)
     d_hidden = nt(cot_s, down)
-    xn_two, second = lift(slab_ref, mixed_all, tok_s, gains_f[1:2], out_w)
-    hidden, d_gate, d_up, d_branch = mlp(xn_two, d_hidden, up_w, min(512, count))
+    if parts == 8:
+        out_near, up_near = after(out_near, d_hidden), after(up_near, d_hidden)
+        out_w = (out_two, out_near, out_core, hop(out_near, CORE))
+        up_w = (up_two, up_near, up_core, hop(up_near, CORE))
+    xn_two, hidden, d_gate, d_up, d_branch, second = middle(
+        slab_ref, mixed_all, tok_s, gains_f[1:2], d_hidden, out_w, up_w
+    )
     d_xn_two = scatter_slabs(d_branch)
     low = lambda array: array.astype(bf16)
     sum_gate = grad_rows(xn_two, d_gate)
@@ -1051,7 +1123,7 @@
     sum_down = grad_rows(cot_s, hidden)
     branch_two = nn(hidden, down).astype(bf16)
     d_xn_two = after(
-        d_xn_two, sum_gate.first(), sum_up.first(), sum_down.first(), branch_two
+        d_xn_two, sum_gate.first(), sum_up.first(), sum_down.first()
     )
     sum_gate.second()
     sum_up.second()

time: 797 us -> 789 us (0.990)
  Pallas kernels: 260 us -> 242 us
  waiting for transfers between devices: 255 us -> 267 us
  other arithmetic: 72.9 us -> 62.4 us
    ppermute x43, waiting for transfers between devices: 130 us -> 150 us  [hop(): lax.ppermute(array, 'tok', [(i, i ^ pairs[i % 2]) for i in range(count)])]
    reduce_scatter x3, waiting for transfers between devices: 44.5 us -> 32 us  [scatter_slabs(): return lax.psum_scatter(array, 'mlp', scatter_dimension=0, tiled=True)]
    unnamed x127 -> x139, local copies, waits for them, and re-layouts: 20.2 us -> 27.7 us
    pallas_call x2 -> x1, Pallas kernels: 59.2 us -> 53.9 us  [middle(): pl.pallas_call(middle_kernel, grid=(slabs,), in_specs=[pl.BlockSpec(memor...]
  transfers between devices with their start and end apart: 54 -> 54, of which waited for: 23 -> 23; matrix products, arithmetic and copies ran while one was open for 21% -> 21% of each run, Pallas kernels for 28% -> 24%
where the time goes in v4:
time: 789 us; the launch traced here: 783 us
  waiting for transfers between devices  267 us (34%)
  Pallas kernels  242 us (31%)
  matrix products  74.3 us (9%)
  other arithmetic  62.4 us (8%)
  local copies, waits for them, and re-layouts  45 us (6%)
  starting transfers between devices  42.5 us (5%)
  blocking collectives  33.1 us (4%)
  between operations  15.6 us (2%)
    ppermute x43, waiting for transfers between devices, hop(): lax.ppermute(array, 'tok', [(i, i ^ pairs[i % 2]) for i in range(count)])  150 us
    pallas_call x4, Pallas kernels, soap(): pl.pallas_call(functools.partial(soap_kernel, turned, swapped), grid=(gro...  85.3 us
    all_gather x3, waiting for transfers between devices, gather_slabs(): return lax.all_gather(array, 'mlp', axis=0, tiled=True)  74.4 us
    pallas_call x1, Pallas kernels, middle(): pl.pallas_call(middle_kernel, grid=(slabs,), in_specs=[pl.BlockSpec(memor...  53.9 us
    dot_general x14, matrix products, tn(): lax.dot_general(left, right, (((0,), (0,)), ((), ())), preferred_element_...  52.5 us
    ppermute x43, starting transfers between devices, hop(): lax.ppermute(array, 'tok', [(i, i ^ pairs[i % 2]) for i in range(count)])  34.9 us
    reduce_scatter x3, waiting for transfers between devices, scatter_slabs(): return lax.psum_scatter(array, 'mlp', scatter_dimension=0, tiled=True)  32 us
    unnamed x139, local copies, waits for them, and re-layouts  27.7 us
  transfers between devices with their start and end apart: 54, of which 23 were waited for; matrix products, arithmetic and copies ran while one was open for 21% of the time, Pallas kernels for 24%

profile of v4, /device:TPU:0, one launch (start us, length us, event | category | flops | bytes accessed | tf_op | source)
XLA Modules:
  0.0 782.7 jit_solution(340707933960780780)
XLA Ops:
  9.8 3.0 collective-permute-start.1
  15.8 4.0 collective-permute-start.6
  25.4 4.9 permute_columns.4.tok
  34.1 2.8 collective-permute-done.2
  41.7 2.2 slice_reduce_fusion.3
  45.7 6.1 fusion.63
  53.1 7.6 collective-permute-done.5.w_1
  65.4 26.1 %front.1 = (bf16[1024,2048]{1,0:T(8,128)(2,1)}, f32[1024,704]{1,0:T(8,128)}, bf16[1024,704]{1,0:T(8,128)(2,1)}, bf16[16,704]{1,0:T(8,128)(2,1)}, bf16[1024,704]{...) custom-call(bf16[1024,2048]{1,0:T(8,128)(2,1)} %permute_columns.4.to, ...), custom_call_target="tpu_custom_call" | custom-call | flops 28600000512 | bytes 85800000 | tf_op jit(solution)/shard_map/front/pallas_call | solution.py:260
  92.3 12.0 %all-gather.4.ends = f32[8,2,704]{2,1,0:T(2,128)} all-gather(f32[1,2,704]{2,1,0:T(2,128)S(1)} %slice_bitcast_fusion.16), channel_id=2, replica_groups=mesh['tok'=8,'mlp'=4] {'tok'}, dimensions={0}, use_global_device_ids=true | all-gather | bytes 50688 | tf_op jit(solution)/shard_map/all_gather | solution.py:1080
  104.8 9.4 %finish_state.1 = (f32[1024,704]{1,0:T(8,128)}, f32[1024,704]{1,0:T(8,128)}, bf16[1024,704]{1,0:T(8,128)(2,1)}, bf16[11,512,128]{2,1,0:T(8,128)(2,1)}) custom-call(s32[1]{0:T(128)} %bitcast.1.rank, f32[8,2,704]{2,1,0:T(2,128)} %all-gather.4.ends, f32[1024,704]{1,0:T(8,128)} %get-tuple-element.125.h_l, f32[1024,704]{1,0:T(8,128)} %get-tuple-element.126.p_l, ...), custom_call_target="tpu_custom_call" | custom-call | flops 8800000000 | bytes 26400000 | tf_op jit(solution)/shard_map/finish_state/pallas_call | solution.py:335
  114.1 2.1 collective-permute-done.9
  122.8 4.9 permute_columns.6
  127.7 3.5 pad_maximum_fusion.u_0
  131.8 6.5 collective-permute-done.10
  139.2 2.1 fusion.74
  141.3 2.1 fusion.73
  147.1 10.6 %fusion.117.dhid = f32[1024,1536]{1,0:T(8,128)} fusion(bf16[1024,2048]{1,0:T(8,128)(2,1)S(1)} %copy-done.28, bf16[1536,2048]{1,0:T(8,128)(2,1)} %fusion.69), kind=kOutput, calls=%fused_computation.267 | convolution fusion | flops 6442450944 | bytes 16777216 | tf_op jit(solution)/shard_map/dot_general | solution.py:49
  157.7 45.1 %collective-permute-done.18.u_1 = bf16[2,2,256,1536]{3,2,1,0:T(8,128)(2,1)S(1)} collective-permute-done((bf16[2,2,256,1536]{3,2,1,0:T(8,128)(2,1)}, bf16[2,2,256,1536]{3,2,1,0:T(8,128)(2,1)S(1)}, u32[]{:S(2)}, u32[]{:S(2)}) %collective-permute-start.18) | collective-permute-done | bytes 3145760 | tf_op jit(solution)/shard_map/ppermute | solution.py:804
  205.0 9.3 %collective-permute-done.15.w_2 = bf16[2,4,704,256]{3,2,1,0:T(8,128)(2,1)} collective-permute-done((bf16[2,4,704,256]{3,2,1,0:T(8,128)(2,1)}, bf16[2,4,704,256]{3,2,1,0:T(8,128)(2,1)}, u32[]{:S(2)}, u32[]{:S(2)}) %collective-permute-start.15) | collective-permute-done | bytes 2883616 | tf_op jit(solution)/shard_map/ppermute | solution.py:804
  214.2 4.5 collective-permute-done.16.w_3
  218.7 10.9 %all-gather.18.cloned.1.call-done = bf16[44,512,128]{2,1,0:T(8,128)(2,1)} async-done(((bf16[11,512,128]{2,1,0:T(8,128)(2,1)}), bf16[44,512,128]{2,1,0:T(8,128)(2,1)}) %all-gather.18.cloned.1.call-update) | async-done | bytes 5767184 | tf_op jit(solution)/shard_map/all_gather | solution.py:1085
  229.6 53.9 %middle.1 = (bf16[1024,2048]{1,0:T(8,128)(2,1)}, bf16[1024,1536]{1,0:T(8,128)(2,1)}, bf16[1024,1536]{1,0:T(8,128)(2,1)}, bf16[1024,1536]{1,0:T(8,128)(2,1)}, bf1...) custom-call(s32[1]{0:T(128)} %bitcast.slab, bf16[4,11,512,128]{3,2,1,0:T(8,128)(2,1)} %bitcast.152, ...), custom_call_target="tpu_custom_call" | custom-call | flops 57200001024 | bytes 171600000 | tf_op jit(solution)/shard_map/middle/pallas_call | solution.py:442
  285.4 5.7 convolution_convert_fusion.3
  292.3 3.7 convolution_convert_fusion.2
  296.5 4.9 convolution_convert_fusion.1
  301.5 5.6 fusion.25
  307.1 6.6 fusion.23
  317.0 6.2 fusion.7
  323.7 2.1 copy-done.2
  327.1 8.3 %collective-permute-done.22 = bf16[512,1536]{1,0:T(8,128)(2,1)S(1)} collective-permute-done((bf16[512,1536]{1,0:T(8,128)(2,1)S(1)}, bf16[512,1536]{1,0:T(8,128)(2,1)S(1)}, u32[]{:S(2)}, u32[]{:S(2)}) %collective-permute-start.22) | collective-permute-done | bytes 1572896 | tf_op jit(solution)/shard_map/ppermute | solution.py:804
  338.2 22.4 %collective-permute-done.25 = bf16[512,1536]{1,0:T(8,128)(2,1)S(1)} collective-permute-done((bf16[512,1536]{1,0:T(8,128)(2,1)S(1)}, bf16[512,1536]{1,0:T(8,128)(2,1)S(1)}, u32[]{:S(2)}, u32[]{:S(2)}) %collective-permute-start.25) | collective-permute-done | bytes 1572896 | tf_op jit(solution)/shard_map/ppermute | solution.py:804
  363.7 4.2 settle.2
  368.0 11.1 %convolution_convert_fusion = bf16[1024,2048]{1,0:T(8,128)(2,1)} fusion(bf16[1024,1536]{1,0:T(8,128)(2,1)} %get-tuple-element.142, bf16[1536,2048]{1,0:T(8,128)(2,1)} %fusion.69), kind=kOutput, calls=%fused_computation.4 | convolution fusion | flops 6444548096 | bytes 13631488 | tf_op jit(solution)/shard_map/dot_general | solution.py:45
  379.1 2.6 fusion.67
  381.7 2.2 fusion.68
  385.2 33.4 %soap.4 = (f32[2,256,1536]{2,1,0:T(8,128)}, f32[2,256,1536]{2,1,0:T(8,128)}, f32[2,256,1536]{2,1,0:T(8,128)}) custom-call(f32[2,256,1536]{2,1,0:T(8,128)} %w.1, f32[2,256,1536]{2,1,0:T(8,128)} %m.1, f32[2,256,1536]{2,1,0:T(8,128)} %v.1, bf16[2,256,1536]{2,1,0:T(8,128)(2,1)} %pad_maximum_fusion.5.g, f32[2,4,24,2,64,64]{5,4,3,2,1,0:T(8,128)} %q.2), custom_call_target="tpu_custom_call" | custom-call | flops 36044800000 | bytes 108134400 | tf_op jit(solution)/shard_map/soap/pallas_call | solution.py:769
  418.6 27.5 %all-gather.12.cloned.1.call-done.d_rec = bf16[1024,2048]{1,0:T(8,128)(2,1)} async-done(((bf16[256,2048]{1,0:T(8,128)(2,1)}), bf16[1024,2048]{1,0:T(8,128)(2,1)}) %all-gather.12.cloned.1.call-update) | async-done | bytes 4194320 | tf_op jit(solution)/shard_map/all_gather | solution.py:795
  446.1 13.9 %back_scan.1 = (bf16[1024,704]{1,0:T(8,128)(2,1)}, f32[1024,704]{1,0:T(8,128)}, f32[1024,704]{1,0:T(8,128)}, f32[8,704]{1,0:T(8,128)}) custom-call(s32[1]{0:T(128)} %bitcast.slab, bf16[1024,2048]{1,0:T(8,128)(2,1)} %all-gather.12.cloned.1.call-done.d_rec, bf16[2,4,704,256]{3,2,1,0:T(8,128)(2,1)} %pad_maximum_fusion.1.w_0, ...), custom_call_target="tpu_custom_call" | custom-call | flops 13200000000 | bytes 39600000 | tf_op jit(solution)/shard_map/back_scan/pallas_call | solution.py:499
  460.8 10.2 %all-gather.5.ends = f32[8,2,704]{2,1,0:T(2,128)} all-gather(f32[1,2,704]{2,1,0:T(2,128)S(1)} %slice_bitcast_fusion.15), channel_id=5, replica_groups=mesh['tok'=8,'mlp'=4] {'tok'}, dimensions={0}, use_global_device_ids=true | all-gather | bytes 50688 | tf_op jit(solution)/shard_map/all_gather | solution.py:1150
  471.0 18.9 %gates_back.1 = (bf16[1024,704]{1,0:T(8,128)(2,1)}, bf16[1024,704]{1,0:T(8,128)(2,1)}, bf16[1024,704]{1,0:T(8,128)(2,1)}, f32[16,704]{1,0:T(8,128)}, f32[16,704]{1,0:T(8,128)}, /*index=5*/f32[8,704]{1,0:T(8,128)}) custom-call(s32[1]{0:T(128)} %bitcast.1.rank, f32[8,2,704]{2,1,0:T(2,128)} %all-gather.5.ends, f32[1024,704]{1,0:T(8,128)} %get-tuple-element.156.g_l, ...), custom_call_target="tpu_custom_call" | custom-call | flops 20899999744 | bytes 62700000 | tf_op jit(solution)/shard_map/gates_back/pallas_call | solution.py:608
  491.1 2.6 collective-permute-start.32
  494.4 12.3 %pair_back.1 = (bf16[1024,2048]{1,0:T(8,128)(2,1)}, bf16[1024,704]{1,0:T(8,128)(2,1)}) custom-call(bf16[1024,704]{1,0:T(8,128)(2,1)} %get-tuple-element.175.left, bf16[1024,704]{1,0:T(8,128)(2,1)} %get-tuple-element.164.right, f32[16,704]{1,0:T(8,128)} %get-tuple-element.165.tail, f32[16,704]{1,0:T(8,128)} %copy-done.48, ...), custom_call_target="tpu_custom_call" | custom-call | flops 13200000000 | bytes 39600000 | tf_op jit(solution)/shard_map/pair_back/pallas_call | solution.py:658
  506.8 16.9 %reduce-scatter.4.cloned.1.call-done = bf16[256,2048]{1,0:T(8,128)(2,1)} async-done(((bf16[1024,2048]{1,0:T(8,128)(2,1)}), bf16[256,2048]{1,0:T(8,128)(2,1)}) %reduce-scatter.4.cloned.1.call-update) | async-done | bytes 1048592 | tf_op jit(solution)/shard_map/reduce_scatter | solution.py:799
  527.3 2.3 constant_dynamic-slice_fusion.1.value
  529.6 8.2 %collective-permute-done.33 = bf16[256,1536]{1,0:T(8,128)(2,1)S(1)} collective-permute-done((bf16[256,1536]{1,0:T(8,128)(2,1)S(1)}, bf16[256,1536]{1,0:T(8,128)(2,1)S(1)}, u32[]{:S(2)}, u32[]{:S(2)}) %collective-permute-start.33) | collective-permute-done | bytes 786464 | tf_op jit(solution)/shard_map/ppermute | solution.py:804
  537.7 2.9 fusion.44
  540.8 5.1 fusion.34
  550.5 23.9 %soap.5 = (f32[1,1536,256]{2,1,0:T(8,128)}, f32[1,1536,256]{2,1,0:T(8,128)}, f32[1,1536,256]{2,1,0:T(8,128)}) custom-call(f32[1,1536,256]{2,1,0:T(8,128)} %bitcast.135, f32[1,1536,256]{2,1,0:T(8,128)} %bitcast.154, f32[1,1536,256]{2,1,0:T(8,128)} %bitcast.155, bf16[1,256,1536]{2,1,0:T(8,128)(2,1)} %bitcast.139, f32[1,24,4,2,64,64]{5,4,3,2,1,0:T(8,128)} %bitcast.151), custom_call_target="tpu_custom_call" | custom-call | flops 18022400000 | bytes 54067200 | tf_op jit(solution)/shard_map/soap/pallas_call | solution.py:769
  574.3 3.9 fusion.17
  588.7 15.1 %reduce-scatter.8.cloned.1.call-done.upstream = bf16[256,2048]{1,0:T(8,128)(2,1)} async-done(((bf16[1024,2048]{1,0:T(8,128)(2,1)}), bf16[256,2048]{1,0:T(8,128)(2,1)}) %reduce-scatter.8.cloned.1.call-update) | async-done | bytes 1048592 | tf_op jit(solution)/shard_map/reduce_scatter | solution.py:799
  603.7 4.4 settle.3
  608.4 2.7 fusion.118
  620.5 3.5 collective-permute-done.41
  625.7 2.3 permute_columns.7
  634.4 6.4 collective-permute-done.34
  643.8 10.4 %collective-permute-done.36 = bf16[704,512]{1,0:T(8,128)(2,1)} collective-permute-done((bf16[704,512]{1,0:T(8,128)(2,1)}, bf16[704,512]{1,0:T(8,128)(2,1)}, u32[]{:S(2)}, u32[]{:S(2)}) %collective-permute-start.36) | collective-permute-done | bytes 720928 | tf_op jit(solution)/shard_map/ppermute | solution.py:804
  657.0 9.0 %collective-permute-done.38 = bf16[704,512]{1,0:T(8,128)(2,1)S(1)} collective-permute-done((bf16[704,512]{1,0:T(8,128)(2,1)}, bf16[704,512]{1,0:T(8,128)(2,1)S(1)}, u32[]{:S(2)}, u32[]{:S(2)}) %collective-permute-start.38) | collective-permute-done | bytes 720928 | tf_op jit(solution)/shard_map/ppermute | solution.py:804
  673.4 17.2 %soap.6 = (f32[2,704,256]{2,1,0:T(8,128)}, f32[2,704,256]{2,1,0:T(8,128)}, f32[2,704,256]{2,1,0:T(8,128)}) custom-call(f32[2,704,256]{2,1,0:T(8,128)} %bitcast.136, f32[2,704,256]{2,1,0:T(8,128)} %bitcast.156, f32[2,704,256]{2,1,0:T(8,128)} %bitcast.157, bf16[2,704,256]{2,1,0:T(8,128)(2,1)} %pad_maximum_fusion.12.g, f32[2,4,11,2,64,64]{5,4,3,2,1,0:T(8,128)} %q.3), custom_call_target="tpu_custom_call" | custom-call | flops 16520532992 | bytes 49561600 | tf_op jit(solution)/shard_map/soap/pallas_call | solution.py:769
  692.1 1.9 fusion.98.g
  694.8 10.8 %soap.7 = (f32[1,704,256]{2,1,0:T(8,128)}, f32[1,704,256]{2,1,0:T(8,128)}, f32[1,704,256]{2,1,0:T(8,128)}) custom-call(f32[1,704,256]{2,1,0:T(8,128)} %bitcast.140, f32[1,704,256]{2,1,0:T(8,128)} %bitcast.158, f32[1,704,256]{2,1,0:T(8,128)} %bitcast.159, bf16[1,704,256]{2,1,0:T(8,128)(2,1)} %fusion.98.g, f32[1,11,4,2,64,64]{5,4,3,2,1,0:T(8,128)} %bitcast.153), custom_call_target="tpu_custom_call" | custom-call | flops 8260266496 | bytes 24780800 | tf_op jit(solution)/shard_map/soap/pallas_call | solution.py:769
  705.7 11.0 %psum.7 = f32[2,256]{1,0:T(2,128)S(1)} all-reduce(f32[2,256]{1,0:T(2,128)S(1)} %fusion.106), channel_id=1, replica_groups=mesh['tok'=8,'mlp'=4] {'mlp'}, use_global_device_ids=true, to_apply=%region_5.6 | all-reduce | flops 512 | bytes 4096 | tf_op jit(solution)/shard_map/psum | solution.py:1197
  717.3 6.7 convert_element_type.330
  723.9 46.9 %all-gather.14.cloned.1.call-done = bf16[1024,2048]{1,0:T(8,128)(2,1)} async-done(((bf16[256,2048]{1,0:T(8,128)(2,1)}), bf16[1024,2048]{1,0:T(8,128)(2,1)}) %all-gather.14.cloned.1.call-update) | async-done | bytes 4194320 | tf_op jit(solution)/shard_map/all_gather | solution.py:795
  770.8 4.8 copy.87
  (346 shorter events, 113.0 us)
Async XLA Ops:
  7.2 57.7 %all-gather.20.cloned.1.call-start = ((), (), s32[]{:S(2)}) async-start(), calls=%async_computation.10 | async-start | bytes 1802240 | tf_op jit(solution)/shard_map/all_gather | solution.py:1033
  9.8 22.1 %collective-permute-start.1 = (bf16[1,8,4024]{2,1,0:T(8,128)(2,1)S(1)}, bf16[1,8,4024]{2,1,0:T(8,128)(2,1)S(1)}, u32[]{:S(2)}, u32[]{:S(2)}) collective-permute-start(bf16[1,8,4024]{2,1,0:T(8,128)(2,1)S(1)} %concatenate.92), channel_id=1, source_target_pairs={{0,16},{4,12},{8,24},{12,4},{16,0},{20,28},{24,8},{28,20},{1,17},{... | collective-permute-start | bytes 193160 | tf_op jit(solution)/shard_map/ppermute | solution.py:804
  13.6 18.4 %collective-permute-start = (bf16[16,2048]{1,0:T(8,128)(2,1)S(1)}, bf16[16,2048]{1,0:T(8,128)(2,1)S(1)}, u32[]{:S(2)}, u32[]{:S(2)}) collective-permute-start(bf16[16,2048]{1,0:T(8,128)(2,1)S(1)} %slice.470), channel_id=1, source_target_pairs={{0,4},{4,8},{8,12},{12,16},{16,20},{20,24},{24,28},{1,5},{5,9},{9,... | collective-permute-start | bytes 196616 | tf_op jit(solution)/shard_map/ppermute | solution.py:1056
  15.8 14.4 %collective-permute-start.6 = (s32[16]{0:T(128)S(1)}, s32[16]{0:T(128)S(1)}, u32[]{:S(2)}, u32[]{:S(2)}) collective-permute-start(s32[16]{0:T(128)S(1)} %slice.478), channel_id=1, source_target_pairs={{0,4},{4,8},{8,12},{12,16},{16,20},{20,24},{24,28},{1,5},{5,9},{9,... | collective-permute-start | bytes 200 | tf_op jit(solution)/shard_map/ppermute | solution.py:1058
  21.3 18.9 %collective-permute-start.4 = (bf16[1,2,704,256]{3,2,1,0:T(8,128)(2,1)S(1)}, bf16[1,2,704,256]{3,2,1,0:T(8,128)(2,1)S(1)}, u32[]{:S(2)}, u32[]{:S(2)}) collective-permute-start(bf16[1,2,704,256]{3,2,1,0:T(8,128)(2,1)S(1)} %convert_bitcast_fusion.1), channel_id=1, source_target_pairs={{0,16},{4,12},{8,24},{12,4},{16,0},{20,28},{24,8},{28,20},{1,17},{... | collective-permute-start | bytes 2162696 | tf_op jit(solution)/shard_map/ppermute | solution.py:804
  22.6 206.9 %all-gather.18.cloned.1.call-start = ((), (), s32[]{:S(2)}) async-start(), calls=%async_computation.9 | async-start | bytes 7208960 | tf_op jit(solution)/shard_map/all_gather | solution.py:1085
  31.9 5.0 collective-permute-start.2
  37.0 1.6 collective-permute-start.3
  41.4 19.3 %collective-permute-start.5 = (bf16[2,2,704,256]{3,2,1,0:T(8,128)(2,1)}, bf16[2,2,704,256]{3,2,1,0:T(8,128)(2,1)}, u32[]{:S(2)}, u32[]{:S(2)}) collective-permute-start(bf16[2,2,704,256]{3,2,1,0:T(8,128)(2,1)} %pad_maximum_fusion.7.w_0), channel_id=1, source_target_pairs={{0,8},{4,20},{8,0},{12,28},{16,24},{20,4},{24,16},{28,12},{1,9},{5... | collective-permute-start | bytes 4325384 | tf_op jit(solution)/shard_map/ppermute | solution.py:804
  51.8 13.6 %collective-permute-start.7 = (bf16[2,2,704,256]{3,2,1,0:T(8,128)(2,1)}, bf16[2,2,704,256]{3,2,1,0:T(8,128)(2,1)}, u32[]{:S(2)}, u32[]{:S(2)}) collective-permute-start(bf16[2,2,704,256]{3,2,1,0:T(8,128)(2,1)} %pad_maximum_fusion.7.w_0), channel_id=1, source_target_pairs={{0,4},{4,0},{8,12},{12,8},{16,20},{20,16},{24,28},{28,24},{1,5},{5... | collective-permute-start | bytes 4325384 | tf_op jit(solution)/shard_map/ppermute | solution.py:804
  60.7 4.7 collective-permute-start.8
  63.4 64.3 %collective-permute-start.17 = (bf16[1,2,256,1536]{3,2,1,0:T(8,128)(2,1)S(1)}, bf16[1,2,256,1536]{3,2,1,0:T(8,128)(2,1)}, u32[]{:S(2)}, u32[]{:S(2)}) collective-permute-start(bf16[1,2,256,1536]{3,2,1,0:T(8,128)(2,1)S(1)} %convert_bitcast_fusion), channel_id=1, source_target_pairs={{0,16},{4,12},{8,24},{12,4},{16,0},{20,28},{24,8},{28,20},{1,17},{... | collective-permute-start | bytes 4718600 | tf_op jit(solution)/shard_map/ppermute | solution.py:804
  64.9 54.2 %collective-permute-start.13 = (bf16[1,4,704,256]{3,2,1,0:T(8,128)(2,1)}, bf16[1,4,704,256]{3,2,1,0:T(8,128)(2,1)S(1)}, u32[]{:S(2)}, u32[]{:S(2)}) collective-permute-start(bf16[1,4,704,256]{3,2,1,0:T(8,128)(2,1)} %bitcast.137), channel_id=1, source_target_pairs={{0,16},{4,12},{8,24},{12,4},{16,0},{20,28},{24,8},{28,20},{1,17},{... | collective-permute-start | bytes 4325384 | tf_op jit(solution)/shard_map/ppermute | solution.py:804
  65.4 38.9 %copy-start.10 = (bf16[1,1536,256]{2,1,0:T(8,128)(2,1)S(1)}, bf16[1,1536,256]{2,1,0:T(8,128)(2,1)}, u32[]{:S(2)}) copy-start(bf16[1,1536,256]{2,1,0:T(8,128)(2,1)} %convert_bitcast_fusion.2) | copy-start | bytes 2359300
  104.3 12.0 %collective-permute-start.9 = (bf16[1,1536,256]{2,1,0:T(8,128)(2,1)S(1)}, bf16[1,1536,256]{2,1,0:T(8,128)(2,1)S(1)}, u32[]{:S(2)}, u32[]{:S(2)}) collective-permute-start(bf16[1,1536,256]{2,1,0:T(8,128)(2,1)S(1)} %copy-done.10), channel_id=1, source_target_pairs={{0,16},{4,12},{8,24},{12,4},{16,0},{20,28},{24,8},{28,20},{1,17},{... | collective-permute-start | bytes 2359304 | tf_op jit(solution)/shard_map/ppermute | solution.py:804
  117.5 20.7 %collective-permute-start.10 = (bf16[2,1536,256]{2,1,0:T(8,128)(2,1)}, bf16[2,1536,256]{2,1,0:T(8,128)(2,1)}, u32[]{:S(2)}, u32[]{:S(2)}) collective-permute-start(bf16[2,1536,256]{2,1,0:T(8,128)(2,1)} %pad_maximum_fusion.2), channel_id=1, source_target_pairs={{0,8},{4,20},{8,0},{12,28},{16,24},{20,4},{24,16},{28,12},{1,9},{5... | collective-permute-start | bytes 4718600 | tf_op jit(solution)/shard_map/ppermute | solution.py:804
  120.9 84.1 %collective-permute-start.14 = (bf16[2,4,704,256]{3,2,1,0:T(8,128)(2,1)}, bf16[2,4,704,256]{3,2,1,0:T(8,128)(2,1)}, u32[]{:S(2)}, u32[]{:S(2)}) collective-permute-start(bf16[2,4,704,256]{3,2,1,0:T(8,128)(2,1)} %pad_maximum_fusion.1.w_0), channel_id=1, source_target_pairs={{0,8},{4,20},{8,0},{12,28},{16,24},{20,4},{24,16},{28,12},{1,9},{5... | collective-permute-start | bytes 8650760 | tf_op jit(solution)/shard_map/ppermute | solution.py:804
  122.4 241.4 %reduce-scatter.6.cloned.1.call-start = ((), (), s32[]{:S(2)}) async-start(), calls=%async_computation.4 | async-start | bytes 5242880 | tf_op jit(solution)/shard_map/reduce_scatter | solution.py:799
  127.7 15.6 %collective-permute-start.11 = (bf16[2,1536,256]{2,1,0:T(8,128)(2,1)}, bf16[2,1536,256]{2,1,0:T(8,128)(2,1)S(1)}, u32[]{:S(2)}, u32[]{:S(2)}) collective-permute-start(bf16[2,1536,256]{2,1,0:T(8,128)(2,1)} %pad_maximum_fusion.2), channel_id=1, source_target_pairs={{0,4},{4,0},{8,12},{12,8},{16,20},{20,16},{24,28},{28,24},{1,5},{5... | collective-permute-start | bytes 4718600 | tf_op jit(solution)/shard_map/ppermute | solution.py:804
  131.2 71.6 %collective-permute-start.18 = (bf16[2,2,256,1536]{3,2,1,0:T(8,128)(2,1)}, bf16[2,2,256,1536]{3,2,1,0:T(8,128)(2,1)S(1)}, u32[]{:S(2)}, u32[]{:S(2)}) collective-permute-start(bf16[2,2,256,1536]{3,2,1,0:T(8,128)(2,1)} %pad_maximum_fusion.u_0), channel_id=1, source_target_pairs={{0,8},{4,20},{8,0},{12,28},{16,24},{20,4},{24,16},{28,12},{1,9},{5... | collective-permute-start | bytes 9437192 | tf_op jit(solution)/shard_map/ppermute | solution.py:804
  131.7 82.5 %collective-permute-start.19 = (bf16[2,2,256,1536]{3,2,1,0:T(8,128)(2,1)}, bf16[2,2,256,1536]{3,2,1,0:T(8,128)(2,1)}, u32[]{:S(2)}, u32[]{:S(2)}) collective-permute-start(bf16[2,2,256,1536]{3,2,1,0:T(8,128)(2,1)} %pad_maximum_fusion.u_0), channel_id=1, source_target_pairs={{0,4},{4,0},{8,12},{12,8},{16,20},{20,16},{24,28},{28,24},{1,5},{5... | collective-permute-start | bytes 9437192 | tf_op jit(solution)/shard_map/ppermute | solution.py:804
  138.3 6.0 collective-permute-start.12
  204.4 14.3 %collective-permute-start.20 = (bf16[2,2,256,1536]{3,2,1,0:T(8,128)(2,1)S(1)}, bf16[2,2,256,1536]{3,2,1,0:T(8,128)(2,1)}, u32[]{:S(2)}, u32[]{:S(2)}) collective-permute-start(bf16[2,2,256,1536]{3,2,1,0:T(8,128)(2,1)S(1)} %collective-permute-done.18.u_1), channel_id=1, source_target_pairs={{0,4},{4,0},{8,12},{12,8},{16,20},{20,16},{24,28},{28,24},{1,5},{5... | collective-permute-start | bytes 9437192 | tf_op jit(solution)/shard_map/ppermute | solution.py:804
  204.4 9.8 %collective-permute-start.15 = (bf16[2,4,704,256]{3,2,1,0:T(8,128)(2,1)}, bf16[2,4,704,256]{3,2,1,0:T(8,128)(2,1)}, u32[]{:S(2)}, u32[]{:S(2)}) collective-permute-start(bf16[2,4,704,256]{3,2,1,0:T(8,128)(2,1)} %pad_maximum_fusion.1.w_0), channel_id=1, source_target_pairs={{0,4},{4,0},{8,12},{12,8},{16,20},{20,16},{24,28},{28,24},{1,5},{5... | collective-permute-start | bytes 8650760 | tf_op jit(solution)/shard_map/ppermute | solution.py:804
  205.0 13.7 %collective-permute-start.16 = (bf16[2,4,704,256]{3,2,1,0:T(8,128)(2,1)}, bf16[2,4,704,256]{3,2,1,0:T(8,128)(2,1)}, u32[]{:S(2)}, u32[]{:S(2)}) collective-permute-start(bf16[2,4,704,256]{3,2,1,0:T(8,128)(2,1)} %collective-permute-done.14.w_1), channel_id=1, source_target_pairs={{0,4},{4,0},{8,12},{12,8},{16,20},{20,16},{24,28},{28,24},{1,5},{5... | collective-permute-start | bytes 8650760 | tf_op jit(solution)/shard_map/ppermute | solution.py:804
  283.5 162.6 %all-gather.12.cloned.1.call-start = ((), (), s32[]{:S(2)}) async-start(), calls=%async_computation.5 | async-start | bytes 5242880 | tf_op jit(solution)/shard_map/all_gather | solution.py:795
  291.1 22.6 %collective-permute-start.21 = (bf16[1024,1536]{1,0:T(8,128)(2,1)S(1)}, bf16[1024,1536]{1,0:T(8,128)(2,1)S(1)}, u32[]{:S(2)}, u32[]{:S(2)}) collective-permute-start(bf16[1024,1536]{1,0:T(8,128)(2,1)S(1)} %convolution_convert_fusion.3), channel_id=1, source_target_pairs={{0,4},{4,0},{8,12},{12,8},{16,20},{20,16},{24,28},{28,24},{1,5},{5... | collective-permute-start | bytes 9437192 | tf_op jit(solution)/shard_map/ppermute | solution.py:804
  296.0 18.3 %collective-permute-start.24 = (bf16[1024,1536]{1,0:T(8,128)(2,1)S(1)}, bf16[1024,1536]{1,0:T(8,128)(2,1)S(1)}, u32[]{:S(2)}, u32[]{:S(2)}) collective-permute-start(bf16[1024,1536]{1,0:T(8,128)(2,1)S(1)} %convolution_convert_fusion.2), channel_id=1, source_target_pairs={{0,4},{4,0},{8,12},{12,8},{16,20},{20,16},{24,28},{28,24},{1,5},{5... | collective-permute-start | bytes 9437192 | tf_op jit(solution)/shard_map/ppermute | solution.py:804
  301.4 21.8 %collective-permute-start.27 = (bf16[1024,1536]{1,0:T(8,128)(2,1)}, bf16[1024,1536]{1,0:T(8,128)(2,1)S(1)}, u32[]{:S(2)}, u32[]{:S(2)}) collective-permute-start(bf16[1024,1536]{1,0:T(8,128)(2,1)} %convolution_convert_fusion.1), channel_id=1, source_target_pairs={{0,4},{4,0},{8,12},{12,8},{16,20},{20,16},{24,28},{28,24},{1,5},{5... | collective-permute-start | bytes 9437192 | tf_op jit(solution)/shard_map/ppermute | solution.py:804
  307.0 28.4 %copy-start.4 = (f32[1024,1536]{1,0:T(8,128)}, f32[1024,1536]{1,0:T(8,128)S(1)}, u32[]{:S(2)}) copy-start(f32[1024,1536]{1,0:T(8,128)S(1)} %fusion.25) | copy-start | bytes 18874372
  313.7 47.0 %copy-start.3 = (f32[1024,1536]{1,0:T(8,128)}, f32[1024,1536]{1,0:T(8,128)S(1)}, u32[]{:S(2)}) copy-start(f32[1024,1536]{1,0:T(8,128)S(1)} %fusion.23) | copy-start | bytes 18874372
  313.7 21.7 %copy-start.9 = (bf16[1024,1536]{1,0:T(8,128)(2,1)}, bf16[1024,1536]{1,0:T(8,128)(2,1)S(1)}, u32[]{:S(2)}) copy-start(bf16[1024,1536]{1,0:T(8,128)(2,1)S(1)} %collective-permute-done.21) | copy-start | bytes 9437188
  314.3 46.4 %copy-start.8 = (bf16[1024,1536]{1,0:T(8,128)(2,1)}, bf16[1024,1536]{1,0:T(8,128)(2,1)S(1)}, u32[]{:S(2)}) copy-start(bf16[1024,1536]{1,0:T(8,128)(2,1)S(1)} %collective-permute-done.24) | copy-start | bytes 9437188
  314.9 20.5 %collective-permute-start.22 = (bf16[512,1536]{1,0:T(8,128)(2,1)S(1)}, bf16[512,1536]{1,0:T(8,128)(2,1)S(1)}, u32[]{:S(2)}, u32[]{:S(2)}) collective-permute-start(bf16[512,1536]{1,0:T(8,128)(2,1)S(1)} %pad_maximum_fusion.3), channel_id=1, source_target_pairs={{0,8},{4,20},{8,0},{12,28},{16,24},{20,4},{24,16},{28,12},{1,9},{5... | collective-permute-start | bytes 4718600 | tf_op jit(solution)/shard_map/ppermute | solution.py:804
  316.5 44.2 %collective-permute-start.25 = (bf16[512,1536]{1,0:T(8,128)(2,1)S(1)}, bf16[512,1536]{1,0:T(8,128)(2,1)S(1)}, u32[]{:S(2)}, u32[]{:S(2)}) collective-permute-start(bf16[512,1536]{1,0:T(8,128)(2,1)S(1)} %pad_maximum_fusion.4), channel_id=1, source_target_pairs={{0,8},{4,20},{8,0},{12,28},{16,24},{20,4},{24,16},{28,12},{1,9},{5... | collective-permute-start | bytes 4718600 | tf_op jit(solution)/shard_map/ppermute | solution.py:804
  335.4 26.9 %copy-start.19 = (bf16[512,1536]{1,0:T(8,128)(2,1)}, bf16[512,1536]{1,0:T(8,128)(2,1)S(1)}, u32[]{:S(2)}) copy-start(bf16[512,1536]{1,0:T(8,128)(2,1)S(1)} %collective-permute-done.22) | copy-start | bytes 4718596
  336.8 42.3 %collective-permute-start.23 = (bf16[256,1536]{1,0:T(8,128)(2,1)}, bf16[256,1536]{1,0:T(8,128)(2,1)}, u32[]{:S(2)}, u32[]{:S(2)}) collective-permute-start(bf16[256,1536]{1,0:T(8,128)(2,1)} %fusion.55), channel_id=1, source_target_pairs={{0,16},{4,12},{8,24},{12,4},{16,0},{20,28},{24,8},{28,20},{1,17},{... | collective-permute-start | bytes 2359304 | tf_op jit(solution)/shard_map/ppermute | solution.py:804
  362.3 19.4 %collective-permute-start.26 = (bf16[256,1536]{1,0:T(8,128)(2,1)}, bf16[256,1536]{1,0:T(8,128)(2,1)}, u32[]{:S(2)}, u32[]{:S(2)}) collective-permute-start(bf16[256,1536]{1,0:T(8,128)(2,1)} %fusion.48), channel_id=1, source_target_pairs={{0,16},{4,12},{8,24},{12,4},{16,0},{20,28},{24,8},{28,20},{1,17},{... | collective-permute-start | bytes 2359304 | tf_op jit(solution)/shard_map/ppermute | solution.py:804
  367.9 155.8 %reduce-scatter.4.cloned.1.call-start = ((), (), s32[]{:S(2)}) async-start(), calls=%async_computation.3 | async-start | bytes 5242880 | tf_op jit(solution)/shard_map/reduce_scatter | solution.py:799
  418.6 185.1 %reduce-scatter.8.cloned.1.call-start = ((), (), s32[]{:S(2)}) async-start(), calls=%async_computation.6 | async-start | bytes 5242880 | tf_op jit(solution)/shard_map/reduce_scatter | solution.py:799
  489.8 3.9 collective-permute-start.28
  491.1 32.6 %collective-permute-start.32 = (bf16[512,1536]{1,0:T(8,128)(2,1)}, bf16[512,1536]{1,0:T(8,128)(2,1)}, u32[]{:S(2)}, u32[]{:S(2)}) collective-permute-start(bf16[512,1536]{1,0:T(8,128)(2,1)} %pad_maximum_fusion.6), channel_id=1, source_target_pairs={{0,8},{4,20},{8,0},{12,28},{16,24},{20,4},{24,16},{28,12},{1,9},{5... | collective-permute-start | bytes 4718600 | tf_op jit(solution)/shard_map/ppermute | solution.py:804
  523.7 193.5 %all-gather.16.cloned.1.call-start = ((), (), s32[]{:S(2)}) async-start(), calls=%async_computation.8 | async-start | bytes 5242880 | tf_op jit(solution)/shard_map/all_gather | solution.py:795
  525.7 12.1 %collective-permute-start.33 = (bf16[256,1536]{1,0:T(8,128)(2,1)S(1)}, bf16[256,1536]{1,0:T(8,128)(2,1)S(1)}, u32[]{:S(2)}, u32[]{:S(2)}) collective-permute-start(bf16[256,1536]{1,0:T(8,128)(2,1)S(1)} %fusion.41), channel_id=1, source_target_pairs={{0,16},{4,12},{8,24},{12,4},{16,0},{20,28},{24,8},{28,20},{1,17},{... | collective-permute-start | bytes 2359304 | tf_op jit(solution)/shard_map/ppermute | solution.py:804
  545.9 37.8 %collective-permute-start.31 = (bf16[704,1024]{1,0:T(8,128)(2,1)}, bf16[704,1024]{1,0:T(8,128)(2,1)S(1)}, u32[]{:S(2)}, u32[]{:S(2)}) collective-permute-start(bf16[704,1024]{1,0:T(8,128)(2,1)} %fusion.34), channel_id=1, source_target_pairs={{0,4},{4,0},{8,12},{12,8},{16,20},{20,16},{24,28},{28,24},{1,5},{5... | collective-permute-start | bytes 4325384 | tf_op jit(solution)/shard_map/ppermute | solution.py:804
  547.7 37.5 %collective-permute-start.30 = (bf16[704,1024]{1,0:T(8,128)(2,1)S(1)}, bf16[704,1024]{1,0:T(8,128)(2,1)S(1)}, u32[]{:S(2)}, u32[]{:S(2)}) collective-permute-start(bf16[704,1024]{1,0:T(8,128)(2,1)S(1)} %fusion.31), channel_id=1, source_target_pairs={{0,4},{4,0},{8,12},{12,8},{16,20},{20,16},{24,28},{28,24},{1,5},{5... | collective-permute-start | bytes 4325384 | tf_op jit(solution)/shard_map/ppermute | solution.py:804
  550.4 36.3 %collective-permute-start.29 = (bf16[704,1024]{1,0:T(8,128)(2,1)S(1)}, bf16[704,1024]{1,0:T(8,128)(2,1)S(1)}, u32[]{:S(2)}, u32[]{:S(2)}) collective-permute-start(bf16[704,1024]{1,0:T(8,128)(2,1)S(1)} %fusion.37), channel_id=1, source_target_pairs={{0,4},{4,0},{8,12},{12,8},{16,20},{20,16},{24,28},{28,24},{1,5},{5... | collective-permute-start | bytes 4325384 | tf_op jit(solution)/shard_map/ppermute | solution.py:804
  608.1 162.7 %all-gather.14.cloned.1.call-start = ((), (), s32[]{:S(2)}) async-start(), calls=%async_computation.7 | async-start | bytes 5242880 | tf_op jit(solution)/shard_map/all_gather | solution.py:795
  615.7 2.0 collective-permute-start.40
  617.7 6.3 collective-permute-start.41
  624.1 5.0 collective-permute-start.42
  629.1 25.1 %copy-start.14 = (f32[704,1024]{1,0:T(8,128)S(1)}, f32[704,1024]{1,0:T(8,128)}, u32[]{:S(2)}) copy-start(f32[704,1024]{1,0:T(8,128)} %copy-done.13) | copy-start | bytes 8650756
  629.2 11.7 %collective-permute-start.34 = (bf16[704,512]{1,0:T(8,128)(2,1)}, bf16[704,512]{1,0:T(8,128)(2,1)}, u32[]{:S(2)}, u32[]{:S(2)}) collective-permute-start(bf16[704,512]{1,0:T(8,128)(2,1)} %pad_maximum_fusion.10), channel_id=1, source_target_pairs={{0,8},{4,20},{8,0},{12,28},{16,24},{20,4},{24,16},{28,12},{1,9},{5... | collective-permute-start | bytes 2162696 | tf_op jit(solution)/shard_map/ppermute | solution.py:804
  630.7 23.5 %collective-permute-start.36 = (bf16[704,512]{1,0:T(8,128)(2,1)}, bf16[704,512]{1,0:T(8,128)(2,1)}, u32[]{:S(2)}, u32[]{:S(2)}) collective-permute-start(bf16[704,512]{1,0:T(8,128)(2,1)} %pad_maximum_fusion.11), channel_id=1, source_target_pairs={{0,8},{4,20},{8,0},{12,28},{16,24},{20,4},{24,16},{28,12},{1,9},{5... | collective-permute-start | bytes 2162696 | tf_op jit(solution)/shard_map/ppermute | solution.py:804
  631.3 34.7 %copy-start.12 = (f32[704,1024]{1,0:T(8,128)S(1)}, f32[704,1024]{1,0:T(8,128)}, u32[]{:S(2)}) copy-start(f32[704,1024]{1,0:T(8,128)} %copy-done.11) | copy-start | bytes 8650756
  632.3 33.8 %collective-permute-start.38 = (bf16[704,512]{1,0:T(8,128)(2,1)}, bf16[704,512]{1,0:T(8,128)(2,1)S(1)}, u32[]{:S(2)}, u32[]{:S(2)}) collective-permute-start(bf16[704,512]{1,0:T(8,128)(2,1)} %pad_maximum_fusion.9), channel_id=1, source_target_pairs={{0,8},{4,20},{8,0},{12,28},{16,24},{20,4},{24,16},{28,12},{1,9},{5... | collective-permute-start | bytes 2162696 | tf_op jit(solution)/shard_map/ppermute | solution.py:804
  642.3 26.4 %collective-permute-start.35 = (bf16[704,256]{1,0:T(8,128)(2,1)S(1)}, bf16[704,256]{1,0:T(8,128)(2,1)S(1)}, u32[]{:S(2)}, u32[]{:S(2)}) collective-permute-start(bf16[704,256]{1,0:T(8,128)(2,1)S(1)} %fusion.86), channel_id=1, source_target_pairs={{0,16},{4,12},{8,24},{12,4},{16,0},{20,28},{24,8},{28,20},{1,17},{... | collective-permute-start | bytes 1081352 | tf_op jit(solution)/shard_map/ppermute | solution.py:804
  655.5 14.7 %collective-permute-start.37 = (bf16[704,256]{1,0:T(8,128)(2,1)S(1)}, bf16[704,256]{1,0:T(8,128)(2,1)S(1)}, u32[]{:S(2)}, u32[]{:S(2)}) collective-permute-start(bf16[704,256]{1,0:T(8,128)(2,1)S(1)} %fusion.81), channel_id=1, source_target_pairs={{0,16},{4,12},{8,24},{12,4},{16,0},{20,28},{24,8},{28,20},{1,17},{... | collective-permute-start | bytes 1081352 | tf_op jit(solution)/shard_map/ppermute | solution.py:804
  667.2 25.0 %collective-permute-start.39 = (bf16[704,256]{1,0:T(8,128)(2,1)S(1)}, bf16[704,256]{1,0:T(8,128)(2,1)S(1)}, u32[]{:S(2)}, u32[]{:S(2)}) collective-permute-start(bf16[704,256]{1,0:T(8,128)(2,1)S(1)} %fusion.76), channel_id=1, source_target_pairs={{0,16},{4,12},{8,24},{12,4},{16,0},{20,28},{24,8},{28,20},{1,17},{... | collective-permute-start | bytes 1081352 | tf_op jit(solution)/shard_map/ppermute | solution.py:804
  673.3 17.3 %collective-permute-start.43 = (f32[4,2,256]{2,1,0:T(2,128)S(1)}, f32[4,2,256]{2,1,0:T(2,128)S(1)}, u32[]{:S(2)}, u32[]{:S(2)}) collective-permute-start(f32[4,2,256]{2,1,0:T(2,128)S(1)} %slice.722), channel_id=1, source_target_pairs={{0,4},{4,0},{8,12},{12,8},{16,20},{20,16},{24,28},{28,24},{1,5},{5... | collective-permute-start | bytes 24584 | tf_op jit(solution)/shard_map/ppermute | solution.py:804
  690.6 3.7 collective-permute-start.44
  694.3 11.4 %collective-permute-start.45 = (f32[1,2,256]{2,1,0:T(2,128)S(1)}, f32[1,2,256]{2,1,0:T(2,128)S(1)}, u32[]{:S(2)}, u32[]{:S(2)}) collective-permute-start(f32[1,2,256]{2,1,0:T(2,128)S(1)} %slice_add_fusion.30), channel_id=1, source_target_pairs={{0,16},{4,12},{8,24},{12,4},{16,0},{20,28},{24,8},{28,20},{1,17},{... | collective-permute-start | bytes 6152 | tf_op jit(solution)/shard_map/ppermute | solution.py:804
  694.8 21.8 %copy-start.39 = (f32[2,256]{1,0:T(2,128)S(1)}, f32[2,256]{1,0:T(2,128)}, u32[]{:S(2)}) copy-start(f32[2,256]{1,0:T(2,128)} %param.61) | copy-start | bytes 6148
  694.8 21.8 %copy-start.40 = (f32[2,256]{1,0:T(2,128)S(1)}, f32[2,256]{1,0:T(2,128)}, u32[]{:S(2)}) copy-start(f32[2,256]{1,0:T(2,128)} %param.60) | copy-start | bytes 6148
  (52 other events, 265.9 us)
Sparse Core Ops, SparseCore 0:
  22.8 35.2 all-gather.19
  122.5 107.0 all-gather.17
  283.7 75.0 reduce-scatter.5
  368.1 78.0 all-gather.11
  448.4 75.2 reduce-scatter.3
  526.4 77.2 reduce-scatter.7
  608.2 81.4 all-gather.15
  691.3 79.4 all-gather.13

commit v5 on v4

--- a/solution.py
+++ b/solution.py
@@ -290,7 +290,7 @@
 
 
 def state_kernel(
-    rank, ends, h_l, p_l, y, h_o, hp_o, o_o, packed_o, hin, hbuf
+    rank, ends, h_l, p_l, y, h_o, hp_o, o_o, hin, hbuf
 ):
     step = pl.program_id(0)
     rows = h_l.shape[0]
@@ -309,27 +309,11 @@
     hbuf[8 : 8 + rows, :] = state
     hp_o[...] = hbuf[7 : 7 + rows, :]
     hbuf[7:8, :] = state[rows - 1 :, :]
-    mixed = (state * gelu_tanh(y[...])).astype(bf16)
-    o_o[...] = mixed
-    odd = step % 2
-    full = mixed.shape[1] // LANES
-    for tile in range(full):
-        packed_o[2 * tile + odd] = mixed[:, tile * LANES : (tile + 1) * LANES]
-    rest = mixed[:, full * LANES :]
-    side = LANES // 2
-
-    @pl.when(odd == 0)
-    def _():
-        packed_o[2 * full, :, :side] = rest
-
-    @pl.when(odd == 1)
-    def _():
-        packed_o[2 * full, :, side:] = rest
+    o_o[...] = (state * gelu_tanh(y[...])).astype(bf16)
 
 
 def finish_state(rank, ends, h_l, p_l, y, rows):
     count, width = h_l.shape
-    assert width % LANES == LANES // 2 and count // rows % 2 == 0
     row = lambda size: pl.BlockSpec((rows, size), lambda i: (i, 0))
     like = lambda size, kind: jax.ShapeDtypeStruct((count, size), kind)
     return pl.pallas_call(
@@ -339,14 +323,8 @@
             pl.BlockSpec(memory_space=pltpu.SMEM), whole(ends.shape), row(width), row(width),
             row(width),
         ],
-        out_specs=[
-            row(width), row(width), row(width),
-            pl.BlockSpec((2 * width // LANES, rows, LANES), lambda i: (0, i // 2, 0)),
-        ],
-        out_shape=[
-            like(width, f32), like(width, f32), like(width, bf16),
-            jax.ShapeDtypeStruct((2 * width // LANES, count // 2, LANES), bf16),
-        ],
+        out_specs=[row(width), row(width), row(width)],
+        out_shape=[like(width, f32), like(width, f32), like(width, bf16)],
         scratch_shapes=[
             pltpu.VMEM((8, width), f32),
             pltpu.VMEM((8 + rows, width), f32),
@@ -360,7 +338,7 @@
 def middle_kernel(
     slab, mixed, tok, gain, dhid, w_0, w_1, w_2, w_3, u_0, u_1, u_2, u_3, *rest
 ):
-    xn_o, hm_o, dg_o, du_o, part_o, own_o, low, w_o, w_up, o_sems, up_sem = rest[-11:]
+    xn_o, hm_o, dg_o, du_o, part_o, own_o, w_o, w_up, o_sems, up_sem = rest[-10:]
     step = pl.program_id(0)
     kinds = w_o.shape[0]
     out_copies = lambda kind: piece_copies(
@@ -378,17 +356,6 @@
         for copy in up_copies():
             copy.start()
 
-    odd = step % 2
-    full = low.shape[2] // LANES
-    for kind in range(kinds):
-        for tile in range(full):
-            low[kind, :, tile * LANES : (tile + 1) * LANES] = mixed[kind, 2 * tile + odd]
-        both = mixed[kind, 2 * full].astype(f32)
-        side = LANES // 2
-        low[kind, :, full * LANES :] = jnp.where(
-            odd == 0, both[:, :side], both[:, side:]
-        ).astype(bf16)
-
     total = None
     for kind in range(kinds):
 
@@ -397,7 +364,7 @@
             for copy in out_copies(kind):
                 copy.wait()
 
-        more = nn(low[kind], w_o[kind])
+        more = nn(mixed[kind], w_o[kind])
         total = more if kind == 0 else total + more
     rows, model = xn_o.shape
     second = tok[...].astype(f32) + total
@@ -432,9 +399,8 @@
 
 
 def middle(slab, mixed, tok, gain, dhid, out_w, up_w):
-    slabs = mixed.shape[0]
-    width = out_w[0].shape[2]
-    count, hidden = dhid.shape
+    slabs, count, width = mixed.shape
+    hidden = dhid.shape[1]
     model = gain.shape[1]
     rows = count // slabs
     row = lambda size: pl.BlockSpec((rows, size), lambda i: (i, 0))
@@ -444,7 +410,7 @@
         grid=(slabs,),
         in_specs=[
             pl.BlockSpec(memory_space=pltpu.SMEM),
-            pl.BlockSpec((slabs, mixed.shape[1], rows, LANES), lambda i: (0, 0, i // 2, 0)),
+            pl.BlockSpec((slabs, rows, width), lambda i: (0, i, 0)),
             row(model), whole(gain.shape), row(hidden), *any_specs(), *any_specs(),
         ],
         out_specs=[
@@ -455,7 +421,6 @@
             jax.ShapeDtypeStruct((rows, model), f32),
         ],
         scratch_shapes=[
-            pltpu.VMEM((slabs, rows, width), bf16),
             pltpu.VMEM((slabs, width, model), bf16),
             pltpu.VMEM((2, model, hidden), bf16),
             pltpu.SemaphoreType.DMA((slabs,)),
@@ -1078,11 +1043,11 @@
         tok_s, halo, gains_f[0:1], rec_w, w_a, w_i, vec, mask, rows
     )
     ends_all = lax.all_gather(ends[0:2], "tok", axis=0, tiled=False)
-    state, state_prev, mixed, packed = finish_state(rank_ref, ends_all, h_loc, p_loc, y_pre, rows)
+    state, state_prev, mixed = finish_state(rank_ref, ends_all, h_loc, p_loc, y_pre, rows)
     own = lambda array: lax.dynamic_slice_in_dim(array, slab * share, share, 0)
     slab_ref = slab.reshape(1).astype(jnp.int32)
     own_tok = own(tok_s)
-    mixed_all = lax.all_gather(packed, "mlp", axis=0, tiled=False)
+    mixed_all = lax.all_gather(mixed, "mlp", axis=0, tiled=False)
     down_own = w_out_mlp.astype(bf16)[None]
     if parts == 8:
         out_two = join(out_own, after(out_far, ends))
@@ -1091,10 +1056,12 @@
         up_near = hop(up_two, NEAR)
         down_far = hop(after(down_own, ends), FAR)
         out_core = hop(after(out_two, mixed), CORE)
+        out_w = (out_two, out_near, out_core, hop(after(out_near, mixed), CORE))
         down_two = join(down_own, after(down_far, mixed))
         down_near = hop(down_two, NEAR)
         down_core = hop(down_two, CORE)
         up_core = hop(after(up_two, mixed), CORE)
+        up_w = (up_two, up_near, up_core, hop(after(up_near, mixed), CORE))
         down_last = hop(down_near, CORE)
         down = jnp.concatenate(
             [
@@ -1109,10 +1076,6 @@
         up_w = (lax.all_gather(up_own, "tok", axis=1, tiled=True)[None],) * 4
     cot_s = permute_columns(after(cotangent, mixed), into_local)
     d_hidden = nt(cot_s, down)
-    if parts == 8:
-        out_near, up_near = after(out_near, d_hidden), after(up_near, d_hidden)
-        out_w = (out_two, out_near, out_core, hop(out_near, CORE))
-        up_w = (up_two, up_near, up_core, hop(up_near, CORE))
     xn_two, hidden, d_gate, d_up, d_branch, second = middle(
         slab_ref, mixed_all, tok_s, gains_f[1:2], d_hidden, out_w, up_w
     )

time: 789 us -> 792 us (level)
    all_gather x1, waiting for transfers between devices: 10.9 us -> 0.01 us  [on_device(): mixed_all = lax.all_gather(mixed, 'mlp', axis=0, tiled=False)]
    ppermute x43, waiting for transfers between devices: 150 us -> 159 us  [hop(): lax.ppermute(array, 'tok', [(i, i ^ pairs[i % 2]) for i in range(count)])]
  transfers between devices with their start and end apart: 54 -> 54, of which waited for: 23 -> 20; matrix products, arithmetic and copies ran while one was open for 21% -> 21% of each run, Pallas kernels for 24% -> 23%
where the time goes in v5:
time: 792 us; the launch traced here: 786 us
  waiting for transfers between devices  267 us (34%)
  Pallas kernels  240 us (30%)
  matrix products  77.2 us (10%)
  other arithmetic  63.4 us (8%)
  local copies, waits for them, and re-layouts  47.8 us (6%)
  starting transfers between devices  41.7 us (5%)
  blocking collectives  33.2 us (4%)
  between operations  15.6 us (2%)
    ppermute x43, waiting for transfers between devices, hop(): lax.ppermute(array, 'tok', [(i, i ^ pairs[i % 2]) for i in range(count)])  159 us
    pallas_call x4, Pallas kernels, soap(): pl.pallas_call(functools.partial(soap_kernel, turned, swapped), grid=(gro...  85.3 us
    all_gather x3, waiting for transfers between devices, gather_slabs(): return lax.all_gather(array, 'mlp', axis=0, tiled=True)  77.5 us
    dot_general x14, matrix products, tn(): lax.dot_general(left, right, (((0,), (0,)), ((), ())), preferred_element_...  55.6 us
    pallas_call x1, Pallas kernels, middle(): pl.pallas_call(middle_kernel, grid=(slabs,), in_specs=[pl.BlockSpec(memor...  52.9 us
    ppermute x43, starting transfers between devices, hop(): lax.ppermute(array, 'tok', [(i, i ^ pairs[i % 2]) for i in range(count)])  34.5 us
    reduce_scatter x3, waiting for transfers between devices, scatter_slabs(): return lax.psum_scatter(array, 'mlp', scatter_dimension=0, tiled=True)  30.8 us
    unnamed x139, local copies, waits for them, and re-layouts  30.4 us
  transfers between devices with their start and end apart: 54, of which 20 were waited for; matrix products, arithmetic and copies ran while one was open for 21% of the time, Pallas kernels for 23%

profile of v5, /device:TPU:0, one launch (start us, length us, event | category | flops | bytes accessed | tf_op | source)
XLA Modules:
  0.0 785.9 jit_solution(8037673206787156014)
XLA Ops:
  9.8 3.0 collective-permute-start.1
  15.8 4.0 collective-permute-start.6
  25.4 4.9 permute_columns.4.tok
  34.1 2.8 collective-permute-done.2
  41.9 2.2 slice_reduce_fusion.3
  45.7 6.1 fusion.63
  53.1 7.5 collective-permute-done.5.w_1
  60.6 2.1 convert_bitcast_fusion
  66.2 26.0 %front.1 = (bf16[1024,2048]{1,0:T(8,128)(2,1)}, f32[1024,704]{1,0:T(8,128)}, bf16[1024,704]{1,0:T(8,128)(2,1)}, bf16[16,704]{1,0:T(8,128)(2,1)}, bf16[1024,704]{...) custom-call(bf16[1024,2048]{1,0:T(8,128)(2,1)} %permute_columns.4.to, ...), custom_call_target="tpu_custom_call" | custom-call | flops 28600000512 | bytes 85800000 | tf_op jit(solution)/shard_map/front/pallas_call | solution.py:260
  93.0 12.0 %all-gather.4.ends = f32[8,2,704]{2,1,0:T(2,128)} all-gather(f32[1,2,704]{2,1,0:T(2,128)S(1)} %slice_bitcast_fusion.16), channel_id=2, replica_groups=mesh['tok'=8,'mlp'=4] {'tok'}, dimensions={0}, use_global_device_ids=true | all-gather | bytes 50688 | tf_op jit(solution)/shard_map/all_gather | solution.py:1045
  105.1 7.4 finish_state.1
  114.6 11.5 %collective-permute-done.9 = bf16[1,1536,256]{2,1,0:T(8,128)(2,1)S(1)} collective-permute-done((bf16[1,1536,256]{2,1,0:T(8,128)(2,1)S(1)}, bf16[1,1536,256]{2,1,0:T(8,128)(2,1)S(1)}, u32[]{:S(2)}, u32[]{:S(2)}) %collective-permute-start.9) | collective-permute-done | bytes 786464 | tf_op jit(solution)/shard_map/ppermute | solution.py:769
  132.1 3.2 pad_maximum_fusion.1.w_0
  137.8 5.3 permute_columns.6
  143.1 5.8 collective-permute-done.10
  149.8 2.1 fusion.74
  151.9 2.1 fusion.73
  155.4 58.1 %collective-permute-done.14.w_1 = bf16[2,4,704,256]{3,2,1,0:T(8,128)(2,1)} collective-permute-done((bf16[2,4,704,256]{3,2,1,0:T(8,128)(2,1)}, bf16[2,4,704,256]{3,2,1,0:T(8,128)(2,1)}, u32[]{:S(2)}, u32[]{:S(2)}) %collective-permute-start.14) | collective-permute-done | bytes 2883616 | tf_op jit(solution)/shard_map/ppermute | solution.py:769
  216.8 10.5 %fusion.117.dhid = f32[1024,1536]{1,0:T(8,128)} fusion(bf16[1024,2048]{1,0:T(8,128)(2,1)S(1)} %copy-done.29, bf16[1536,2048]{1,0:T(8,128)(2,1)} %fusion.69), kind=kOutput, calls=%fused_computation.267 | convolution fusion | flops 6442450944 | bytes 16777216 | tf_op jit(solution)/shard_map/dot_general | solution.py:49
  230.6 52.9 %middle.1 = (bf16[1024,2048]{1,0:T(8,128)(2,1)}, bf16[1024,1536]{1,0:T(8,128)(2,1)}, bf16[1024,1536]{1,0:T(8,128)(2,1)}, bf16[1024,1536]{1,0:T(8,128)(2,1)}, bf1...) custom-call(s32[1]{0:T(128)} %bitcast.slab, bf16[4,1024,704]{2,1,0:T(8,128)(2,1)} %bitcast.152, ...), custom_call_target="tpu_custom_call" | custom-call | flops 57200001024 | bytes 171600000 | tf_op jit(solution)/shard_map/middle/pallas_call | solution.py:408
  285.4 5.5 convolution_convert_fusion.3
  292.2 3.7 convolution_convert_fusion.2
  296.5 5.1 convolution_convert_fusion.1
  301.7 6.2 fusion.25
  308.0 6.7 fusion.23
  318.0 6.2 fusion.7
  324.9 2.0 copy-done.2
  328.1 8.3 %collective-permute-done.22 = bf16[512,1536]{1,0:T(8,128)(2,1)S(1)} collective-permute-done((bf16[512,1536]{1,0:T(8,128)(2,1)S(1)}, bf16[512,1536]{1,0:T(8,128)(2,1)S(1)}, u32[]{:S(2)}, u32[]{:S(2)}) %collective-permute-start.22) | collective-permute-done | bytes 1572896 | tf_op jit(solution)/shard_map/ppermute | solution.py:769
  338.4 23.3 %collective-permute-done.25 = bf16[512,1536]{1,0:T(8,128)(2,1)S(1)} collective-permute-done((bf16[512,1536]{1,0:T(8,128)(2,1)S(1)}, bf16[512,1536]{1,0:T(8,128)(2,1)S(1)}, u32[]{:S(2)}, u32[]{:S(2)}) %collective-permute-start.25) | collective-permute-done | bytes 1572896 | tf_op jit(solution)/shard_map/ppermute | solution.py:769
  363.9 4.2 settle.2
  368.1 11.1 %convolution_convert_fusion = bf16[1024,2048]{1,0:T(8,128)(2,1)} fusion(bf16[1024,1536]{1,0:T(8,128)(2,1)} %get-tuple-element.140, bf16[1536,2048]{1,0:T(8,128)(2,1)} %fusion.69), kind=kOutput, calls=%fused_computation.4 | convolution fusion | flops 6444548096 | bytes 13631488 | tf_op jit(solution)/shard_map/dot_general | solution.py:45
  379.2 2.6 fusion.67
  381.8 2.2 fusion.68
  385.3 33.3 %soap.4 = (f32[2,256,1536]{2,1,0:T(8,128)}, f32[2,256,1536]{2,1,0:T(8,128)}, f32[2,256,1536]{2,1,0:T(8,128)}) custom-call(f32[2,256,1536]{2,1,0:T(8,128)} %w.1, f32[2,256,1536]{2,1,0:T(8,128)} %m.1, f32[2,256,1536]{2,1,0:T(8,128)} %v.1, bf16[2,256,1536]{2,1,0:T(8,128)(2,1)} %pad_maximum_fusion.5.g, f32[2,4,24,2,64,64]{5,4,3,2,1,0:T(8,128)} %q.2), custom_call_target="tpu_custom_call" | custom-call | flops 36044800000 | bytes 108134400 | tf_op jit(solution)/shard_map/soap/pallas_call | solution.py:734
  418.7 30.7 %all-gather.12.cloned.1.call-done.d_rec = bf16[1024,2048]{1,0:T(8,128)(2,1)} async-done(((bf16[256,2048]{1,0:T(8,128)(2,1)}), bf16[1024,2048]{1,0:T(8,128)(2,1)}) %all-gather.12.cloned.1.call-update) | async-done | bytes 4194320 | tf_op jit(solution)/shard_map/all_gather | solution.py:760
  449.4 13.9 %back_scan.1 = (bf16[1024,704]{1,0:T(8,128)(2,1)}, f32[1024,704]{1,0:T(8,128)}, f32[1024,704]{1,0:T(8,128)}, f32[8,704]{1,0:T(8,128)}) custom-call(s32[1]{0:T(128)} %bitcast.slab, bf16[1024,2048]{1,0:T(8,128)(2,1)} %all-gather.12.cloned.1.call-done.d_rec, bf16[2,4,704,256]{3,2,1,0:T(8,128)(2,1)} %pad_maximum_fusion.1.w_0, ...), custom_call_target="tpu_custom_call" | custom-call | flops 13200000000 | bytes 39600000 | tf_op jit(solution)/shard_map/back_scan/pallas_call | solution.py:464
  464.0 10.2 %all-gather.5.ends = f32[8,2,704]{2,1,0:T(2,128)} all-gather(f32[1,2,704]{2,1,0:T(2,128)S(1)} %slice_bitcast_fusion.15), channel_id=5, replica_groups=mesh['tok'=8,'mlp'=4] {'tok'}, dimensions={0}, use_global_device_ids=true | all-gather | bytes 50688 | tf_op jit(solution)/shard_map/all_gather | solution.py:1113
  474.2 18.9 %gates_back.1 = (bf16[1024,704]{1,0:T(8,128)(2,1)}, bf16[1024,704]{1,0:T(8,128)(2,1)}, bf16[1024,704]{1,0:T(8,128)(2,1)}, f32[16,704]{1,0:T(8,128)}, f32[16,704]{1,0:T(8,128)}, /*index=5*/f32[8,704]{1,0:T(8,128)}) custom-call(s32[1]{0:T(128)} %bitcast.1.rank, f32[8,2,704]{2,1,0:T(2,128)} %all-gather.5.ends, f32[1024,704]{1,0:T(8,128)} %get-tuple-element.154.g_l, ...), custom_call_target="tpu_custom_call" | custom-call | flops 20899999744 | bytes 62700000 | tf_op jit(solution)/shard_map/gates_back/pallas_call | solution.py:573
  494.4 2.6 collective-permute-start.32
  497.6 12.3 %pair_back.1 = (bf16[1024,2048]{1,0:T(8,128)(2,1)}, bf16[1024,704]{1,0:T(8,128)(2,1)}) custom-call(bf16[1024,704]{1,0:T(8,128)(2,1)} %get-tuple-element.173.left, bf16[1024,704]{1,0:T(8,128)(2,1)} %get-tuple-element.162.right, f32[16,704]{1,0:T(8,128)} %get-tuple-element.163.tail, f32[16,704]{1,0:T(8,128)} %copy-done.50, ...), custom_call_target="tpu_custom_call" | custom-call | flops 13200000000 | bytes 39600000 | tf_op jit(solution)/shard_map/pair_back/pallas_call | solution.py:623
  510.0 17.0 %reduce-scatter.4.cloned.1.call-done = bf16[256,2048]{1,0:T(8,128)(2,1)} async-done(((bf16[1024,2048]{1,0:T(8,128)(2,1)}), bf16[256,2048]{1,0:T(8,128)(2,1)}) %reduce-scatter.4.cloned.1.call-update) | async-done | bytes 1048592 | tf_op jit(solution)/shard_map/reduce_scatter | solution.py:764
  530.5 2.3 constant_dynamic-slice_fusion.1.value
  532.8 8.2 %collective-permute-done.33 = bf16[256,1536]{1,0:T(8,128)(2,1)S(1)} collective-permute-done((bf16[256,1536]{1,0:T(8,128)(2,1)S(1)}, bf16[256,1536]{1,0:T(8,128)(2,1)S(1)}, u32[]{:S(2)}, u32[]{:S(2)}) %collective-permute-start.33) | collective-permute-done | bytes 786464 | tf_op jit(solution)/shard_map/ppermute | solution.py:769
  541.0 2.9 fusion.44
  544.1 5.1 fusion.34
  549.2 2.8 fusion.31
  552.5 2.8 fusion.37
  555.4 23.9 %soap.5 = (f32[1,1536,256]{2,1,0:T(8,128)}, f32[1,1536,256]{2,1,0:T(8,128)}, f32[1,1536,256]{2,1,0:T(8,128)}) custom-call(f32[1,1536,256]{2,1,0:T(8,128)} %bitcast.135, f32[1,1536,256]{2,1,0:T(8,128)} %bitcast.154, f32[1,1536,256]{2,1,0:T(8,128)} %bitcast.155, bf16[1,256,1536]{2,1,0:T(8,128)(2,1)} %bitcast.139, f32[1,24,4,2,64,64]{5,4,3,2,1,0:T(8,128)} %bitcast.151), custom_call_target="tpu_custom_call" | custom-call | flops 18022400000 | bytes 54067200 | tf_op jit(solution)/shard_map/soap/pallas_call | solution.py:734
  579.3 3.9 fusion.17
  593.1 13.8 %reduce-scatter.8.cloned.1.call-done.upstream = bf16[256,2048]{1,0:T(8,128)(2,1)} async-done(((bf16[1024,2048]{1,0:T(8,128)(2,1)}), bf16[256,2048]{1,0:T(8,128)(2,1)}) %reduce-scatter.8.cloned.1.call-update) | async-done | bytes 1048592 | tf_op jit(solution)/shard_map/reduce_scatter | solution.py:764
  607.0 4.4 settle.3
  611.6 2.7 fusion.118
  623.8 3.5 collective-permute-done.41
  628.9 2.3 permute_columns.7
  637.7 6.4 collective-permute-done.34
  647.1 10.4 %collective-permute-done.36 = bf16[704,512]{1,0:T(8,128)(2,1)} collective-permute-done((bf16[704,512]{1,0:T(8,128)(2,1)}, bf16[704,512]{1,0:T(8,128)(2,1)}, u32[]{:S(2)}, u32[]{:S(2)}) %collective-permute-start.36) | collective-permute-done | bytes 720928 | tf_op jit(solution)/shard_map/ppermute | solution.py:769
  660.3 9.0 %collective-permute-done.38 = bf16[704,512]{1,0:T(8,128)(2,1)S(1)} collective-permute-done((bf16[704,512]{1,0:T(8,128)(2,1)}, bf16[704,512]{1,0:T(8,128)(2,1)S(1)}, u32[]{:S(2)}, u32[]{:S(2)}) %collective-permute-start.38) | collective-permute-done | bytes 720928 | tf_op jit(solution)/shard_map/ppermute | solution.py:769
  676.6 17.2 %soap.6 = (f32[2,704,256]{2,1,0:T(8,128)}, f32[2,704,256]{2,1,0:T(8,128)}, f32[2,704,256]{2,1,0:T(8,128)}) custom-call(f32[2,704,256]{2,1,0:T(8,128)} %bitcast.136, f32[2,704,256]{2,1,0:T(8,128)} %bitcast.156, f32[2,704,256]{2,1,0:T(8,128)} %bitcast.157, bf16[2,704,256]{2,1,0:T(8,128)(2,1)} %pad_maximum_fusion.12.g, f32[2,4,11,2,64,64]{5,4,3,2,1,0:T(8,128)} %q.3), custom_call_target="tpu_custom_call" | custom-call | flops 16520532992 | bytes 49561600 | tf_op jit(solution)/shard_map/soap/pallas_call | solution.py:734
  695.4 1.9 fusion.98.g
  698.1 10.8 %soap.7 = (f32[1,704,256]{2,1,0:T(8,128)}, f32[1,704,256]{2,1,0:T(8,128)}, f32[1,704,256]{2,1,0:T(8,128)}) custom-call(f32[1,704,256]{2,1,0:T(8,128)} %bitcast.140, f32[1,704,256]{2,1,0:T(8,128)} %bitcast.158, f32[1,704,256]{2,1,0:T(8,128)} %bitcast.159, bf16[1,704,256]{2,1,0:T(8,128)(2,1)} %fusion.98.g, f32[1,11,4,2,64,64]{5,4,3,2,1,0:T(8,128)} %bitcast.153), custom_call_target="tpu_custom_call" | custom-call | flops 8260266496 | bytes 24780800 | tf_op jit(solution)/shard_map/soap/pallas_call | solution.py:734
  708.9 11.0 %psum.7 = f32[2,256]{1,0:T(2,128)S(1)} all-reduce(f32[2,256]{1,0:T(2,128)S(1)} %fusion.106), channel_id=1, replica_groups=mesh['tok'=8,'mlp'=4] {'mlp'}, use_global_device_ids=true, to_apply=%region_5.6 | all-reduce | flops 512 | bytes 4096 | tf_op jit(solution)/shard_map/psum | solution.py:1160
  720.5 6.7 convert_element_type.330
  727.2 46.9 %all-gather.14.cloned.1.call-done = bf16[1024,2048]{1,0:T(8,128)(2,1)} async-done(((bf16[256,2048]{1,0:T(8,128)(2,1)}), bf16[1024,2048]{1,0:T(8,128)(2,1)}) %all-gather.14.cloned.1.call-update) | async-done | bytes 4194320 | tf_op jit(solution)/shard_map/all_gather | solution.py:760
  774.1 4.8 copy.87
  (346 shorter events, 111.0 us)
Async XLA Ops:
  7.2 58.5 %all-gather.20.cloned.1.call-start = ((), (), s32[]{:S(2)}) async-start(), calls=%async_computation.10 | async-start | bytes 1802240 | tf_op jit(solution)/shard_map/all_gather | solution.py:998
  9.8 22.1 %collective-permute-start.1 = (bf16[1,8,4024]{2,1,0:T(8,128)(2,1)S(1)}, bf16[1,8,4024]{2,1,0:T(8,128)(2,1)S(1)}, u32[]{:S(2)}, u32[]{:S(2)}) collective-permute-start(bf16[1,8,4024]{2,1,0:T(8,128)(2,1)S(1)} %concatenate.92), channel_id=1, source_target_pairs={{0,16},{4,12},{8,24},{12,4},{16,0},{20,28},{24,8},{28,20},{1,17},{... | collective-permute-start | bytes 193160 | tf_op jit(solution)/shard_map/ppermute | solution.py:769
  13.6 18.4 %collective-permute-start = (bf16[16,2048]{1,0:T(8,128)(2,1)S(1)}, bf16[16,2048]{1,0:T(8,128)(2,1)S(1)}, u32[]{:S(2)}, u32[]{:S(2)}) collective-permute-start(bf16[16,2048]{1,0:T(8,128)(2,1)S(1)} %slice.470), channel_id=1, source_target_pairs={{0,4},{4,8},{8,12},{12,16},{16,20},{20,24},{24,28},{1,5},{5,9},{9,... | collective-permute-start | bytes 196616 | tf_op jit(solution)/shard_map/ppermute | solution.py:1021
  15.8 14.4 %collective-permute-start.6 = (s32[16]{0:T(128)S(1)}, s32[16]{0:T(128)S(1)}, u32[]{:S(2)}, u32[]{:S(2)}) collective-permute-start(s32[16]{0:T(128)S(1)} %slice.478), channel_id=1, source_target_pairs={{0,4},{4,8},{8,12},{12,16},{16,20},{20,24},{24,28},{1,5},{5,9},{9,... | collective-permute-start | bytes 200 | tf_op jit(solution)/shard_map/ppermute | solution.py:1023
  21.3 18.9 %collective-permute-start.4 = (bf16[1,2,704,256]{3,2,1,0:T(8,128)(2,1)S(1)}, bf16[1,2,704,256]{3,2,1,0:T(8,128)(2,1)}, u32[]{:S(2)}, u32[]{:S(2)}) collective-permute-start(bf16[1,2,704,256]{3,2,1,0:T(8,128)(2,1)S(1)} %convert_bitcast_fusion.1), channel_id=1, source_target_pairs={{0,16},{4,12},{8,24},{12,4},{16,0},{20,28},{24,8},{28,20},{1,17},{... | collective-permute-start | bytes 2162696 | tf_op jit(solution)/shard_map/ppermute | solution.py:769
  22.6 208.0 %all-gather.18.cloned.1.call-start = ((), (), s32[]{:S(2)}) async-start(), calls=%async_computation.9 | async-start | bytes 7864320 | tf_op jit(solution)/shard_map/all_gather | solution.py:1050
  31.9 5.0 collective-permute-start.2
  37.0 1.6 collective-permute-start.3
  41.4 19.2 %collective-permute-start.5 = (bf16[2,2,704,256]{3,2,1,0:T(8,128)(2,1)S(1)}, bf16[2,2,704,256]{3,2,1,0:T(8,128)(2,1)}, u32[]{:S(2)}, u32[]{:S(2)}) collective-permute-start(bf16[2,2,704,256]{3,2,1,0:T(8,128)(2,1)S(1)} %pad_maximum_fusion.7.w_0), channel_id=1, source_target_pairs={{0,8},{4,20},{8,0},{12,28},{16,24},{20,4},{24,16},{28,12},{1,9},{5... | collective-permute-start | bytes 4325384 | tf_op jit(solution)/shard_map/ppermute | solution.py:769
  51.8 14.4 %collective-permute-start.7 = (bf16[2,2,704,256]{3,2,1,0:T(8,128)(2,1)S(1)}, bf16[2,2,704,256]{3,2,1,0:T(8,128)(2,1)}, u32[]{:S(2)}, u32[]{:S(2)}) collective-permute-start(bf16[2,2,704,256]{3,2,1,0:T(8,128)(2,1)S(1)} %pad_maximum_fusion.7.w_0), channel_id=1, source_target_pairs={{0,4},{4,0},{8,12},{12,8},{16,20},{20,16},{24,28},{28,24},{1,5},{5... | collective-permute-start | bytes 4325384 | tf_op jit(solution)/shard_map/ppermute | solution.py:769
  60.6 5.7 collective-permute-start.8
  64.2 64.6 %collective-permute-start.17 = (bf16[1,2,256,1536]{3,2,1,0:T(8,128)(2,1)S(1)}, bf16[1,2,256,1536]{3,2,1,0:T(8,128)(2,1)}, u32[]{:S(2)}, u32[]{:S(2)}) collective-permute-start(bf16[1,2,256,1536]{3,2,1,0:T(8,128)(2,1)S(1)} %convert_bitcast_fusion), channel_id=1, source_target_pairs={{0,16},{4,12},{8,24},{12,4},{16,0},{20,28},{24,8},{28,20},{1,17},{... | collective-permute-start | bytes 4718600 | tf_op jit(solution)/shard_map/ppermute | solution.py:769
  65.7 63.1 %collective-permute-start.13 = (bf16[1,4,704,256]{3,2,1,0:T(8,128)(2,1)}, bf16[1,4,704,256]{3,2,1,0:T(8,128)(2,1)}, u32[]{:S(2)}, u32[]{:S(2)}) collective-permute-start(bf16[1,4,704,256]{3,2,1,0:T(8,128)(2,1)} %bitcast.137), channel_id=1, source_target_pairs={{0,16},{4,12},{8,24},{12,4},{16,0},{20,28},{24,8},{28,20},{1,17},{... | collective-permute-start | bytes 4325384 | tf_op jit(solution)/shard_map/ppermute | solution.py:769
  112.5 251.4 %reduce-scatter.6.cloned.1.call-start = ((), (), s32[]{:S(2)}) async-start(), calls=%async_computation.4 | async-start | bytes 5242880 | tf_op jit(solution)/shard_map/reduce_scatter | solution.py:764
  114.0 12.1 %collective-permute-start.9 = (bf16[1,1536,256]{2,1,0:T(8,128)(2,1)S(1)}, bf16[1,1536,256]{2,1,0:T(8,128)(2,1)S(1)}, u32[]{:S(2)}, u32[]{:S(2)}) collective-permute-start(bf16[1,1536,256]{2,1,0:T(8,128)(2,1)S(1)} %convert_bitcast_fusion.2), channel_id=1, source_target_pairs={{0,16},{4,12},{8,24},{12,4},{16,0},{20,28},{24,8},{28,20},{1,17},{... | collective-permute-start | bytes 2359304 | tf_op jit(solution)/shard_map/ppermute | solution.py:769
  128.2 20.7 %collective-permute-start.10 = (bf16[2,1536,256]{2,1,0:T(8,128)(2,1)}, bf16[2,1536,256]{2,1,0:T(8,128)(2,1)}, u32[]{:S(2)}, u32[]{:S(2)}) collective-permute-start(bf16[2,1536,256]{2,1,0:T(8,128)(2,1)} %pad_maximum_fusion.2), channel_id=1, source_target_pairs={{0,8},{4,20},{8,0},{12,28},{16,24},{20,4},{24,16},{28,12},{1,9},{5... | collective-permute-start | bytes 4718600 | tf_op jit(solution)/shard_map/ppermute | solution.py:769
  130.6 23.4 %copy-start.5 = (bf16[2,2,256,1536]{3,2,1,0:T(8,128)(2,1)}, bf16[2,2,256,1536]{3,2,1,0:T(8,128)(2,1)S(1)}, u32[]{:S(2)}) copy-start(bf16[2,2,256,1536]{3,2,1,0:T(8,128)(2,1)S(1)} %pad_maximum_fusion.u_0) | copy-start | bytes 9437188
  130.6 82.9 %collective-permute-start.18 = (bf16[2,2,256,1536]{3,2,1,0:T(8,128)(2,1)S(1)}, bf16[2,2,256,1536]{3,2,1,0:T(8,128)(2,1)}, u32[]{:S(2)}, u32[]{:S(2)}) collective-permute-start(bf16[2,2,256,1536]{3,2,1,0:T(8,128)(2,1)S(1)} %pad_maximum_fusion.u_0), channel_id=1, source_target_pairs={{0,8},{4,20},{8,0},{12,28},{16,24},{20,4},{24,16},{28,12},{1,9},{5... | collective-permute-start | bytes 9437192 | tf_op jit(solution)/shard_map/ppermute | solution.py:769
  135.3 78.2 %collective-permute-start.14 = (bf16[2,4,704,256]{3,2,1,0:T(8,128)(2,1)}, bf16[2,4,704,256]{3,2,1,0:T(8,128)(2,1)}, u32[]{:S(2)}, u32[]{:S(2)}) collective-permute-start(bf16[2,4,704,256]{3,2,1,0:T(8,128)(2,1)} %pad_maximum_fusion.1.w_0), channel_id=1, source_target_pairs={{0,8},{4,20},{8,0},{12,28},{16,24},{20,4},{24,16},{28,12},{1,9},{5... | collective-permute-start | bytes 8650760 | tf_op jit(solution)/shard_map/ppermute | solution.py:769
  137.3 90.1 %collective-permute-start.15 = (bf16[2,4,704,256]{3,2,1,0:T(8,128)(2,1)}, bf16[2,4,704,256]{3,2,1,0:T(8,128)(2,1)}, u32[]{:S(2)}, u32[]{:S(2)}) collective-permute-start(bf16[2,4,704,256]{3,2,1,0:T(8,128)(2,1)} %pad_maximum_fusion.1.w_0), channel_id=1, source_target_pairs={{0,4},{4,0},{8,12},{12,8},{16,20},{20,16},{24,28},{28,24},{1,5},{5... | collective-permute-start | bytes 8650760 | tf_op jit(solution)/shard_map/ppermute | solution.py:769
  137.3 16.7 %collective-permute-start.11 = (bf16[2,1536,256]{2,1,0:T(8,128)(2,1)}, bf16[2,1536,256]{2,1,0:T(8,128)(2,1)S(1)}, u32[]{:S(2)}, u32[]{:S(2)}) collective-permute-start(bf16[2,1536,256]{2,1,0:T(8,128)(2,1)} %pad_maximum_fusion.2), channel_id=1, source_target_pairs={{0,4},{4,0},{8,12},{12,8},{16,20},{20,16},{24,28},{28,24},{1,5},{5... | collective-permute-start | bytes 4718600 | tf_op jit(solution)/shard_map/ppermute | solution.py:769
  148.9 65.1 %collective-permute-start.12 = (bf16[2,1536,256]{2,1,0:T(8,128)(2,1)}, bf16[2,1536,256]{2,1,0:T(8,128)(2,1)S(1)}, u32[]{:S(2)}, u32[]{:S(2)}) collective-permute-start(bf16[2,1536,256]{2,1,0:T(8,128)(2,1)} %collective-permute-done.10), channel_id=1, source_target_pairs={{0,4},{4,0},{8,12},{12,8},{16,20},{20,16},{24,28},{28,24},{1,5},{5... | collective-permute-start | bytes 4718600 | tf_op jit(solution)/shard_map/ppermute | solution.py:769
  154.0 73.4 %collective-permute-start.19 = (bf16[2,2,256,1536]{3,2,1,0:T(8,128)(2,1)S(1)}, bf16[2,2,256,1536]{3,2,1,0:T(8,128)(2,1)S(1)}, u32[]{:S(2)}, u32[]{:S(2)}) collective-permute-start(bf16[2,2,256,1536]{3,2,1,0:T(8,128)(2,1)S(1)} %pad_maximum_fusion.u_0), channel_id=1, source_target_pairs={{0,4},{4,0},{8,12},{12,8},{16,20},{20,16},{24,28},{28,24},{1,5},{5... | collective-permute-start | bytes 9437192 | tf_op jit(solution)/shard_map/ppermute | solution.py:769
  155.4 61.4 %copy-start.29 = (bf16[1024,2048]{1,0:T(8,128)(2,1)S(1)}, bf16[1024,2048]{1,0:T(8,128)(2,1)}, u32[]{:S(2)}) copy-start(bf16[1024,2048]{1,0:T(8,128)(2,1)} %permute_columns.6) | copy-start | bytes 12582916
  213.5 15.5 %collective-permute-start.16 = (bf16[2,4,704,256]{3,2,1,0:T(8,128)(2,1)}, bf16[2,4,704,256]{3,2,1,0:T(8,128)(2,1)S(1)}, u32[]{:S(2)}, u32[]{:S(2)}) collective-permute-start(bf16[2,4,704,256]{3,2,1,0:T(8,128)(2,1)} %collective-permute-done.14.w_1), channel_id=1, source_target_pairs={{0,4},{4,0},{8,12},{12,8},{16,20},{20,16},{24,28},{28,24},{1,5},{5... | collective-permute-start | bytes 8650760 | tf_op jit(solution)/shard_map/ppermute | solution.py:769
  213.5 17.1 %collective-permute-start.20 = (bf16[2,2,256,1536]{3,2,1,0:T(8,128)(2,1)}, bf16[2,2,256,1536]{3,2,1,0:T(8,128)(2,1)}, u32[]{:S(2)}, u32[]{:S(2)}) collective-permute-start(bf16[2,2,256,1536]{3,2,1,0:T(8,128)(2,1)} %collective-permute-done.18.u_1), channel_id=1, source_target_pairs={{0,4},{4,0},{8,12},{12,8},{16,20},{20,16},{24,28},{28,24},{1,5},{5... | collective-permute-start | bytes 9437192 | tf_op jit(solution)/shard_map/ppermute | solution.py:769
  283.6 165.8 %all-gather.12.cloned.1.call-start = ((), (), s32[]{:S(2)}) async-start(), calls=%async_computation.5 | async-start | bytes 5242880 | tf_op jit(solution)/shard_map/all_gather | solution.py:760
  291.0 23.7 %collective-permute-start.21 = (bf16[1024,1536]{1,0:T(8,128)(2,1)S(1)}, bf16[1024,1536]{1,0:T(8,128)(2,1)S(1)}, u32[]{:S(2)}, u32[]{:S(2)}) collective-permute-start(bf16[1024,1536]{1,0:T(8,128)(2,1)S(1)} %convolution_convert_fusion.3), channel_id=1, source_target_pairs={{0,4},{4,0},{8,12},{12,8},{16,20},{20,16},{24,28},{28,24},{1,5},{5... | collective-permute-start | bytes 9437192 | tf_op jit(solution)/shard_map/ppermute | solution.py:769
  295.9 19.4 %collective-permute-start.24 = (bf16[1024,1536]{1,0:T(8,128)(2,1)S(1)}, bf16[1024,1536]{1,0:T(8,128)(2,1)S(1)}, u32[]{:S(2)}, u32[]{:S(2)}) collective-permute-start(bf16[1024,1536]{1,0:T(8,128)(2,1)S(1)} %convolution_convert_fusion.2), channel_id=1, source_target_pairs={{0,4},{4,0},{8,12},{12,8},{16,20},{20,16},{24,28},{28,24},{1,5},{5... | collective-permute-start | bytes 9437192 | tf_op jit(solution)/shard_map/ppermute | solution.py:769
  301.6 22.7 %collective-permute-start.27 = (bf16[1024,1536]{1,0:T(8,128)(2,1)}, bf16[1024,1536]{1,0:T(8,128)(2,1)S(1)}, u32[]{:S(2)}, u32[]{:S(2)}) collective-permute-start(bf16[1024,1536]{1,0:T(8,128)(2,1)} %convolution_convert_fusion.1), channel_id=1, source_target_pairs={{0,4},{4,0},{8,12},{12,8},{16,20},{20,16},{24,28},{28,24},{1,5},{5... | collective-permute-start | bytes 9437192 | tf_op jit(solution)/shard_map/ppermute | solution.py:769
  308.0 28.5 %copy-start.4 = (f32[1024,1536]{1,0:T(8,128)}, f32[1024,1536]{1,0:T(8,128)S(1)}, u32[]{:S(2)}) copy-start(f32[1024,1536]{1,0:T(8,128)S(1)} %fusion.25) | copy-start | bytes 18874372
  314.7 47.0 %copy-start.3 = (f32[1024,1536]{1,0:T(8,128)}, f32[1024,1536]{1,0:T(8,128)S(1)}, u32[]{:S(2)}) copy-start(f32[1024,1536]{1,0:T(8,128)S(1)} %fusion.23) | copy-start | bytes 18874372
  315.3 46.4 %copy-start.8 = (bf16[1024,1536]{1,0:T(8,128)(2,1)}, bf16[1024,1536]{1,0:T(8,128)(2,1)S(1)}, u32[]{:S(2)}) copy-start(bf16[1024,1536]{1,0:T(8,128)(2,1)S(1)} %collective-permute-done.24) | copy-start | bytes 9437188
  315.9 20.5 %collective-permute-start.22 = (bf16[512,1536]{1,0:T(8,128)(2,1)S(1)}, bf16[512,1536]{1,0:T(8,128)(2,1)S(1)}, u32[]{:S(2)}, u32[]{:S(2)}) collective-permute-start(bf16[512,1536]{1,0:T(8,128)(2,1)S(1)} %pad_maximum_fusion.3), channel_id=1, source_target_pairs={{0,8},{4,20},{8,0},{12,28},{16,24},{20,4},{24,16},{28,12},{1,9},{5... | collective-permute-start | bytes 4718600 | tf_op jit(solution)/shard_map/ppermute | solution.py:769
  316.6 45.1 %collective-permute-start.25 = (bf16[512,1536]{1,0:T(8,128)(2,1)S(1)}, bf16[512,1536]{1,0:T(8,128)(2,1)S(1)}, u32[]{:S(2)}, u32[]{:S(2)}) collective-permute-start(bf16[512,1536]{1,0:T(8,128)(2,1)S(1)} %pad_maximum_fusion.4), channel_id=1, source_target_pairs={{0,8},{4,20},{8,0},{12,28},{16,24},{20,4},{24,16},{28,12},{1,9},{5... | collective-permute-start | bytes 4718600 | tf_op jit(solution)/shard_map/ppermute | solution.py:769
  336.4 26.9 %copy-start.19 = (bf16[512,1536]{1,0:T(8,128)(2,1)}, bf16[512,1536]{1,0:T(8,128)(2,1)S(1)}, u32[]{:S(2)}) copy-start(bf16[512,1536]{1,0:T(8,128)(2,1)S(1)} %collective-permute-done.22) | copy-start | bytes 4718596
  337.8 41.4 %collective-permute-start.23 = (bf16[256,1536]{1,0:T(8,128)(2,1)}, bf16[256,1536]{1,0:T(8,128)(2,1)}, u32[]{:S(2)}, u32[]{:S(2)}) collective-permute-start(bf16[256,1536]{1,0:T(8,128)(2,1)} %fusion.55), channel_id=1, source_target_pairs={{0,16},{4,12},{8,24},{12,4},{16,0},{20,28},{24,8},{28,20},{1,17},{... | collective-permute-start | bytes 2359304 | tf_op jit(solution)/shard_map/ppermute | solution.py:769
  363.3 18.5 %collective-permute-start.26 = (bf16[256,1536]{1,0:T(8,128)(2,1)}, bf16[256,1536]{1,0:T(8,128)(2,1)}, u32[]{:S(2)}, u32[]{:S(2)}) collective-permute-start(bf16[256,1536]{1,0:T(8,128)(2,1)} %fusion.48), channel_id=1, source_target_pairs={{0,16},{4,12},{8,24},{12,4},{16,0},{20,28},{24,8},{28,20},{1,17},{... | collective-permute-start | bytes 2359304 | tf_op jit(solution)/shard_map/ppermute | solution.py:769
  368.1 158.9 %reduce-scatter.4.cloned.1.call-start = ((), (), s32[]{:S(2)}) async-start(), calls=%async_computation.3 | async-start | bytes 5242880 | tf_op jit(solution)/shard_map/reduce_scatter | solution.py:764
  418.7 188.3 %reduce-scatter.8.cloned.1.call-start = ((), (), s32[]{:S(2)}) async-start(), calls=%async_computation.6 | async-start | bytes 5242880 | tf_op jit(solution)/shard_map/reduce_scatter | solution.py:764
  493.1 3.9 collective-permute-start.28
  494.4 32.7 %collective-permute-start.32 = (bf16[512,1536]{1,0:T(8,128)(2,1)}, bf16[512,1536]{1,0:T(8,128)(2,1)}, u32[]{:S(2)}, u32[]{:S(2)}) collective-permute-start(bf16[512,1536]{1,0:T(8,128)(2,1)} %pad_maximum_fusion.6), channel_id=1, source_target_pairs={{0,8},{4,20},{8,0},{12,28},{16,24},{20,4},{24,16},{28,12},{1,9},{5... | collective-permute-start | bytes 4718600 | tf_op jit(solution)/shard_map/ppermute | solution.py:769
  527.0 193.5 %all-gather.16.cloned.1.call-start = ((), (), s32[]{:S(2)}) async-start(), calls=%async_computation.8 | async-start | bytes 5242880 | tf_op jit(solution)/shard_map/all_gather | solution.py:760
  529.0 12.1 %collective-permute-start.33 = (bf16[256,1536]{1,0:T(8,128)(2,1)S(1)}, bf16[256,1536]{1,0:T(8,128)(2,1)S(1)}, u32[]{:S(2)}, u32[]{:S(2)}) collective-permute-start(bf16[256,1536]{1,0:T(8,128)(2,1)S(1)} %fusion.41), channel_id=1, source_target_pairs={{0,16},{4,12},{8,24},{12,4},{16,0},{20,28},{24,8},{28,20},{1,17},{... | collective-permute-start | bytes 2359304 | tf_op jit(solution)/shard_map/ppermute | solution.py:769
  549.2 39.0 %collective-permute-start.31 = (bf16[704,1024]{1,0:T(8,128)(2,1)}, bf16[704,1024]{1,0:T(8,128)(2,1)S(1)}, u32[]{:S(2)}, u32[]{:S(2)}) collective-permute-start(bf16[704,1024]{1,0:T(8,128)(2,1)} %fusion.34), channel_id=1, source_target_pairs={{0,4},{4,0},{8,12},{12,8},{16,20},{20,16},{24,28},{28,24},{1,5},{5... | collective-permute-start | bytes 4325384 | tf_op jit(solution)/shard_map/ppermute | solution.py:769
  552.0 37.6 %collective-permute-start.30 = (bf16[704,1024]{1,0:T(8,128)(2,1)}, bf16[704,1024]{1,0:T(8,128)(2,1)S(1)}, u32[]{:S(2)}, u32[]{:S(2)}) collective-permute-start(bf16[704,1024]{1,0:T(8,128)(2,1)} %fusion.31), channel_id=1, source_target_pairs={{0,4},{4,0},{8,12},{12,8},{16,20},{20,16},{24,28},{28,24},{1,5},{5... | collective-permute-start | bytes 4325384 | tf_op jit(solution)/shard_map/ppermute | solution.py:769
  555.4 35.8 %collective-permute-start.29 = (bf16[704,1024]{1,0:T(8,128)(2,1)}, bf16[704,1024]{1,0:T(8,128)(2,1)S(1)}, u32[]{:S(2)}, u32[]{:S(2)}) collective-permute-start(bf16[704,1024]{1,0:T(8,128)(2,1)} %fusion.37), channel_id=1, source_target_pairs={{0,4},{4,0},{8,12},{12,8},{16,20},{20,16},{24,28},{28,24},{1,5},{5... | collective-permute-start | bytes 4325384 | tf_op jit(solution)/shard_map/ppermute | solution.py:769
  611.3 162.7 %all-gather.14.cloned.1.call-start = ((), (), s32[]{:S(2)}) async-start(), calls=%async_computation.7 | async-start | bytes 5242880 | tf_op jit(solution)/shard_map/all_gather | solution.py:760
  618.9 2.0 collective-permute-start.40
  620.9 6.3 collective-permute-start.41
  627.3 5.0 collective-permute-start.42
  632.4 25.1 %copy-start.13 = (f32[704,1024]{1,0:T(8,128)S(1)}, f32[704,1024]{1,0:T(8,128)}, u32[]{:S(2)}) copy-start(f32[704,1024]{1,0:T(8,128)} %copy-done.12) | copy-start | bytes 8650756
  632.4 11.7 %collective-permute-start.34 = (bf16[704,512]{1,0:T(8,128)(2,1)}, bf16[704,512]{1,0:T(8,128)(2,1)}, u32[]{:S(2)}, u32[]{:S(2)}) collective-permute-start(bf16[704,512]{1,0:T(8,128)(2,1)} %pad_maximum_fusion.10), channel_id=1, source_target_pairs={{0,8},{4,20},{8,0},{12,28},{16,24},{20,4},{24,16},{28,12},{1,9},{5... | collective-permute-start | bytes 2162696 | tf_op jit(solution)/shard_map/ppermute | solution.py:769
  634.0 23.5 %collective-permute-start.36 = (bf16[704,512]{1,0:T(8,128)(2,1)}, bf16[704,512]{1,0:T(8,128)(2,1)}, u32[]{:S(2)}, u32[]{:S(2)}) collective-permute-start(bf16[704,512]{1,0:T(8,128)(2,1)} %pad_maximum_fusion.11), channel_id=1, source_target_pairs={{0,8},{4,20},{8,0},{12,28},{16,24},{20,4},{24,16},{28,12},{1,9},{5... | collective-permute-start | bytes 2162696 | tf_op jit(solution)/shard_map/ppermute | solution.py:769
  634.6 34.7 %copy-start.11 = (f32[704,1024]{1,0:T(8,128)S(1)}, f32[704,1024]{1,0:T(8,128)}, u32[]{:S(2)}) copy-start(f32[704,1024]{1,0:T(8,128)} %copy-done.10) | copy-start | bytes 8650756
  635.5 33.8 %collective-permute-start.38 = (bf16[704,512]{1,0:T(8,128)(2,1)}, bf16[704,512]{1,0:T(8,128)(2,1)S(1)}, u32[]{:S(2)}, u32[]{:S(2)}) collective-permute-start(bf16[704,512]{1,0:T(8,128)(2,1)} %pad_maximum_fusion.9), channel_id=1, source_target_pairs={{0,8},{4,20},{8,0},{12,28},{16,24},{20,4},{24,16},{28,12},{1,9},{5... | collective-permute-start | bytes 2162696 | tf_op jit(solution)/shard_map/ppermute | solution.py:769
  645.5 26.4 %collective-permute-start.35 = (bf16[704,256]{1,0:T(8,128)(2,1)S(1)}, bf16[704,256]{1,0:T(8,128)(2,1)S(1)}, u32[]{:S(2)}, u32[]{:S(2)}) collective-permute-start(bf16[704,256]{1,0:T(8,128)(2,1)S(1)} %fusion.86), channel_id=1, source_target_pairs={{0,16},{4,12},{8,24},{12,4},{16,0},{20,28},{24,8},{28,20},{1,17},{... | collective-permute-start | bytes 1081352 | tf_op jit(solution)/shard_map/ppermute | solution.py:769
  658.7 14.7 %collective-permute-start.37 = (bf16[704,256]{1,0:T(8,128)(2,1)S(1)}, bf16[704,256]{1,0:T(8,128)(2,1)S(1)}, u32[]{:S(2)}, u32[]{:S(2)}) collective-permute-start(bf16[704,256]{1,0:T(8,128)(2,1)S(1)} %fusion.81), channel_id=1, source_target_pairs={{0,16},{4,12},{8,24},{12,4},{16,0},{20,28},{24,8},{28,20},{1,17},{... | collective-permute-start | bytes 1081352 | tf_op jit(solution)/shard_map/ppermute | solution.py:769
  670.4 25.0 %collective-permute-start.39 = (bf16[704,256]{1,0:T(8,128)(2,1)S(1)}, bf16[704,256]{1,0:T(8,128)(2,1)S(1)}, u32[]{:S(2)}, u32[]{:S(2)}) collective-permute-start(bf16[704,256]{1,0:T(8,128)(2,1)S(1)} %fusion.76), channel_id=1, source_target_pairs={{0,16},{4,12},{8,24},{12,4},{16,0},{20,28},{24,8},{28,20},{1,17},{... | collective-permute-start | bytes 1081352 | tf_op jit(solution)/shard_map/ppermute | solution.py:769
  676.5 17.3 %collective-permute-start.43 = (f32[4,2,256]{2,1,0:T(2,128)S(1)}, f32[4,2,256]{2,1,0:T(2,128)S(1)}, u32[]{:S(2)}, u32[]{:S(2)}) collective-permute-start(f32[4,2,256]{2,1,0:T(2,128)S(1)} %slice.722), channel_id=1, source_target_pairs={{0,4},{4,0},{8,12},{12,8},{16,20},{20,16},{24,28},{28,24},{1,5},{5... | collective-permute-start | bytes 24584 | tf_op jit(solution)/shard_map/ppermute | solution.py:769
  693.8 3.7 collective-permute-start.44
  697.5 11.4 %collective-permute-start.45 = (f32[1,2,256]{2,1,0:T(2,128)S(1)}, f32[1,2,256]{2,1,0:T(2,128)S(1)}, u32[]{:S(2)}, u32[]{:S(2)}) collective-permute-start(f32[1,2,256]{2,1,0:T(2,128)S(1)} %slice_add_fusion.30), channel_id=1, source_target_pairs={{0,16},{4,12},{8,24},{12,4},{16,0},{20,28},{24,8},{28,20},{1,17},{... | collective-permute-start | bytes 6152 | tf_op jit(solution)/shard_map/ppermute | solution.py:769
  698.1 21.8 %copy-start.40 = (f32[2,256]{1,0:T(2,128)S(1)}, f32[2,256]{1,0:T(2,128)}, u32[]{:S(2)}) copy-start(f32[2,256]{1,0:T(2,128)} %param.61) | copy-start | bytes 6148
  698.1 21.8 %copy-start.41 = (f32[2,256]{1,0:T(2,128)S(1)}, f32[2,256]{1,0:T(2,128)}, u32[]{:S(2)}) copy-start(f32[2,256]{1,0:T(2,128)} %param.60) | copy-start | bytes 6148
  (52 other events, 271.4 us)
Sparse Core Ops, SparseCore 0:
  22.8 35.2 all-gather.19
  112.6 115.6 all-gather.17
  283.7 77.0 reduce-scatter.5
  368.2 81.1 all-gather.11
  451.6 75.2 reduce-scatter.3
  529.7 77.2 reduce-scatter.7
  611.5 81.4 all-gather.15
  694.6 79.4 all-gather.13
